TPU v7x, 256 devices: a whole 4x4x8 slice. The times are simulated.
256 devices in a mesh: expert: 128 (over x, z, y), tensor: 2 (over core).
Axes of the slice: x: 4, y: 4, z: 8, core: 2. Of those that a mesh axis runs over, the one named last changes fastest.
Arguments:
- context: bfloat16 [32768, 1664], P('expert', 'tensor'), may hold values from -6 to 6
- out_weight: bfloat16 [1664, 1664], P('tensor'), may hold values from -0.15625 to 0.15625
- residual: bfloat16 [32768, 1664], P(('expert', 'tensor')), may hold values from -6 to 6
- norm_gain: float32 [1664], replicated, may hold values from 0.1 to 1.9
- expert_in: bfloat16 [128, 1664, 2048], P('expert', None, 'tensor'), may hold values from -0.15625 to 0.15625
- expert_out: bfloat16 [128, 2048, 1664], P('expert', 'tensor'), may hold values from -0.0625 to 0.0625
- patch_index: int32 [32, 512], replicated, may hold values from 0 to 32767, as said below
- patch_count: int32 [32], replicated, may hold values from 256 to 512, as said below
- gate_value: float32 [32, 512], replicated, may hold values from 0.2 to 1
- upstream: bfloat16 [32768, 1664], P(('expert', 'tensor')), may hold values from -6 to 6
Outputs:
- layer_out: bfloat16 [32768, 1664], P(('expert', 'tensor'))
- stream_grad: bfloat16 [32768, 1664], P(('expert', 'tensor'))
Inputs may be any that keep to these rules, and one draw needn't show every extreme that they name: `patch_index`: the first patch_count[e] slots of expert e's list hold distinct patch numbers below 32768, the other slots 0. Among the patches of one aligned block of 256 patches, at most 4 are listed by one expert, and some expert lists exactly 4 from every block. `patch_count`: some expert's list is full.
All inputs are finite; a program needn't handle non-finite values.
Results may differ from a plain program's by a relative error of at most 0.0045.
Values may be sent and summed in bfloat16 or wider, within the bound.
No kernel may reach another device: no remote copies, remote signals or barrier semaphores. Data moves between devices by JAX's collectives and lax.ppermute only.
A program may use at most 64 MiB of HBM per device.

v0:
```python
import jax
import jax.numpy as jnp
from jax import lax
from jax.sharding import PartitionSpec as P

SHARDS = 4


def norm_rows(stream, norm_gain):
    center_mean = jnp.mean(stream, axis=-1, keepdims=True)
    centered = stream - center_mean
    variance = jnp.mean(centered * centered, axis=-1, keepdims=True)
    return norm_gain * centered * lax.rsqrt(variance + 1e-06)


def gelu_act(values):
    return jax.nn.gelu(values, approximate=True)


def per_device(
    context,
    out_weight,
    residual,
    norm_gain,
    expert_in,
    expert_out,
    patch_index,
    patch_count,
    gate_value,
    upstream,
):
    tok_dev = context.shape[0]
    model_width = residual.shape[1]
    sources = lax.axis_size("expert")
    my_index = lax.axis_index("expert")
    experts = patch_index.shape[0]
    capacity = patch_index.shape[1]
    send_slots = capacity // sources
    attended = lax.psum_scatter(
        jnp.dot(context, out_weight, preferred_element_type=jnp.float32),
        "tensor",
        scatter_dimension=0,
        tiled=True,
    )
    stream = residual.astype(jnp.float32) + attended
    normed_own = norm_rows(stream, norm_gain).astype(jnp.bfloat16)
    normed = lax.all_gather(normed_own, "tensor", axis=0, tiled=True)
    slot_ids = jnp.arange(capacity)
    listed_live = slot_ids[None, :] < patch_count[:, None]
    local_row = patch_index - my_index * tok_dev
    is_mine = listed_live & (local_row >= 0) & (local_row < tok_dev)
    slot_rank = jnp.cumsum(is_mine.astype(jnp.int32), axis=1) - 1
    picked = is_mine[:, None, :] & (slot_rank[:, None, :] == jnp.arange(send_slots)[None, :, None])
    row_of = jnp.sum(jnp.where(picked, local_row[:, None, :], 0), axis=2).reshape(-1)
    present = jnp.any(picked, axis=2).reshape(-1)
    weight_of = jnp.sum(
        jnp.where(picked, gate_value[:, None, :], jnp.zeros((), jnp.float32)), axis=2
    ).reshape(-1)
    weight_of = jnp.where(present, weight_of, jnp.zeros((), jnp.float32))

    def dispatch(rows_full):
        chosen = jnp.where(present[:, None], rows_full[row_of], jnp.zeros((), jnp.bfloat16))
        chosen = chosen.reshape(experts, send_slots, model_width)
        outgoing = jnp.broadcast_to(chosen[:, None], (experts, SHARDS, send_slots, model_width))
        outgoing = outgoing.reshape(sources, send_slots, model_width)
        gathered = lax.all_to_all(outgoing, "expert", split_axis=0, concat_axis=0, tiled=True)
        return gathered

    def collect(part_out):
        returned = lax.all_to_all(part_out, "expert", split_axis=0, concat_axis=0, tiled=True)
        summed = jnp.sum(
            returned.reshape(experts, SHARDS, send_slots, model_width).astype(jnp.float32), axis=1
        )
        return summed

    def merge_rows(slot_values):
        flat_rows = slot_values.reshape(-1, model_width)
        scattered = (
            jnp.zeros((tok_dev, model_width), jnp.float32)
            .at[row_of]
            .add(weight_of[:, None] * flat_rows)
        )
        return lax.psum_scatter(
            scattered.astype(jnp.bfloat16), "tensor", scatter_dimension=0, tiled=True
        ).astype(jnp.float32)

    weight_in = expert_in[0]
    weight_out = expert_out[0]
    received = dispatch(normed).reshape(-1, model_width)
    pre_act = jnp.dot(received, weight_in, preferred_element_type=jnp.float32)
    hidden = gelu_act(pre_act).astype(jnp.bfloat16)
    part_out = jnp.dot(hidden, weight_out, preferred_element_type=jnp.float32).astype(jnp.bfloat16)
    mixed_rows = merge_rows(collect(part_out.reshape(sources, send_slots, model_width)))
    layer_out = (stream + mixed_rows).astype(jnp.bfloat16)
    down_rows = lax.all_gather(upstream, "tensor", axis=0, tiled=True)
    down_recv = dispatch(down_rows).reshape(-1, model_width)
    hidden_grad = lax.dot_general(
        down_recv, weight_out, (((1,), (1,)), ((), ())), preferred_element_type=jnp.float32
    )
    pre_grad = jax.vjp(gelu_act, pre_act)[1](hidden_grad)[0].astype(jnp.bfloat16)
    input_part = lax.dot_general(
        pre_grad, weight_in, (((1,), (1,)), ((), ())), preferred_element_type=jnp.float32
    )
    input_part = input_part.astype(jnp.bfloat16)
    back_rows = merge_rows(collect(input_part.reshape(sources, send_slots, model_width)))
    pull_back = jax.vjp(lambda values: norm_rows(values, norm_gain), stream)[1]
    stream_grad = (upstream.astype(jnp.float32) + pull_back(back_rows)[0]).astype(jnp.bfloat16)
    return (layer_out, stream_grad)


def solution(mesh):
    return jax.shard_map(
        per_device,
        mesh=mesh,
        in_specs=(
            P("expert", "tensor"),
            P("tensor", None),
            P(("expert", "tensor"), None),
            P(),
            P("expert", None, "tensor"),
            P("expert", "tensor", None),
            P(),
            P(),
            P(),
            P(("expert", "tensor"), None),
        ),
        out_specs=(P(("expert", "tensor"), None), P(("expert", "tensor"), None)),
        check_vma=False,
    )
```

profile of v0, /device:TPU:1, one launch (start us, length us, event | category | flops | bytes accessed | tf_op | source)
XLA Modules:
  0.0 302.0 jit_solution(13166018126139753824)
XLA Ops:
  7.2 4.4 %fusion.58 = f32[256,1664]{1,0:T(8,128)} fusion(bf16[256,832]{0,1:T(8,128)(2,1)} %param.10, bf16[832,1664]{1,0:T(8,128)(2,1)} %param.11), kind=kOutput, calls=%fused_computation.85 | convolution fusion | flops 708837376 | bytes 4898816 | tf_op jit(solution)/shard_map/dot_general | solution.py:40
  15.3 7.2 %all_gather.7 = bf16[256,1664]{1,0:T(8,128)(2,1)} all-gather(bf16[128,1664]{1,0:T(8,128)(2,1)} %param.19), channel_id=1, replica_groups=mesh['expert'=128,'tensor'=2] {'tensor'}, dimensions={0}, use_global_device_ids=true | all-gather | bytes 1277952 | tf_op jit(solution)/shard_map/all_gather | solution.py:95
  22.6 3.3 %gather_fusion.1 = bf16[128,1664]{1,0:T(8,128)(2,1)} fusion(bf16[256,1664]{1,0:T(8,128)(2,1)} %all_gather.7, s32[1024]{0:T(1024)S(1)} %pad_clamp_fusion), kind=kCustom, calls=%fused_computation.1 | custom fusion | bytes 852480 | tf_op jit(solution)/shard_map/gather | solution.py:62
  25.9 1.9 gather.13
  27.8 3.0 reduce-scatter.4.cloned.1.call-done
  33.3 2.5 all_gather.6
  35.9 3.3 %gather_fusion = bf16[128,1664]{1,0:T(8,128)(2,1)} fusion(bf16[256,1664]{1,0:T(8,128)(2,1)} %all_gather.6, s32[1024]{0:T(1024)S(1)} %pad_clamp_fusion), kind=kCustom, calls=%fused_computation | custom fusion | bytes 852480 | tf_op jit(solution)/shard_map/gather | solution.py:62
  39.2 1.9 gather.11
  43.1 54.7 %all_to_all.20 = bf16[128,4,1664]{2,1,0:T(4,128)(2,1)} all-to-all(bf16[128,4,1664]{2,1,0:T(4,128)(2,1)S(1)} %bitcast.43), channel_id=1, replica_groups=mesh['expert'=128,'tensor'=2] {'expert'}, dimensions={0} | all-to-all | bytes 3407872 | tf_op jit(solution)/shard_map/all_to_all | solution.py:66
  99.4 10.6 %all-to-all-start.2 = ((bf16[128,4,1664]{2,1,0:T(4,128)(2,1)}), bf16[128,4,1664]{2,1,0:T(4,128)(2,1)}, u32[]{:S(2)}, u32[]{:S(2)}) async-start(bf16[128,4,1664]{2,1,0:T(4,128)(2,1)} %bitcast.42), calls=%async_computation.4 | async-start | bytes 3407872 | tf_op jit(solution)/shard_map/all_to_all | solution.py:66
  110.1 3.8 %reshape.155 = bf16[512,1664]{1,0:T(8,128)(2,1)} reshape(bf16[128,4,1664]{2,1,0:T(4,128)(2,1)} %all_to_all.20) | data formatting | bytes 3407872 | tf_op jit(solution)/shard_map/reshape | solution.py:89
  113.9 5.9 %fusion.6 = f32[512,1024]{1,0:T(8,128)} fusion(bf16[512,1664]{1,0:T(8,128)(2,1)} %reshape.155, bf16[1,1664,1024]{2,1,0:T(8,128)(2,1)} %param.14), kind=kOutput, calls=%fused_computation.12 | convolution fusion | flops 1744830464 | bytes 7208960 | tf_op jit(solution)/shard_map/dot_general | solution.py:90
  119.8 31.0 %all-to-all-done.2 = bf16[128,4,1664]{2,1,0:T(4,128)(2,1)} async-done(((bf16[128,4,1664]{2,1,0:T(4,128)(2,1)}), bf16[128,4,1664]{2,1,0:T(4,128)(2,1)}, u32[]{:S(2)}, u32[]{:S(2)}) %all-to-all-start.2) | async-done | bytes 1703968 | tf_op jit(solution)/shard_map/all_to_all | solution.py:66
  150.8 3.8 %reshape.159 = bf16[512,1664]{1,0:T(8,128)(2,1)} reshape(bf16[128,4,1664]{2,1,0:T(4,128)(2,1)} %all-to-all-done.2) | data formatting | bytes 3407872 | tf_op jit(solution)/shard_map/reshape | solution.py:96
  154.7 9.0 %fusion.8 = bf16[512,1664]{1,0:T(8,128)(2,1)} fusion(bf16[1,1664,1024]{2,1,0:T(8,128)(2,1)} %param.14, f32[512,1024]{1,0:T(8,128)} %fusion.6, bf16[512,1664]{1,0:T(8,128)(2,1)} %reshape.159, bf16[1,1024,1664]{2,1,0:T(8,128)(2,1)S(1)} %copy-done), kind=kOutput, calls=%fused_computation.16 | convolution fusion | flops 3500998656 | bytes 12320768 | tf_op jit(solution)/shard_map/dot_general | solution.py:101
  163.7 3.9 %reshape.160 = bf16[128,4,1664]{2,1,0:T(4,128)(2,1)} reshape(bf16[512,1664]{1,0:T(8,128)(2,1)} %fusion.8) | data formatting | bytes 3407872 | tf_op jit(solution)/shard_map/reshape | solution.py:105
  167.6 9.6 %all-to-all-start.3 = ((bf16[128,4,1664]{2,1,0:T(4,128)(2,1)}), bf16[128,4,1664]{2,1,0:T(4,128)(2,1)}, u32[]{:S(2)}, u32[]{:S(2)}) async-start(bf16[128,4,1664]{2,1,0:T(4,128)(2,1)} %reshape.160), calls=%async_computation.5 | async-start | bytes 3407872 | tf_op jit(solution)/shard_map/all_to_all | solution.py:70
  177.2 5.3 %fusion.11 = bf16[512,1664]{1,0:T(8,128)(2,1)} fusion(bf16[1,1024,1664]{2,1,0:T(8,128)(2,1)S(1)} %copy-done, f32[512,1024]{1,0:T(8,128)} %fusion.6), kind=kOutput, calls=%fused_computation.17 | convolution fusion | flops 1750401024 | bytes 7208960 | tf_op jit(solution)/shard_map/dot_general | solution.py:92
  182.5 3.9 %reshape.156 = bf16[128,4,1664]{2,1,0:T(4,128)(2,1)} reshape(bf16[512,1664]{1,0:T(8,128)(2,1)} %fusion.11) | data formatting | bytes 3407872 | tf_op jit(solution)/shard_map/reshape | solution.py:93
  186.4 30.9 %all-to-all-done.3 = bf16[128,4,1664]{2,1,0:T(4,128)(2,1)} async-done(((bf16[128,4,1664]{2,1,0:T(4,128)(2,1)}), bf16[128,4,1664]{2,1,0:T(4,128)(2,1)}, u32[]{:S(2)}, u32[]{:S(2)}) %all-to-all-start.3) | async-done | bytes 1703968 | tf_op jit(solution)/shard_map/all_to_all | solution.py:70
  217.3 10.1 %all-to-all-start.1 = ((bf16[128,4,1664]{2,1,0:T(4,128)(2,1)}), bf16[128,4,1664]{2,1,0:T(4,128)(2,1)}, u32[]{:S(2)}, u32[]{:S(2)}) async-start(bf16[128,4,1664]{2,1,0:T(4,128)(2,1)} %reshape.156), calls=%async_computation.2 | async-start | bytes 3407872 | tf_op jit(solution)/shard_map/all_to_all | solution.py:70
  228.7 3.4 %convert_reduce_fusion = f32[32,4,1664]{2,1,0:T(4,128)} fusion(bf16[128,4,1664]{2,1,0:T(4,128)(2,1)} %all-to-all-done.3), kind=kLoop, calls=%fused_computation.4 | loop fusion | flops 1490944 | bytes 2555904 | tf_op jit(solution)/shard_map/reduce_sum | solution.py:71
  232.1 2.4 reshape.161
  234.5 4.0 %scatter_custom_fusion.1 = f32[256,1664]{1,0:T(8,128)} fusion(s32[128]{0:T(128)S(1)} %fusion.43, f32[128,1664]{1,0:T(8,128)} %reshape.161, f32[]{:T(128)} %constant.17.clone.1, f32[128]{0:T(128)S(1)} %select_n.51), kind=kCustom, calls=%fused_computation.36 | custom fusion | flops 425984 | bytes 2556420 | tf_op jit(solution)/shard_map/scatter-add | solution.py:81
  238.5 2.5 convert_element_type.66
  241.0 26.2 %all-to-all-done.1 = bf16[128,4,1664]{2,1,0:T(4,128)(2,1)} async-done(((bf16[128,4,1664]{2,1,0:T(4,128)(2,1)}), bf16[128,4,1664]{2,1,0:T(4,128)(2,1)}, u32[]{:S(2)}, u32[]{:S(2)}) %all-to-all-start.1) | async-done | bytes 1703968 | tf_op jit(solution)/shard_map/all_to_all | solution.py:70
  267.3 3.4 %convert_reduce_fusion.1 = f32[32,4,1664]{2,1,0:T(4,128)} fusion(bf16[128,4,1664]{2,1,0:T(4,128)(2,1)} %all-to-all-done.1), kind=kLoop, calls=%fused_computation.5 | loop fusion | flops 1490944 | bytes 2555904 | tf_op jit(solution)/shard_map/reduce_sum | solution.py:71
  270.7 2.4 reshape.157
  273.0 4.0 %scatter_custom_fusion = f32[256,1664]{1,0:T(8,128)} fusion(s32[128]{0:T(128)S(1)} %fusion.43, f32[128,1664]{1,0:T(8,128)} %reshape.157, f32[]{:T(128)} %constant.17.clone.1, f32[128]{0:T(128)S(1)} %select_n.51), kind=kCustom, calls=%fused_computation.39 | custom fusion | flops 425984 | bytes 2556420 | tf_op jit(solution)/shard_map/scatter-add | solution.py:81
  277.0 2.4 convert_element_type.58
  282.8 9.8 %reduce-scatter.6.cloned.1.call-done = bf16[128,1664]{1,0:T(8,128)(2,1)} async-done(((bf16[256,1664]{1,0:T(8,128)(2,1)}), bf16[128,1664]{1,0:T(8,128)(2,1)}) %reduce-scatter.6.cloned.1.call-update) | async-done | bytes 426000 | tf_op jit(solution)/shard_map/reduce_scatter | solution.py:83
  292.5 2.9 add_convert_fusion
  (47 shorter events, 14.4 us)
Async XLA Ops:
  7.2 147.5 %copy-start = (bf16[1,1024,1664]{2,1,0:T(8,128)(2,1)S(1)}, bf16[1,1024,1664]{2,1,0:T(8,128)(2,1)}, u32[]{:S(2)}) copy-start(bf16[1,1024,1664]{2,1,0:T(8,128)(2,1)} %param.15) | copy-start | bytes 10223620
  7.2 4.5 %copy-start.4 = (s32[32]{0:T(128)S(1)}, s32[32]{0:T(128)}, u32[]{:S(2)}) copy-start(s32[32]{0:T(128)} %param.17) | copy-start | bytes 388
  7.2 4.5 %copy-start.3 = (s32[32,512]{1,0:T(8,128)S(1)}, s32[32,512]{1,0:T(8,128)}, u32[]{:S(2)}) copy-start(s32[32,512]{1,0:T(8,128)} %param.16) | copy-start | bytes 196612
  7.2 23.6 %reduce-scatter.4.cloned.1.call-start = ((), (), s32[]{:S(2)}) async-start(), calls=%async_computation.7 | async-start | bytes 2555904 | tf_op jit(solution)/shard_map/reduce_scatter | solution.py:39
  25.9 7.2 %copy-start.2 = (f32[1664]{0:T(1024)S(1)}, f32[1664]{0:T(1024)}, u32[]{:S(2)}) copy-start(f32[1664]{0:T(1024)} %param.13) | copy-start | bytes 19972
  32.2 0.9 copy-start.1
  99.4 51.4 %all-to-all-start.2 = ((bf16[128,4,1664]{2,1,0:T(4,128)(2,1)}), bf16[128,4,1664]{2,1,0:T(4,128)(2,1)}, u32[]{:S(2)}, u32[]{:S(2)}) async-start(bf16[128,4,1664]{2,1,0:T(4,128)(2,1)} %bitcast.42), calls=%async_computation.4 | async-start | bytes 3407872 | tf_op jit(solution)/shard_map/all_to_all | solution.py:66
  167.6 49.7 %all-to-all-start.3 = ((bf16[128,4,1664]{2,1,0:T(4,128)(2,1)}), bf16[128,4,1664]{2,1,0:T(4,128)(2,1)}, u32[]{:S(2)}, u32[]{:S(2)}) async-start(bf16[128,4,1664]{2,1,0:T(4,128)(2,1)} %reshape.160), calls=%async_computation.5 | async-start | bytes 3407872 | tf_op jit(solution)/shard_map/all_to_all | solution.py:70
  217.3 49.9 %all-to-all-start.1 = ((bf16[128,4,1664]{2,1,0:T(4,128)(2,1)}), bf16[128,4,1664]{2,1,0:T(4,128)(2,1)}, u32[]{:S(2)}, u32[]{:S(2)}) async-start(bf16[128,4,1664]{2,1,0:T(4,128)(2,1)} %reshape.156), calls=%async_computation.2 | async-start | bytes 3407872 | tf_op jit(solution)/shard_map/all_to_all | solution.py:70
  227.5 52.0 %reduce-scatter.8.cloned.1.call-start = ((), (), s32[]{:S(2)}) async-start(), calls=%async_computation.9 | async-start | bytes 1277952 | tf_op jit(solution)/shard_map/reduce_scatter | solution.py:83
  241.0 51.6 %reduce-scatter.6.cloned.1.call-start = ((), (), s32[]{:S(2)}) async-start(), calls=%async_computation.8 | async-start | bytes 1277952 | tf_op jit(solution)/shard_map/reduce_scatter | solution.py:83
Sparse Core Ops, SparseCore 0:
  11.8 18.9 reduce-scatter.3
  241.1 16.5 reduce-scatter.7
  279.6 12.8 reduce-scatter.5
where the time goes:
time: 303 us; the launch traced here: 302 us
  waiting for transfers between devices  101 us (33%)
  blocking collectives  64.5 us (21%)
  local copies, waits for them, and re-layouts  34.2 us (11%)
  other arithmetic  33.4 us (11%)
  starting transfers between devices  30.4 us (10%)
  matrix products  24.6 us (8%)
  between operations  13.9 us (5%)
    all_to_all x2, waiting for transfers between devices, collect(): lax.all_to_all(part_out, 'expert', split_axis=0, concat_axis=0, tiled=True)  57.1 us
    all_to_all x1, blocking collectives, dispatch(): lax.all_to_all(outgoing, 'expert', split_axis=0, concat_axis=0, tiled=True)  54.7 us
    all_to_all x1, waiting for transfers between devices, dispatch(): lax.all_to_all(outgoing, 'expert', split_axis=0, concat_axis=0, tiled=True)  31 us
    all_to_all x2, starting transfers between devices, collect(): lax.all_to_all(part_out, 'expert', split_axis=0, concat_axis=0, tiled=True)  19.7 us
    all_to_all x1, starting transfers between devices, dispatch(): lax.all_to_all(outgoing, 'expert', split_axis=0, concat_axis=0, tiled=True)  10.6 us
    gather x4, local copies, waits for them, and re-layouts, dispatch(): rows_full[row_of]  10.4 us
    reduce_scatter x2, waiting for transfers between devices, merge_rows(): lax.psum_scatter(scattered.astype(jnp.bfloat16), 'tensor', scatter_dimens...  9.8 us
    dot_general x1, matrix products, per_device(): lax.dot_general(pre_grad, weight_in, (((1,), (1,)), ((), ())), preferred_...  9.01 us
  transfers between devices with their start and end apart: 6, of which 5 were waited for; matrix products, arithmetic and copies ran while one was open for 19% of the time, Pallas kernels for 0%

commit v1 on v0

v1 whole, which is shorter than its diff:
```python
import jax
import jax.numpy as jnp
from jax import lax
from jax.sharding import Mesh, PartitionSpec as P

SLOTS = 4
HALF = 2
BF = jnp.bfloat16
F32 = jnp.float32


def norm_rows(stream, norm_gain):
    center_mean = jnp.mean(stream, axis=-1, keepdims=True)
    centered = stream - center_mean
    variance = jnp.mean(centered * centered, axis=-1, keepdims=True)
    return norm_gain * centered * lax.rsqrt(variance + 1e-06)


def gelu_act(values):
    return jax.nn.gelu(values, approximate=True)


def mm(a, b):
    return jnp.dot(a, b, preferred_element_type=F32)


def mm_t(a, b):
    return lax.dot_general(a, b, (((1,), (1,)), ((), ())), preferred_element_type=F32)


def swap_core(x):
    return lax.ppermute(x, "core", [(0, 1), (1, 0)])


def shift_y(x, step):
    size = lax.axis_size("y")
    return lax.ppermute(x, "y", [(i, (i + step) % size) for i in range(size)])


def per_device(
    context,
    out_weight,
    residual,
    norm_gain,
    expert_in,
    expert_out,
    patch_index,
    patch_count,
    gate_value,
    upstream,
):
    own_rows, width = residual.shape
    experts, capacity = patch_index.shape
    core = lax.axis_index("core")
    index = lax.axis_index("xz") * lax.axis_size("y") + lax.axis_index("y")
    first_patch = index * (2 * own_rows)

    with jax.named_scope("routing"):
        local_row = patch_index - first_patch
        listed = jnp.arange(capacity)[None, :] < patch_count[:, None]
        mine = listed & (local_row >= 0) & (local_row < 2 * own_rows)
        upto = (jnp.arange(capacity)[:, None] <= jnp.arange(capacity)[None, :]).astype(BF)
        rank = mm(mine.astype(BF), upto).astype(jnp.int32) - 1
        picked = mine[:, None, :] & (rank[:, None, :] == jnp.arange(SLOTS)[None, :, None])
        row_of = jnp.sum(jnp.where(picked, local_row[:, None, :] + 1, 0), axis=2) - 1
        weight_of = jnp.sum(jnp.where(picked, gate_value[:, None, :], 0.0), axis=2)
        row_keep = jnp.where(core == 0, row_of[:, :HALF], row_of[:, HALF:]).reshape(-1)
        row_send = jnp.where(core == 0, row_of[:, HALF:], row_of[:, :HALF]).reshape(-1)
        weight_keep = jnp.where(core == 0, weight_of[:, :HALF], weight_of[:, HALF:]).reshape(-1)
        weight_send = jnp.where(core == 0, weight_of[:, HALF:], weight_of[:, :HALF]).reshape(-1)
        own_ids = core * own_rows + jnp.arange(own_rows)
        hot_keep = row_keep[:, None] == own_ids[None, :]
        hot_send = row_send[:, None] == own_ids[None, :]
        pick_keep = hot_keep.astype(BF)
        pick_send = hot_send.astype(BF)
        spread = jnp.concatenate(
            [
                jnp.where(hot_keep, weight_keep[:, None], 0.0).T,
                jnp.where(hot_send, weight_send[:, None], 0.0).T,
            ],
            axis=1,
        )
        spread_high = spread.astype(BF)
        spread_low = (spread - spread_high.astype(F32)).astype(BF)

    def dispatch(rows_own):
        theirs = swap_core(mm(pick_send, rows_own).astype(BF))
        chosen = mm(pick_keep, rows_own).astype(BF) + theirs
        chosen = chosen.reshape(experts, HALF, width)
        got = lax.all_to_all(chosen, "xz", split_axis=0, concat_axis=0, tiled=True)
        return got.reshape(experts * HALF, width)

    def gather_y(block):
        half = block.shape[0] // 2
        before = shift_y(block, 1)
        after = shift_y(block, -1)
        far_top = shift_y(before[:half], 1)
        far_bottom = shift_y(after[half:], -1)
        return jnp.concatenate([block, after, far_top, far_bottom, before], axis=0)

    def reduce_y(parts):
        block = parts.shape[0] // 4
        half = block // 2
        own, after, far, before = (parts[i * block : (i + 1) * block] for i in range(4))
        from_before = shift_y(far[:half].astype(BF), 1)
        from_after = shift_y(far[half:].astype(BF), -1)
        after = jnp.concatenate([after[:half] + from_before.astype(F32), after[half:]], axis=0)
        before = jnp.concatenate([before[:half], before[half:] + from_after.astype(F32)], axis=0)
        left = shift_y(after.astype(BF), 1)
        right = shift_y(before.astype(BF), -1)
        return own + left.astype(F32) + right.astype(F32)

    def give_back(keep_part, send_part):
        theirs = swap_core(send_part.astype(BF))
        total = reduce_y(keep_part + theirs.astype(F32)).astype(BF)
        total = total.reshape(experts, HALF, width)
        got = lax.all_to_all(total, "xz", split_axis=0, concat_axis=0, tiled=True)
        got = got.reshape(experts * HALF, width)
        rows = jnp.concatenate([got, swap_core(got)], axis=0)
        return mm(spread_high, rows) + mm(spread_low, rows)

    with jax.named_scope("dispatch_upstream"):
        down_keep = gather_y(dispatch(upstream))
        down_send = swap_core(down_keep)

    with jax.named_scope("attend"):
        context_send = lax.dynamic_slice_in_dim(context, (1 - core) * own_rows, own_rows, 0)
        context_keep = lax.dynamic_slice_in_dim(context, core * own_rows, own_rows, 0)
        theirs = swap_core(mm(context_send, out_weight))
        stream = residual.astype(F32) + (mm(context_keep, out_weight) + theirs)
        normed = norm_rows(stream, norm_gain).astype(BF)

    with jax.named_scope("dispatch_normed"):
        rows_keep = gather_y(dispatch(normed))
        rows_send = swap_core(rows_keep)

    weight_in = expert_in[0]
    weight_out = expert_out[0]
    with jax.named_scope("experts"):
        pre_keep = mm(rows_keep, weight_in)
        pre_send = mm(rows_send, weight_in)
        part_send = mm(gelu_act(pre_send).astype(BF), weight_out)
        part_keep = mm(gelu_act(pre_keep).astype(BF), weight_out)
    with jax.named_scope("return_result"):
        mixed = give_back(part_keep, part_send)
        layer_out = (stream + mixed).astype(BF)

    with jax.named_scope("experts_back"):
        hidden_grad_send = mm_t(down_send, weight_out)
        hidden_grad_keep = mm_t(down_keep, weight_out)
        pre_grad_send = jax.vjp(gelu_act, pre_send)[1](hidden_grad_send)[0].astype(BF)
        pre_grad_keep = jax.vjp(gelu_act, pre_keep)[1](hidden_grad_keep)[0].astype(BF)
        back_send = mm_t(pre_grad_send, weight_in)
        back_keep = mm_t(pre_grad_keep, weight_in)
    with jax.named_scope("return_back"):
        back_rows = give_back(back_keep, back_send)
        pull_back = jax.vjp(lambda values: norm_rows(values, norm_gain), stream)[1]
        stream_grad = (upstream.astype(F32) + pull_back(back_rows)[0]).astype(BF)
    return (layer_out, stream_grad)


def solution(mesh):
    sizes = mesh.devices.shape
    shards = 4
    split = Mesh(
        mesh.devices.reshape(sizes[0] // shards, shards, sizes[1]), ("xz", "y", "core")
    )
    return jax.shard_map(
        per_device,
        mesh=split,
        in_specs=(
            P(("xz", "y"), "core"),
            P("core", None),
            P(("xz", "y", "core"), None),
            P(),
            P(("xz", "y"), None, "core"),
            P(("xz", "y"), "core", None),
            P(),
            P(),
            P(),
            P(("xz", "y", "core"), None),
        ),
        out_specs=(P(("xz", "y", "core"), None), P(("xz", "y", "core"), None)),
        check_vma=False,
    )
```

time: 303 us -> 182 us (0.60)
  waiting for transfers between devices: 101 us -> 23.3 us
  blocking collectives: 64.5 us -> 0 us
  starting transfers between devices: 30.4 us -> 67.9 us
  other arithmetic: 33.4 us -> 12.7 us
  matrix products: 24.6 us -> 41.7 us
  between operations: 13.9 us -> 1.14 us
    all_to_all x3 -> x4, waiting for transfers between devices: 88.2 us -> 11.7 us  [the longest x2 6.48 us: give_back(): got = lax.all_to_all(total, 'xz', split_axis=0, concat_axis=0, tiled=True)]
    all_to_all x1 -> x0, blocking collectives: 54.7 us -> none  [dispatch(): lax.all_to_all(outgoing, 'expert', split_axis=0, concat_axis=0, tiled=True)]
    ppermute x0 -> x25, starting transfers between devices: none -> 38.5 us  [the longest x9 19.9 us: swap_core(): return lax.ppermute(x, 'core', [(0, 1), (1, 0)])]
    dot_general x4 -> x17, matrix products: 24.6 us -> 41.7 us  [the longest x15 29.1 us: mm(): return jnp.dot(a, b, preferred_element_type=F32)]
    reduce_scatter x3 -> x0, waiting for transfers between devices: 12.8 us -> none  [the longest x2 9.8 us: merge_rows(): lax.psum_scatter(scattered.astype(jnp.bfloat16), 'tensor', scatter_dimens...]
    ppermute x0 -> x25, waiting for transfers between devices: none -> 11.7 us  [the longest x16 11.6 us: shift_y(): return lax.ppermute(x, 'y', [(i, (i + step) % size) for i in range(size)])]
    unnamed x10 -> x52, local copies, waits for them, and re-layouts: 0.67 us -> 12.1 us
    reduce_sum x6 -> x2, other arithmetic: 11.8 us -> 1.14 us  [the longest x1 0.97 us: per_device(): weight_of = jnp.sum(jnp.where(picked, gate_value[:, None, :], 0.0), axis=2)]
  transfers between devices with their start and end apart: 6 -> 29, of which waited for: 5 -> 8; matrix products, arithmetic and copies ran while one was open for 19% -> 44% of each run, Pallas kernels for 0% -> 0%
where the time goes in v1:
time: 182 us; the launch traced here: 181 us
  starting transfers between devices  67.9 us (37%)
  matrix products  41.7 us (23%)
  local copies, waits for them, and re-layouts  33.9 us (19%)
  waiting for transfers between devices  23.3 us (13%)
  other arithmetic  12.7 us (7%)
    dot_general x15, matrix products, mm(): return jnp.dot(a, b, preferred_element_type=F32)  29.1 us
    ppermute x9, starting transfers between devices, swap_core(): return lax.ppermute(x, 'core', [(0, 1), (1, 0)])  19.9 us
    ppermute x16, starting transfers between devices, shift_y(): return lax.ppermute(x, 'y', [(i, (i + step) % size) for i in range(size)])  18.6 us
    all_to_all x2, starting transfers between devices, dispatch(): got = lax.all_to_all(chosen, 'xz', split_axis=0, concat_axis=0, tiled=True)  15.3 us
    all_to_all x2, starting transfers between devices, give_back(): got = lax.all_to_all(total, 'xz', split_axis=0, concat_axis=0, tiled=True)  14.1 us
    dot_general x2, matrix products, mm_t(): lax.dot_general(a, b, (((1,), (1,)), ((), ())), preferred_element_type=F32)  12.6 us
    unnamed x52, local copies, waits for them, and re-layouts  12.1 us
    ppermute x16, waiting for transfers between devices, shift_y(): return lax.ppermute(x, 'y', [(i, (i + step) % size) for i in range(size)])  11.6 us
  transfers between devices with their start and end apart: 29, of which 8 were waited for; matrix products, arithmetic and copies ran while one was open for 44% of the time, Pallas kernels for 0%

profile of v1, /device:TPU:1, one launch (start us, length us, event | category | flops | bytes accessed | tf_op | source)
XLA Modules:
  0.0 180.7 jit_solution(6073483844867915358)
XLA Ops:
  0.7 3.6 %fusion.87 = f32[128,1664]{1,0:T(8,128)} fusion(bf16[832,1664]{1,0:T(8,128)(2,1)} %param.11, bf16[256,832]{0,1:T(8,128)(2,1)} %param.10, s32[]{:T(128)S(6)} %select_n.46), kind=kOutput, calls=%fused_computation.102 | convolution fusion | flops 354418688 | bytes 3833860 | tf_op jit(solution)/shard_map/attend/dot_general | solution.py:24
  4.3 3.2 %collective-permute-start = (f32[128,1664]{1,0:T(8,128)}, f32[128,1664]{1,0:T(8,128)}, u32[]{:S(2)}, u32[]{:S(2)}) collective-permute-start(f32[128,1664]{1,0:T(8,128)} %fusion.87), channel_id=1, source_target_pairs={{0,1},{1,0},{2,3},{3,2},{4,5},{5,4},{6,7},{7,6},{8,9},{9,8},{10,11... | collective-permute-start | bytes 2555912 | tf_op jit(solution)/shard_map/attend/ppermute | solution.py:32
  8.3 2.0 %convolution_convert_fusion = bf16[64,1664]{1,0:T(8,128)(2,1)} fusion(bf16[128,1664]{1,0:T(8,128)(2,1)} %param.19, s32[128]{0:T(128)S(1)} %iota_add_fusion, s32[64]{0:T(128)S(1)} %eq.67), kind=kOutput, calls=%fused_computation.24 | convolution fusion | flops 27377664 | bytes 639744 | tf_op jit(solution)/shard_map/dispatch_upstream/dot_general | solution.py:24
  10.5 3.0 %fusion.133 = (f32[128]{0:T(128)S(1)}, f32[128,1664]{1,0:T(8,128)S(1)}) fusion(f32[128,1664]{1,0:T(8,128)} %collective-permute-done, bf16[832,1664]{1,0:T(8,128)(2,1)} %param.11, bf16[256,832]{0,1:T(8,128)(2,1)} %param.10, s32[]{:T(128)S(6)} %select_n.45, bf16[128,1664]{1,0:T(8,128)(2,1)} %param.12), kind=kOutput, calls=%fused_computation.176 | convolution fusion | flops 355270528 | bytes 5112324 | tf_op jit(solution)/shard_map/attend/dot_general | solution.py:24
  16.8 1.9 %fusion.26 = bf16[64,1664]{1,0:T(8,128)(2,1)} fusion(bf16[64,1664]{1,0:T(8,128)(2,1)} %collective-permute-done.13, bf16[128,1664]{1,0:T(8,128)(2,1)S(1)} %copy-done.3, s32[128]{0:T(128)S(1)} %iota_add_fusion, s32[64]{0:T(128)S(1)} %eq.63), kind=kOutput, calls=%fused_computation.29 | convolution fusion | flops 27484160 | bytes 852736 | tf_op jit(solution)/shard_map/dispatch_upstream/dot_general | solution.py:24
  20.4 9.4 %all-to-all-start.2 = ((bf16[32,2,1664]{2,1,0:T(2,128)(2,1)}), bf16[32,2,1664]{2,1,0:T(2,128)(2,1)}, u32[]{:S(2)}, u32[]{:S(2)}) async-start(bf16[32,2,1664]{2,1,0:T(2,128)(2,1)} %reshape.75), calls=%async_computation.2 | async-start | bytes 425984 | tf_op jit(solution)/shard_map/dispatch_upstream/all_to_all | solution.py:90
  30.8 2.0 %fusion.25 = bf16[64,1664]{1,0:T(8,128)(2,1)} fusion(bf16[64,1664]{1,0:T(8,128)(2,1)} %collective-permute-done.1, bf16[128,1664]{1,0:T(8,128)(2,1)} %copy-done.5, s32[128]{0:T(128)S(1)} %iota_add_fusion, s32[64]{0:T(128)S(1)} %eq.63), kind=kOutput, calls=%fused_computation.28 | convolution fusion | flops 27484160 | bytes 852736 | tf_op jit(solution)/shard_map/dispatch_normed/dot_general | solution.py:24
  34.5 5.2 %all-to-all-done.2 = bf16[32,2,1664]{2,1,0:T(2,128)(2,1)} async-done(((bf16[32,2,1664]{2,1,0:T(2,128)(2,1)}), bf16[32,2,1664]{2,1,0:T(2,128)(2,1)}, u32[]{:S(2)}, u32[]{:S(2)}) %all-to-all-start.2) | async-done | bytes 213024 | tf_op jit(solution)/shard_map/dispatch_upstream/all_to_all | solution.py:90
  39.7 5.9 %all-to-all-start = ((bf16[32,2,1664]{2,1,0:T(2,128)(2,1)}), bf16[32,2,1664]{2,1,0:T(2,128)(2,1)}, u32[]{:S(2)}, u32[]{:S(2)}) async-start(bf16[32,2,1664]{2,1,0:T(2,128)(2,1)} %reshape.71), calls=%async_computation | async-start | bytes 425984 | tf_op jit(solution)/shard_map/dispatch_normed/all_to_all | solution.py:90
  48.7 2.7 %collective-permute-start.14 = (bf16[64,1664]{1,0:T(8,128)(2,1)}, bf16[64,1664]{1,0:T(8,128)(2,1)S(1)}, u32[]{:S(2)}, u32[]{:S(2)}) collective-permute-start(bf16[64,1664]{1,0:T(8,128)(2,1)} %reshape.76), channel_id=1, source_target_pairs={{0,6},{2,0},{4,2},{6,4},{1,7},{3,1},{5,3},{7,5},{8,14},{10,8},{12,... | collective-permute-start | bytes 638984 | tf_op jit(solution)/shard_map/dispatch_upstream/ppermute | solution.py:37
  53.1 5.0 %collective-permute-done.15 = bf16[64,1664]{1,0:T(8,128)(2,1)S(1)} collective-permute-done((bf16[64,1664]{1,0:T(8,128)(2,1)}, bf16[64,1664]{1,0:T(8,128)(2,1)S(1)}, u32[]{:S(2)}, u32[]{:S(2)}) %collective-permute-start.15) | collective-permute-done | bytes 213024 | tf_op jit(solution)/shard_map/dispatch_upstream/ppermute | solution.py:37
  60.8 2.7 %collective-permute-start.17 = (bf16[32,1664]{1,0:T(8,128)(2,1)}, bf16[32,1664]{1,0:T(8,128)(2,1)}, u32[]{:S(2)}, u32[]{:S(2)}) collective-permute-start(bf16[32,1664]{1,0:T(8,128)(2,1)} %slice.128), channel_id=1, source_target_pairs={{0,6},{2,0},{4,2},{6,4},{1,7},{3,1},{5,3},{7,5},{8,14},{10,8},{12,... | collective-permute-start | bytes 319496 | tf_op jit(solution)/shard_map/dispatch_upstream/ppermute | solution.py:37
  67.6 3.7 %collective-permute-done.3 = bf16[64,1664]{1,0:T(8,128)(2,1)S(1)} collective-permute-done((bf16[64,1664]{1,0:T(8,128)(2,1)}, bf16[64,1664]{1,0:T(8,128)(2,1)S(1)}, u32[]{:S(2)}, u32[]{:S(2)}) %collective-permute-start.3) | collective-permute-done | bytes 213024 | tf_op jit(solution)/shard_map/dispatch_normed/ppermute | solution.py:37
  72.0 2.4 %collective-permute-start.5 = (bf16[32,1664]{1,0:T(8,128)(2,1)S(1)}, bf16[32,1664]{1,0:T(8,128)(2,1)S(1)}, u32[]{:S(2)}, u32[]{:S(2)}) collective-permute-start(bf16[32,1664]{1,0:T(8,128)(2,1)S(1)} %slice.119), channel_id=1, source_target_pairs={{0,6},{2,0},{4,2},{6,4},{1,7},{3,1},{5,3},{7,5},{8,14},{10,8},{12,... | collective-permute-start | bytes 319496 | tf_op jit(solution)/shard_map/dispatch_normed/ppermute | solution.py:37
  74.4 1.8 collective-permute-done.4
  76.2 6.0 %collective-permute-start.6 = (bf16[256,1664]{1,0:T(8,128)(2,1)S(1)}, bf16[256,1664]{1,0:T(8,128)(2,1)S(1)}, u32[]{:S(2)}, u32[]{:S(2)}) collective-permute-start(bf16[256,1664]{1,0:T(8,128)(2,1)S(1)} %constant_dynamic-update-slice_fusion), channel_id=1, source_target_pairs={{0,1},{1,0},{2,3},{3,2},{4,5},{5,4},{6,7},{7,6},{8,9},{9,8},{10,11... | collective-permute-start | bytes 2555912 | tf_op jit(solution)/shard_map/dispatch_normed/ppermute | solution.py:32
  87.8 3.1 %fusion.12 = f32[256,1024]{1,0:T(8,128)S(1)} fusion(bf16[256,1664]{1,0:T(8,128)(2,1)S(1)} %collective-permute-done.6, bf16[1,1664,1024]{2,1,0:T(8,128)(2,1)} %param.14), kind=kOutput, calls=%fused_computation.12 | convolution fusion | flops 872415232 | bytes 5308416 | tf_op jit(solution)/shard_map/experts/dot_general | solution.py:24
  91.0 2.1 %fusion.19 = bf16[256,1664]{1,0:T(8,128)(2,1)} fusion(bf16[1,1024,1664]{2,1,0:T(8,128)(2,1)S(1)} %copy-done, f32[256,1024]{1,0:T(8,128)S(1)} %fusion.12), kind=kOutput, calls=%fused_computation.17 | convolution fusion | flops 875200512 | bytes 5308416 | tf_op jit(solution)/shard_map/experts/dot_general | solution.py:24
  93.6 2.1 %fusion.14 = f32[256,1024]{1,0:T(8,128)} fusion(bf16[256,1664]{1,0:T(8,128)(2,1)S(1)} %constant_dynamic-update-slice_fusion, bf16[1,1664,1024]{2,1,0:T(8,128)(2,1)S(1)} %copy-done.19), kind=kOutput, calls=%fused_computation.14 | convolution fusion | flops 872415232 | bytes 5308416 | tf_op jit(solution)/shard_map/experts/dot_general | solution.py:24
  95.7 5.8 %fusion.16 = bf16[256,1664]{1,0:T(8,128)(2,1)} fusion(bf16[1,1664,1024]{2,1,0:T(8,128)(2,1)} %param.14, f32[256,1024]{1,0:T(8,128)} %copy-done.20, bf16[256,1664]{1,0:T(8,128)(2,1)} %collective-permute-done.18, bf16[1,1024,1664]{2,1,0:T(8,128)(2,1)S(1)} %copy-done), kind=kOutput, calls=%fused_computation.16 | convolution fusion | flops 1750499328 | bytes 9568256 | tf_op jit(solution)/shard_map/experts_back/dot_general | solution.py:28
  102.0 3.9 %fusion.134 = (bf16[256,1664]{1,0:T(8,128)(2,1)S(1)}, f32[256,1664]{1,0:T(8,128)}) fusion(bf16[256,1664]{1,0:T(8,128)(2,1)} %collective-permute-done.7, bf16[1,1024,1664]{2,1,0:T(8,128)(2,1)S(1)} %copy-done, f32[256,1024]{1,0:T(8,128)} %fusion.14), kind=kOutput, calls=%fused_computation.177 | convolution fusion | flops 876052480 | bytes 7864320 | tf_op jit(solution)/shard_map/experts/dot_general | solution.py:24
  106.6 2.7 %collective-permute-start.10 = (bf16[32,1664]{1,0:T(8,128)(2,1)}, bf16[32,1664]{1,0:T(8,128)(2,1)}, u32[]{:S(2)}, u32[]{:S(2)}) collective-permute-start(bf16[32,1664]{1,0:T(8,128)(2,1)} %get-tuple-element.13), channel_id=1, source_target_pairs={{0,6},{2,0},{4,2},{6,4},{1,7},{3,1},{5,3},{7,5},{8,14},{10,8},{12,... | collective-permute-start | bytes 319496 | tf_op jit(solution)/shard_map/return_result/ppermute | solution.py:37
  109.3 6.8 %fusion.135 = (bf16[256,1664]{1,0:T(8,128)(2,1)}, f32[256,1664]{1,0:T(8,128)}) fusion(bf16[256,1664]{1,0:T(8,128)(2,1)} %collective-permute-done.19, bf16[1,1664,1024]{2,1,0:T(8,128)(2,1)} %param.14, f32[256,1024]{1,0:T(8,128)} %fusion.14, bf16[256,1664]{1,0:T(8,128)(2,1)} %constant_dynamic-update-slice_fusion.7, bf16[1,1024,1664]{2,1,0:T(8,128)(2,1)S(1)} %copy-done), kind=kOutput, calls=%fused_computation.178 | convolution fusion | flops 1751351296 | bytes 12124160 | tf_op jit(solution)/shard_map/experts_back/dot_general | solution.py:28
  117.5 2.7 %collective-permute-start.22 = (bf16[32,1664]{1,0:T(8,128)(2,1)S(1)}, bf16[32,1664]{1,0:T(8,128)(2,1)S(1)}, u32[]{:S(2)}, u32[]{:S(2)}) collective-permute-start(bf16[32,1664]{1,0:T(8,128)(2,1)S(1)} %get-tuple-element.9), channel_id=1, source_target_pairs={{0,6},{2,0},{4,2},{6,4},{1,7},{3,1},{5,3},{7,5},{8,14},{10,8},{12,... | collective-permute-start | bytes 319496 | tf_op jit(solution)/shard_map/return_back/ppermute | solution.py:37
  129.0 1.8 fusion.81
  132.5 9.5 %all-to-all-start.1 = ((bf16[32,2,1664]{2,1,0:T(2,128)(2,1)}), bf16[32,2,1664]{2,1,0:T(2,128)(2,1)}, u32[]{:S(2)}, u32[]{:S(2)}) async-start(bf16[32,2,1664]{2,1,0:T(2,128)(2,1)} %reshape.73), calls=%async_computation.1 | async-start | bytes 425984 | tf_op jit(solution)/shard_map/return_result/all_to_all | solution.py:117
  142.1 1.9 %fusion.79 = bf16[64,1664]{1,0:T(8,128)(2,1)} fusion(f32[256,1664]{1,0:T(8,128)} %get-tuple-element.27, bf16[64,1664]{1,0:T(8,128)(2,1)} %collective-permute-done.23, bf16[64,1664]{1,0:T(8,128)(2,1)} %collective-permute-done.21), kind=kLoop, calls=%fused_computation.82 | loop fusion | flops 532480 | bytes 1064960 | tf_op jit(solution)/shard_map/return_back/convert_element_type | solution.py:115
  145.7 5.8 %all-to-all-done.1 = bf16[32,2,1664]{2,1,0:T(2,128)(2,1)} async-done(((bf16[32,2,1664]{2,1,0:T(2,128)(2,1)}), bf16[32,2,1664]{2,1,0:T(2,128)(2,1)}, u32[]{:S(2)}, u32[]{:S(2)}) %all-to-all-start.1) | async-done | bytes 213024 | tf_op jit(solution)/shard_map/return_result/all_to_all | solution.py:117
  151.5 4.6 %all-to-all-start.3 = ((bf16[32,2,1664]{2,1,0:T(2,128)(2,1)}), bf16[32,2,1664]{2,1,0:T(2,128)(2,1)}, u32[]{:S(2)}, u32[]{:S(2)}) async-start(bf16[32,2,1664]{2,1,0:T(2,128)(2,1)} %reshape.77), calls=%async_computation.3 | async-start | bytes 425984 | tf_op jit(solution)/shard_map/return_back/all_to_all | solution.py:117
  159.2 4.0 %collective-permute-start.12 = (bf16[64,1664]{1,0:T(8,128)(2,1)}, bf16[64,1664]{1,0:T(8,128)(2,1)}, u32[]{:S(2)}, u32[]{:S(2)}) collective-permute-start(bf16[64,1664]{1,0:T(8,128)(2,1)} %reshape.74), channel_id=1, source_target_pairs={{0,1},{1,0},{2,3},{3,2},{4,5},{5,4},{6,7},{7,6},{8,9},{9,8},{10,11... | collective-permute-start | bytes 638984 | tf_op jit(solution)/shard_map/return_result/ppermute | solution.py:32
  167.3 5.1 %collective-permute-start.24 = (bf16[64,1664]{1,0:T(8,128)(2,1)}, bf16[64,1664]{1,0:T(8,128)(2,1)S(1)}, u32[]{:S(2)}, u32[]{:S(2)}) collective-permute-start(bf16[64,1664]{1,0:T(8,128)(2,1)} %reshape.78), channel_id=1, source_target_pairs={{0,1},{1,0},{2,3},{3,2},{4,5},{5,4},{6,7},{7,6},{8,9},{9,8},{10,11... | collective-permute-start | bytes 638984 | tf_op jit(solution)/shard_map/return_back/ppermute | solution.py:32
  176.3 2.4 %fusion.24 = bf16[128,1664]{1,0:T(8,128)(2,1)} fusion(f32[128,1664]{1,0:T(8,128)} %copy-done.1, f32[128,1664]{1,0:T(8,128)S(1)} %fusion.138, bf16[128,1664]{1,0:T(8,128)(2,1)} %constant_dynamic-update-slice_fusion.5, f32[128,64]{1,0:T(8,128)S(1)} %get-tuple-element.21, f32[128,64]{1,0:T(8,128)S(1)} %get-tuple-element.20), kind=kOutput, calls=%fused_computation.23 | convolution fusion | flops 55230464 | bytes 2621440 | tf_op jit(solution)/shard_map/return_result/dot_general | solution.py:24
  (147 shorter events, 55.0 us)
Async XLA Ops:
  0.6 90.3 %copy-start = (bf16[1,1024,1664]{2,1,0:T(8,128)(2,1)S(1)}, bf16[1,1024,1664]{2,1,0:T(8,128)(2,1)}, u32[]{:S(2)}) copy-start(bf16[1,1024,1664]{2,1,0:T(8,128)(2,1)} %param.15) | copy-start | bytes 10223620
  4.3 6.2 %collective-permute-start = (f32[128,1664]{1,0:T(8,128)}, f32[128,1664]{1,0:T(8,128)}, u32[]{:S(2)}, u32[]{:S(2)}) collective-permute-start(f32[128,1664]{1,0:T(8,128)} %fusion.87), channel_id=1, source_target_pairs={{0,1},{1,0},{2,3},{3,2},{4,5},{5,4},{6,7},{7,6},{8,9},{9,8},{10,11... | collective-permute-start | bytes 2555912 | tf_op jit(solution)/shard_map/attend/ppermute | solution.py:32
  10.2 6.6 %collective-permute-start.13 = (bf16[64,1664]{1,0:T(8,128)(2,1)}, bf16[64,1664]{1,0:T(8,128)(2,1)}, u32[]{:S(2)}, u32[]{:S(2)}) collective-permute-start(bf16[64,1664]{1,0:T(8,128)(2,1)} %convolution_convert_fusion), channel_id=1, source_target_pairs={{0,1},{1,0},{2,3},{3,2},{4,5},{5,4},{6,7},{7,6},{8,9},{9,8},{10,11... | collective-permute-start | bytes 638984 | tf_op jit(solution)/shard_map/dispatch_upstream/ppermute | solution.py:32
  13.7 26.0 %copy-start.17 = (f32[128]{0:T(128)}, f32[128]{0:T(128)S(1)}, u32[]{:S(2)}) copy-start(f32[128]{0:T(128)S(1)} %multiply_reduce_fusion.1) | copy-start | bytes 1540
  14.4 25.3 %copy-start.14 = (f32[128]{0:T(128)}, f32[128]{0:T(128)S(1)}, u32[]{:S(2)}) copy-start(f32[128]{0:T(128)S(1)} %fusion.107) | copy-start | bytes 1540
  16.3 14.5 %collective-permute-start.1 = (bf16[64,1664]{1,0:T(8,128)(2,1)}, bf16[64,1664]{1,0:T(8,128)(2,1)}, u32[]{:S(2)}, u32[]{:S(2)}) collective-permute-start(bf16[64,1664]{1,0:T(8,128)(2,1)} %convolution_convert_fusion.2), channel_id=1, source_target_pairs={{0,1},{1,0},{2,3},{3,2},{4,5},{5,4},{6,7},{7,6},{8,9},{9,8},{10,11... | collective-permute-start | bytes 638984 | tf_op jit(solution)/shard_map/dispatch_normed/ppermute | solution.py:32
  20.4 19.3 %all-to-all-start.2 = ((bf16[32,2,1664]{2,1,0:T(2,128)(2,1)}), bf16[32,2,1664]{2,1,0:T(2,128)(2,1)}, u32[]{:S(2)}, u32[]{:S(2)}) async-start(bf16[32,2,1664]{2,1,0:T(2,128)(2,1)} %reshape.75), calls=%async_computation.2 | async-start | bytes 425984 | tf_op jit(solution)/shard_map/dispatch_upstream/all_to_all | solution.py:90
  39.7 23.8 %all-to-all-start = ((bf16[32,2,1664]{2,1,0:T(2,128)(2,1)}), bf16[32,2,1664]{2,1,0:T(2,128)(2,1)}, u32[]{:S(2)}, u32[]{:S(2)}) async-start(bf16[32,2,1664]{2,1,0:T(2,128)(2,1)} %reshape.71), calls=%async_computation | async-start | bytes 425984 | tf_op jit(solution)/shard_map/dispatch_normed/all_to_all | solution.py:90
  48.7 10.8 %collective-permute-start.14 = (bf16[64,1664]{1,0:T(8,128)(2,1)}, bf16[64,1664]{1,0:T(8,128)(2,1)S(1)}, u32[]{:S(2)}, u32[]{:S(2)}) collective-permute-start(bf16[64,1664]{1,0:T(8,128)(2,1)} %reshape.76), channel_id=1, source_target_pairs={{0,6},{2,0},{4,2},{6,4},{1,7},{3,1},{5,3},{7,5},{8,14},{10,8},{12,... | collective-permute-start | bytes 638984 | tf_op jit(solution)/shard_map/dispatch_upstream/ppermute | solution.py:37
  51.4 6.7 %collective-permute-start.15 = (bf16[64,1664]{1,0:T(8,128)(2,1)}, bf16[64,1664]{1,0:T(8,128)(2,1)S(1)}, u32[]{:S(2)}, u32[]{:S(2)}) collective-permute-start(bf16[64,1664]{1,0:T(8,128)(2,1)} %reshape.76), channel_id=1, source_target_pairs={{0,2},{2,4},{4,6},{6,0},{1,3},{3,5},{5,7},{7,1},{8,10},{10,12},{12... | collective-permute-start | bytes 638984 | tf_op jit(solution)/shard_map/dispatch_upstream/ppermute | solution.py:37
  59.5 24.4 %collective-permute-start.16 = (bf16[32,1664]{1,0:T(8,128)(2,1)}, bf16[32,1664]{1,0:T(8,128)(2,1)S(1)}, u32[]{:S(2)}, u32[]{:S(2)}) collective-permute-start(bf16[32,1664]{1,0:T(8,128)(2,1)} %slice.127), channel_id=1, source_target_pairs={{0,2},{2,4},{4,6},{6,0},{1,3},{3,5},{5,7},{7,1},{8,10},{10,12},{12... | collective-permute-start | bytes 319496 | tf_op jit(solution)/shard_map/dispatch_upstream/ppermute | solution.py:37
  60.8 23.8 %collective-permute-start.17 = (bf16[32,1664]{1,0:T(8,128)(2,1)}, bf16[32,1664]{1,0:T(8,128)(2,1)}, u32[]{:S(2)}, u32[]{:S(2)}) collective-permute-start(bf16[32,1664]{1,0:T(8,128)(2,1)} %slice.128), channel_id=1, source_target_pairs={{0,6},{2,0},{4,2},{6,4},{1,7},{3,1},{5,3},{7,5},{8,14},{10,8},{12,... | collective-permute-start | bytes 319496 | tf_op jit(solution)/shard_map/dispatch_upstream/ppermute | solution.py:37
  65.2 6.8 %collective-permute-start.2 = (bf16[64,1664]{1,0:T(8,128)(2,1)}, bf16[64,1664]{1,0:T(8,128)(2,1)S(1)}, u32[]{:S(2)}, u32[]{:S(2)}) collective-permute-start(bf16[64,1664]{1,0:T(8,128)(2,1)} %reshape.72), channel_id=1, source_target_pairs={{0,6},{2,0},{4,2},{6,4},{1,7},{3,1},{5,3},{7,5},{8,14},{10,8},{12,... | collective-permute-start | bytes 638984 | tf_op jit(solution)/shard_map/dispatch_normed/ppermute | solution.py:37
  65.2 6.1 %collective-permute-start.3 = (bf16[64,1664]{1,0:T(8,128)(2,1)}, bf16[64,1664]{1,0:T(8,128)(2,1)S(1)}, u32[]{:S(2)}, u32[]{:S(2)}) collective-permute-start(bf16[64,1664]{1,0:T(8,128)(2,1)} %reshape.72), channel_id=1, source_target_pairs={{0,2},{2,4},{4,6},{6,0},{1,3},{3,5},{5,7},{7,1},{8,10},{10,12},{12... | collective-permute-start | bytes 638984 | tf_op jit(solution)/shard_map/dispatch_normed/ppermute | solution.py:37
  71.3 4.8 %collective-permute-start.4 = (bf16[32,1664]{1,0:T(8,128)(2,1)S(1)}, bf16[32,1664]{1,0:T(8,128)(2,1)S(1)}, u32[]{:S(2)}, u32[]{:S(2)}) collective-permute-start(bf16[32,1664]{1,0:T(8,128)(2,1)S(1)} %slice.118), channel_id=1, source_target_pairs={{0,2},{2,4},{4,6},{6,0},{1,3},{3,5},{5,7},{7,1},{8,10},{10,12},{12... | collective-permute-start | bytes 319496 | tf_op jit(solution)/shard_map/dispatch_normed/ppermute | solution.py:37
  72.0 4.2 %collective-permute-start.5 = (bf16[32,1664]{1,0:T(8,128)(2,1)S(1)}, bf16[32,1664]{1,0:T(8,128)(2,1)S(1)}, u32[]{:S(2)}, u32[]{:S(2)}) collective-permute-start(bf16[32,1664]{1,0:T(8,128)(2,1)S(1)} %slice.119), channel_id=1, source_target_pairs={{0,6},{2,0},{4,2},{6,4},{1,7},{3,1},{5,3},{7,5},{8,14},{10,8},{12,... | collective-permute-start | bytes 319496 | tf_op jit(solution)/shard_map/dispatch_normed/ppermute | solution.py:37
  76.2 11.6 %collective-permute-start.6 = (bf16[256,1664]{1,0:T(8,128)(2,1)S(1)}, bf16[256,1664]{1,0:T(8,128)(2,1)S(1)}, u32[]{:S(2)}, u32[]{:S(2)}) collective-permute-start(bf16[256,1664]{1,0:T(8,128)(2,1)S(1)} %constant_dynamic-update-slice_fusion), channel_id=1, source_target_pairs={{0,1},{1,0},{2,3},{3,2},{4,5},{5,4},{6,7},{7,6},{8,9},{9,8},{10,11... | collective-permute-start | bytes 2555912 | tf_op jit(solution)/shard_map/dispatch_normed/ppermute | solution.py:32
  87.8 7.9 %collective-permute-start.18 = (bf16[256,1664]{1,0:T(8,128)(2,1)}, bf16[256,1664]{1,0:T(8,128)(2,1)}, u32[]{:S(2)}, u32[]{:S(2)}) collective-permute-start(bf16[256,1664]{1,0:T(8,128)(2,1)} %constant_dynamic-update-slice_fusion.7), channel_id=1, source_target_pairs={{0,1},{1,0},{2,3},{3,2},{4,5},{5,4},{6,7},{7,6},{8,9},{9,8},{10,11... | collective-permute-start | bytes 2555912 | tf_op jit(solution)/shard_map/dispatch_upstream/ppermute | solution.py:32
  93.1 8.9 %collective-permute-start.7 = (bf16[256,1664]{1,0:T(8,128)(2,1)}, bf16[256,1664]{1,0:T(8,128)(2,1)}, u32[]{:S(2)}, u32[]{:S(2)}) collective-permute-start(bf16[256,1664]{1,0:T(8,128)(2,1)} %fusion.19), channel_id=1, source_target_pairs={{0,1},{1,0},{2,3},{3,2},{4,5},{5,4},{6,7},{7,6},{8,9},{9,8},{10,11... | collective-permute-start | bytes 2555912 | tf_op jit(solution)/shard_map/return_result/ppermute | solution.py:32
  101.5 7.8 %collective-permute-start.19 = (bf16[256,1664]{1,0:T(8,128)(2,1)}, bf16[256,1664]{1,0:T(8,128)(2,1)}, u32[]{:S(2)}, u32[]{:S(2)}) collective-permute-start(bf16[256,1664]{1,0:T(8,128)(2,1)} %fusion.16), channel_id=1, source_target_pairs={{0,1},{1,0},{2,3},{3,2},{4,5},{5,4},{6,7},{7,6},{8,9},{9,8},{10,11... | collective-permute-start | bytes 2555912 | tf_op jit(solution)/shard_map/return_back/ppermute | solution.py:32
  106.6 13.5 %collective-permute-start.8 = (bf16[32,1664]{1,0:T(8,128)(2,1)}, bf16[32,1664]{1,0:T(8,128)(2,1)}, u32[]{:S(2)}, u32[]{:S(2)}) collective-permute-start(bf16[32,1664]{1,0:T(8,128)(2,1)} %get-tuple-element.12), channel_id=1, source_target_pairs={{0,2},{2,4},{4,6},{6,0},{1,3},{3,5},{5,7},{7,1},{8,10},{10,12},{12... | collective-permute-start | bytes 319496 | tf_op jit(solution)/shard_map/return_result/ppermute | solution.py:37
  106.6 13.5 %collective-permute-start.10 = (bf16[32,1664]{1,0:T(8,128)(2,1)}, bf16[32,1664]{1,0:T(8,128)(2,1)}, u32[]{:S(2)}, u32[]{:S(2)}) collective-permute-start(bf16[32,1664]{1,0:T(8,128)(2,1)} %get-tuple-element.13), channel_id=1, source_target_pairs={{0,6},{2,0},{4,2},{6,4},{1,7},{3,1},{5,3},{7,5},{8,14},{10,8},{12,... | collective-permute-start | bytes 319496 | tf_op jit(solution)/shard_map/return_result/ppermute | solution.py:37
  117.1 6.7 %collective-permute-start.20 = (bf16[32,1664]{1,0:T(8,128)(2,1)S(1)}, bf16[32,1664]{1,0:T(8,128)(2,1)S(1)}, u32[]{:S(2)}, u32[]{:S(2)}) collective-permute-start(bf16[32,1664]{1,0:T(8,128)(2,1)S(1)} %get-tuple-element.8), channel_id=1, source_target_pairs={{0,2},{2,4},{4,6},{6,0},{1,3},{3,5},{5,7},{7,1},{8,10},{10,12},{12... | collective-permute-start | bytes 319496 | tf_op jit(solution)/shard_map/return_back/ppermute | solution.py:37
  117.5 6.4 %collective-permute-start.22 = (bf16[32,1664]{1,0:T(8,128)(2,1)S(1)}, bf16[32,1664]{1,0:T(8,128)(2,1)S(1)}, u32[]{:S(2)}, u32[]{:S(2)}) collective-permute-start(bf16[32,1664]{1,0:T(8,128)(2,1)S(1)} %get-tuple-element.9), channel_id=1, source_target_pairs={{0,6},{2,0},{4,2},{6,4},{1,7},{3,1},{5,3},{7,5},{8,14},{10,8},{12,... | collective-permute-start | bytes 319496 | tf_op jit(solution)/shard_map/return_back/ppermute | solution.py:37
  122.2 5.7 %collective-permute-start.11 = (bf16[64,1664]{1,0:T(8,128)(2,1)S(1)}, bf16[64,1664]{1,0:T(8,128)(2,1)S(1)}, u32[]{:S(2)}, u32[]{:S(2)}) collective-permute-start(bf16[64,1664]{1,0:T(8,128)(2,1)S(1)} %pad_maximum_fusion.1), channel_id=1, source_target_pairs={{0,6},{2,0},{4,2},{6,4},{1,7},{3,1},{5,3},{7,5},{8,14},{10,8},{12,... | collective-permute-start | bytes 638984 | tf_op jit(solution)/shard_map/return_result/ppermute | solution.py:37
  122.4 6.6 %collective-permute-start.9 = (bf16[64,1664]{1,0:T(8,128)(2,1)S(1)}, bf16[64,1664]{1,0:T(8,128)(2,1)S(1)}, u32[]{:S(2)}, u32[]{:S(2)}) collective-permute-start(bf16[64,1664]{1,0:T(8,128)(2,1)S(1)} %pad_maximum_fusion), channel_id=1, source_target_pairs={{0,2},{2,4},{4,6},{6,0},{1,3},{3,5},{5,7},{7,1},{8,10},{10,12},{12... | collective-permute-start | bytes 638984 | tf_op jit(solution)/shard_map/return_result/ppermute | solution.py:37
  125.7 16.3 %collective-permute-start.23 = (bf16[64,1664]{1,0:T(8,128)(2,1)}, bf16[64,1664]{1,0:T(8,128)(2,1)}, u32[]{:S(2)}, u32[]{:S(2)}) collective-permute-start(bf16[64,1664]{1,0:T(8,128)(2,1)} %pad_maximum_fusion.3), channel_id=1, source_target_pairs={{0,6},{2,0},{4,2},{6,4},{1,7},{3,1},{5,3},{7,5},{8,14},{10,8},{12,... | collective-permute-start | bytes 638984 | tf_op jit(solution)/shard_map/return_back/ppermute | solution.py:37
  127.7 14.4 %collective-permute-start.21 = (bf16[64,1664]{1,0:T(8,128)(2,1)}, bf16[64,1664]{1,0:T(8,128)(2,1)}, u32[]{:S(2)}, u32[]{:S(2)}) collective-permute-start(bf16[64,1664]{1,0:T(8,128)(2,1)} %pad_maximum_fusion.2), channel_id=1, source_target_pairs={{0,2},{2,4},{4,6},{6,0},{1,3},{3,5},{5,7},{7,1},{8,10},{10,12},{12... | collective-permute-start | bytes 638984 | tf_op jit(solution)/shard_map/return_back/ppermute | solution.py:37
  132.5 19.0 %all-to-all-start.1 = ((bf16[32,2,1664]{2,1,0:T(2,128)(2,1)}), bf16[32,2,1664]{2,1,0:T(2,128)(2,1)}, u32[]{:S(2)}, u32[]{:S(2)}) async-start(bf16[32,2,1664]{2,1,0:T(2,128)(2,1)} %reshape.73), calls=%async_computation.1 | async-start | bytes 425984 | tf_op jit(solution)/shard_map/return_result/all_to_all | solution.py:117
  151.5 14.1 %all-to-all-start.3 = ((bf16[32,2,1664]{2,1,0:T(2,128)(2,1)}), bf16[32,2,1664]{2,1,0:T(2,128)(2,1)}, u32[]{:S(2)}, u32[]{:S(2)}) async-start(bf16[32,2,1664]{2,1,0:T(2,128)(2,1)} %reshape.77), calls=%async_computation.3 | async-start | bytes 425984 | tf_op jit(solution)/shard_map/return_back/all_to_all | solution.py:117
  159.2 14.1 %collective-permute-start.12 = (bf16[64,1664]{1,0:T(8,128)(2,1)}, bf16[64,1664]{1,0:T(8,128)(2,1)}, u32[]{:S(2)}, u32[]{:S(2)}) collective-permute-start(bf16[64,1664]{1,0:T(8,128)(2,1)} %reshape.74), channel_id=1, source_target_pairs={{0,1},{1,0},{2,3},{3,2},{4,5},{5,4},{6,7},{7,6},{8,9},{9,8},{10,11... | collective-permute-start | bytes 638984 | tf_op jit(solution)/shard_map/return_result/ppermute | solution.py:32
  167.3 11.4 %collective-permute-start.24 = (bf16[64,1664]{1,0:T(8,128)(2,1)}, bf16[64,1664]{1,0:T(8,128)(2,1)S(1)}, u32[]{:S(2)}, u32[]{:S(2)}) collective-permute-start(bf16[64,1664]{1,0:T(8,128)(2,1)} %reshape.78), channel_id=1, source_target_pairs={{0,1},{1,0},{2,3},{3,2},{4,5},{5,4},{6,7},{7,6},{8,9},{9,8},{10,11... | collective-permute-start | bytes 638984 | tf_op jit(solution)/shard_map/return_back/ppermute | solution.py:32
  (18 other events, 106.5 us)

commit v2 on v1

v2 whole, which is shorter than its diff:
```python
import jax
import jax.numpy as jnp
from jax import lax
from jax.experimental import pallas as pl
from jax.experimental.pallas import tpu as pltpu
from jax.sharding import Mesh, PartitionSpec as P

SLOTS = 4
HALF = 2
BF = jnp.bfloat16
F32 = jnp.float32
I32 = jnp.int32
VMEM = pl.BlockSpec(memory_space=pltpu.VMEM)
SMEM = pl.BlockSpec(memory_space=pltpu.SMEM)
WIDE = 896
PACK = 8


def mm(a, b):
    return jnp.dot(a, b, preferred_element_type=F32)


def mm_t(a, b):
    return lax.dot_general(a, b, (((1,), (1,)), ((), ())), preferred_element_type=F32)


def cuts(size, step):
    return [(i, min(i + step, size)) for i in range(0, size, step)]


def iota(shape, dim):
    return lax.broadcasted_iota(I32, shape, dim)


def call(kernel, outs, in_specs, scratch=(), flops=0, moved=0, mib=16):
    return pl.pallas_call(
        kernel,
        out_shape=outs,
        in_specs=in_specs,
        out_specs=jax.tree.map(lambda _: VMEM, outs),
        scratch_shapes=list(scratch),
        compiler_params=pltpu.CompilerParams(vmem_limit_bytes=mib * 2**20),
        cost_estimate=pl.CostEstimate(flops=flops, bytes_accessed=moved, transcendentals=0),
    )


def attend_kernel(ids, context, weight, send, keep):
    core = ids[0]
    rows = send.shape[0]
    for out, at in ((send, 1 - core), (keep, core)):
        block = context[pl.ds(pl.multiple_of(at * rows, rows), rows), :]
        for lo, hi in cuts(out.shape[1], 512):
            out[:, lo:hi] = mm(block, weight[:, lo:hi])


def routing_kernel(ids, index, count, gate, pick_keep, pick_send, merge_high, merge_low):
    core = ids[0]
    experts, capacity = index.shape
    packed = experts * PACK
    own_rows = 128
    local = index[...] - ids[1]
    listed = iota((experts, capacity), 1) < count[...]
    mine = listed & (local >= 0) & (local < 2 * own_rows)
    upto = jnp.where(iota((capacity, capacity), 0) <= iota((capacity, capacity), 1), 1.0, 0.0)
    rank = mm(jnp.where(mine, 1.0, 0.0).astype(BF), upto.astype(BF))
    lane = iota((experts, 128), 1)
    rows = jnp.zeros((experts, 128), F32)
    gates = jnp.zeros((experts, 128), F32)
    shifted = (local + 1).astype(F32)
    for slot in range(SLOTS):
        here = mine & (rank == slot + 1.0)
        row = jnp.sum(jnp.where(here, shifted, 0.0), axis=1, keepdims=True) - 1.0
        rows = jnp.where(lane == slot, row, rows)
        weight = jnp.sum(jnp.where(here, gate[...], 0.0), axis=1, keepdims=True)
        gates = jnp.where(lane == slot, weight, gates)
    rows = rows.astype(BF)
    gate_high = gates.astype(BF)
    gate_low = (gates - gate_high.astype(F32)).astype(BF)
    spread = jnp.where(iota((packed, experts), 0) // PACK == iota((packed, experts), 1), 1.0, 0.0).astype(BF)
    down = mm(spread, rows)
    r_col = iota((packed, 128), 0) % PACK
    lane_id = iota((packed, 128), 1)
    k = iota((packed, 2 * own_rows), 1)
    r_wide = iota((packed, 2 * own_rows), 0) % PACK
    same_stream = (r_wide // 2) % 2 == k // own_rows
    patch = (core * own_rows + k % own_rows).astype(F32)
    for out, side in ((pick_keep, core), (pick_send, 1 - core)):
        slot = 2 * side + r_col % 2
        row = jnp.sum(jnp.where(lane_id == slot, down, 0.0), axis=1, keepdims=True)
        hot = same_stream & (row == patch)
        out[:, : 2 * own_rows] = jnp.where(hot & (r_wide < 4), 1.0, 0.0).astype(BF)
        out[:, 2 * own_rows :] = jnp.where(hot & (r_wide >= 4), 1.0, 0.0).astype(BF)
    along = (((0,), (1,)), ((), ()))
    across = [
        lax.dot_general(part, spread, along, preferred_element_type=F32)
        for part in (rows, gate_high, gate_low)
    ]
    q = iota((128, packed), 1) % PACK
    sub = iota((128, packed), 0)
    own = (core * own_rows + iota((own_rows, packed), 0)).astype(F32)
    for which, side in ((0, core), (1, 1 - core)):
        slot = 2 * side + q % 2
        row, high, low = (
            jnp.sum(jnp.where(sub == slot, part, 0.0), axis=0, keepdims=True) for part in across
        )
        hot = row == own
        for group in range(4):
            here = hot & (q // 2 == group)
            at = (slice(group * own_rows, (group + 1) * own_rows), slice(which * packed, (which + 1) * packed))
            merge_high[at] = jnp.where(here, high, 0.0).astype(BF)
            merge_low[at] = jnp.where(here, low, 0.0).astype(BF)


def statistics(stream):
    mean = jnp.mean(stream, axis=-1, keepdims=True)
    centered = stream - mean
    variance = jnp.mean(centered * centered, axis=-1, keepdims=True)
    return centered, lax.rsqrt(variance + 1e-06)


def norm_kernel(att_keep, att_got, residual, gain, upstream, pick_keep, pick_send, stream, keep, send, both):
    rows, width = residual.shape
    total = residual[...].astype(F32) + (att_keep[...] + att_got[...])
    stream[...] = total
    centered, inverse = statistics(total)
    both[:rows, :] = (gain[...] * centered * inverse).astype(BF)
    both[rows:, :] = upstream[...]
    rest = width - WIDE
    for pick, out in ((pick_send, send), (pick_keep, keep)):
        first, second = pick[:, : 2 * rows], pick[:, 2 * rows :]
        out[:, :rest] = (mm(first, both[:, :rest]) + mm(second, both[:, WIDE:])).astype(BF)
        out[:, rest:] = mm(first, both[:, rest:WIDE]).astype(BF)


def place(packed):
    q = packed
    return (q % 64 // 2) * PACK + q // 64 * 2 + q % 2


def unpack_kernel(got, first, second):
    n = got.shape[0]
    order = jnp.where(place(iota((n, n), 0)) == iota((n, n), 1), 1.0, 0.0).astype(BF)
    flat = mm(order, got[...]).astype(BF)
    quarter = n // 4
    rest = first.shape[1] - WIDE
    for stream, out in enumerate((first, second)):
        out[:, :WIDE] = flat[stream * quarter : (stream + 1) * quarter, :]
        out[:, WIDE:] = flat[(2 + stream) * quarter : (3 + stream) * quarter, :rest]


def pack_kernel(own_r, one_r, two_r, own_b, one_b, two_b, out, flat):
    n = out.shape[0]
    quarter = n // 4
    rest = own_r.shape[1] - WIDE
    flat[2 * quarter :, rest:] = jnp.zeros((2 * quarter, WIDE - rest), BF)
    for stream, (own, one, two) in enumerate(((own_r, one_r, two_r), (own_b, one_b, two_b))):
        total = (own[...] + one[...].astype(F32) + two[...].astype(F32)).astype(BF)
        flat[stream * quarter : (stream + 1) * quarter, :] = total[:, :WIDE]
        flat[(2 + stream) * quarter : (3 + stream) * quarter, :rest] = total[:, WIDE:]
    order = jnp.where(iota((n, n), 0) == place(iota((n, n), 1)), 1.0, 0.0).astype(BF)
    out[...] = mm(order, flat[...]).astype(BF)


def forward_kernel(x0, x1, x2, x3, w1, w2, slope, part, x, hidden):
    block = x0.shape[0]
    for i, ref in enumerate((x0, x1, x2, x3)):
        x[i * block : (i + 1) * block, :] = ref[...]
    for lo, hi in cuts(hidden.shape[1], 256):
        v = mm(x[...], w1[:, lo:hi])
        square = v * v
        t = jnp.tanh(0.7978845608 * v * (1.0 + 0.044715 * square))
        gate = 0.5 + 0.5 * t
        hidden[:, lo:hi] = (v * gate).astype(BF)
        slope[:, lo:hi] = gate + 0.5 * v * (1.0 - t * t) * (0.7978845608 * (1.0 + 0.134145 * square))
    for lo, hi in cuts(part.shape[1], 512):
        part[:, lo:hi] = mm(hidden[...], w2[:, lo:hi]).astype(part.dtype)


def backward_kernel(x0, x1, x2, x3, w1, w2, slope, part, x, grad):
    block = x0.shape[0]
    for i, ref in enumerate((x0, x1, x2, x3)):
        x[i * block : (i + 1) * block, :] = ref[...]
    for lo, hi in cuts(grad.shape[1], 256):
        grad[:, lo:hi] = (mm_t(x[...], w2[lo:hi, :]) * slope[:, lo:hi]).astype(BF)
    for lo, hi in cuts(part.shape[1], 512):
        part[:, lo:hi] = mm_t(grad[...], w1[lo:hi, :]).astype(part.dtype)


def combine_kernel(keep, got, own, one, two, far):
    block = own.shape[0]
    for i, out in enumerate((own, one, two, far)):
        at = slice(i * block, (i + 1) * block)
        out[...] = (keep[at, :] + got[at, :].astype(F32)).astype(out.dtype)


def add_kernel(a, b, out):
    out[...] = (a[...].astype(F32) + b[...].astype(F32)).astype(BF)


def final_kernel(mine, theirs, merge_high, merge_low, stream, gain, upstream, layer_out, stream_grad, back):
    rows, width = stream.shape
    n = mine.shape[0]
    rest = width - WIDE
    total = stream[...]
    centered, inverse = statistics(total)
    x_hat = centered * inverse
    for group in range(4):
        at = slice(group * rows, (group + 1) * rows)
        summed = mm(merge_high[at, :n], mine[...]) + mm(merge_high[at, n:], theirs[...])
        summed += mm(merge_low[at, :n], mine[...]) + mm(merge_low[at, n:], theirs[...])
        cols = slice(0, WIDE) if group < 2 else slice(WIDE, width)
        summed = summed if group < 2 else summed[:, :rest]
        if group % 2 == 0:
            layer_out[:, cols] = (total[:, cols] + summed).astype(BF)
        else:
            back[:, cols] = summed
    scaled = gain[...] * back[...]
    mean = jnp.mean(scaled, axis=-1, keepdims=True)
    along = jnp.mean(scaled * x_hat, axis=-1, keepdims=True)
    pulled = inverse * (scaled - mean - x_hat * along)
    stream_grad[...] = (upstream[...].astype(F32) + pulled).astype(BF)


def per_device(
    context,
    out_weight,
    residual,
    norm_gain,
    expert_in,
    expert_out,
    patch_index,
    patch_count,
    gate_value,
    upstream,
):
    rows, width = residual.shape
    experts, capacity = patch_index.shape
    shards = lax.axis_size("y")
    packed = experts * PACK
    block = experts * HALF
    units = expert_in.shape[2]
    sds = jax.ShapeDtypeStruct
    core = lax.axis_index("core")
    index = lax.axis_index("xz") * shards + lax.axis_index("y")
    ids = jnp.stack([core, index * (2 * rows)]).astype(I32)
    gain = norm_gain.reshape(1, width)

    def swap_core(x):
        return lax.ppermute(x, "core", [(0, 1), (1, 0)])

    def ring(x, way):
        pairs = []
        for y in range(shards):
            for c in range(2):
                step = way if c == 0 else -way
                pairs.append((y * 2 + c, (y + step) % shards * 2 + c))
        return lax.ppermute(x, ("y", "core"), pairs)

    def exchange(x):
        got = lax.all_to_all(
            x.reshape(experts, PACK, WIDE), "xz", split_axis=0, concat_axis=0, tiled=True
        )
        return got.reshape(packed, WIDE)

    with jax.named_scope("attend"):
        att_send, att_keep = call(
            attend_kernel,
            [sds((rows, width), F32)] * 2,
            [SMEM, VMEM, VMEM],
            flops=4 * rows * width * context.shape[1],
            moved=5 * 10**6,
        )(ids, context, out_weight)
        att_got = swap_core(att_send)
    with jax.named_scope("routing"):
        pick_keep, pick_send, merge_high, merge_low = call(
            routing_kernel,
            [sds((packed, 4 * rows), BF)] * 2 + [sds((4 * rows, 2 * packed), BF)] * 2,
            [SMEM] + [VMEM] * 3,
            flops=10**9,
            moved=2 * 10**6,
        )(ids, patch_index, patch_count.reshape(experts, 1), gate_value)
    with jax.named_scope("norm"):
        stream, keep, send = call(
            norm_kernel,
            [sds((rows, width), F32)] + [sds((packed, WIDE), BF)] * 2,
            [VMEM] * 7,
            [pltpu.VMEM((2 * rows, width), BF)],
            flops=10**9,
            moved=3 * 10**6,
        )(att_keep, att_got, residual, gain, upstream, pick_keep, pick_send)
    with jax.named_scope("dispatch"):
        got = exchange(keep + swap_core(send))
        normed_rows, down_rows = call(
            unpack_kernel, [sds((block, width), BF)] * 2, [VMEM], flops=10**8, moved=10**6
        )(got)

    def gather_y(own):
        one = ring(own, 1)
        two = ring(own, -1)
        far = ring(one, 1)
        keeps = [own, one, two, far]
        return keeps, [swap_core(x) for x in keeps]

    def combine(keep_part, send_part):
        return call(
            combine_kernel,
            [sds((block, width), F32)] * 2 + [sds((block, width), BF)] * 2,
            [VMEM] * 2,
            flops=10**6,
            moved=4 * 10**6,
        )(keep_part, swap_core(send_part))

    def reduce_y(parts):
        own, one, two, far = parts
        from_two = ring(two, 1)
        from_far = ring(far, -1)
        one = call(add_kernel, sds((block, width), BF), [VMEM] * 2, flops=10**5, moved=10**6)(one, from_far)
        return own, ring(one, -1), from_two

    weight_in = expert_in[0]
    weight_out = expert_out[0]
    tall = shards * block
    flops = 4 * tall * width * units

    def forward(xs, kind):
        return call(
            forward_kernel,
            [sds((tall, units), F32), sds((tall, width), kind)],
            [VMEM] * 6,
            [pltpu.VMEM((tall, width), BF), pltpu.VMEM((tall, units), BF)],
            flops=flops,
            moved=10**7,
            mib=24,
        )(*xs, weight_in, weight_out)

    def backward(xs, slope, kind):
        return call(
            backward_kernel,
            sds((tall, width), kind),
            [VMEM] * 7,
            [pltpu.VMEM((tall, width), BF), pltpu.VMEM((tall, units), BF)],
            flops=flops,
            moved=10**7,
            mib=24,
        )(*xs, weight_in, weight_out, slope)

    with jax.named_scope("gather_normed"):
        keeps, sends = gather_y(normed_rows)
    with jax.named_scope("gather_down"):
        down_keeps, down_sends = gather_y(down_rows)
    with jax.named_scope("forward"):
        slope_send, part_send = forward(sends, BF)
        slope_keep, part_keep = forward(keeps, F32)
    with jax.named_scope("return_result"):
        result = reduce_y(combine(part_keep, part_send))
    with jax.named_scope("backward"):
        back_send = backward(down_sends, slope_send, BF)
        back_keep = backward(down_keeps, slope_keep, F32)
    with jax.named_scope("return_back"):
        back = reduce_y(combine(back_keep, back_send))
    with jax.named_scope("collect"):
        ready = call(
            pack_kernel,
            sds((packed, WIDE), BF),
            [VMEM] * 6,
            [pltpu.VMEM((packed, WIDE), BF)],
            flops=10**8,
            moved=10**6,
        )(*result, *back)
        mine = exchange(ready)
        theirs = swap_core(mine)
    with jax.named_scope("final"):
        layer_out, stream_grad = call(
            final_kernel,
            [sds((rows, width), BF)] * 2,
            [VMEM] * 7,
            [pltpu.VMEM((rows, width), F32)],
            flops=10**9,
            moved=4 * 10**6,
        )(mine, theirs, merge_high, merge_low, stream, gain, upstream)
    return (layer_out, stream_grad)


def solution(mesh):
    sizes = mesh.devices.shape
    shards = 4
    split = Mesh(
        mesh.devices.reshape(sizes[0] // shards, shards, sizes[1]), ("xz", "y", "core")
    )
    return jax.shard_map(
        per_device,
        mesh=split,
        in_specs=(
            P(("xz", "y"), "core"),
            P("core", None),
            P(("xz", "y", "core"), None),
            P(),
            P(("xz", "y"), None, "core"),
            P(("xz", "y"), "core", None),
            P(),
            P(),
            P(),
            P(("xz", "y", "core"), None),
        ),
        out_specs=(P(("xz", "y", "core"), None), P(("xz", "y", "core"), None)),
        check_vma=False,
    )
```

time: 182 us -> 114 us (0.63)
  matrix products: 41.7 us -> 0 us
  blocking collectives: 0 us -> 38.8 us
  starting transfers between devices: 67.9 us -> 36.2 us
  local copies, waits for them, and re-layouts: 33.9 us -> 4.03 us
  Pallas kernels: 0 us -> 17.3 us
  other arithmetic: 12.7 us -> 0.15 us
  waiting for transfers between devices: 23.3 us -> 16.3 us
    dot_general x17 -> x0, matrix products: 41.7 us -> none  [the longest x15 29.1 us: mm(): return jnp.dot(a, b, preferred_element_type=F32)]
    all_to_all x0 -> x2, blocking collectives: none -> 38.8 us  [exchange(): lax.all_to_all(x.reshape(experts, PACK, WIDE), 'xz', split_axis=0, concat...]
    all_to_all x4 -> x0, starting transfers between devices: 29.4 us -> none  [the longest x2 15.3 us: dispatch(): got = lax.all_to_all(chosen, 'xz', split_axis=0, concat_axis=0, tiled=True)]
    pallas_call x0 -> x14, Pallas kernels: none -> 17.3 us  [the longest x2 5.14 us: forward(): call(forward_kernel, [sds((tall, units), F32), sds((tall, width), kind)],...]
    reshape x8 -> x2, local copies, waits for them, and re-layouts: 13.6 us -> 0.09 us  [the longest x1 0.09 us: per_device(): patch_count.reshape(experts, 1)]
    all_to_all x4 -> x0, waiting for transfers between devices: 11.7 us -> none  [the longest x2 6.48 us: give_back(): got = lax.all_to_all(total, 'xz', split_axis=0, concat_axis=0, tiled=True)]
    ppermute x16 -> x12, starting transfers between devices: 18.6 us -> 10.4 us  [ring(): return lax.ppermute(x, ('y', 'core'), pairs)]
    unnamed x52 -> x19, local copies, waits for them, and re-layouts: 12.1 us -> 3.94 us
  transfers between devices with their start and end apart: 29 -> 25, of which waited for: 8 -> 8; matrix products, arithmetic and copies ran while one was open for 44% -> 0% of each run, Pallas kernels for 0% -> 10%
where the time goes in v2:
time: 114 us
  blocking collectives  38.8 us (34%)
  starting transfers between devices  36.2 us (32%)
  Pallas kernels  17.3 us (15%)
  waiting for transfers between devices  16.3 us (14%)
  local copies, waits for them, and re-layouts  4.03 us (4%)
    all_to_all x2, blocking collectives, exchange(): lax.all_to_all(x.reshape(experts, PACK, WIDE), 'xz', split_axis=0, concat...  38.8 us
    ppermute x13, starting transfers between devices, swap_core(): return lax.ppermute(x, 'core', [(0, 1), (1, 0)])  25.8 us
    ppermute x12, waiting for transfers between devices, ring(): return lax.ppermute(x, ('y', 'core'), pairs)  13.1 us
    ppermute x12, starting transfers between devices, ring(): return lax.ppermute(x, ('y', 'core'), pairs)  10.4 us
    pallas_call x2, Pallas kernels, forward(): call(forward_kernel, [sds((tall, units), F32), sds((tall, width), kind)],...  5.14 us
    pallas_call x2, Pallas kernels, backward(): call(backward_kernel, sds((tall, width), kind), [VMEM] * 7, [pltpu.VMEM((...  4.43 us
    unnamed x19, local copies, waits for them, and re-layouts  3.94 us
    ppermute x13, waiting for transfers between devices, swap_core(): return lax.ppermute(x, 'core', [(0, 1), (1, 0)])  3.26 us
  transfers between devices with their start and end apart: 25, of which 8 were waited for; matrix products, arithmetic and copies ran while one was open for 0% of the time, Pallas kernels for 10%

profile of v2, /device:TPU:1, one launch (start us, length us, event | category | flops | bytes accessed | tf_op | source)
XLA Modules:
  0.0 113.6 jit_solution(3408939438521501840)
XLA Ops:
  0.7 1.3 %copy.12.context = bf16[256,832]{1,0:T(8,128)(2,1)S(1)} copy(bf16[256,832]{0,1:T(8,128)(2,1)} %param.10) | data formatting | bytes 851968 | tf_op args[0]
  2.0 1.8 %copy-done.2 = bf16[832,1664]{1,0:T(8,128)(2,1)S(1)} copy-done((bf16[832,1664]{1,0:T(8,128)(2,1)S(1)}, bf16[832,1664]{1,0:T(8,128)(2,1)}, u32[]{:S(2)}) %copy-start.2) | copy-done | bytes 2768920
  3.8 1.7 %attend.1 = (f32[128,1664]{1,0:T(8,128)S(1)}, f32[128,1664]{1,0:T(8,128)S(1)}) custom-call(s32[2]{0:T(128)S(1)} %pad_add_fusion.ids, bf16[256,832]{1,0:T(8,128)(2,1)S(1)} %copy.12.context, bf16[832,1664]{1,0:T(8,128)(2,1)S(1)} %copy-done.2), custom_call_target="tpu_custom_call" | custom-call | flops 708837376 | bytes 5000000 | tf_op jit(solution)/shard_map/attend/pallas_call | solution.py:266
  5.5 3.3 %collective-permute-start = (f32[128,1664]{1,0:T(8,128)S(1)}, f32[128,1664]{1,0:T(8,128)S(1)}, u32[]{:S(2)}, u32[]{:S(2)}) collective-permute-start(f32[128,1664]{1,0:T(8,128)S(1)} %get-tuple-element.26), channel_id=1, source_target_pairs={{0,1},{1,0},{2,3},{3,2},{4,5},{5,4},{6,7},{7,6},{8,9},{9,8},{10,11... | collective-permute-start | bytes 2555912 | tf_op jit(solution)/shard_map/attend/ppermute | solution.py:249
  9.0 0.8 copy-done.6
  9.8 1.7 %routing.1 = (bf16[256,512]{1,0:T(8,128)(2,1)S(1)}, bf16[256,512]{1,0:T(8,128)(2,1)S(1)}, bf16[512,512]{1,0:T(8,128)(2,1)S(1)}, bf16[512,512]{1,0:T(8,128)(2,1)S(1)}) custom-call(s32[2]{0:T(128)S(1)} %pad_add_fusion.ids, s32[32,512]{1,0:T(8,128)S(1)} %copy-done.5, s32[32,1]{1,0:T(8,128)S(1)} %copy.13.count, f32[32,512]{1,0:T(8,128)S(1)} %copy-done.6), custom_call_target="tpu_custom_call" | custom-call | flops 1000000000 | bytes 2000000 | tf_op jit(solution)/shard_map/routing/pallas_call | solution.py:275
  11.5 1.0 norm.1
  12.6 1.8 %collective-permute-done.1 = bf16[256,896]{1,0:T(8,128)(2,1)S(1)} collective-permute-done((bf16[256,896]{1,0:T(8,128)(2,1)S(1)}, bf16[256,896]{1,0:T(8,128)(2,1)S(1)}, u32[]{:S(2)}, u32[]{:S(2)}) %collective-permute-start.1) | collective-permute-done | bytes 458784 | tf_op jit(solution)/shard_map/dispatch/ppermute | solution.py:249
  14.5 22.2 %all_to_all.10 = bf16[32,8,896]{2,1,0:T(8,128)(2,1)S(1)} all-to-all(bf16[32,8,896]{2,1,0:T(8,128)(2,1)S(1)} %add_bitcast_fusion), channel_id=1, replica_groups=mesh['xz'=32,'y'=4,'core'=2] {'xz'}, dimensions={0} | all-to-all | bytes 917504 | tf_op jit(solution)/shard_map/dispatch/all_to_all | solution.py:260
  37.0 2.8 %collective-permute-start.2 = (bf16[64,1664]{1,0:T(8,128)(2,1)S(1)}, bf16[64,1664]{1,0:T(8,128)(2,1)S(1)}, u32[]{:S(2)}, u32[]{:S(2)}) collective-permute-start(bf16[64,1664]{1,0:T(8,128)(2,1)S(1)} %get-tuple-element.31.x0), channel_id=1, source_target_pairs={{0,2},{1,7},{2,4},{3,1},{4,6},{5,3},{6,0},{7,5},{8,10},{9,15},{10,... | collective-permute-start | bytes 638984 | tf_op jit(solution)/shard_map/gather_normed/ppermute | solution.py:257
  39.8 3.8 %collective-permute-start.5 = (bf16[64,1664]{1,0:T(8,128)(2,1)S(1)}, bf16[64,1664]{1,0:T(8,128)(2,1)S(1)}, u32[]{:S(2)}, u32[]{:S(2)}) collective-permute-start(bf16[64,1664]{1,0:T(8,128)(2,1)S(1)} %get-tuple-element.31.x0), channel_id=1, source_target_pairs={{0,1},{1,0},{2,3},{3,2},{4,5},{5,4},{6,7},{7,6},{8,9},{9,8},{10,11... | collective-permute-start | bytes 638984 | tf_op jit(solution)/shard_map/gather_normed/ppermute | solution.py:249
  43.6 1.5 %collective-permute-start.13 = (bf16[64,1664]{1,0:T(8,128)(2,1)S(1)}, bf16[64,1664]{1,0:T(8,128)(2,1)S(1)}, u32[]{:S(2)}, u32[]{:S(2)}) collective-permute-start(bf16[64,1664]{1,0:T(8,128)(2,1)S(1)} %get-tuple-element.38.x0), channel_id=1, source_target_pairs={{0,2},{1,7},{2,4},{3,1},{4,6},{5,3},{6,0},{7,5},{8,10},{9,15},{10,... | collective-permute-start | bytes 638984 | tf_op jit(solution)/shard_map/gather_down/ppermute | solution.py:257
  45.7 0.9 collective-permute-start.14
  47.2 4.7 %collective-permute-start.6 = (bf16[64,1664]{1,0:T(8,128)(2,1)S(1)}, bf16[64,1664]{1,0:T(8,128)(2,1)S(1)}, u32[]{:S(2)}, u32[]{:S(2)}) collective-permute-start(bf16[64,1664]{1,0:T(8,128)(2,1)S(1)} %collective-permute-done.2.x1), channel_id=1, source_target_pairs={{0,1},{1,0},{2,3},{3,2},{4,5},{5,4},{6,7},{7,6},{8,9},{9,8},{10,11... | collective-permute-start | bytes 638984 | tf_op jit(solution)/shard_map/gather_normed/ppermute | solution.py:249
  52.0 3.7 %collective-permute-start.8 = (bf16[64,1664]{1,0:T(8,128)(2,1)S(1)}, bf16[64,1664]{1,0:T(8,128)(2,1)S(1)}, u32[]{:S(2)}, u32[]{:S(2)}) collective-permute-start(bf16[64,1664]{1,0:T(8,128)(2,1)S(1)} %collective-permute-done.4.x3), channel_id=1, source_target_pairs={{0,1},{1,0},{2,3},{3,2},{4,5},{5,4},{6,7},{7,6},{8,9},{9,8},{10,11... | collective-permute-start | bytes 638984 | tf_op jit(solution)/shard_map/gather_normed/ppermute | solution.py:249
  55.7 1.8 %collective-permute-start.16 = (bf16[64,1664]{1,0:T(8,128)(2,1)S(1)}, bf16[64,1664]{1,0:T(8,128)(2,1)S(1)}, u32[]{:S(2)}, u32[]{:S(2)}) collective-permute-start(bf16[64,1664]{1,0:T(8,128)(2,1)S(1)} %get-tuple-element.38.x0), channel_id=1, source_target_pairs={{0,1},{1,0},{2,3},{3,2},{4,5},{5,4},{6,7},{7,6},{8,9},{9,8},{10,11... | collective-permute-start | bytes 638984 | tf_op jit(solution)/shard_map/gather_down/ppermute | solution.py:249
  58.0 1.5 %collective-permute-start.19 = (bf16[64,1664]{1,0:T(8,128)(2,1)S(1)}, bf16[64,1664]{1,0:T(8,128)(2,1)S(1)}, u32[]{:S(2)}, u32[]{:S(2)}) collective-permute-start(bf16[64,1664]{1,0:T(8,128)(2,1)S(1)} %collective-permute-done.15.x3), channel_id=1, source_target_pairs={{0,1},{1,0},{2,3},{3,2},{4,5},{5,4},{6,7},{7,6},{8,9},{9,8},{10,11... | collective-permute-start | bytes 638984 | tf_op jit(solution)/shard_map/gather_down/ppermute | solution.py:249
  59.5 2.6 %forward.3 = (f32[256,1024]{1,0:T(8,128)S(1)}, bf16[256,1664]{1,0:T(8,128)(2,1)S(1)}) custom-call(bf16[64,1664]{1,0:T(8,128)(2,1)S(1)} %collective-permute-done.5.x0, bf16[64,1664]{1,0:T(8,128)(2,1)S(1)} %collective-permute-done.6.x1, bf16[64,1664]{1,0:T(8,128)(2,1)S(1)} %collective-permute-done.7.x2, bf16[64,1664]{1,0:T(8,128)(2,1)S(1)} %collective-permute-done.8.x3, ...), custom_call_target="tpu_custom_call" | custom-call | flops 1744830464 | bytes 10000000 | tf_op jit(solution)/shard_map/forward/pallas_call | solution.py:326
  62.2 2.2 %backward.3 = bf16[256,1664]{1,0:T(8,128)(2,1)S(1)} custom-call(bf16[64,1664]{1,0:T(8,128)(2,1)S(1)} %collective-permute-done.16.x0, bf16[64,1664]{1,0:T(8,128)(2,1)S(1)} %collective-permute-done.17.x1, bf16[64,1664]{1,0:T(8,128)(2,1)S(1)} %collective-permute-done.18.x2, bf16[64,1664]{1,0:T(8,128)(2,1)S(1)} %collective-permute-done.19.x3, ...), custom_call_target="tpu_custom_call" | custom-call | flops 1744830464 | bytes 10000000 | tf_op jit(solution)/shard_map/backward/pallas_call | solution.py:337
  65.0 2.6 %forward.2 = (f32[256,1024]{1,0:T(8,128)S(1)}, f32[256,1664]{1,0:T(8,128)S(1)}) custom-call(bf16[64,1664]{1,0:T(8,128)(2,1)S(1)} %get-tuple-element.31.x0, bf16[64,1664]{1,0:T(8,128)(2,1)S(1)} %collective-permute-done.2.x1, bf16[64,1664]{1,0:T(8,128)(2,1)S(1)} %collective-permute-done.3.x2, bf16[64,1664]{1,0:T(8,128)(2,1)S(1)} %collective-permute-done.4.x3, ...), custom_call_target="tpu_custom_call" | custom-call | flops 1744830464 | bytes 10000000 | tf_op jit(solution)/shard_map/forward/pallas_call | solution.py:326
  67.6 2.2 %backward.2.keep = f32[256,1664]{1,0:T(8,128)S(1)} custom-call(bf16[64,1664]{1,0:T(8,128)(2,1)S(1)} %get-tuple-element.38.x0, bf16[64,1664]{1,0:T(8,128)(2,1)S(1)} %collective-permute-done.13.x1, bf16[64,1664]{1,0:T(8,128)(2,1)S(1)} %collective-permute-done.14.x2, bf16[64,1664]{1,0:T(8,128)(2,1)S(1)} %collective-permute-done.15.x3, ...), custom_call_target="tpu_custom_call" | custom-call | flops 1744830464 | bytes 10000000 | tf_op jit(solution)/shard_map/backward/pallas_call | solution.py:337
  70.5 2.7 %collective-permute-start.12 = (bf16[64,1664]{1,0:T(8,128)(2,1)S(1)}, bf16[64,1664]{1,0:T(8,128)(2,1)S(1)}, u32[]{:S(2)}, u32[]{:S(2)}) collective-permute-start(bf16[64,1664]{1,0:T(8,128)(2,1)S(1)} %get-tuple-element.37), channel_id=1, source_target_pairs={{0,2},{1,7},{2,4},{3,1},{4,6},{5,3},{6,0},{7,5},{8,10},{9,15},{10,... | collective-permute-start | bytes 638984 | tf_op jit(solution)/shard_map/return_result/ppermute | solution.py:257
  73.2 1.4 %collective-permute-start.23 = (bf16[64,1664]{1,0:T(8,128)(2,1)S(1)}, bf16[64,1664]{1,0:T(8,128)(2,1)S(1)}, u32[]{:S(2)}, u32[]{:S(2)}) collective-permute-start(bf16[64,1664]{1,0:T(8,128)(2,1)S(1)} %get-tuple-element.44), channel_id=1, source_target_pairs={{0,2},{1,7},{2,4},{3,1},{4,6},{5,3},{6,0},{7,5},{8,10},{9,15},{10,... | collective-permute-start | bytes 638984 | tf_op jit(solution)/shard_map/return_back/ppermute | solution.py:257
  74.6 1.3 %collective-permute-done.10.b = bf16[64,1664]{1,0:T(8,128)(2,1)S(1)} collective-permute-done((bf16[64,1664]{1,0:T(8,128)(2,1)S(1)}, bf16[64,1664]{1,0:T(8,128)(2,1)S(1)}, u32[]{:S(2)}, u32[]{:S(2)}) %collective-permute-start.10) | collective-permute-done | bytes 213024 | tf_op jit(solution)/shard_map/return_result/ppermute | solution.py:257
  76.1 3.2 %collective-permute-done.21.b = bf16[64,1664]{1,0:T(8,128)(2,1)S(1)} collective-permute-done((bf16[64,1664]{1,0:T(8,128)(2,1)S(1)}, bf16[64,1664]{1,0:T(8,128)(2,1)S(1)}, u32[]{:S(2)}, u32[]{:S(2)}) %collective-permute-start.21) | collective-permute-done | bytes 213024 | tf_op jit(solution)/shard_map/return_back/ppermute | solution.py:257
  79.4 3.8 %collective-permute-done.23.two_b = bf16[64,1664]{1,0:T(8,128)(2,1)S(1)} collective-permute-done((bf16[64,1664]{1,0:T(8,128)(2,1)S(1)}, bf16[64,1664]{1,0:T(8,128)(2,1)S(1)}, u32[]{:S(2)}, u32[]{:S(2)}) %collective-permute-start.23) | collective-permute-done | bytes 213024 | tf_op jit(solution)/shard_map/return_back/ppermute | solution.py:257
  83.3 1.3 %collective-permute-done.11.one_r = bf16[64,1664]{1,0:T(8,128)(2,1)S(1)} collective-permute-done((bf16[64,1664]{1,0:T(8,128)(2,1)S(1)}, bf16[64,1664]{1,0:T(8,128)(2,1)S(1)}, u32[]{:S(2)}, u32[]{:S(2)}) %collective-permute-start.11) | collective-permute-done | bytes 213024 | tf_op jit(solution)/shard_map/return_result/ppermute | solution.py:257
  84.6 2.7 %collective-permute-done.22.one_b = bf16[64,1664]{1,0:T(8,128)(2,1)S(1)} collective-permute-done((bf16[64,1664]{1,0:T(8,128)(2,1)S(1)}, bf16[64,1664]{1,0:T(8,128)(2,1)S(1)}, u32[]{:S(2)}, u32[]{:S(2)}) %collective-permute-start.22) | collective-permute-done | bytes 213024 | tf_op jit(solution)/shard_map/return_back/ppermute | solution.py:257
  87.7 16.6 %all_to_all.11 = bf16[32,8,896]{2,1,0:T(8,128)(2,1)S(1)} all-to-all(bf16[32,8,896]{2,1,0:T(8,128)(2,1)S(1)} %bitcast.18), channel_id=1, replica_groups=mesh['xz'=32,'y'=4,'core'=2] {'xz'}, dimensions={0} | all-to-all | bytes 917504 | tf_op jit(solution)/shard_map/collect/all_to_all | solution.py:260
  104.3 5.6 %collective-permute-start.24 = (bf16[256,896]{1,0:T(8,128)(2,1)S(1)}, bf16[256,896]{1,0:T(8,128)(2,1)S(1)}, u32[]{:S(2)}, u32[]{:S(2)}) collective-permute-start(bf16[256,896]{1,0:T(8,128)(2,1)S(1)} %bitcast.20), channel_id=1, source_target_pairs={{0,1},{1,0},{2,3},{3,2},{4,5},{5,4},{6,7},{7,6},{8,9},{9,8},{10,11... | collective-permute-start | bytes 1376264 | tf_op jit(solution)/shard_map/collect/ppermute | solution.py:249
  109.9 1.4 %collective-permute-done.24.theirs = bf16[256,896]{1,0:T(8,128)(2,1)S(1)} collective-permute-done((bf16[256,896]{1,0:T(8,128)(2,1)S(1)}, bf16[256,896]{1,0:T(8,128)(2,1)S(1)}, u32[]{:S(2)}, u32[]{:S(2)}) %collective-permute-start.24) | collective-permute-done | bytes 458784 | tf_op jit(solution)/shard_map/collect/ppermute | solution.py:249
  111.3 2.3 %final.1 = (bf16[128,1664]{1,0:T(8,128)(2,1)}, bf16[128,1664]{1,0:T(8,128)(2,1)}) custom-call(bf16[256,896]{1,0:T(8,128)(2,1)S(1)} %bitcast.21, bf16[256,896]{1,0:T(8,128)(2,1)S(1)} %collective-permute-done.24.theirs, bf16[512,512]{1,0:T(8,128)(2,1)S(1)} %get-tuple-element.45.merge_high, bf16[512,512]{1,0:T(8,128)(2,1)S(1)} %get-tuple-element.46.merge_low, ...), custom_call_target="tpu_custom_call" | custom-call | flops 1000000000 | bytes 4000000 | tf_op jit(solution)/shard_map/final/pallas_call | solution.py:373
  (57 shorter events, 4.5 us)
Async XLA Ops:
  0.6 8.2 %copy-start.7 = (f32[1664]{0:T(1024)S(1)}, f32[1664]{0:T(1024)}, u32[]{:S(2)}) copy-start(f32[1664]{0:T(1024)} %param.13) | copy-start | bytes 19972
  0.6 8.2 %copy-start.8 = (s32[32]{0:T(128)S(1)}, s32[32]{0:T(128)}, u32[]{:S(2)}) copy-start(s32[32]{0:T(128)} %param.17) | copy-start | bytes 388
  0.7 8.3 %copy-start.5 = (s32[32,512]{1,0:T(8,128)S(1)}, s32[32,512]{1,0:T(8,128)}, u32[]{:S(2)}) copy-start(s32[32,512]{1,0:T(8,128)} %index.1) | copy-start | bytes 196612
  3.8 7.7 %copy-start.3 = (bf16[128,1664]{1,0:T(8,128)(2,1)S(1)}, bf16[128,1664]{1,0:T(8,128)(2,1)}, u32[]{:S(2)}) copy-start(bf16[128,1664]{1,0:T(8,128)(2,1)} %residual.1) | copy-start | bytes 1277956
  5.5 6.0 %copy-start.4 = (bf16[128,1664]{1,0:T(8,128)(2,1)S(1)}, bf16[128,1664]{1,0:T(8,128)(2,1)}, u32[]{:S(2)}) copy-start(bf16[128,1664]{1,0:T(8,128)(2,1)} %upstream.3) | copy-start | bytes 1277956
  5.5 6.0 %collective-permute-start = (f32[128,1664]{1,0:T(8,128)S(1)}, f32[128,1664]{1,0:T(8,128)S(1)}, u32[]{:S(2)}, u32[]{:S(2)}) collective-permute-start(f32[128,1664]{1,0:T(8,128)S(1)} %get-tuple-element.26), channel_id=1, source_target_pairs={{0,1},{1,0},{2,3},{3,2},{4,5},{5,4},{6,7},{7,6},{8,9},{9,8},{10,11... | collective-permute-start | bytes 2555912 | tf_op jit(solution)/shard_map/attend/ppermute | solution.py:249
  9.8 49.7 %copy-start.1 = (bf16[1,1024,1664]{2,1,0:T(8,128)(2,1)S(1)}, bf16[1,1024,1664]{2,1,0:T(8,128)(2,1)}, u32[]{:S(2)}) copy-start(bf16[1,1024,1664]{2,1,0:T(8,128)(2,1)} %param.15) | copy-start | bytes 10223620
  11.5 48.0 %copy-start = (bf16[1,1664,1024]{2,1,0:T(8,128)(2,1)S(1)}, bf16[1,1664,1024]{2,1,0:T(8,128)(2,1)}, u32[]{:S(2)}) copy-start(bf16[1,1664,1024]{2,1,0:T(8,128)(2,1)} %param.14) | copy-start | bytes 10223620
  12.5 1.9 %collective-permute-start.1 = (bf16[256,896]{1,0:T(8,128)(2,1)S(1)}, bf16[256,896]{1,0:T(8,128)(2,1)S(1)}, u32[]{:S(2)}, u32[]{:S(2)}) collective-permute-start(bf16[256,896]{1,0:T(8,128)(2,1)S(1)} %get-tuple-element.30), channel_id=1, source_target_pairs={{0,1},{1,0},{2,3},{3,2},{4,5},{5,4},{6,7},{7,6},{8,9},{9,8},{10,11... | collective-permute-start | bytes 1376264 | tf_op jit(solution)/shard_map/dispatch/ppermute | solution.py:249
  37.0 8.2 %collective-permute-start.2 = (bf16[64,1664]{1,0:T(8,128)(2,1)S(1)}, bf16[64,1664]{1,0:T(8,128)(2,1)S(1)}, u32[]{:S(2)}, u32[]{:S(2)}) collective-permute-start(bf16[64,1664]{1,0:T(8,128)(2,1)S(1)} %get-tuple-element.31.x0), channel_id=1, source_target_pairs={{0,2},{1,7},{2,4},{3,1},{4,6},{5,3},{6,0},{7,5},{8,10},{9,15},{10,... | collective-permute-start | bytes 638984 | tf_op jit(solution)/shard_map/gather_normed/ppermute | solution.py:257
  39.8 7.4 %collective-permute-start.3 = (bf16[64,1664]{1,0:T(8,128)(2,1)S(1)}, bf16[64,1664]{1,0:T(8,128)(2,1)S(1)}, u32[]{:S(2)}, u32[]{:S(2)}) collective-permute-start(bf16[64,1664]{1,0:T(8,128)(2,1)S(1)} %get-tuple-element.31.x0), channel_id=1, source_target_pairs={{0,6},{1,3},{2,0},{3,5},{4,2},{5,7},{6,4},{7,1},{8,14},{9,11},{10,... | collective-permute-start | bytes 638984 | tf_op jit(solution)/shard_map/gather_normed/ppermute | solution.py:257
  39.8 12.1 %collective-permute-start.5 = (bf16[64,1664]{1,0:T(8,128)(2,1)S(1)}, bf16[64,1664]{1,0:T(8,128)(2,1)S(1)}, u32[]{:S(2)}, u32[]{:S(2)}) collective-permute-start(bf16[64,1664]{1,0:T(8,128)(2,1)S(1)} %get-tuple-element.31.x0), channel_id=1, source_target_pairs={{0,1},{1,0},{2,3},{3,2},{4,5},{5,4},{6,7},{7,6},{8,9},{9,8},{10,11... | collective-permute-start | bytes 638984 | tf_op jit(solution)/shard_map/gather_normed/ppermute | solution.py:249
  43.6 8.4 %collective-permute-start.13 = (bf16[64,1664]{1,0:T(8,128)(2,1)S(1)}, bf16[64,1664]{1,0:T(8,128)(2,1)S(1)}, u32[]{:S(2)}, u32[]{:S(2)}) collective-permute-start(bf16[64,1664]{1,0:T(8,128)(2,1)S(1)} %get-tuple-element.38.x0), channel_id=1, source_target_pairs={{0,2},{1,7},{2,4},{3,1},{4,6},{5,3},{6,0},{7,5},{8,10},{9,15},{10,... | collective-permute-start | bytes 638984 | tf_op jit(solution)/shard_map/gather_down/ppermute | solution.py:257
  45.1 6.9 %collective-permute-start.4 = (bf16[64,1664]{1,0:T(8,128)(2,1)S(1)}, bf16[64,1664]{1,0:T(8,128)(2,1)S(1)}, u32[]{:S(2)}, u32[]{:S(2)}) collective-permute-start(bf16[64,1664]{1,0:T(8,128)(2,1)S(1)} %collective-permute-done.2.x1), channel_id=1, source_target_pairs={{0,2},{1,7},{2,4},{3,1},{4,6},{5,3},{6,0},{7,5},{8,10},{9,15},{10,... | collective-permute-start | bytes 638984 | tf_op jit(solution)/shard_map/gather_normed/ppermute | solution.py:257
  45.7 10.0 %collective-permute-start.14 = (bf16[64,1664]{1,0:T(8,128)(2,1)S(1)}, bf16[64,1664]{1,0:T(8,128)(2,1)S(1)}, u32[]{:S(2)}, u32[]{:S(2)}) collective-permute-start(bf16[64,1664]{1,0:T(8,128)(2,1)S(1)} %get-tuple-element.38.x0), channel_id=1, source_target_pairs={{0,6},{1,3},{2,0},{3,5},{4,2},{5,7},{6,4},{7,1},{8,14},{9,11},{10,... | collective-permute-start | bytes 638984 | tf_op jit(solution)/shard_map/gather_down/ppermute | solution.py:257
  47.2 10.3 %collective-permute-start.6 = (bf16[64,1664]{1,0:T(8,128)(2,1)S(1)}, bf16[64,1664]{1,0:T(8,128)(2,1)S(1)}, u32[]{:S(2)}, u32[]{:S(2)}) collective-permute-start(bf16[64,1664]{1,0:T(8,128)(2,1)S(1)} %collective-permute-done.2.x1), channel_id=1, source_target_pairs={{0,1},{1,0},{2,3},{3,2},{4,5},{5,4},{6,7},{7,6},{8,9},{9,8},{10,11... | collective-permute-start | bytes 638984 | tf_op jit(solution)/shard_map/gather_normed/ppermute | solution.py:249
  51.9 5.6 %collective-permute-start.7 = (bf16[64,1664]{1,0:T(8,128)(2,1)S(1)}, bf16[64,1664]{1,0:T(8,128)(2,1)S(1)}, u32[]{:S(2)}, u32[]{:S(2)}) collective-permute-start(bf16[64,1664]{1,0:T(8,128)(2,1)S(1)} %collective-permute-done.3.x2), channel_id=1, source_target_pairs={{0,1},{1,0},{2,3},{3,2},{4,5},{5,4},{6,7},{7,6},{8,9},{9,8},{10,11... | collective-permute-start | bytes 638984 | tf_op jit(solution)/shard_map/gather_normed/ppermute | solution.py:249
  52.0 6.0 %collective-permute-start.15 = (bf16[64,1664]{1,0:T(8,128)(2,1)S(1)}, bf16[64,1664]{1,0:T(8,128)(2,1)S(1)}, u32[]{:S(2)}, u32[]{:S(2)}) collective-permute-start(bf16[64,1664]{1,0:T(8,128)(2,1)S(1)} %collective-permute-done.13.x1), channel_id=1, source_target_pairs={{0,2},{1,7},{2,4},{3,1},{4,6},{5,3},{6,0},{7,5},{8,10},{9,15},{10,... | collective-permute-start | bytes 638984 | tf_op jit(solution)/shard_map/gather_down/ppermute | solution.py:257
  52.0 7.5 %collective-permute-start.8 = (bf16[64,1664]{1,0:T(8,128)(2,1)S(1)}, bf16[64,1664]{1,0:T(8,128)(2,1)S(1)}, u32[]{:S(2)}, u32[]{:S(2)}) collective-permute-start(bf16[64,1664]{1,0:T(8,128)(2,1)S(1)} %collective-permute-done.4.x3), channel_id=1, source_target_pairs={{0,1},{1,0},{2,3},{3,2},{4,5},{5,4},{6,7},{7,6},{8,9},{9,8},{10,11... | collective-permute-start | bytes 638984 | tf_op jit(solution)/shard_map/gather_normed/ppermute | solution.py:249
  55.7 6.5 %collective-permute-start.16 = (bf16[64,1664]{1,0:T(8,128)(2,1)S(1)}, bf16[64,1664]{1,0:T(8,128)(2,1)S(1)}, u32[]{:S(2)}, u32[]{:S(2)}) collective-permute-start(bf16[64,1664]{1,0:T(8,128)(2,1)S(1)} %get-tuple-element.38.x0), channel_id=1, source_target_pairs={{0,1},{1,0},{2,3},{3,2},{4,5},{5,4},{6,7},{7,6},{8,9},{9,8},{10,11... | collective-permute-start | bytes 638984 | tf_op jit(solution)/shard_map/gather_down/ppermute | solution.py:249
  57.5 4.7 %collective-permute-start.17 = (bf16[64,1664]{1,0:T(8,128)(2,1)S(1)}, bf16[64,1664]{1,0:T(8,128)(2,1)S(1)}, u32[]{:S(2)}, u32[]{:S(2)}) collective-permute-start(bf16[64,1664]{1,0:T(8,128)(2,1)S(1)} %collective-permute-done.13.x1), channel_id=1, source_target_pairs={{0,1},{1,0},{2,3},{3,2},{4,5},{5,4},{6,7},{7,6},{8,9},{9,8},{10,11... | collective-permute-start | bytes 638984 | tf_op jit(solution)/shard_map/gather_down/ppermute | solution.py:249
  57.5 4.7 %collective-permute-start.18 = (bf16[64,1664]{1,0:T(8,128)(2,1)S(1)}, bf16[64,1664]{1,0:T(8,128)(2,1)S(1)}, u32[]{:S(2)}, u32[]{:S(2)}) collective-permute-start(bf16[64,1664]{1,0:T(8,128)(2,1)S(1)} %collective-permute-done.14.x2), channel_id=1, source_target_pairs={{0,1},{1,0},{2,3},{3,2},{4,5},{5,4},{6,7},{7,6},{8,9},{9,8},{10,11... | collective-permute-start | bytes 638984 | tf_op jit(solution)/shard_map/gather_down/ppermute | solution.py:249
  58.0 4.2 %collective-permute-start.19 = (bf16[64,1664]{1,0:T(8,128)(2,1)S(1)}, bf16[64,1664]{1,0:T(8,128)(2,1)S(1)}, u32[]{:S(2)}, u32[]{:S(2)}) collective-permute-start(bf16[64,1664]{1,0:T(8,128)(2,1)S(1)} %collective-permute-done.15.x3), channel_id=1, source_target_pairs={{0,1},{1,0},{2,3},{3,2},{4,5},{5,4},{6,7},{7,6},{8,9},{9,8},{10,11... | collective-permute-start | bytes 638984 | tf_op jit(solution)/shard_map/gather_down/ppermute | solution.py:249
  62.1 7.7 %collective-permute-start.9 = (bf16[256,1664]{1,0:T(8,128)(2,1)S(1)}, bf16[256,1664]{1,0:T(8,128)(2,1)S(1)}, u32[]{:S(2)}, u32[]{:S(2)}) collective-permute-start(bf16[256,1664]{1,0:T(8,128)(2,1)S(1)} %get-tuple-element.33), channel_id=1, source_target_pairs={{0,1},{1,0},{2,3},{3,2},{4,5},{5,4},{6,7},{7,6},{8,9},{9,8},{10,11... | collective-permute-start | bytes 2555912 | tf_op jit(solution)/shard_map/return_result/ppermute | solution.py:249
  64.4 5.6 %collective-permute-start.20 = (bf16[256,1664]{1,0:T(8,128)(2,1)S(1)}, bf16[256,1664]{1,0:T(8,128)(2,1)S(1)}, u32[]{:S(2)}, u32[]{:S(2)}) collective-permute-start(bf16[256,1664]{1,0:T(8,128)(2,1)S(1)} %backward.3), channel_id=1, source_target_pairs={{0,1},{1,0},{2,3},{3,2},{4,5},{5,4},{6,7},{7,6},{8,9},{9,8},{10,11... | collective-permute-start | bytes 2555912 | tf_op jit(solution)/shard_map/return_back/ppermute | solution.py:249
  70.0 6.0 %collective-permute-start.10 = (bf16[64,1664]{1,0:T(8,128)(2,1)S(1)}, bf16[64,1664]{1,0:T(8,128)(2,1)S(1)}, u32[]{:S(2)}, u32[]{:S(2)}) collective-permute-start(bf16[64,1664]{1,0:T(8,128)(2,1)S(1)} %get-tuple-element.36), channel_id=1, source_target_pairs={{0,6},{1,3},{2,0},{3,5},{4,2},{5,7},{6,4},{7,1},{8,14},{9,11},{10,... | collective-permute-start | bytes 638984 | tf_op jit(solution)/shard_map/return_result/ppermute | solution.py:257
  70.2 9.1 %collective-permute-start.21 = (bf16[64,1664]{1,0:T(8,128)(2,1)S(1)}, bf16[64,1664]{1,0:T(8,128)(2,1)S(1)}, u32[]{:S(2)}, u32[]{:S(2)}) collective-permute-start(bf16[64,1664]{1,0:T(8,128)(2,1)S(1)} %get-tuple-element.43), channel_id=1, source_target_pairs={{0,6},{1,3},{2,0},{3,5},{4,2},{5,7},{6,4},{7,1},{8,14},{9,11},{10,... | collective-permute-start | bytes 638984 | tf_op jit(solution)/shard_map/return_back/ppermute | solution.py:257
  70.5 8.9 %collective-permute-start.12 = (bf16[64,1664]{1,0:T(8,128)(2,1)S(1)}, bf16[64,1664]{1,0:T(8,128)(2,1)S(1)}, u32[]{:S(2)}, u32[]{:S(2)}) collective-permute-start(bf16[64,1664]{1,0:T(8,128)(2,1)S(1)} %get-tuple-element.37), channel_id=1, source_target_pairs={{0,2},{1,7},{2,4},{3,1},{4,6},{5,3},{6,0},{7,5},{8,10},{9,15},{10,... | collective-permute-start | bytes 638984 | tf_op jit(solution)/shard_map/return_result/ppermute | solution.py:257
  73.2 10.0 %collective-permute-start.23 = (bf16[64,1664]{1,0:T(8,128)(2,1)S(1)}, bf16[64,1664]{1,0:T(8,128)(2,1)S(1)}, u32[]{:S(2)}, u32[]{:S(2)}) collective-permute-start(bf16[64,1664]{1,0:T(8,128)(2,1)S(1)} %get-tuple-element.44), channel_id=1, source_target_pairs={{0,2},{1,7},{2,4},{3,1},{4,6},{5,3},{6,0},{7,5},{8,10},{9,15},{10,... | collective-permute-start | bytes 638984 | tf_op jit(solution)/shard_map/return_back/ppermute | solution.py:257
  76.0 8.6 %collective-permute-start.11 = (bf16[64,1664]{1,0:T(8,128)(2,1)S(1)}, bf16[64,1664]{1,0:T(8,128)(2,1)S(1)}, u32[]{:S(2)}, u32[]{:S(2)}) collective-permute-start(bf16[64,1664]{1,0:T(8,128)(2,1)S(1)} %return_result.3), channel_id=1, source_target_pairs={{0,6},{1,3},{2,0},{3,5},{4,2},{5,7},{6,4},{7,1},{8,14},{9,11},{10,... | collective-permute-start | bytes 638984 | tf_op jit(solution)/shard_map/return_result/ppermute | solution.py:257
  79.3 8.0 %collective-permute-start.22 = (bf16[64,1664]{1,0:T(8,128)(2,1)S(1)}, bf16[64,1664]{1,0:T(8,128)(2,1)S(1)}, u32[]{:S(2)}, u32[]{:S(2)}) collective-permute-start(bf16[64,1664]{1,0:T(8,128)(2,1)S(1)} %return_back.3), channel_id=1, source_target_pairs={{0,6},{1,3},{2,0},{3,5},{4,2},{5,7},{6,4},{7,1},{8,14},{9,11},{10,... | collective-permute-start | bytes 638984 | tf_op jit(solution)/shard_map/return_back/ppermute | solution.py:257
  104.3 7.0 %collective-permute-start.24 = (bf16[256,896]{1,0:T(8,128)(2,1)S(1)}, bf16[256,896]{1,0:T(8,128)(2,1)S(1)}, u32[]{:S(2)}, u32[]{:S(2)}) collective-permute-start(bf16[256,896]{1,0:T(8,128)(2,1)S(1)} %bitcast.20), channel_id=1, source_target_pairs={{0,1},{1,0},{2,3},{3,2},{4,5},{5,4},{6,7},{7,6},{8,9},{9,8},{10,11... | collective-permute-start | bytes 1376264 | tf_op jit(solution)/shard_map/collect/ppermute | solution.py:249
  (2 other events, 2.6 us)

commit v3 on v2

--- a/solution.py
+++ b/solution.py
@@ -1,3 +1,5 @@
+import functools
+
 import jax
 import jax.numpy as jnp
 from jax import lax
@@ -12,6 +14,7 @@
 I32 = jnp.int32
 VMEM = pl.BlockSpec(memory_space=pltpu.VMEM)
 SMEM = pl.BlockSpec(memory_space=pltpu.SMEM)
+ANY = pl.BlockSpec(memory_space=pl.ANY)
 WIDE = 896
 PACK = 8
 
@@ -22,6 +25,10 @@
 
 def mm_t(a, b):
     return lax.dot_general(a, b, (((1,), (1,)), ((), ())), preferred_element_type=F32)
+
+
+def mm_a(a, b):
+    return lax.dot_general(a, b, (((0,), (0,)), ((), ())), preferred_element_type=F32)
 
 
 def cuts(size, step):
@@ -44,60 +51,85 @@
     )
 
 
-def attend_kernel(ids, context, weight, send, keep):
-    core = ids[0]
-    rows = send.shape[0]
-    for out, at in ((send, 1 - core), (keep, core)):
-        block = context[pl.ds(pl.multiple_of(at * rows, rows), rows), :]
-        for lo, hi in cuts(out.shape[1], 512):
-            out[:, lo:hi] = mm(block, weight[:, lo:hi])
-
-
-def routing_kernel(ids, index, count, gate, pick_keep, pick_send, merge_high, merge_low):
+def open_kernel(ids, index, count, gate, context, weight, send, keep, pick_keep, pick_send, slots, ctx, w, sems):
+    width = weight.shape[1]
+    chunks = cuts(width, 512)
+    load = pltpu.make_async_copy(context, ctx, sems.at[0])
+    load.start()
+    loads = []
+    for i, (lo, hi) in enumerate(chunks):
+        loads.append(pltpu.make_async_copy(weight.at[:, lo:hi], w.at[:, lo:hi], sems.at[i + 1]))
+        loads[-1].start()
     core = ids[0]
     experts, capacity = index.shape
     packed = experts * PACK
-    own_rows = 128
+    rows = send.shape[0]
     local = index[...] - ids[1]
     listed = iota((experts, capacity), 1) < count[...]
-    mine = listed & (local >= 0) & (local < 2 * own_rows)
+    mine = listed & (local >= 0) & (local < 2 * rows)
     upto = jnp.where(iota((capacity, capacity), 0) <= iota((capacity, capacity), 1), 1.0, 0.0)
     rank = mm(jnp.where(mine, 1.0, 0.0).astype(BF), upto.astype(BF))
     lane = iota((experts, 128), 1)
-    rows = jnp.zeros((experts, 128), F32)
+    at_row = jnp.zeros((experts, 128), F32)
     gates = jnp.zeros((experts, 128), F32)
     shifted = (local + 1).astype(F32)
     for slot in range(SLOTS):
         here = mine & (rank == slot + 1.0)
         row = jnp.sum(jnp.where(here, shifted, 0.0), axis=1, keepdims=True) - 1.0
-        rows = jnp.where(lane == slot, row, rows)
-        weight = jnp.sum(jnp.where(here, gate[...], 0.0), axis=1, keepdims=True)
-        gates = jnp.where(lane == slot, weight, gates)
-    rows = rows.astype(BF)
+        at_row = jnp.where(lane == slot, row, at_row)
+        value = jnp.sum(jnp.where(here, gate[...], 0.0), axis=1, keepdims=True)
+        gates = jnp.where(lane == slot, value, gates)
+    at_row = at_row.astype(BF)
     gate_high = gates.astype(BF)
-    gate_low = (gates - gate_high.astype(F32)).astype(BF)
-    spread = jnp.where(iota((packed, experts), 0) // PACK == iota((packed, experts), 1), 1.0, 0.0).astype(BF)
-    down = mm(spread, rows)
+    slots[:experts, :] = at_row
+    slots[experts : 2 * experts, :] = gate_high
+    slots[2 * experts :, :] = (gates - gate_high.astype(F32)).astype(BF)
+    down = mm(spread_of(experts), at_row)
     r_col = iota((packed, 128), 0) % PACK
     lane_id = iota((packed, 128), 1)
-    k = iota((packed, 2 * own_rows), 1)
-    r_wide = iota((packed, 2 * own_rows), 0) % PACK
-    same_stream = (r_wide // 2) % 2 == k // own_rows
-    patch = (core * own_rows + k % own_rows).astype(F32)
+    k = iota((packed, 2 * rows), 1)
+    r_wide = iota((packed, 2 * rows), 0) % PACK
+    same_stream = (r_wide // 2) % 2 == k // rows
+    patch = (core * rows + k % rows).astype(F32)
     for out, side in ((pick_keep, core), (pick_send, 1 - core)):
         slot = 2 * side + r_col % 2
         row = jnp.sum(jnp.where(lane_id == slot, down, 0.0), axis=1, keepdims=True)
         hot = same_stream & (row == patch)
-        out[:, : 2 * own_rows] = jnp.where(hot & (r_wide < 4), 1.0, 0.0).astype(BF)
-        out[:, 2 * own_rows :] = jnp.where(hot & (r_wide >= 4), 1.0, 0.0).astype(BF)
-    along = (((0,), (1,)), ((), ()))
+        out[:, : 2 * rows] = jnp.where(hot & (r_wide < 4), 1.0, 0.0).astype(BF)
+        out[:, 2 * rows :] = jnp.where(hot & (r_wide >= 4), 1.0, 0.0).astype(BF)
+    load.wait()
+    theirs = ctx[:, pl.ds(pl.multiple_of((1 - core) * rows, rows), rows)]
+    ours = ctx[:, pl.ds(pl.multiple_of(core * rows, rows), rows)]
+    for i, (lo, hi) in enumerate(chunks):
+        loads[i].wait()
+        send[:, lo:hi] = mm_a(theirs, w[:, lo:hi])
+        keep[:, lo:hi] = mm_a(ours, w[:, lo:hi])
+
+
+def spread_of(experts):
+    shape = (experts * PACK, experts)
+    return jnp.where(iota(shape, 0) // PACK == iota(shape, 1), 1.0, 0.0).astype(BF)
+
+
+def merge_kernel(ids, slots, merge_high, merge_low):
+    core = ids[0]
+    experts = slots.shape[0] // 3
+    packed = experts * PACK
+    rows = merge_high.shape[0] // 4
+    spread = spread_of(experts)
     across = [
-        lax.dot_general(part, spread, along, preferred_element_type=F32)
-        for part in (rows, gate_high, gate_low)
+        lax.dot_general(
+            slots[i * experts : (i + 1) * experts, :],
+            spread,
+            (((0,), (1,)), ((), ())),
+            preferred_element_type=F32,
+        )
+        for i in range(3)
     ]
     q = iota((128, packed), 1) % PACK
     sub = iota((128, packed), 0)
-    own = (core * own_rows + iota((own_rows, packed), 0)).astype(F32)
+    own = (core * rows + iota((rows, packed), 0)).astype(F32)
+    q_rows = iota((rows, packed), 1) % PACK
     for which, side in ((0, core), (1, 1 - core)):
         slot = 2 * side + q % 2
         row, high, low = (
@@ -105,8 +137,8 @@
         )
         hot = row == own
         for group in range(4):
-            here = hot & (q // 2 == group)
-            at = (slice(group * own_rows, (group + 1) * own_rows), slice(which * packed, (which + 1) * packed))
+            here = hot & (q_rows // 2 == group)
+            at = (slice(group * rows, (group + 1) * rows), slice(which * packed, (which + 1) * packed))
             merge_high[at] = jnp.where(here, high, 0.0).astype(BF)
             merge_low[at] = jnp.where(here, low, 0.0).astype(BF)
 
@@ -137,15 +169,16 @@
     return (q % 64 // 2) * PACK + q // 64 * 2 + q % 2
 
 
-def unpack_kernel(got, first, second):
+def unpack_kernel(stream, got, *rest):
+    out = rest[-1]
     n = got.shape[0]
-    order = jnp.where(place(iota((n, n), 0)) == iota((n, n), 1), 1.0, 0.0).astype(BF)
+    quarter = n // 4
+    q = iota((2 * quarter, n), 0)
+    q = q + (q // quarter + stream) * quarter
+    order = jnp.where(place(q) == iota((2 * quarter, n), 1), 1.0, 0.0).astype(BF)
     flat = mm(order, got[...]).astype(BF)
-    quarter = n // 4
-    rest = first.shape[1] - WIDE
-    for stream, out in enumerate((first, second)):
-        out[:, :WIDE] = flat[stream * quarter : (stream + 1) * quarter, :]
-        out[:, WIDE:] = flat[(2 + stream) * quarter : (3 + stream) * quarter, :rest]
+    out[:, :WIDE] = flat[:quarter, :]
+    out[:, WIDE:] = flat[quarter:, : out.shape[1] - WIDE]
 
 
 def pack_kernel(own_r, one_r, two_r, own_b, one_b, two_b, out, flat):
@@ -161,7 +194,8 @@
     out[...] = mm(order, flat[...]).astype(BF)
 
 
-def forward_kernel(x0, x1, x2, x3, w1, w2, slope, part, x, hidden):
+def forward_kernel(x0, x1, x2, x3, w1, w2, *rest):
+    slope, part, x, hidden = rest[-4:]
     block = x0.shape[0]
     for i, ref in enumerate((x0, x1, x2, x3)):
         x[i * block : (i + 1) * block, :] = ref[...]
@@ -176,7 +210,8 @@
         part[:, lo:hi] = mm(hidden[...], w2[:, lo:hi]).astype(part.dtype)
 
 
-def backward_kernel(x0, x1, x2, x3, w1, w2, slope, part, x, grad):
+def backward_kernel(x0, x1, x2, x3, w1, w2, slope, *rest):
+    part, x, grad = rest[-3:]
     block = x0.shape[0]
     for i, ref in enumerate((x0, x1, x2, x3)):
         x[i * block : (i + 1) * block, :] = ref[...]
@@ -262,23 +297,28 @@
         )
         return got.reshape(packed, WIDE)
 
-    with jax.named_scope("attend"):
-        att_send, att_keep = call(
-            attend_kernel,
-            [sds((rows, width), F32)] * 2,
-            [SMEM, VMEM, VMEM],
+    with jax.named_scope("open"):
+        att_send, att_keep, pick_keep, pick_send, slots = call(
+            open_kernel,
+            [sds((rows, width), F32)] * 2 + [sds((packed, 4 * rows), BF)] * 2 + [sds((3 * experts, 128), BF)],
+            [SMEM] + [VMEM] * 3 + [ANY] * 2,
+            [
+                pltpu.VMEM((context.shape[1], 2 * rows), BF),
+                pltpu.VMEM(out_weight.shape, BF),
+                pltpu.SemaphoreType.DMA((1 + len(cuts(width, 512)),)),
+            ],
             flops=4 * rows * width * context.shape[1],
             moved=5 * 10**6,
-        )(ids, context, out_weight)
+        )(ids, patch_index, patch_count.reshape(experts, 1), gate_value, context.T, out_weight)
         att_got = swap_core(att_send)
-    with jax.named_scope("routing"):
-        pick_keep, pick_send, merge_high, merge_low = call(
-            routing_kernel,
-            [sds((packed, 4 * rows), BF)] * 2 + [sds((4 * rows, 2 * packed), BF)] * 2,
-            [SMEM] + [VMEM] * 3,
-            flops=10**9,
-            moved=2 * 10**6,
-        )(ids, patch_index, patch_count.reshape(experts, 1), gate_value)
+    with jax.named_scope("merge"):
+        merge_high, merge_low = call(
+            merge_kernel,
+            [sds((4 * rows, 2 * packed), BF)] * 2,
+            [SMEM, VMEM],
+            flops=10**8,
+            moved=10**6,
+        )(ids, slots)
     with jax.named_scope("norm"):
         stream, keep, send = call(
             norm_kernel,
@@ -290,9 +330,15 @@
         )(att_keep, att_got, residual, gain, upstream, pick_keep, pick_send)
     with jax.named_scope("dispatch"):
         got = exchange(keep + swap_core(send))
-        normed_rows, down_rows = call(
-            unpack_kernel, [sds((block, width), BF)] * 2, [VMEM], flops=10**8, moved=10**6
-        )(got)
+
+    def unpack(stream, *after):
+        return call(
+            functools.partial(unpack_kernel, stream),
+            sds((block, width), BF),
+            [VMEM] + [ANY] * len(after),
+            flops=10**8,
+            moved=10**6,
+        )(got, *after)
 
     def gather_y(own):
         one = ring(own, 1)
@@ -312,52 +358,52 @@
 
     def reduce_y(parts):
         own, one, two, far = parts
+        from_far = ring(far, -1)
         from_two = ring(two, 1)
-        from_far = ring(far, -1)
         one = call(add_kernel, sds((block, width), BF), [VMEM] * 2, flops=10**5, moved=10**6)(one, from_far)
-        return own, ring(one, -1), from_two
+        return (own, ring(one, -1), from_two), (far, one, from_two)
 
     weight_in = expert_in[0]
     weight_out = expert_out[0]
     tall = shards * block
-    flops = 4 * tall * width * units
-
-    def forward(xs, kind):
+    flops = 16 * tall * width * units
+
+    def forward(xs, kind, *after):
         return call(
             forward_kernel,
             [sds((tall, units), F32), sds((tall, width), kind)],
-            [VMEM] * 6,
+            [VMEM] * 6 + [ANY] * len(after),
             [pltpu.VMEM((tall, width), BF), pltpu.VMEM((tall, units), BF)],
             flops=flops,
             moved=10**7,
             mib=24,
-        )(*xs, weight_in, weight_out)
-
-    def backward(xs, slope, kind):
+        )(*xs, weight_in, weight_out, *after)
+
+    def backward(xs, slope, kind, *after):
         return call(
             backward_kernel,
             sds((tall, width), kind),
-            [VMEM] * 7,
+            [VMEM] * 7 + [ANY] * len(after),
             [pltpu.VMEM((tall, width), BF), pltpu.VMEM((tall, units), BF)],
             flops=flops,
             moved=10**7,
             mib=24,
-        )(*xs, weight_in, weight_out, slope)
+        )(*xs, weight_in, weight_out, slope, *after)
 
     with jax.named_scope("gather_normed"):
-        keeps, sends = gather_y(normed_rows)
+        keeps, sends = gather_y(unpack(0))
     with jax.named_scope("gather_down"):
-        down_keeps, down_sends = gather_y(down_rows)
+        down_keeps, down_sends = gather_y(unpack(1, keeps[1], keeps[2]))
     with jax.named_scope("forward"):
         slope_send, part_send = forward(sends, BF)
-        slope_keep, part_keep = forward(keeps, F32)
+        slope_keep, part_keep = forward(keeps, F32, down_keeps[1], down_keeps[2])
     with jax.named_scope("return_result"):
-        result = reduce_y(combine(part_keep, part_send))
+        result, passed = reduce_y(combine(part_keep, part_send))
     with jax.named_scope("backward"):
-        back_send = backward(down_sends, slope_send, BF)
-        back_keep = backward(down_keeps, slope_keep, F32)
+        back_send = backward(down_sends, slope_send, BF, passed[0])
+        back_keep = backward(down_keeps, slope_keep, F32, *passed[1:])
     with jax.named_scope("return_back"):
-        back = reduce_y(combine(back_keep, back_send))
+        back, _ = reduce_y(combine(back_keep, back_send))
     with jax.named_scope("collect"):
         ready = call(
             pack_kernel,

time: 114 us -> 122 us (1.070)
  waiting for transfers between devices: 16.3 us -> 19.1 us
  blocking collectives: 38.8 us -> 41.1 us
  Pallas kernels: 17.3 us -> 19 us
    ppermute x13, starting transfers between devices: 25.8 us -> 18.5 us  [swap_core(): return lax.ppermute(x, 'core', [(0, 1), (1, 0)])]
    ppermute x12, starting transfers between devices: 10.4 us -> 17.3 us  [ring(): return lax.ppermute(x, ('y', 'core'), pairs)]
    ppermute x12, waiting for transfers between devices: 13.1 us -> 15.4 us  [ring(): return lax.ppermute(x, ('y', 'core'), pairs)]
    all_to_all x2, blocking collectives: 38.8 us -> 41.1 us  [exchange(): lax.all_to_all(x.reshape(experts, PACK, WIDE), 'xz', split_axis=0, concat...]
    pallas_call x5 -> x6, Pallas kernels: 8.06 us -> 9.76 us  [the longest x2 4.61 us: backward(): call(backward_kernel, sds((tall, width), kind), [VMEM] * 7 + [ANY] * len(...]
    unnamed x19 -> x18, local copies, waits for them, and re-layouts: 3.94 us -> 4.49 us
where the time goes in v3:
time: 122 us; the launch traced here: 121 us
  blocking collectives  41.1 us (34%)
  starting transfers between devices  35.8 us (29%)
  waiting for transfers between devices  19.1 us (16%)
  Pallas kernels  19 us (16%)
  local copies, waits for them, and re-layouts  5.23 us (4%)
    all_to_all x2, blocking collectives, exchange(): lax.all_to_all(x.reshape(experts, PACK, WIDE), 'xz', split_axis=0, concat...  41.1 us
    ppermute x13, starting transfers between devices, swap_core(): return lax.ppermute(x, 'core', [(0, 1), (1, 0)])  18.5 us
    ppermute x12, starting transfers between devices, ring(): return lax.ppermute(x, ('y', 'core'), pairs)  17.3 us
    ppermute x12, waiting for transfers between devices, ring(): return lax.ppermute(x, ('y', 'core'), pairs)  15.4 us
    pallas_call x2, Pallas kernels, forward(): call(forward_kernel, [sds((tall, units), F32), sds((tall, width), kind)],...  5.27 us
    pallas_call x2, Pallas kernels, backward(): call(backward_kernel, sds((tall, width), kind), [VMEM] * 7 + [ANY] * len(...  4.61 us
    unnamed x18, local copies, waits for them, and re-layouts  4.49 us
    ppermute x13, waiting for transfers between devices, swap_core(): return lax.ppermute(x, 'core', [(0, 1), (1, 0)])  3.75 us
  transfers between devices with their start and end apart: 25, of which 8 were waited for; matrix products, arithmetic and copies ran while one was open for 0% of the time, Pallas kernels for 10%

profile of v3, /device:TPU:1, one launch (start us, length us, event | category | flops | bytes accessed | tf_op | source)
XLA Modules:
  0.0 121.3 jit_solution(4711287752735200910)
XLA Ops:
  1.5 1.8 %copy-done = bf16[832,1664]{1,0:T(8,128)(2,1)S(1)} copy-done((bf16[832,1664]{1,0:T(8,128)(2,1)S(1)}, bf16[832,1664]{1,0:T(8,128)(2,1)}, u32[]{:S(2)}) %copy-start) | copy-done | bytes 2768920
  3.2 1.0 copy-done.1
  4.3 0.8 copy-done.2
  5.9 3.4 %open.1 = (f32[128,1664]{1,0:T(8,128)S(1)}, f32[128,1664]{1,0:T(8,128)S(1)}, bf16[256,512]{1,0:T(8,128)(2,1)S(1)}, bf16[256,512]{1,0:T(8,128)(2,1)S(1)}, bf16[96,128]{1,0:T(8,128)(2,1)S(1)}) custom-call(s32[2]{0:T(128)S(1)} %pad_add_fusion.ids, s32[32,512]{1,0:T(8,128)S(1)} %copy-done.2, s32[32,1]{1,0:T(8,128)S(1)} %copy.12.count, f32[32,512]{1,0:T(8,128)S(1)} %copy-done.3, ...), custom_call_target="tpu_custom_call" | custom-call | flops 708837376 | bytes 5000000 | tf_op jit(solution)/shard_map/open/pallas_call | solution.py:301
  9.3 3.3 %collective-permute-start = (f32[128,1664]{1,0:T(8,128)S(1)}, f32[128,1664]{1,0:T(8,128)S(1)}, u32[]{:S(2)}, u32[]{:S(2)}) collective-permute-start(f32[128,1664]{1,0:T(8,128)S(1)} %get-tuple-element.25), channel_id=1, source_target_pairs={{0,1},{1,0},{2,3},{3,2},{4,5},{5,4},{6,7},{7,6},{8,9},{9,8},{10,11... | collective-permute-start | bytes 2555912 | tf_op jit(solution)/shard_map/open/ppermute | solution.py:284
  12.7 2.0 %collective-permute-done.att_got = f32[128,1664]{1,0:T(8,128)S(1)} collective-permute-done((f32[128,1664]{1,0:T(8,128)S(1)}, f32[128,1664]{1,0:T(8,128)S(1)}, u32[]{:S(2)}, u32[]{:S(2)}) %collective-permute-start) | collective-permute-done | bytes 852000 | tf_op jit(solution)/shard_map/open/ppermute | solution.py:284
  14.7 1.0 norm.1
  16.2 1.4 %collective-permute-done.1 = bf16[256,896]{1,0:T(8,128)(2,1)S(1)} collective-permute-done((bf16[256,896]{1,0:T(8,128)(2,1)S(1)}, bf16[256,896]{1,0:T(8,128)(2,1)S(1)}, u32[]{:S(2)}, u32[]{:S(2)}) %collective-permute-start.1) | collective-permute-done | bytes 458784 | tf_op jit(solution)/shard_map/dispatch/ppermute | solution.py:284
  17.7 22.2 %all_to_all.10 = bf16[32,8,896]{2,1,0:T(8,128)(2,1)S(1)} all-to-all(bf16[32,8,896]{2,1,0:T(8,128)(2,1)S(1)} %add_bitcast_fusion), channel_id=1, replica_groups=mesh['xz'=32,'y'=4,'core'=2] {'xz'}, dimensions={0} | all-to-all | bytes 917504 | tf_op jit(solution)/shard_map/dispatch/all_to_all | solution.py:295
  40.2 2.8 %collective-permute-start.2 = (bf16[64,1664]{1,0:T(8,128)(2,1)S(1)}, bf16[64,1664]{1,0:T(8,128)(2,1)S(1)}, u32[]{:S(2)}, u32[]{:S(2)}) collective-permute-start(bf16[64,1664]{1,0:T(8,128)(2,1)S(1)} %gather_normed.1.x0), channel_id=1, source_target_pairs={{0,2},{1,7},{2,4},{3,1},{4,6},{5,3},{6,0},{7,5},{8,10},{9,15},{10,... | collective-permute-start | bytes 638984 | tf_op jit(solution)/shard_map/gather_normed/ppermute | solution.py:292
  43.0 2.8 %collective-permute-done.2.rest_0_.x1 = bf16[64,1664]{1,0:T(8,128)(2,1)S(1)} collective-permute-done((bf16[64,1664]{1,0:T(8,128)(2,1)S(1)}, bf16[64,1664]{1,0:T(8,128)(2,1)S(1)}, u32[]{:S(2)}, u32[]{:S(2)}) %collective-permute-start.2) | collective-permute-done | bytes 213024 | tf_op jit(solution)/shard_map/gather_normed/ppermute | solution.py:292
  45.8 3.1 %collective-permute-start.4 = (bf16[64,1664]{1,0:T(8,128)(2,1)S(1)}, bf16[64,1664]{1,0:T(8,128)(2,1)S(1)}, u32[]{:S(2)}, u32[]{:S(2)}) collective-permute-start(bf16[64,1664]{1,0:T(8,128)(2,1)S(1)} %collective-permute-done.2.rest_0_.x1), channel_id=1, source_target_pairs={{0,2},{1,7},{2,4},{3,1},{4,6},{5,3},{6,0},{7,5},{8,10},{9,15},{10,... | collective-permute-start | bytes 638984 | tf_op jit(solution)/shard_map/gather_normed/ppermute | solution.py:292
  48.9 3.0 %collective-permute-start.7 = (bf16[64,1664]{1,0:T(8,128)(2,1)S(1)}, bf16[64,1664]{1,0:T(8,128)(2,1)S(1)}, u32[]{:S(2)}, u32[]{:S(2)}) collective-permute-start(bf16[64,1664]{1,0:T(8,128)(2,1)S(1)} %gather_normed.1.x0), channel_id=1, source_target_pairs={{0,1},{1,0},{2,3},{3,2},{4,5},{5,4},{6,7},{7,6},{8,9},{9,8},{10,11... | collective-permute-start | bytes 638984 | tf_op jit(solution)/shard_map/gather_normed/ppermute | solution.py:284
  52.2 3.0 %collective-permute-start.5 = (bf16[64,1664]{1,0:T(8,128)(2,1)S(1)}, bf16[64,1664]{1,0:T(8,128)(2,1)S(1)}, u32[]{:S(2)}, u32[]{:S(2)}) collective-permute-start(bf16[64,1664]{1,0:T(8,128)(2,1)S(1)} %gather_down.1.x0), channel_id=1, source_target_pairs={{0,2},{1,7},{2,4},{3,1},{4,6},{5,3},{6,0},{7,5},{8,10},{9,15},{10,... | collective-permute-start | bytes 638984 | tf_op jit(solution)/shard_map/gather_down/ppermute | solution.py:292
  55.8 3.2 %collective-permute-start.10 = (bf16[64,1664]{1,0:T(8,128)(2,1)S(1)}, bf16[64,1664]{1,0:T(8,128)(2,1)S(1)}, u32[]{:S(2)}, u32[]{:S(2)}) collective-permute-start(bf16[64,1664]{1,0:T(8,128)(2,1)S(1)} %collective-permute-done.4.x3), channel_id=1, source_target_pairs={{0,1},{1,0},{2,3},{3,2},{4,5},{5,4},{6,7},{7,6},{8,9},{9,8},{10,11... | collective-permute-start | bytes 638984 | tf_op jit(solution)/shard_map/gather_normed/ppermute | solution.py:284
  59.0 2.7 %collective-permute-start.15 = (bf16[64,1664]{1,0:T(8,128)(2,1)S(1)}, bf16[64,1664]{1,0:T(8,128)(2,1)S(1)}, u32[]{:S(2)}, u32[]{:S(2)}) collective-permute-start(bf16[64,1664]{1,0:T(8,128)(2,1)S(1)} %collective-permute-done.5.rest_0_.x1), channel_id=1, source_target_pairs={{0,2},{1,7},{2,4},{3,1},{4,6},{5,3},{6,0},{7,5},{8,10},{9,15},{10,... | collective-permute-start | bytes 638984 | tf_op jit(solution)/shard_map/gather_down/ppermute | solution.py:292
  61.7 2.6 %forward.3 = (f32[256,1024]{1,0:T(8,128)S(1)}, bf16[256,1664]{1,0:T(8,128)(2,1)S(1)}) custom-call(bf16[64,1664]{1,0:T(8,128)(2,1)S(1)} %collective-permute-done.7.x0, bf16[64,1664]{1,0:T(8,128)(2,1)S(1)} %collective-permute-done.8.x1, bf16[64,1664]{1,0:T(8,128)(2,1)S(1)} %collective-permute-done.9.x2, bf16[64,1664]{1,0:T(8,128)(2,1)S(1)} %collective-permute-done.10.x3, ...), custom_call_target="tpu_custom_call" | custom-call | flops 6979321856 | bytes 10000000 | tf_op jit(solution)/shard_map/forward/pallas_call | solution.py:372
  65.0 1.9 %collective-permute-start.18 = (bf16[64,1664]{1,0:T(8,128)(2,1)S(1)}, bf16[64,1664]{1,0:T(8,128)(2,1)S(1)}, u32[]{:S(2)}, u32[]{:S(2)}) collective-permute-start(bf16[64,1664]{1,0:T(8,128)(2,1)S(1)} %collective-permute-done.6.rest_1_.x2), channel_id=1, source_target_pairs={{0,1},{1,0},{2,3},{3,2},{4,5},{5,4},{6,7},{7,6},{8,9},{9,8},{10,11... | collective-permute-start | bytes 638984 | tf_op jit(solution)/shard_map/gather_down/ppermute | solution.py:284
  66.9 1.4 %collective-permute-start.19 = (bf16[64,1664]{1,0:T(8,128)(2,1)S(1)}, bf16[64,1664]{1,0:T(8,128)(2,1)S(1)}, u32[]{:S(2)}, u32[]{:S(2)}) collective-permute-start(bf16[64,1664]{1,0:T(8,128)(2,1)S(1)} %collective-permute-done.15.x3), channel_id=1, source_target_pairs={{0,1},{1,0},{2,3},{3,2},{4,5},{5,4},{6,7},{7,6},{8,9},{9,8},{10,11... | collective-permute-start | bytes 638984 | tf_op jit(solution)/shard_map/gather_down/ppermute | solution.py:284
  68.3 2.6 %forward.2 = (f32[256,1024]{1,0:T(8,128)S(1)}, f32[256,1664]{1,0:T(8,128)S(1)}) custom-call(bf16[64,1664]{1,0:T(8,128)(2,1)S(1)} %gather_normed.1.x0, bf16[64,1664]{1,0:T(8,128)(2,1)S(1)} %collective-permute-done.2.rest_0_.x1, bf16[64,1664]{1,0:T(8,128)(2,1)S(1)} %collective-permute-done.3.rest_1_.x2, bf16[64,1664]{1,0:T(8,128)(2,1)S(1)} %collective-permute-done.4.x3, ...), custom_call_target="tpu_custom_call" | custom-call | flops 6979321856 | bytes 10000000 | tf_op jit(solution)/shard_map/forward/pallas_call | solution.py:372
  71.2 2.7 %collective-permute-start.14 = (bf16[64,1664]{1,0:T(8,128)(2,1)S(1)}, bf16[64,1664]{1,0:T(8,128)(2,1)S(1)}, u32[]{:S(2)}, u32[]{:S(2)}) collective-permute-start(bf16[64,1664]{1,0:T(8,128)(2,1)S(1)} %get-tuple-element.35), channel_id=1, source_target_pairs={{0,2},{1,7},{2,4},{3,1},{4,6},{5,3},{6,0},{7,5},{8,10},{9,15},{10,... | collective-permute-start | bytes 638984 | tf_op jit(solution)/shard_map/return_result/ppermute | solution.py:292
  73.9 2.3 %backward.3 = bf16[256,1664]{1,0:T(8,128)(2,1)S(1)} custom-call(bf16[64,1664]{1,0:T(8,128)(2,1)S(1)} %collective-permute-done.16.x0, bf16[64,1664]{1,0:T(8,128)(2,1)S(1)} %collective-permute-done.17.x1, bf16[64,1664]{1,0:T(8,128)(2,1)S(1)} %collective-permute-done.18.x2, bf16[64,1664]{1,0:T(8,128)(2,1)S(1)} %collective-permute-done.19.x3, ...), custom_call_target="tpu_custom_call" | custom-call | flops 6979321856 | bytes 10000000 | tf_op jit(solution)/shard_map/backward/pallas_call | solution.py:383
  76.5 2.6 %collective-permute-done.12.b = bf16[64,1664]{1,0:T(8,128)(2,1)S(1)} collective-permute-done((bf16[64,1664]{1,0:T(8,128)(2,1)S(1)}, bf16[64,1664]{1,0:T(8,128)(2,1)S(1)}, u32[]{:S(2)}, u32[]{:S(2)}) %collective-permute-start.12) | collective-permute-done | bytes 213024 | tf_op jit(solution)/shard_map/return_result/ppermute | solution.py:292
  79.2 2.3 %backward.2.keep = f32[256,1664]{1,0:T(8,128)S(1)} custom-call(bf16[64,1664]{1,0:T(8,128)(2,1)S(1)} %gather_down.1.x0, bf16[64,1664]{1,0:T(8,128)(2,1)S(1)} %collective-permute-done.5.rest_0_.x1, bf16[64,1664]{1,0:T(8,128)(2,1)S(1)} %collective-permute-done.6.rest_1_.x2, bf16[64,1664]{1,0:T(8,128)(2,1)S(1)} %collective-permute-done.15.x3, ...), custom_call_target="tpu_custom_call" | custom-call | flops 6979321856 | bytes 10000000 | tf_op jit(solution)/shard_map/backward/pallas_call | solution.py:383
  81.8 2.7 %collective-permute-start.23 = (bf16[64,1664]{1,0:T(8,128)(2,1)S(1)}, bf16[64,1664]{1,0:T(8,128)(2,1)S(1)}, u32[]{:S(2)}, u32[]{:S(2)}) collective-permute-start(bf16[64,1664]{1,0:T(8,128)(2,1)S(1)} %get-tuple-element.41), channel_id=1, source_target_pairs={{0,2},{1,7},{2,4},{3,1},{4,6},{5,3},{6,0},{7,5},{8,10},{9,15},{10,... | collective-permute-start | bytes 638984 | tf_op jit(solution)/shard_map/return_back/ppermute | solution.py:292
  84.5 4.1 %collective-permute-done.21.b = bf16[64,1664]{1,0:T(8,128)(2,1)S(1)} collective-permute-done((bf16[64,1664]{1,0:T(8,128)(2,1)S(1)}, bf16[64,1664]{1,0:T(8,128)(2,1)S(1)}, u32[]{:S(2)}, u32[]{:S(2)}) %collective-permute-start.21) | collective-permute-done | bytes 213024 | tf_op jit(solution)/shard_map/return_back/ppermute | solution.py:292
  88.7 3.5 %collective-permute-done.13.one_r = bf16[64,1664]{1,0:T(8,128)(2,1)S(1)} collective-permute-done((bf16[64,1664]{1,0:T(8,128)(2,1)S(1)}, bf16[64,1664]{1,0:T(8,128)(2,1)S(1)}, u32[]{:S(2)}, u32[]{:S(2)}) %collective-permute-start.13) | collective-permute-done | bytes 213024 | tf_op jit(solution)/shard_map/return_result/ppermute | solution.py:292
  92.2 2.4 %collective-permute-done.22.one_b = bf16[64,1664]{1,0:T(8,128)(2,1)S(1)} collective-permute-done((bf16[64,1664]{1,0:T(8,128)(2,1)S(1)}, bf16[64,1664]{1,0:T(8,128)(2,1)S(1)}, u32[]{:S(2)}, u32[]{:S(2)}) %collective-permute-start.22) | collective-permute-done | bytes 213024 | tf_op jit(solution)/shard_map/return_back/ppermute | solution.py:292
  95.0 18.8 %all_to_all.11 = bf16[32,8,896]{2,1,0:T(8,128)(2,1)S(1)} all-to-all(bf16[32,8,896]{2,1,0:T(8,128)(2,1)S(1)} %bitcast.13), channel_id=1, replica_groups=mesh['xz'=32,'y'=4,'core'=2] {'xz'}, dimensions={0} | all-to-all | bytes 917504 | tf_op jit(solution)/shard_map/collect/all_to_all | solution.py:295
  113.8 3.8 %collective-permute-start.24 = (bf16[256,896]{1,0:T(8,128)(2,1)S(1)}, bf16[256,896]{1,0:T(8,128)(2,1)S(1)}, u32[]{:S(2)}, u32[]{:S(2)}) collective-permute-start(bf16[256,896]{1,0:T(8,128)(2,1)S(1)} %bitcast.14), channel_id=1, source_target_pairs={{0,1},{1,0},{2,3},{3,2},{4,5},{5,4},{6,7},{7,6},{8,9},{9,8},{10,11... | collective-permute-start | bytes 1376264 | tf_op jit(solution)/shard_map/collect/ppermute | solution.py:284
  117.6 1.2 merge.1
  119.0 2.2 %final.1 = (bf16[128,1664]{1,0:T(8,128)(2,1)}, bf16[128,1664]{1,0:T(8,128)(2,1)}) custom-call(bf16[256,896]{1,0:T(8,128)(2,1)S(1)} %bitcast.15, bf16[256,896]{1,0:T(8,128)(2,1)S(1)} %collective-permute-done.24.theirs, bf16[512,512]{1,0:T(8,128)(2,1)S(1)} %get-tuple-element.43.merge_high, bf16[512,512]{1,0:T(8,128)(2,1)S(1)} %get-tuple-element.44.merge_low, ...), custom_call_target="tpu_custom_call" | custom-call | flops 1000000000 | bytes 4000000 | tf_op jit(solution)/shard_map/final/pallas_call | solution.py:419
  (57 shorter events, 5.7 us)
Async XLA Ops:
  0.6 12.0 %copy-start.8 = (f32[1664]{0:T(1024)S(1)}, f32[1664]{0:T(1024)}, u32[]{:S(2)}) copy-start(f32[1664]{0:T(1024)} %param.13) | copy-start | bytes 19972
  1.5 1.8 %copy-start = (bf16[832,1664]{1,0:T(8,128)(2,1)S(1)}, bf16[832,1664]{1,0:T(8,128)(2,1)}, u32[]{:S(2)}) copy-start(bf16[832,1664]{1,0:T(8,128)(2,1)} %weight.1) | copy-start | bytes 8306692
  3.2 1.0 copy-start.1
  5.9 8.7 %copy-start.6 = (bf16[128,1664]{1,0:T(8,128)(2,1)S(1)}, bf16[128,1664]{1,0:T(8,128)(2,1)}, u32[]{:S(2)}) copy-start(bf16[128,1664]{1,0:T(8,128)(2,1)} %residual.1) | copy-start | bytes 1277956
  5.9 8.7 %copy-start.7 = (bf16[128,1664]{1,0:T(8,128)(2,1)S(1)}, bf16[128,1664]{1,0:T(8,128)(2,1)}, u32[]{:S(2)}) copy-start(bf16[128,1664]{1,0:T(8,128)(2,1)} %upstream.3) | copy-start | bytes 1277956
  9.3 5.3 %collective-permute-start = (f32[128,1664]{1,0:T(8,128)S(1)}, f32[128,1664]{1,0:T(8,128)S(1)}, u32[]{:S(2)}, u32[]{:S(2)}) collective-permute-start(f32[128,1664]{1,0:T(8,128)S(1)} %get-tuple-element.25), channel_id=1, source_target_pairs={{0,1},{1,0},{2,3},{3,2},{4,5},{5,4},{6,7},{7,6},{8,9},{9,8},{10,11... | collective-permute-start | bytes 2555912 | tf_op jit(solution)/shard_map/open/ppermute | solution.py:284
  14.7 47.0 %copy-start.5 = (bf16[1,1024,1664]{2,1,0:T(8,128)(2,1)S(1)}, bf16[1,1024,1664]{2,1,0:T(8,128)(2,1)}, u32[]{:S(2)}) copy-start(bf16[1,1024,1664]{2,1,0:T(8,128)(2,1)} %param.15) | copy-start | bytes 10223620
  15.7 46.0 %copy-start.4 = (bf16[1,1664,1024]{2,1,0:T(8,128)(2,1)S(1)}, bf16[1,1664,1024]{2,1,0:T(8,128)(2,1)}, u32[]{:S(2)}) copy-start(bf16[1,1664,1024]{2,1,0:T(8,128)(2,1)} %param.14) | copy-start | bytes 10223620
  15.7 1.9 %collective-permute-start.1 = (bf16[256,896]{1,0:T(8,128)(2,1)S(1)}, bf16[256,896]{1,0:T(8,128)(2,1)S(1)}, u32[]{:S(2)}, u32[]{:S(2)}) collective-permute-start(bf16[256,896]{1,0:T(8,128)(2,1)S(1)} %get-tuple-element.29), channel_id=1, source_target_pairs={{0,1},{1,0},{2,3},{3,2},{4,5},{5,4},{6,7},{7,6},{8,9},{9,8},{10,11... | collective-permute-start | bytes 1376264 | tf_op jit(solution)/shard_map/dispatch/ppermute | solution.py:284
  40.2 5.6 %collective-permute-start.2 = (bf16[64,1664]{1,0:T(8,128)(2,1)S(1)}, bf16[64,1664]{1,0:T(8,128)(2,1)S(1)}, u32[]{:S(2)}, u32[]{:S(2)}) collective-permute-start(bf16[64,1664]{1,0:T(8,128)(2,1)S(1)} %gather_normed.1.x0), channel_id=1, source_target_pairs={{0,2},{1,7},{2,4},{3,1},{4,6},{5,3},{6,0},{7,5},{8,10},{9,15},{10,... | collective-permute-start | bytes 638984 | tf_op jit(solution)/shard_map/gather_normed/ppermute | solution.py:292
  43.0 8.9 %collective-permute-start.3 = (bf16[64,1664]{1,0:T(8,128)(2,1)S(1)}, bf16[64,1664]{1,0:T(8,128)(2,1)S(1)}, u32[]{:S(2)}, u32[]{:S(2)}) collective-permute-start(bf16[64,1664]{1,0:T(8,128)(2,1)S(1)} %gather_normed.1.x0), channel_id=1, source_target_pairs={{0,6},{1,3},{2,0},{3,5},{4,2},{5,7},{6,4},{7,1},{8,14},{9,11},{10,... | collective-permute-start | bytes 638984 | tf_op jit(solution)/shard_map/gather_normed/ppermute | solution.py:292
  45.8 9.9 %collective-permute-start.4 = (bf16[64,1664]{1,0:T(8,128)(2,1)S(1)}, bf16[64,1664]{1,0:T(8,128)(2,1)S(1)}, u32[]{:S(2)}, u32[]{:S(2)}) collective-permute-start(bf16[64,1664]{1,0:T(8,128)(2,1)S(1)} %collective-permute-done.2.rest_0_.x1), channel_id=1, source_target_pairs={{0,2},{1,7},{2,4},{3,1},{4,6},{5,3},{6,0},{7,5},{8,10},{9,15},{10,... | collective-permute-start | bytes 638984 | tf_op jit(solution)/shard_map/gather_normed/ppermute | solution.py:292
  48.9 10.0 %collective-permute-start.7 = (bf16[64,1664]{1,0:T(8,128)(2,1)S(1)}, bf16[64,1664]{1,0:T(8,128)(2,1)S(1)}, u32[]{:S(2)}, u32[]{:S(2)}) collective-permute-start(bf16[64,1664]{1,0:T(8,128)(2,1)S(1)} %gather_normed.1.x0), channel_id=1, source_target_pairs={{0,1},{1,0},{2,3},{3,2},{4,5},{5,4},{6,7},{7,6},{8,9},{9,8},{10,11... | collective-permute-start | bytes 638984 | tf_op jit(solution)/shard_map/gather_normed/ppermute | solution.py:284
  52.2 6.8 %collective-permute-start.5 = (bf16[64,1664]{1,0:T(8,128)(2,1)S(1)}, bf16[64,1664]{1,0:T(8,128)(2,1)S(1)}, u32[]{:S(2)}, u32[]{:S(2)}) collective-permute-start(bf16[64,1664]{1,0:T(8,128)(2,1)S(1)} %gather_down.1.x0), channel_id=1, source_target_pairs={{0,2},{1,7},{2,4},{3,1},{4,6},{5,3},{6,0},{7,5},{8,10},{9,15},{10,... | collective-permute-start | bytes 638984 | tf_op jit(solution)/shard_map/gather_down/ppermute | solution.py:292
  55.3 6.4 %collective-permute-start.8 = (bf16[64,1664]{1,0:T(8,128)(2,1)S(1)}, bf16[64,1664]{1,0:T(8,128)(2,1)S(1)}, u32[]{:S(2)}, u32[]{:S(2)}) collective-permute-start(bf16[64,1664]{1,0:T(8,128)(2,1)S(1)} %collective-permute-done.2.rest_0_.x1), channel_id=1, source_target_pairs={{0,1},{1,0},{2,3},{3,2},{4,5},{5,4},{6,7},{7,6},{8,9},{9,8},{10,11... | collective-permute-start | bytes 638984 | tf_op jit(solution)/shard_map/gather_normed/ppermute | solution.py:284
  55.3 6.4 %collective-permute-start.9 = (bf16[64,1664]{1,0:T(8,128)(2,1)S(1)}, bf16[64,1664]{1,0:T(8,128)(2,1)S(1)}, u32[]{:S(2)}, u32[]{:S(2)}) collective-permute-start(bf16[64,1664]{1,0:T(8,128)(2,1)S(1)} %collective-permute-done.3.rest_1_.x2), channel_id=1, source_target_pairs={{0,1},{1,0},{2,3},{3,2},{4,5},{5,4},{6,7},{7,6},{8,9},{9,8},{10,11... | collective-permute-start | bytes 638984 | tf_op jit(solution)/shard_map/gather_normed/ppermute | solution.py:284
  55.8 5.9 %collective-permute-start.10 = (bf16[64,1664]{1,0:T(8,128)(2,1)S(1)}, bf16[64,1664]{1,0:T(8,128)(2,1)S(1)}, u32[]{:S(2)}, u32[]{:S(2)}) collective-permute-start(bf16[64,1664]{1,0:T(8,128)(2,1)S(1)} %collective-permute-done.4.x3), channel_id=1, source_target_pairs={{0,1},{1,0},{2,3},{3,2},{4,5},{5,4},{6,7},{7,6},{8,9},{9,8},{10,11... | collective-permute-start | bytes 638984 | tf_op jit(solution)/shard_map/gather_normed/ppermute | solution.py:284
  59.0 6.1 %collective-permute-start.6 = (bf16[64,1664]{1,0:T(8,128)(2,1)S(1)}, bf16[64,1664]{1,0:T(8,128)(2,1)S(1)}, u32[]{:S(2)}, u32[]{:S(2)}) collective-permute-start(bf16[64,1664]{1,0:T(8,128)(2,1)S(1)} %gather_down.1.x0), channel_id=1, source_target_pairs={{0,6},{1,3},{2,0},{3,5},{4,2},{5,7},{6,4},{7,1},{8,14},{9,11},{10,... | collective-permute-start | bytes 638984 | tf_op jit(solution)/shard_map/gather_down/ppermute | solution.py:292
  59.0 7.9 %collective-permute-start.15 = (bf16[64,1664]{1,0:T(8,128)(2,1)S(1)}, bf16[64,1664]{1,0:T(8,128)(2,1)S(1)}, u32[]{:S(2)}, u32[]{:S(2)}) collective-permute-start(bf16[64,1664]{1,0:T(8,128)(2,1)S(1)} %collective-permute-done.5.rest_0_.x1), channel_id=1, source_target_pairs={{0,2},{1,7},{2,4},{3,1},{4,6},{5,3},{6,0},{7,5},{8,10},{9,15},{10,... | collective-permute-start | bytes 638984 | tf_op jit(solution)/shard_map/gather_down/ppermute | solution.py:292
  64.3 6.6 %collective-permute-start.11 = (bf16[256,1664]{1,0:T(8,128)(2,1)S(1)}, bf16[256,1664]{1,0:T(8,128)(2,1)S(1)}, u32[]{:S(2)}, u32[]{:S(2)}) collective-permute-start(bf16[256,1664]{1,0:T(8,128)(2,1)S(1)} %get-tuple-element.31), channel_id=1, source_target_pairs={{0,1},{1,0},{2,3},{3,2},{4,5},{5,4},{6,7},{7,6},{8,9},{9,8},{10,11... | collective-permute-start | bytes 2555912 | tf_op jit(solution)/shard_map/return_result/ppermute | solution.py:284
  64.4 6.8 %collective-permute-start.16 = (bf16[64,1664]{1,0:T(8,128)(2,1)S(1)}, bf16[64,1664]{1,0:T(8,128)(2,1)S(1)}, u32[]{:S(2)}, u32[]{:S(2)}) collective-permute-start(bf16[64,1664]{1,0:T(8,128)(2,1)S(1)} %gather_down.1.x0), channel_id=1, source_target_pairs={{0,1},{1,0},{2,3},{3,2},{4,5},{5,4},{6,7},{7,6},{8,9},{9,8},{10,11... | collective-permute-start | bytes 638984 | tf_op jit(solution)/shard_map/gather_down/ppermute | solution.py:284
  64.9 8.9 %collective-permute-start.17 = (bf16[64,1664]{1,0:T(8,128)(2,1)S(1)}, bf16[64,1664]{1,0:T(8,128)(2,1)S(1)}, u32[]{:S(2)}, u32[]{:S(2)}) collective-permute-start(bf16[64,1664]{1,0:T(8,128)(2,1)S(1)} %collective-permute-done.5.rest_0_.x1), channel_id=1, source_target_pairs={{0,1},{1,0},{2,3},{3,2},{4,5},{5,4},{6,7},{7,6},{8,9},{9,8},{10,11... | collective-permute-start | bytes 638984 | tf_op jit(solution)/shard_map/gather_down/ppermute | solution.py:284
  65.0 8.8 %collective-permute-start.18 = (bf16[64,1664]{1,0:T(8,128)(2,1)S(1)}, bf16[64,1664]{1,0:T(8,128)(2,1)S(1)}, u32[]{:S(2)}, u32[]{:S(2)}) collective-permute-start(bf16[64,1664]{1,0:T(8,128)(2,1)S(1)} %collective-permute-done.6.rest_1_.x2), channel_id=1, source_target_pairs={{0,1},{1,0},{2,3},{3,2},{4,5},{5,4},{6,7},{7,6},{8,9},{9,8},{10,11... | collective-permute-start | bytes 638984 | tf_op jit(solution)/shard_map/gather_down/ppermute | solution.py:284
  66.9 7.0 %collective-permute-start.19 = (bf16[64,1664]{1,0:T(8,128)(2,1)S(1)}, bf16[64,1664]{1,0:T(8,128)(2,1)S(1)}, u32[]{:S(2)}, u32[]{:S(2)}) collective-permute-start(bf16[64,1664]{1,0:T(8,128)(2,1)S(1)} %collective-permute-done.15.x3), channel_id=1, source_target_pairs={{0,1},{1,0},{2,3},{3,2},{4,5},{5,4},{6,7},{7,6},{8,9},{9,8},{10,11... | collective-permute-start | bytes 638984 | tf_op jit(solution)/shard_map/gather_down/ppermute | solution.py:284
  71.1 8.0 %collective-permute-start.12 = (bf16[64,1664]{1,0:T(8,128)(2,1)S(1)}, bf16[64,1664]{1,0:T(8,128)(2,1)S(1)}, u32[]{:S(2)}, u32[]{:S(2)}) collective-permute-start(bf16[64,1664]{1,0:T(8,128)(2,1)S(1)} %get-tuple-element.34.rest_0_), channel_id=1, source_target_pairs={{0,6},{1,3},{2,0},{3,5},{4,2},{5,7},{6,4},{7,1},{8,14},{9,11},{10,... | collective-permute-start | bytes 638984 | tf_op jit(solution)/shard_map/return_result/ppermute | solution.py:292
  71.2 8.0 %collective-permute-start.14 = (bf16[64,1664]{1,0:T(8,128)(2,1)S(1)}, bf16[64,1664]{1,0:T(8,128)(2,1)S(1)}, u32[]{:S(2)}, u32[]{:S(2)}) collective-permute-start(bf16[64,1664]{1,0:T(8,128)(2,1)S(1)} %get-tuple-element.35), channel_id=1, source_target_pairs={{0,2},{1,7},{2,4},{3,1},{4,6},{5,3},{6,0},{7,5},{8,10},{9,15},{10,... | collective-permute-start | bytes 638984 | tf_op jit(solution)/shard_map/return_result/ppermute | solution.py:292
  76.2 5.3 %collective-permute-start.20 = (bf16[256,1664]{1,0:T(8,128)(2,1)S(1)}, bf16[256,1664]{1,0:T(8,128)(2,1)S(1)}, u32[]{:S(2)}, u32[]{:S(2)}) collective-permute-start(bf16[256,1664]{1,0:T(8,128)(2,1)S(1)} %backward.3), channel_id=1, source_target_pairs={{0,1},{1,0},{2,3},{3,2},{4,5},{5,4},{6,7},{7,6},{8,9},{9,8},{10,11... | collective-permute-start | bytes 2555912 | tf_op jit(solution)/shard_map/return_back/ppermute | solution.py:284
  81.6 7.0 %collective-permute-start.21 = (bf16[64,1664]{1,0:T(8,128)(2,1)S(1)}, bf16[64,1664]{1,0:T(8,128)(2,1)S(1)}, u32[]{:S(2)}, u32[]{:S(2)}) collective-permute-start(bf16[64,1664]{1,0:T(8,128)(2,1)S(1)} %get-tuple-element.40), channel_id=1, source_target_pairs={{0,6},{1,3},{2,0},{3,5},{4,2},{5,7},{6,4},{7,1},{8,14},{9,11},{10,... | collective-permute-start | bytes 638984 | tf_op jit(solution)/shard_map/return_back/ppermute | solution.py:292
  81.7 10.5 %collective-permute-start.13 = (bf16[64,1664]{1,0:T(8,128)(2,1)S(1)}, bf16[64,1664]{1,0:T(8,128)(2,1)S(1)}, u32[]{:S(2)}, u32[]{:S(2)}) collective-permute-start(bf16[64,1664]{1,0:T(8,128)(2,1)S(1)} %return_result.3.rest_0_), channel_id=1, source_target_pairs={{0,6},{1,3},{2,0},{3,5},{4,2},{5,7},{6,4},{7,1},{8,14},{9,11},{10,... | collective-permute-start | bytes 638984 | tf_op jit(solution)/shard_map/return_result/ppermute | solution.py:292
  81.8 10.4 %collective-permute-start.23 = (bf16[64,1664]{1,0:T(8,128)(2,1)S(1)}, bf16[64,1664]{1,0:T(8,128)(2,1)S(1)}, u32[]{:S(2)}, u32[]{:S(2)}) collective-permute-start(bf16[64,1664]{1,0:T(8,128)(2,1)S(1)} %get-tuple-element.41), channel_id=1, source_target_pairs={{0,2},{1,7},{2,4},{3,1},{4,6},{5,3},{6,0},{7,5},{8,10},{9,15},{10,... | collective-permute-start | bytes 638984 | tf_op jit(solution)/shard_map/return_back/ppermute | solution.py:292
  88.6 6.0 %collective-permute-start.22 = (bf16[64,1664]{1,0:T(8,128)(2,1)S(1)}, bf16[64,1664]{1,0:T(8,128)(2,1)S(1)}, u32[]{:S(2)}, u32[]{:S(2)}) collective-permute-start(bf16[64,1664]{1,0:T(8,128)(2,1)S(1)} %return_back.3), channel_id=1, source_target_pairs={{0,6},{1,3},{2,0},{3,5},{4,2},{5,7},{6,4},{7,1},{8,14},{9,11},{10,... | collective-permute-start | bytes 638984 | tf_op jit(solution)/shard_map/return_back/ppermute | solution.py:292
  113.8 5.2 %collective-permute-start.24 = (bf16[256,896]{1,0:T(8,128)(2,1)S(1)}, bf16[256,896]{1,0:T(8,128)(2,1)S(1)}, u32[]{:S(2)}, u32[]{:S(2)}) collective-permute-start(bf16[256,896]{1,0:T(8,128)(2,1)S(1)} %bitcast.14), channel_id=1, source_target_pairs={{0,1},{1,0},{2,3},{3,2},{4,5},{5,4},{6,7},{7,6},{8,9},{9,8},{10,11... | collective-permute-start | bytes 1376264 | tf_op jit(solution)/shard_map/collect/ppermute | solution.py:284
  (2 other events, 1.7 us)

commit v4 on v3

v4 whole, which is shorter than its diff:
```python
import jax
import jax.numpy as jnp
from jax import lax
from jax.experimental import pallas as pl
from jax.experimental.pallas import tpu as pltpu
from jax.sharding import Mesh, PartitionSpec as P

SLOTS = 4
HALF = 2
BF = jnp.bfloat16
F32 = jnp.float32
I32 = jnp.int32
VMEM = pl.BlockSpec(memory_space=pltpu.VMEM)
SMEM = pl.BlockSpec(memory_space=pltpu.SMEM)
ANY = pl.BlockSpec(memory_space=pl.ANY)
WIDE = 896
PACK = 8
PARTS = ((0, 512), (512, 896), (896, 1280), (1280, 1664))


def mm(a, b):
    return jnp.dot(a, b, preferred_element_type=F32)


def mm_t(a, b):
    return lax.dot_general(a, b, (((1,), (1,)), ((), ())), preferred_element_type=F32)


def mm_a(a, b):
    return lax.dot_general(a, b, (((0,), (0,)), ((), ())), preferred_element_type=F32)


def cuts(size, step):
    return [(i, min(i + step, size)) for i in range(0, size, step)]


def iota(shape, dim):
    return lax.broadcasted_iota(I32, shape, dim)


def call(kernel, outs, in_specs, scratch=(), flops=0, moved=0, mib=16):
    return pl.pallas_call(
        kernel,
        out_shape=outs,
        in_specs=in_specs,
        out_specs=jax.tree.map(lambda _: VMEM, outs),
        scratch_shapes=list(scratch),
        compiler_params=pltpu.CompilerParams(vmem_limit_bytes=mib * 2**20),
        cost_estimate=pl.CostEstimate(flops=flops, bytes_accessed=moved, transcendentals=0),
    )


def select(hot, rows, out):
    part = iota(hot.shape, 0) % PACK // 2
    picks = [jnp.where(part == i, hot[...], 0.0).astype(BF) for i in range(len(PARTS))]
    low = PARTS[-1][1] - PARTS[-1][0]
    total = mm(picks[0], rows[:, :low])
    for pick, (lo, hi) in zip(picks[1:], PARTS[1:]):
        total += mm(pick, rows[:, lo:hi])
    out[:, :low] = total.astype(BF)
    out[:, low:] = mm(picks[0], rows[:, low : PARTS[0][1]]).astype(BF)


def open_kernel(ids, index, count, gate, upstream, hot_keep, hot_send, slots, keep, send):
    core = ids[0]
    experts, capacity = index.shape
    packed = experts * PACK
    rows = upstream.shape[0]
    local = index[...] - ids[1]
    listed = iota((experts, capacity), 1) < count[...]
    mine = listed & (local >= 0) & (local < 2 * rows)
    upto = jnp.where(iota((capacity, capacity), 0) <= iota((capacity, capacity), 1), 1.0, 0.0)
    rank = mm(jnp.where(mine, 1.0, 0.0).astype(BF), upto.astype(BF))
    lane = iota((experts, 128), 1)
    at_row = jnp.zeros((experts, 128), F32)
    gates = jnp.zeros((experts, 128), F32)
    shifted = (local + 1).astype(F32)
    for slot in range(SLOTS):
        here = mine & (rank == slot + 1.0)
        row = jnp.sum(jnp.where(here, shifted, 0.0), axis=1, keepdims=True) - 1.0
        at_row = jnp.where(lane == slot, row, at_row)
        value = jnp.sum(jnp.where(here, gate[...], 0.0), axis=1, keepdims=True)
        gates = jnp.where(lane == slot, value, gates)
    at_row = at_row.astype(BF)
    gate_high = gates.astype(BF)
    slots[:experts, :] = at_row
    slots[experts : 2 * experts, :] = gate_high
    slots[2 * experts :, :] = (gates - gate_high.astype(F32)).astype(BF)
    down = mm(spread_of(experts), at_row)
    r = iota((packed, 128), 0) % PACK
    lane_id = iota((packed, 128), 1)
    patch = (core * rows + iota((packed, rows), 1)).astype(F32)
    for hot, out, side in ((hot_send, send, 1 - core), (hot_keep, keep, core)):
        row = jnp.sum(jnp.where(lane_id == 2 * side + r % 2, down, 0.0), axis=1, keepdims=True)
        hot[...] = jnp.where(row == patch, 1.0, 0.0).astype(BF)
        select(hot, upstream, out)


def attend_kernel(ids, context, weight, after, send, keep, w, sems):
    chunks = cuts(weight.shape[1], 512)
    loads = []
    for i, (lo, hi) in enumerate(chunks):
        loads.append(pltpu.make_async_copy(weight.at[:, lo:hi], w.at[:, lo:hi], sems.at[i]))
        loads[-1].start()
    core = ids[0]
    rows = send.shape[0]
    theirs = context[:, pl.ds(pl.multiple_of((1 - core) * rows, rows), rows)]
    ours = context[:, pl.ds(pl.multiple_of(core * rows, rows), rows)]
    for i, (lo, hi) in enumerate(chunks):
        loads[i].wait()
        send[:, lo:hi] = mm_a(theirs, w[:, lo:hi])
        keep[:, lo:hi] = mm_a(ours, w[:, lo:hi])


def spread_of(experts):
    shape = (experts * PACK, experts)
    return jnp.where(iota(shape, 0) // PACK == iota(shape, 1), 1.0, 0.0).astype(BF)


def merge_kernel(ids, slots, merge_high, merge_low):
    core = ids[0]
    experts = slots.shape[0] // 3
    packed = experts * PACK
    rows = merge_high.shape[0] // 4
    spread = spread_of(experts)
    across = [
        lax.dot_general(
            slots[i * experts : (i + 1) * experts, :],
            spread,
            (((0,), (1,)), ((), ())),
            preferred_element_type=F32,
        )
        for i in range(3)
    ]
    q = iota((128, packed), 1) % PACK
    sub = iota((128, packed), 0)
    own = (core * rows + iota((rows, packed), 0)).astype(F32)
    q_rows = iota((rows, packed), 1) % PACK
    for which, side in ((0, core), (1, 1 - core)):
        slot = 2 * side + q % 2
        row, high, low = (
            jnp.sum(jnp.where(sub == slot, part, 0.0), axis=0, keepdims=True) for part in across
        )
        hot = row == own
        for group in range(4):
            here = hot & (q_rows // 2 == group)
            at = (slice(group * rows, (group + 1) * rows), slice(which * packed, (which + 1) * packed))
            merge_high[at] = jnp.where(here, high, 0.0).astype(BF)
            merge_low[at] = jnp.where(here, low, 0.0).astype(BF)


def statistics(stream):
    mean = jnp.mean(stream, axis=-1, keepdims=True)
    centered = stream - mean
    variance = jnp.mean(centered * centered, axis=-1, keepdims=True)
    return centered, lax.rsqrt(variance + 1e-06)


def norm_kernel(att_keep, att_got, residual, gain, hot_keep, hot_send, stream, keep, send, normed):
    total = residual[...].astype(F32) + (att_keep[...] + att_got[...])
    stream[...] = total
    centered, inverse = statistics(total)
    normed[...] = (gain[...] * centered * inverse).astype(BF)
    select(hot_send, normed, send)
    select(hot_keep, normed, keep)


def unpack_kernel(got, *rest):
    out = rest[-1]
    n = got.shape[0]
    q = iota((n // 4, n), 0)
    for i, (lo, hi) in enumerate(PARTS):
        order = jnp.where(q // 2 * PACK + i * 2 + q % 2 == iota((n // 4, n), 1), 1.0, 0.0).astype(BF)
        out[:, lo:hi] = mm(order, got[:, : hi - lo]).astype(BF)


def stack_kernel(*refs):
    block = refs[0].shape[0]
    for i, ref in enumerate(refs[:-1]):
        refs[-1][i * block : (i + 1) * block, :] = ref[...]


def place(packed):
    q = packed
    return (q % 64 // 2) * PACK + q // 64 * 2 + q % 2


def pack_kernel(own, one, two, out, flat):
    n = out.shape[0]
    quarter = n // 4
    rest = own.shape[1] - WIDE
    total = (own[...] + one[...].astype(F32) + two[...].astype(F32)).astype(BF)
    flat[: 2 * quarter, :] = total[:, :WIDE]
    flat[2 * quarter :, :rest] = total[:, WIDE:]
    flat[2 * quarter :, rest:] = jnp.zeros((2 * quarter, WIDE - rest), BF)
    order = jnp.where(iota((n, n), 0) == place(iota((n, n), 1)), 1.0, 0.0).astype(BF)
    out[...] = mm(order, flat[...]).astype(BF)


def lift_kernel(u, w2, out):
    for lo, hi in cuts(out.shape[1], 256):
        out[:, lo:hi] = mm_t(u[...], w2[lo:hi, :])


def expert(x, lifted, w1, w2, hidden, grad, store):
    for lo, hi in cuts(hidden.shape[1], 256):
        v = mm(x[...], w1[:, lo:hi])
        square = v * v
        t = jnp.tanh(0.7978845608 * v * (1.0 + 0.044715 * square))
        gate = 0.5 + 0.5 * t
        hidden[:, lo:hi] = (v * gate).astype(BF)
        slope = gate + 0.5 * v * (1.0 - t * t) * (0.7978845608 * (1.0 + 0.134145 * square))
        grad[:, lo:hi] = (lifted(lo, hi) * slope).astype(BF)
    for lo, hi in cuts(w2.shape[1], 512):
        store(0, lo, hi, mm(hidden[...], w2[:, lo:hi]))
        store(1, lo, hi, mm_t(grad[...], w1[lo:hi, :]))


def near_kernel(x, lifted, w1, w2, part, hidden, grad):
    rows = x.shape[0]

    def store(stream, lo, hi, value):
        part[stream * rows : (stream + 1) * rows, lo:hi] = value.astype(part.dtype)

    expert(x, lambda lo, hi: lifted[:rows, lo:hi], w1, w2, hidden, grad, store)


def far_kernel(x_keep, x_send, lifted_keep, lifted_send, w1, w2, keep, send, x, hidden, grad, lifted):
    rows = x_keep.shape[0]
    x[:rows, :] = x_keep[...]
    x[rows:, :] = x_send[...]
    lifted[:rows, :] = lifted_keep[-rows:, :]
    lifted[rows:, :] = lifted_send[-rows:, :]

    def store(stream, lo, hi, value):
        at = slice(stream * rows, (stream + 1) * rows)
        keep[at, lo:hi] = value[:rows, :]
        send[at, lo:hi] = value[rows:, :].astype(send.dtype)

    expert(x, lambda lo, hi: lifted[:, lo:hi], w1, w2, hidden, grad, store)


def combine_kernel(keep, got, *outs):
    block = outs[0].shape[0] // 2
    for stream in range(2):
        for i, out in enumerate(outs):
            lo = (stream * len(outs) + i) * block
            at = slice(lo, lo + block)
            total = keep[at, :] + got[at, :].astype(F32)
            out[stream * block : (stream + 1) * block, :] = total.astype(out.dtype)


def add_kernel(a, b, out):
    out[...] = (a[...].astype(F32) + b[...].astype(F32)).astype(BF)


def final_kernel(mine, theirs, merge_high, merge_low, stream, gain, upstream, layer_out, stream_grad, back):
    rows, width = stream.shape
    n = mine.shape[0]
    rest = width - WIDE
    total = stream[...]
    centered, inverse = statistics(total)
    x_hat = centered * inverse
    for group in range(4):
        at = slice(group * rows, (group + 1) * rows)
        summed = mm(merge_high[at, :n], mine[...]) + mm(merge_high[at, n:], theirs[...])
        summed += mm(merge_low[at, :n], mine[...]) + mm(merge_low[at, n:], theirs[...])
        cols = slice(0, WIDE) if group < 2 else slice(WIDE, width)
        summed = summed if group < 2 else summed[:, :rest]
        if group % 2 == 0:
            layer_out[:, cols] = (total[:, cols] + summed).astype(BF)
        else:
            back[:, cols] = summed
    scaled = gain[...] * back[...]
    mean = jnp.mean(scaled, axis=-1, keepdims=True)
    along = jnp.mean(scaled * x_hat, axis=-1, keepdims=True)
    pulled = inverse * (scaled - mean - x_hat * along)
    stream_grad[...] = (upstream[...].astype(F32) + pulled).astype(BF)


def per_device(
    context,
    out_weight,
    residual,
    norm_gain,
    expert_in,
    expert_out,
    patch_index,
    patch_count,
    gate_value,
    upstream,
):
    rows, width = residual.shape
    experts, capacity = patch_index.shape
    shards = lax.axis_size("y")
    packed = experts * PACK
    block = experts * HALF
    units = expert_in.shape[2]
    sds = jax.ShapeDtypeStruct
    core = lax.axis_index("core")
    index = lax.axis_index("xz") * shards + lax.axis_index("y")
    ids = jnp.stack([core, index * (2 * rows)]).astype(I32)
    gain = norm_gain.reshape(1, width)

    def swap_core(x):
        return lax.ppermute(x, "core", [(0, 1), (1, 0)])

    def ring(x, way):
        pairs = []
        for y in range(shards):
            for c in range(2):
                step = way if c == 0 else -way
                pairs.append((y * 2 + c, (y + step) % shards * 2 + c))
        return lax.ppermute(x, ("y", "core"), pairs)

    def exchange(x):
        got = lax.all_to_all(
            x.reshape(experts, PACK, x.shape[1]), "xz", split_axis=0, concat_axis=0, tiled=True
        )
        return got.reshape(x.shape)

    weight_in = expert_in[0]
    weight_out = expert_out[0]
    tall = shards * block
    thin = PARTS[0][1]
    pack_sds = sds((packed, thin), BF)

    def unpack(got, *after):
        out = sds((block, width), BF)
        specs = [VMEM] + [ANY] * len(after)
        return call(unpack_kernel, out, specs, flops=10**8, moved=10**6)(got, *after)

    def stack(*xs):
        out = sds((block * len(xs), width), BF)
        return call(stack_kernel, out, [VMEM] * len(xs), flops=10**5, moved=10**6)(*xs)

    with jax.named_scope("open"):
        hot_keep, hot_send, slots, down_keep, down_send = call(
            open_kernel,
            [sds((packed, rows), BF)] * 2 + [sds((3 * experts, 128), BF)] + [pack_sds] * 2,
            [SMEM] + [VMEM] * 4,
            flops=10**9,
            moved=10**6,
            mib=56,
        )(ids, patch_index, patch_count.reshape(experts, 1), gate_value, upstream)
        down_packed = down_keep + swap_core(down_send)
    with jax.named_scope("attend"):
        att_send, att_keep = call(
            attend_kernel,
            [sds((rows, width), F32)] * 2,
            [SMEM, VMEM, ANY, ANY],
            [pltpu.VMEM(out_weight.shape, BF), pltpu.SemaphoreType.DMA((len(cuts(width, 512)),))],
            flops=4 * rows * width * context.shape[1],
            moved=5 * 10**6,
            mib=56,
        )(ids, context.T, out_weight, slots)
        att_got = swap_core(att_send)
    with jax.named_scope("norm"):
        stream, keep, send = call(
            norm_kernel,
            [sds((rows, width), F32)] + [pack_sds] * 2,
            [VMEM] * 6,
            [pltpu.VMEM((rows, width), BF)],
            flops=10**9,
            moved=3 * 10**6,
        )(att_keep, att_got, residual, gain, hot_keep, hot_send)
    with jax.named_scope("dispatch_normed"):
        packed_rows = keep + swap_core(send)
        own = unpack(exchange(packed_rows))
    with jax.named_scope("dispatch_down"):
        down_rows = unpack(exchange(down_packed), packed_rows)
    with jax.named_scope("merge"):
        merge_high, merge_low = call(
            merge_kernel,
            [sds((4 * rows, 2 * packed), BF)] * 2,
            [SMEM, VMEM],
            flops=10**8,
            moved=10**6,
        )(ids, slots)

    def lift(u):
        return call(
            lift_kernel,
            sds((tall, units), F32),
            [VMEM] * 2,
            flops=4 * tall * width * units,
            moved=6 * 10**6,
            mib=16,
        )(u, weight_out)

    def near_part(x, lifted, kind):
        tall = x.shape[0]
        return call(
            near_kernel,
            sds((2 * tall, width), kind),
            [VMEM] * 4,
            [pltpu.VMEM((tall, units), BF)] * 2,
            flops=20 * tall * width * units,
            moved=10**7,
            mib=20,
        )(x, lifted, weight_in, weight_out)

    with jax.named_scope("gather_down"):
        down_one = ring(down_rows, 1)
        down_two = ring(down_rows, -1)
        down_far = ring(down_one, 1)
        downs = stack(down_rows, down_one, down_two, down_far)
        lifted_send = lift(swap_core(downs))
        lifted_keep = lift(downs)
    with jax.named_scope("gather_normed"):
        one = ring(own, 1)
        two = ring(own, -1)
        far = ring(one, 1)
        near = stack(own, one, two)
        near_send = swap_core(near)
        far_send = swap_core(far)
    pair = (2 * block, width)
    with jax.named_scope("experts"):
        near_keep = near_part(near, lifted_keep, F32)
        near_got = swap_core(near_part(near_send, lifted_send, BF))
        far_keep, far_out = call(
            far_kernel,
            [sds(pair, F32), sds(pair, BF)],
            [VMEM] * 6,
            [pltpu.VMEM(pair, BF)]
            + [pltpu.VMEM((2 * block, units), BF)] * 2
            + [pltpu.VMEM((2 * block, units), F32)],
            flops=40 * block * width * units,
            moved=10**7,
            mib=20,
        )(far, far_send, lifted_keep, lifted_send, weight_in, weight_out)
        far_got = swap_core(far_out)
    with jax.named_scope("reduce"):

        def combine(keep, got, *kinds):
            outs = [sds(pair, kind) for kind in kinds]
            return call(combine_kernel, outs, [VMEM] * 2, flops=10**6, moved=10**6)(keep, got)

        own_sum, one_sum, two_sum = combine(near_keep, near_got, F32, F32, BF)
        (far_sum,) = combine(far_keep, far_got, BF)
        from_far = ring(far_sum, -1)
        from_two = ring(two_sum, 1)
        one_sum = call(add_kernel, sds(pair, BF), [VMEM] * 2, flops=10**5, moved=10**6)(one_sum, from_far)
        from_one = ring(one_sum, -1)
    with jax.named_scope("collect"):
        ready = call(
            pack_kernel,
            sds((packed, WIDE), BF),
            [VMEM] * 3,
            [pltpu.VMEM((packed, WIDE), BF)],
            flops=10**8,
            moved=10**6,
        )(own_sum, from_one, from_two)
        mine = exchange(ready)
        theirs = swap_core(mine)
    with jax.named_scope("final"):
        layer_out, stream_grad = call(
            final_kernel,
            [sds((rows, width), BF)] * 2,
            [VMEM] * 7,
            [pltpu.VMEM((rows, width), F32)],
            flops=10**9,
            moved=4 * 10**6,
        )(mine, theirs, merge_high, merge_low, stream, gain, upstream)
    return (layer_out, stream_grad)


def solution(mesh):
    sizes = mesh.devices.shape
    shards = 4
    split = Mesh(
        mesh.devices.reshape(sizes[0] // shards, shards, sizes[1]), ("xz", "y", "core")
    )
    return jax.shard_map(
        per_device,
        mesh=split,
        in_specs=(
            P(("xz", "y"), "core"),
            P("core", None),
            P(("xz", "y", "core"), None),
            P(),
            P(("xz", "y"), None, "core"),
            P(("xz", "y"), "core", None),
            P(),
            P(),
            P(),
            P(("xz", "y", "core"), None),
        ),
        out_specs=(P(("xz", "y", "core"), None), P(("xz", "y", "core"), None)),
        check_vma=False,
    )
```

time: 122 us -> 132 us (1.082)
  blocking collectives: 41.1 us -> 20 us
  waiting for transfers between devices: 19.1 us -> 34.9 us
  starting transfers between devices: 35.8 us -> 44.5 us
  Pallas kernels: 19 us -> 24.4 us
  other arithmetic: 0.15 us -> 2.11 us
    all_to_all x2 -> x1, blocking collectives: 41.1 us -> 20 us  [exchange(): lax.all_to_all(x.reshape(experts, PACK, x.shape[1]), 'xz', split_axis=0,...]
    all_to_all x0 -> x2, starting transfers between devices: none -> 16 us  [exchange(): lax.all_to_all(x.reshape(experts, PACK, x.shape[1]), 'xz', split_axis=0,...]
    ppermute x12 -> x9, waiting for transfers between devices: 15.4 us -> 23.8 us  [ring(): return lax.ppermute(x, ('y', 'core'), pairs)]
    all_to_all x0 -> x2, waiting for transfers between devices: none -> 5.99 us  [exchange(): lax.all_to_all(x.reshape(experts, PACK, x.shape[1]), 'xz', split_axis=0,...]
    pallas_call x13 -> x16, Pallas kernels: 15.6 us -> 21 us  [the longest x2 5.78 us: near_part(): call(near_kernel, sds((2 * tall, width), kind), [VMEM] * 4, [pltpu.VMEM((...]
    ppermute x12 -> x9, starting transfers between devices: 17.3 us -> 12.8 us  [ring(): return lax.ppermute(x, ('y', 'core'), pairs)]
    ppermute x13 -> x9, starting transfers between devices: 18.5 us -> 15.7 us  [swap_core(): return lax.ppermute(x, 'core', [(0, 1), (1, 0)])]
    ppermute x13 -> x9, waiting for transfers between devices: 3.75 us -> 5.12 us  [swap_core(): return lax.ppermute(x, 'core', [(0, 1), (1, 0)])]
  transfers between devices with their start and end apart: 25 -> 20, of which waited for: 8 -> 13; matrix products, arithmetic and copies ran while one was open for 0% -> 1% of each run, Pallas kernels for 10% -> 10%
where the time goes in v4:
time: 132 us; the launch traced here: 131 us
  starting transfers between devices  44.5 us (34%)
  waiting for transfers between devices  34.9 us (26%)
  Pallas kernels  24.4 us (18%)
  blocking collectives  20 us (15%)
  local copies, waits for them, and re-layouts  4.5 us (3%)
  other arithmetic  2.11 us (2%)
    ppermute x9, waiting for transfers between devices, ring(): return lax.ppermute(x, ('y', 'core'), pairs)  23.8 us
    all_to_all x1, blocking collectives, exchange(): lax.all_to_all(x.reshape(experts, PACK, x.shape[1]), 'xz', split_axis=0,...  20 us
    all_to_all x2, starting transfers between devices, exchange(): lax.all_to_all(x.reshape(experts, PACK, x.shape[1]), 'xz', split_axis=0,...  16 us
    ppermute x9, starting transfers between devices, swap_core(): return lax.ppermute(x, 'core', [(0, 1), (1, 0)])  15.7 us
    ppermute x9, starting transfers between devices, ring(): return lax.ppermute(x, ('y', 'core'), pairs)  12.8 us
    all_to_all x2, waiting for transfers between devices, exchange(): lax.all_to_all(x.reshape(experts, PACK, x.shape[1]), 'xz', split_axis=0,...  5.99 us
    pallas_call x2, Pallas kernels, near_part(): call(near_kernel, sds((2 * tall, width), kind), [VMEM] * 4, [pltpu.VMEM((...  5.78 us
    ppermute x9, waiting for transfers between devices, swap_core(): return lax.ppermute(x, 'core', [(0, 1), (1, 0)])  5.12 us
  transfers between devices with their start and end apart: 20, of which 13 were waited for; matrix products, arithmetic and copies ran while one was open for 1% of the time, Pallas kernels for 10%

profile of v4, /device:TPU:1, one launch (start us, length us, event | category | flops | bytes accessed | tf_op | source)
XLA Modules:
  0.0 131.3 jit_solution(8153437163272643408)
XLA Ops:
  0.6 1.3 %copy.12.count = s32[32,1]{1,0:T(8,128)} copy(s32[32,1]{0,1:T(1,128)} %bitcast.27) | data formatting | bytes 256 | tf_op jit(solution)/shard_map/open/reshape | solution.py:345
  2.6 3.1 %open.1 = (bf16[256,128]{1,0:T(8,128)(2,1)}, bf16[256,128]{1,0:T(8,128)(2,1)}, bf16[96,128]{1,0:T(8,128)(2,1)}, bf16[256,512]{1,0:T(8,128)(2,1)}, bf16[256,512]{1,0:T(8,128)(2,1)}) custom-call(s32[2]{0:T(128)} %pad_add_fusion.ids, s32[32,512]{1,0:T(8,128)} %index.1, s32[32,1]{1,0:T(8,128)} %copy.12.count, f32[32,512]{1,0:T(8,128)} %gate.1, ...), custom_call_target="tpu_custom_call" | custom-call | flops 1000000000 | bytes 1000000 | tf_op jit(solution)/shard_map/open/pallas_call | solution.py:338
  5.7 5.1 %attend.1 = (f32[128,1664]{1,0:T(8,128)}, f32[128,1664]{1,0:T(8,128)}) custom-call(s32[2]{0:T(128)} %pad_add_fusion.ids, bf16[832,256]{1,0:T(8,128)(2,1)} %bitcast.26, bf16[832,1664]{1,0:T(8,128)(2,1)} %weight.1, bf16[96,128]{1,0:T(8,128)(2,1)} %get-tuple-element.19.after.slots), custom_call_target="tpu_custom_call" | custom-call | flops 708837376 | bytes 5000000 | tf_op jit(solution)/shard_map/attend/pallas_call | solution.py:348
  10.8 3.3 %collective-permute-start = (f32[128,1664]{1,0:T(8,128)}, f32[128,1664]{1,0:T(8,128)S(1)}, u32[]{:S(2)}, u32[]{:S(2)}) collective-permute-start(f32[128,1664]{1,0:T(8,128)} %get-tuple-element.21), channel_id=1, source_target_pairs={{0,1},{1,0},{2,3},{3,2},{4,5},{5,4},{6,7},{7,6},{8,9},{9,8},{10,11... | collective-permute-start | bytes 2555912 | tf_op jit(solution)/shard_map/attend/ppermute | solution.py:306
  14.2 2.3 %collective-permute-done.4 = bf16[256,512]{1,0:T(8,128)(2,1)S(1)} collective-permute-done((bf16[256,512]{1,0:T(8,128)(2,1)S(1)}, bf16[256,512]{1,0:T(8,128)(2,1)S(1)}, u32[]{:S(2)}, u32[]{:S(2)}) %collective-permute-start.4) | collective-permute-done | bytes 262176 | tf_op jit(solution)/shard_map/open/ppermute | solution.py:306
  17.2 9.3 %all-to-all-start.1 = ((bf16[32,8,512]{2,1,0:T(8,128)(2,1)}), bf16[32,8,512]{2,1,0:T(8,128)(2,1)S(1)}, u32[]{:S(2)}, u32[]{:S(2)}) async-start(bf16[32,8,512]{2,1,0:T(8,128)(2,1)} %add_bitcast_fusion), calls=%async_computation.1 | async-start | bytes 524288 | tf_op jit(solution)/shard_map/dispatch_down/all_to_all | solution.py:317
  29.4 1.2 collective-permute-done.1
  31.4 4.8 %all-to-all-done.1 = bf16[32,8,512]{2,1,0:T(8,128)(2,1)S(1)} async-done(((bf16[32,8,512]{2,1,0:T(8,128)(2,1)}), bf16[32,8,512]{2,1,0:T(8,128)(2,1)S(1)}, u32[]{:S(2)}, u32[]{:S(2)}) %all-to-all-start.1) | async-done | bytes 262176 | tf_op jit(solution)/shard_map/dispatch_down/all_to_all | solution.py:317
  36.5 2.8 %collective-permute-start.5 = (bf16[64,1664]{1,0:T(8,128)(2,1)S(1)}, bf16[64,1664]{1,0:T(8,128)(2,1)S(1)}, u32[]{:S(2)}, u32[]{:S(2)}) collective-permute-start(bf16[64,1664]{1,0:T(8,128)(2,1)S(1)} %dispatch_down.1.refs_0_), channel_id=1, source_target_pairs={{0,2},{1,7},{2,4},{3,1},{4,6},{5,3},{6,0},{7,5},{8,10},{9,15},{10,... | collective-permute-start | bytes 638984 | tf_op jit(solution)/shard_map/gather_down/ppermute | solution.py:314
  39.3 6.7 %all-to-all-start = ((bf16[32,8,512]{2,1,0:T(8,128)(2,1)}), bf16[32,8,512]{2,1,0:T(8,128)(2,1)S(1)}, u32[]{:S(2)}, u32[]{:S(2)}) async-start(bf16[32,8,512]{2,1,0:T(8,128)(2,1)} %bitcast.4), calls=%async_computation | async-start | bytes 524288 | tf_op jit(solution)/shard_map/dispatch_normed/all_to_all | solution.py:317
  46.1 2.7 %collective-permute-start.7 = (bf16[64,1664]{1,0:T(8,128)(2,1)S(1)}, bf16[64,1664]{1,0:T(8,128)(2,1)S(1)}, u32[]{:S(2)}, u32[]{:S(2)}) collective-permute-start(bf16[64,1664]{1,0:T(8,128)(2,1)S(1)} %collective-permute-done.5.refs_1_), channel_id=1, source_target_pairs={{0,2},{1,7},{2,4},{3,1},{4,6},{5,3},{6,0},{7,5},{8,10},{9,15},{10,... | collective-permute-start | bytes 638984 | tf_op jit(solution)/shard_map/gather_down/ppermute | solution.py:314
  48.8 3.2 %collective-permute-done.6.refs_2_ = bf16[64,1664]{1,0:T(8,128)(2,1)S(1)} collective-permute-done((bf16[64,1664]{1,0:T(8,128)(2,1)S(1)}, bf16[64,1664]{1,0:T(8,128)(2,1)S(1)}, u32[]{:S(2)}, u32[]{:S(2)}) %collective-permute-start.6) | collective-permute-done | bytes 213024 | tf_op jit(solution)/shard_map/gather_down/ppermute | solution.py:314
  52.0 1.3 collective-permute-done.7.refs_3_
  53.3 1.9 %collective-permute-start.9 = (bf16[256,1664]{1,0:T(8,128)(2,1)S(1)}, bf16[256,1664]{1,0:T(8,128)(2,1)S(1)}, u32[]{:S(2)}, u32[]{:S(2)}) collective-permute-start(bf16[256,1664]{1,0:T(8,128)(2,1)S(1)} %gather_down.3.u), channel_id=1, source_target_pairs={{0,1},{1,0},{2,3},{3,2},{4,5},{5,4},{6,7},{7,6},{8,9},{9,8},{10,11... | collective-permute-start | bytes 2555912 | tf_op jit(solution)/shard_map/gather_down/ppermute | solution.py:306
  58.2 3.2 %collective-permute-done.2.refs_1_ = bf16[64,1664]{1,0:T(8,128)(2,1)S(1)} collective-permute-done((bf16[64,1664]{1,0:T(8,128)(2,1)S(1)}, bf16[64,1664]{1,0:T(8,128)(2,1)S(1)}, u32[]{:S(2)}, u32[]{:S(2)}) %collective-permute-start.2) | collective-permute-done | bytes 213024 | tf_op jit(solution)/shard_map/gather_normed/ppermute | solution.py:314
  61.4 2.0 %collective-permute-done.3.refs_2_ = bf16[64,1664]{1,0:T(8,128)(2,1)S(1)} collective-permute-done((bf16[64,1664]{1,0:T(8,128)(2,1)S(1)}, bf16[64,1664]{1,0:T(8,128)(2,1)S(1)}, u32[]{:S(2)}, u32[]{:S(2)}) %collective-permute-start.3) | collective-permute-done | bytes 213024 | tf_op jit(solution)/shard_map/gather_normed/ppermute | solution.py:314
  63.4 2.8 %collective-permute-start.8 = (bf16[192,1664]{1,0:T(8,128)(2,1)S(1)}, bf16[192,1664]{1,0:T(8,128)(2,1)S(1)}, u32[]{:S(2)}, u32[]{:S(2)}) collective-permute-start(bf16[192,1664]{1,0:T(8,128)(2,1)S(1)} %gather_normed.1.x), channel_id=1, source_target_pairs={{0,1},{1,0},{2,3},{3,2},{4,5},{5,4},{6,7},{7,6},{8,9},{9,8},{10,11... | collective-permute-start | bytes 1916936 | tf_op jit(solution)/shard_map/gather_normed/ppermute | solution.py:306
  66.2 2.9 %collective-permute-start.11 = (bf16[64,1664]{1,0:T(8,128)(2,1)S(1)}, bf16[64,1664]{1,0:T(8,128)(2,1)S(1)}, u32[]{:S(2)}, u32[]{:S(2)}) collective-permute-start(bf16[64,1664]{1,0:T(8,128)(2,1)S(1)} %collective-permute-done.2.refs_1_), channel_id=1, source_target_pairs={{0,2},{1,7},{2,4},{3,1},{4,6},{5,3},{6,0},{7,5},{8,10},{9,15},{10,... | collective-permute-start | bytes 638984 | tf_op jit(solution)/shard_map/gather_normed/ppermute | solution.py:314
  69.1 2.0 %copy-done.2 = bf16[1,1024,1664]{2,1,0:T(8,128)(2,1)S(1)} copy-done((bf16[1,1024,1664]{2,1,0:T(8,128)(2,1)S(1)}, bf16[1,1024,1664]{2,1,0:T(8,128)(2,1)}, u32[]{:S(2)}) %copy-start.2) | copy-done | bytes 3407896
  72.2 1.3 %collective-permute-start.12 = (bf16[64,1664]{1,0:T(8,128)(2,1)S(1)}, bf16[64,1664]{1,0:T(8,128)(2,1)S(1)}, u32[]{:S(2)}, u32[]{:S(2)}) collective-permute-start(bf16[64,1664]{1,0:T(8,128)(2,1)S(1)} %collective-permute-done.11.x_keep), channel_id=1, source_target_pairs={{0,1},{1,0},{2,3},{3,2},{4,5},{5,4},{6,7},{7,6},{8,9},{9,8},{10,11... | collective-permute-start | bytes 638984 | tf_op jit(solution)/shard_map/gather_normed/ppermute | solution.py:306
  74.7 2.9 %experts.4 = bf16[384,1664]{1,0:T(8,128)(2,1)S(1)} custom-call(bf16[192,1664]{1,0:T(8,128)(2,1)S(1)} %collective-permute-done.8.x, f32[256,1024]{1,0:T(8,128)S(1)} %gather_down.5.lifted.lifted_send, bf16[1664,1024]{1,0:T(8,128)(2,1)S(1)} %bitcast.23, bf16[1024,1664]{1,0:T(8,128)(2,1)S(1)} %bitcast.20), custom_call_target="tpu_custom_call" | custom-call | flops 6543114240 | bytes 10000000 | tf_op jit(solution)/shard_map/experts/pallas_call | solution.py:393
  77.7 2.5 %experts.5 = (f32[128,1664]{1,0:T(8,128)S(1)}, bf16[128,1664]{1,0:T(8,128)(2,1)S(1)}) custom-call(bf16[64,1664]{1,0:T(8,128)(2,1)S(1)} %collective-permute-done.11.x_keep, bf16[64,1664]{1,0:T(8,128)(2,1)S(1)} %collective-permute-done.12.x_send, f32[256,1024]{1,0:T(8,128)S(1)} %gather_down.4.lifted.lifted_keep, ...), custom_call_target="tpu_custom_call" | custom-call | flops 4362076160 | bytes 10000000 | tf_op jit(solution)/shard_map/experts/pallas_call | solution.py:421
  80.8 1.4 %collective-permute-done.13.got = bf16[128,1664]{1,0:T(8,128)(2,1)S(1)} collective-permute-done((bf16[128,1664]{1,0:T(8,128)(2,1)S(1)}, bf16[128,1664]{1,0:T(8,128)(2,1)S(1)}, u32[]{:S(2)}, u32[]{:S(2)}) %collective-permute-start.13) | collective-permute-done | bytes 426016 | tf_op jit(solution)/shard_map/experts/ppermute | solution.py:306
  82.4 2.9 %experts.3.keep = f32[384,1664]{1,0:T(8,128)S(1)} custom-call(bf16[192,1664]{1,0:T(8,128)(2,1)S(1)} %gather_normed.1.x, f32[256,1024]{1,0:T(8,128)S(1)} %gather_down.4.lifted.lifted_keep, bf16[1664,1024]{1,0:T(8,128)(2,1)S(1)} %bitcast.25, bf16[1024,1664]{1,0:T(8,128)(2,1)S(1)} %bitcast.22), custom_call_target="tpu_custom_call" | custom-call | flops 6543114240 | bytes 10000000 | tf_op jit(solution)/shard_map/experts/pallas_call | solution.py:393
  85.5 5.0 %collective-permute-done.14.b = bf16[128,1664]{1,0:T(8,128)(2,1)S(1)} collective-permute-done((bf16[128,1664]{1,0:T(8,128)(2,1)S(1)}, bf16[128,1664]{1,0:T(8,128)(2,1)S(1)}, u32[]{:S(2)}, u32[]{:S(2)}) %collective-permute-start.14) | collective-permute-done | bytes 426016 | tf_op jit(solution)/shard_map/reduce/ppermute | solution.py:314
  90.7 2.7 %collective-permute-start.16 = (bf16[128,1664]{1,0:T(8,128)(2,1)S(1)}, bf16[128,1664]{1,0:T(8,128)(2,1)S(1)}, u32[]{:S(2)}, u32[]{:S(2)}) collective-permute-start(bf16[128,1664]{1,0:T(8,128)(2,1)S(1)} %get-tuple-element.32), channel_id=1, source_target_pairs={{0,2},{1,7},{2,4},{3,1},{4,6},{5,3},{6,0},{7,5},{8,10},{9,15},{10,... | collective-permute-start | bytes 1277960 | tf_op jit(solution)/shard_map/reduce/ppermute | solution.py:314
  93.4 6.4 %collective-permute-done.15.one = bf16[128,1664]{1,0:T(8,128)(2,1)S(1)} collective-permute-done((bf16[128,1664]{1,0:T(8,128)(2,1)S(1)}, bf16[128,1664]{1,0:T(8,128)(2,1)S(1)}, u32[]{:S(2)}, u32[]{:S(2)}) %collective-permute-start.15) | collective-permute-done | bytes 426016 | tf_op jit(solution)/shard_map/reduce/ppermute | solution.py:314
  99.7 2.7 %collective-permute-done.16.two = bf16[128,1664]{1,0:T(8,128)(2,1)S(1)} collective-permute-done((bf16[128,1664]{1,0:T(8,128)(2,1)S(1)}, bf16[128,1664]{1,0:T(8,128)(2,1)S(1)}, u32[]{:S(2)}, u32[]{:S(2)}) %collective-permute-start.16) | collective-permute-done | bytes 426016 | tf_op jit(solution)/shard_map/reduce/ppermute | solution.py:314
  102.8 20.0 %all_to_all.15 = bf16[32,8,896]{2,1,0:T(8,128)(2,1)S(1)} all-to-all(bf16[32,8,896]{2,1,0:T(8,128)(2,1)S(1)} %bitcast.13), channel_id=1, replica_groups=mesh['xz'=32,'y'=4,'core'=2] {'xz'}, dimensions={0} | all-to-all | bytes 917504 | tf_op jit(solution)/shard_map/collect/all_to_all | solution.py:317
  122.8 4.8 %collective-permute-start.17 = (bf16[256,896]{1,0:T(8,128)(2,1)S(1)}, bf16[256,896]{1,0:T(8,128)(2,1)S(1)}, u32[]{:S(2)}, u32[]{:S(2)}) collective-permute-start(bf16[256,896]{1,0:T(8,128)(2,1)S(1)} %bitcast.16), channel_id=1, source_target_pairs={{0,1},{1,0},{2,3},{3,2},{4,5},{5,4},{6,7},{7,6},{8,9},{9,8},{10,11... | collective-permute-start | bytes 1376264 | tf_op jit(solution)/shard_map/collect/ppermute | solution.py:306
  127.6 1.2 merge.1
  129.1 2.2 %final.1 = (bf16[128,1664]{1,0:T(8,128)(2,1)}, bf16[128,1664]{1,0:T(8,128)(2,1)}) custom-call(bf16[256,896]{1,0:T(8,128)(2,1)S(1)} %bitcast.17, bf16[256,896]{1,0:T(8,128)(2,1)S(1)} %collective-permute-done.17.theirs, bf16[512,512]{1,0:T(8,128)(2,1)S(1)} %get-tuple-element.33.merge_high, bf16[512,512]{1,0:T(8,128)(2,1)S(1)} %get-tuple-element.34.merge_low, ...), custom_call_target="tpu_custom_call" | custom-call | flops 1000000000 | bytes 4000000 | tf_op jit(solution)/shard_map/final/pallas_call | solution.py:457
  (58 shorter events, 12.6 us)
Async XLA Ops:
  5.7 8.5 %copy-start.12 = (bf16[256,512]{1,0:T(8,128)(2,1)S(1)}, bf16[256,512]{1,0:T(8,128)(2,1)}, u32[]{:S(2)}) copy-start(bf16[256,512]{1,0:T(8,128)(2,1)} %get-tuple-element.27) | copy-start | bytes 786436
  5.7 10.8 %copy-start.10 = (bf16[256,512]{1,0:T(8,128)(2,1)S(1)}, bf16[256,512]{1,0:T(8,128)(2,1)}, u32[]{:S(2)}) copy-start(bf16[256,512]{1,0:T(8,128)(2,1)} %get-tuple-element.26) | copy-start | bytes 786436
  5.7 20.9 %copy-start.11 = (f32[1664]{0:T(1024)S(1)}, f32[1664]{0:T(1024)}, u32[]{:S(2)}) copy-start(f32[1664]{0:T(1024)} %param.13) | copy-start | bytes 19972
  5.7 20.9 %copy-start.6 = (bf16[128,1664]{1,0:T(8,128)(2,1)S(1)}, bf16[128,1664]{1,0:T(8,128)(2,1)}, u32[]{:S(2)}) copy-start(bf16[128,1664]{1,0:T(8,128)(2,1)} %residual.1) | copy-start | bytes 1277956
  5.7 20.9 %copy-start.8 = (bf16[256,128]{1,0:T(8,128)(2,1)S(1)}, bf16[256,128]{1,0:T(8,128)(2,1)}, u32[]{:S(2)}) copy-start(bf16[256,128]{1,0:T(8,128)(2,1)} %get-tuple-element.22.hot_keep) | copy-start | bytes 196612
  5.7 20.9 %copy-start.9 = (bf16[256,128]{1,0:T(8,128)(2,1)S(1)}, bf16[256,128]{1,0:T(8,128)(2,1)}, u32[]{:S(2)}) copy-start(bf16[256,128]{1,0:T(8,128)(2,1)} %get-tuple-element.23.hot_send) | copy-start | bytes 196612
  10.8 15.8 %collective-permute-start = (f32[128,1664]{1,0:T(8,128)}, f32[128,1664]{1,0:T(8,128)S(1)}, u32[]{:S(2)}, u32[]{:S(2)}) collective-permute-start(f32[128,1664]{1,0:T(8,128)} %get-tuple-element.21), channel_id=1, source_target_pairs={{0,1},{1,0},{2,3},{3,2},{4,5},{5,4},{6,7},{7,6},{8,9},{9,8},{10,11... | collective-permute-start | bytes 2555912 | tf_op jit(solution)/shard_map/attend/ppermute | solution.py:306
  14.1 2.4 %collective-permute-start.4 = (bf16[256,512]{1,0:T(8,128)(2,1)S(1)}, bf16[256,512]{1,0:T(8,128)(2,1)S(1)}, u32[]{:S(2)}, u32[]{:S(2)}) collective-permute-start(bf16[256,512]{1,0:T(8,128)(2,1)S(1)} %copy-done.12), channel_id=1, source_target_pairs={{0,1},{1,0},{2,3},{3,2},{4,5},{5,4},{6,7},{7,6},{8,9},{9,8},{10,11... | collective-permute-start | bytes 786440 | tf_op jit(solution)/shard_map/open/ppermute | solution.py:306
  17.2 19.0 %all-to-all-start.1 = ((bf16[32,8,512]{2,1,0:T(8,128)(2,1)}), bf16[32,8,512]{2,1,0:T(8,128)(2,1)S(1)}, u32[]{:S(2)}, u32[]{:S(2)}) async-start(bf16[32,8,512]{2,1,0:T(8,128)(2,1)} %add_bitcast_fusion), calls=%async_computation.1 | async-start | bytes 524288 | tf_op jit(solution)/shard_map/dispatch_down/all_to_all | solution.py:317
  28.7 1.9 %collective-permute-start.1 = (bf16[256,512]{1,0:T(8,128)(2,1)S(1)}, bf16[256,512]{1,0:T(8,128)(2,1)S(1)}, u32[]{:S(2)}, u32[]{:S(2)}) collective-permute-start(bf16[256,512]{1,0:T(8,128)(2,1)S(1)} %get-tuple-element.25), channel_id=1, source_target_pairs={{0,1},{1,0},{2,3},{3,2},{4,5},{5,4},{6,7},{7,6},{8,9},{9,8},{10,11... | collective-permute-start | bytes 786440 | tf_op jit(solution)/shard_map/dispatch_normed/ppermute | solution.py:306
  36.5 9.6 %collective-permute-start.5 = (bf16[64,1664]{1,0:T(8,128)(2,1)S(1)}, bf16[64,1664]{1,0:T(8,128)(2,1)S(1)}, u32[]{:S(2)}, u32[]{:S(2)}) collective-permute-start(bf16[64,1664]{1,0:T(8,128)(2,1)S(1)} %dispatch_down.1.refs_0_), channel_id=1, source_target_pairs={{0,2},{1,7},{2,4},{3,1},{4,6},{5,3},{6,0},{7,5},{8,10},{9,15},{10,... | collective-permute-start | bytes 638984 | tf_op jit(solution)/shard_map/gather_down/ppermute | solution.py:314
  39.3 17.1 %all-to-all-start = ((bf16[32,8,512]{2,1,0:T(8,128)(2,1)}), bf16[32,8,512]{2,1,0:T(8,128)(2,1)S(1)}, u32[]{:S(2)}, u32[]{:S(2)}) async-start(bf16[32,8,512]{2,1,0:T(8,128)(2,1)} %bitcast.4), calls=%async_computation | async-start | bytes 524288 | tf_op jit(solution)/shard_map/dispatch_normed/all_to_all | solution.py:317
  46.0 6.0 %collective-permute-start.6 = (bf16[64,1664]{1,0:T(8,128)(2,1)S(1)}, bf16[64,1664]{1,0:T(8,128)(2,1)S(1)}, u32[]{:S(2)}, u32[]{:S(2)}) collective-permute-start(bf16[64,1664]{1,0:T(8,128)(2,1)S(1)} %dispatch_down.1.refs_0_), channel_id=1, source_target_pairs={{0,6},{1,3},{2,0},{3,5},{4,2},{5,7},{6,4},{7,1},{8,14},{9,11},{10,... | collective-permute-start | bytes 638984 | tf_op jit(solution)/shard_map/gather_down/ppermute | solution.py:314
  46.1 7.1 %collective-permute-start.7 = (bf16[64,1664]{1,0:T(8,128)(2,1)S(1)}, bf16[64,1664]{1,0:T(8,128)(2,1)S(1)}, u32[]{:S(2)}, u32[]{:S(2)}) collective-permute-start(bf16[64,1664]{1,0:T(8,128)(2,1)S(1)} %collective-permute-done.5.refs_1_), channel_id=1, source_target_pairs={{0,2},{1,7},{2,4},{3,1},{4,6},{5,3},{6,0},{7,5},{8,10},{9,15},{10,... | collective-permute-start | bytes 638984 | tf_op jit(solution)/shard_map/gather_down/ppermute | solution.py:314
  53.3 20.2 %collective-permute-start.9 = (bf16[256,1664]{1,0:T(8,128)(2,1)S(1)}, bf16[256,1664]{1,0:T(8,128)(2,1)S(1)}, u32[]{:S(2)}, u32[]{:S(2)}) collective-permute-start(bf16[256,1664]{1,0:T(8,128)(2,1)S(1)} %gather_down.3.u), channel_id=1, source_target_pairs={{0,1},{1,0},{2,3},{3,2},{4,5},{5,4},{6,7},{7,6},{8,9},{9,8},{10,11... | collective-permute-start | bytes 2555912 | tf_op jit(solution)/shard_map/gather_down/ppermute | solution.py:306
  56.6 4.8 %collective-permute-start.2 = (bf16[64,1664]{1,0:T(8,128)(2,1)S(1)}, bf16[64,1664]{1,0:T(8,128)(2,1)S(1)}, u32[]{:S(2)}, u32[]{:S(2)}) collective-permute-start(bf16[64,1664]{1,0:T(8,128)(2,1)S(1)} %dispatch_normed.1.refs_0_), channel_id=1, source_target_pairs={{0,2},{1,7},{2,4},{3,1},{4,6},{5,3},{6,0},{7,5},{8,10},{9,15},{10,... | collective-permute-start | bytes 638984 | tf_op jit(solution)/shard_map/gather_normed/ppermute | solution.py:314
  57.2 6.2 %collective-permute-start.3 = (bf16[64,1664]{1,0:T(8,128)(2,1)S(1)}, bf16[64,1664]{1,0:T(8,128)(2,1)S(1)}, u32[]{:S(2)}, u32[]{:S(2)}) collective-permute-start(bf16[64,1664]{1,0:T(8,128)(2,1)S(1)} %dispatch_normed.1.refs_0_), channel_id=1, source_target_pairs={{0,6},{1,3},{2,0},{3,5},{4,2},{5,7},{6,4},{7,1},{8,14},{9,11},{10,... | collective-permute-start | bytes 638984 | tf_op jit(solution)/shard_map/gather_normed/ppermute | solution.py:314
  63.4 11.2 %collective-permute-start.8 = (bf16[192,1664]{1,0:T(8,128)(2,1)S(1)}, bf16[192,1664]{1,0:T(8,128)(2,1)S(1)}, u32[]{:S(2)}, u32[]{:S(2)}) collective-permute-start(bf16[192,1664]{1,0:T(8,128)(2,1)S(1)} %gather_normed.1.x), channel_id=1, source_target_pairs={{0,1},{1,0},{2,3},{3,2},{4,5},{5,4},{6,7},{7,6},{8,9},{9,8},{10,11... | collective-permute-start | bytes 1916936 | tf_op jit(solution)/shard_map/gather_normed/ppermute | solution.py:306
  66.2 6.0 %collective-permute-start.11 = (bf16[64,1664]{1,0:T(8,128)(2,1)S(1)}, bf16[64,1664]{1,0:T(8,128)(2,1)S(1)}, u32[]{:S(2)}, u32[]{:S(2)}) collective-permute-start(bf16[64,1664]{1,0:T(8,128)(2,1)S(1)} %collective-permute-done.2.refs_1_), channel_id=1, source_target_pairs={{0,2},{1,7},{2,4},{3,1},{4,6},{5,3},{6,0},{7,5},{8,10},{9,15},{10,... | collective-permute-start | bytes 638984 | tf_op jit(solution)/shard_map/gather_normed/ppermute | solution.py:314
  69.1 2.0 %copy-start.2 = (bf16[1,1024,1664]{2,1,0:T(8,128)(2,1)S(1)}, bf16[1,1024,1664]{2,1,0:T(8,128)(2,1)}, u32[]{:S(2)}) copy-start(bf16[1,1024,1664]{2,1,0:T(8,128)(2,1)} %param.15) | copy-start | bytes 10223620
  71.0 2.5 %copy-start.3 = (bf16[1,1024,1664]{2,1,0:T(8,128)(2,1)S(1)}, bf16[1,1024,1664]{2,1,0:T(8,128)(2,1)}, u32[]{:S(2)}) copy-start(bf16[1,1024,1664]{2,1,0:T(8,128)(2,1)} %param.15) | copy-start | bytes 10223620
  72.2 2.5 %copy-start.4 = (bf16[1,1664,1024]{2,1,0:T(8,128)(2,1)S(1)}, bf16[1,1664,1024]{2,1,0:T(8,128)(2,1)}, u32[]{:S(2)}) copy-start(bf16[1,1664,1024]{2,1,0:T(8,128)(2,1)} %param.14) | copy-start | bytes 10223620
  72.2 5.5 %collective-permute-start.12 = (bf16[64,1664]{1,0:T(8,128)(2,1)S(1)}, bf16[64,1664]{1,0:T(8,128)(2,1)S(1)}, u32[]{:S(2)}, u32[]{:S(2)}) collective-permute-start(bf16[64,1664]{1,0:T(8,128)(2,1)S(1)} %collective-permute-done.11.x_keep), channel_id=1, source_target_pairs={{0,1},{1,0},{2,3},{3,2},{4,5},{5,4},{6,7},{7,6},{8,9},{9,8},{10,11... | collective-permute-start | bytes 638984 | tf_op jit(solution)/shard_map/gather_normed/ppermute | solution.py:306
  77.6 7.7 %collective-permute-start.10 = (bf16[384,1664]{1,0:T(8,128)(2,1)S(1)}, bf16[384,1664]{1,0:T(8,128)(2,1)S(1)}, u32[]{:S(2)}, u32[]{:S(2)}) collective-permute-start(bf16[384,1664]{1,0:T(8,128)(2,1)S(1)} %experts.4), channel_id=1, source_target_pairs={{0,1},{1,0},{2,3},{3,2},{4,5},{5,4},{6,7},{7,6},{8,9},{9,8},{10,11... | collective-permute-start | bytes 3833864 | tf_op jit(solution)/shard_map/experts/ppermute | solution.py:306
  80.2 2.0 %collective-permute-start.13 = (bf16[128,1664]{1,0:T(8,128)(2,1)S(1)}, bf16[128,1664]{1,0:T(8,128)(2,1)S(1)}, u32[]{:S(2)}, u32[]{:S(2)}) collective-permute-start(bf16[128,1664]{1,0:T(8,128)(2,1)S(1)} %get-tuple-element.31), channel_id=1, source_target_pairs={{0,1},{1,0},{2,3},{3,2},{4,5},{5,4},{6,7},{7,6},{8,9},{9,8},{10,11... | collective-permute-start | bytes 1277960 | tf_op jit(solution)/shard_map/experts/ppermute | solution.py:306
  82.3 8.3 %collective-permute-start.14 = (bf16[128,1664]{1,0:T(8,128)(2,1)S(1)}, bf16[128,1664]{1,0:T(8,128)(2,1)S(1)}, u32[]{:S(2)}, u32[]{:S(2)}) collective-permute-start(bf16[128,1664]{1,0:T(8,128)(2,1)S(1)} %reduce.4), channel_id=1, source_target_pairs={{0,6},{1,3},{2,0},{3,5},{4,2},{5,7},{6,4},{7,1},{8,14},{9,11},{10,... | collective-permute-start | bytes 1277960 | tf_op jit(solution)/shard_map/reduce/ppermute | solution.py:314
  85.5 42.2 %copy-start = (bf16[96,128]{1,0:T(8,128)(2,1)S(1)}, bf16[96,128]{1,0:T(8,128)(2,1)}, u32[]{:S(2)}) copy-start(bf16[96,128]{1,0:T(8,128)(2,1)} %get-tuple-element.19.after.slots) | copy-start | bytes 73732
  85.5 42.2 %copy-start.1 = (s32[2]{0:T(128)S(1)}, s32[2]{0:T(128)}, u32[]{:S(2)}) copy-start(s32[2]{0:T(128)} %pad_add_fusion.ids) | copy-start | bytes 28
  85.5 43.6 %copy-start.7 = (bf16[128,1664]{1,0:T(8,128)(2,1)S(1)}, bf16[128,1664]{1,0:T(8,128)(2,1)}, u32[]{:S(2)}) copy-start(bf16[128,1664]{1,0:T(8,128)(2,1)} %upstream.3) | copy-start | bytes 1277956
  90.6 9.1 %collective-permute-start.15 = (bf16[128,1664]{1,0:T(8,128)(2,1)S(1)}, bf16[128,1664]{1,0:T(8,128)(2,1)S(1)}, u32[]{:S(2)}, u32[]{:S(2)}) collective-permute-start(bf16[128,1664]{1,0:T(8,128)(2,1)S(1)} %reduce.5), channel_id=1, source_target_pairs={{0,6},{1,3},{2,0},{3,5},{4,2},{5,7},{6,4},{7,1},{8,14},{9,11},{10,... | collective-permute-start | bytes 1277960 | tf_op jit(solution)/shard_map/reduce/ppermute | solution.py:314
  90.7 11.7 %collective-permute-start.16 = (bf16[128,1664]{1,0:T(8,128)(2,1)S(1)}, bf16[128,1664]{1,0:T(8,128)(2,1)S(1)}, u32[]{:S(2)}, u32[]{:S(2)}) collective-permute-start(bf16[128,1664]{1,0:T(8,128)(2,1)S(1)} %get-tuple-element.32), channel_id=1, source_target_pairs={{0,2},{1,7},{2,4},{3,1},{4,6},{5,3},{6,0},{7,5},{8,10},{9,15},{10,... | collective-permute-start | bytes 1277960 | tf_op jit(solution)/shard_map/reduce/ppermute | solution.py:314
  122.8 6.3 %collective-permute-start.17 = (bf16[256,896]{1,0:T(8,128)(2,1)S(1)}, bf16[256,896]{1,0:T(8,128)(2,1)S(1)}, u32[]{:S(2)}, u32[]{:S(2)}) collective-permute-start(bf16[256,896]{1,0:T(8,128)(2,1)S(1)} %bitcast.16), channel_id=1, source_target_pairs={{0,1},{1,0},{2,3},{3,2},{4,5},{5,4},{6,7},{7,6},{8,9},{9,8},{10,11... | collective-permute-start | bytes 1376264 | tf_op jit(solution)/shard_map/collect/ppermute | solution.py:306
  (1 other events, 1.2 us)

commit v5 on v4

v5 whole, which is shorter than its diff:
```python
import jax
import jax.numpy as jnp
from jax import lax
from jax.experimental import pallas as pl
from jax.experimental.pallas import tpu as pltpu
from jax.sharding import Mesh, PartitionSpec as P

SLOTS = 4
HALF = 2
BF = jnp.bfloat16
F32 = jnp.float32
I32 = jnp.int32
VMEM = pl.BlockSpec(memory_space=pltpu.VMEM)
SMEM = pl.BlockSpec(memory_space=pltpu.SMEM)
ANY = pl.BlockSpec(memory_space=pl.ANY)
WIDE = 896
PACK = 8


def mm(a, b):
    return jnp.dot(a, b, preferred_element_type=F32)


def mm_t(a, b):
    return lax.dot_general(a, b, (((1,), (1,)), ((), ())), preferred_element_type=F32)


def mm_a(a, b):
    return lax.dot_general(a, b, (((0,), (0,)), ((), ())), preferred_element_type=F32)


def cuts(size, step):
    return [(i, min(i + step, size)) for i in range(0, size, step)]


def iota(shape, dim):
    return lax.broadcasted_iota(I32, shape, dim)


def call(kernel, outs, in_specs, scratch=(), flops=0, moved=0, mib=16):
    return pl.pallas_call(
        kernel,
        out_shape=outs,
        in_specs=in_specs,
        out_specs=jax.tree.map(lambda _: VMEM, outs),
        scratch_shapes=list(scratch),
        compiler_params=pltpu.CompilerParams(vmem_limit_bytes=mib * 2**20),
        cost_estimate=pl.CostEstimate(flops=flops, bytes_accessed=moved, transcendentals=0),
    )


def routing_kernel(ids, index, count, gate, pick_keep, pick_send, slots):
    core = ids[0]
    experts, capacity = index.shape
    packed = experts * PACK
    rows = pick_keep.shape[1] // 4
    local = index[...] - ids[1]
    diagonal = iota((experts, experts), 0) == iota((experts, experts), 1)
    counts = jnp.sum(jnp.where(diagonal, count[...].astype(F32), 0.0), axis=1, keepdims=True)
    listed = iota((experts, capacity), 1).astype(F32) < counts
    mine = listed & (local >= 0) & (local < 2 * rows)
    upto = jnp.where(iota((capacity, capacity), 0) <= iota((capacity, capacity), 1), 1.0, 0.0)
    rank = mm(jnp.where(mine, 1.0, 0.0).astype(BF), upto.astype(BF))
    lane = iota((experts, 128), 1)
    at_row = jnp.zeros((experts, 128), F32)
    gates = jnp.zeros((experts, 128), F32)
    shifted = (local + 1).astype(F32)
    for slot in range(SLOTS):
        here = mine & (rank == slot + 1.0)
        row = jnp.sum(jnp.where(here, shifted, 0.0), axis=1, keepdims=True) - 1.0
        at_row = jnp.where(lane == slot, row, at_row)
        value = jnp.sum(jnp.where(here, gate[...], 0.0), axis=1, keepdims=True)
        gates = jnp.where(lane == slot, value, gates)
    at_row = at_row.astype(BF)
    gate_high = gates.astype(BF)
    slots[:experts, :] = at_row
    slots[experts : 2 * experts, :] = gate_high
    slots[2 * experts :, :] = (gates - gate_high.astype(F32)).astype(BF)
    down = mm(spread_of(experts), at_row)
    r_col = iota((packed, 128), 0) % PACK
    lane_id = iota((packed, 128), 1)
    k = iota((packed, 2 * rows), 1)
    r_wide = iota((packed, 2 * rows), 0) % PACK
    same_stream = (r_wide // 2) % 2 == k // rows
    patch = (core * rows + k % rows).astype(F32)
    for out, side in ((pick_keep, core), (pick_send, 1 - core)):
        slot = 2 * side + r_col % 2
        row = jnp.sum(jnp.where(lane_id == slot, down, 0.0), axis=1, keepdims=True)
        hot = same_stream & (row == patch)
        out[:, : 2 * rows] = jnp.where(hot & (r_wide < 4), 1.0, 0.0).astype(BF)
        out[:, 2 * rows :] = jnp.where(hot & (r_wide >= 4), 1.0, 0.0).astype(BF)


def attend_kernel(ids, context, weight, after, send, keep):
    core = ids[0]
    rows = send.shape[0]
    for out, at in ((send, 1 - core), (keep, core)):
        block = context[:, pl.ds(pl.multiple_of(at * rows, rows), rows)]
        for lo, hi in cuts(out.shape[1], 512):
            out[:, lo:hi] = mm_a(block, weight[:, lo:hi])


def spread_of(experts):
    shape = (experts * PACK, experts)
    return jnp.where(iota(shape, 0) // PACK == iota(shape, 1), 1.0, 0.0).astype(BF)


def merge_kernel(ids, slots, merge_high, merge_low):
    core = ids[0]
    experts = slots.shape[0] // 3
    packed = experts * PACK
    rows = merge_high.shape[0] // 4
    spread = spread_of(experts)
    across = [
        lax.dot_general(
            slots[i * experts : (i + 1) * experts, :],
            spread,
            (((0,), (1,)), ((), ())),
            preferred_element_type=F32,
        )
        for i in range(3)
    ]
    q = iota((128, packed), 1) % PACK
    sub = iota((128, packed), 0)
    own = (core * rows + iota((rows, packed), 0)).astype(F32)
    q_rows = iota((rows, packed), 1) % PACK
    for which, side in ((0, core), (1, 1 - core)):
        slot = 2 * side + q % 2
        row, high, low = (
            jnp.sum(jnp.where(sub == slot, part, 0.0), axis=0, keepdims=True) for part in across
        )
        hot = row == own
        for group in range(4):
            here = hot & (q_rows // 2 == group)
            at = (slice(group * rows, (group + 1) * rows), slice(which * packed, (which + 1) * packed))
            merge_high[at] = jnp.where(here, high, 0.0).astype(BF)
            merge_low[at] = jnp.where(here, low, 0.0).astype(BF)


def statistics(stream):
    mean = jnp.mean(stream, axis=-1, keepdims=True)
    centered = stream - mean
    variance = jnp.mean(centered * centered, axis=-1, keepdims=True)
    return centered, lax.rsqrt(variance + 1e-06)


def norm_kernel(att_keep, att_got, residual, gain, upstream, pick_keep, pick_send, stream, keep, send, both):
    rows, width = residual.shape
    total = residual[...].astype(F32) + (att_keep[...] + att_got[...])
    stream[...] = total
    centered, inverse = statistics(total)
    both[:rows, :] = (gain[...] * centered * inverse).astype(BF)
    both[rows:, :] = upstream[...]
    rest = width - WIDE
    for pick, out in ((pick_send, send), (pick_keep, keep)):
        first, second = pick[:, : 2 * rows], pick[:, 2 * rows :]
        out[:, :rest] = (mm(first, both[:, :rest]) + mm(second, both[:, WIDE:])).astype(BF)
        out[:, rest:] = mm(first, both[:, rest:WIDE]).astype(BF)


def place(packed):
    q = packed
    return (q % 64 // 2) * PACK + q // 64 * 2 + q % 2


def unpack_kernel(got, out):
    n = got.shape[0]
    half = n // 2
    order = jnp.where(place(iota((n, n), 0)) == iota((n, n), 1), 1.0, 0.0).astype(BF)
    flat = mm(order, got[...]).astype(BF)
    out[:, :WIDE] = flat[:half, :]
    out[:, WIDE:] = flat[half:, : out.shape[1] - WIDE]


def stack_kernel(*refs):
    out = refs[-1]
    block = refs[0].shape[0] // 2
    for stream in range(2):
        for i, ref in enumerate(refs[:-1]):
            lo = (stream * (len(refs) - 1) + i) * block
            out[lo : lo + block, :] = ref[stream * block : (stream + 1) * block, :]


def pack_kernel(own, one, two, out, flat):
    n = out.shape[0]
    quarter = n // 4
    rest = own.shape[1] - WIDE
    total = (own[...] + one[...].astype(F32) + two[...].astype(F32)).astype(BF)
    flat[: 2 * quarter, :] = total[:, :WIDE]
    flat[2 * quarter :, :rest] = total[:, WIDE:]
    flat[2 * quarter :, rest:] = jnp.zeros((2 * quarter, WIDE - rest), BF)
    order = jnp.where(iota((n, n), 0) == place(iota((n, n), 1)), 1.0, 0.0).astype(BF)
    out[...] = mm(order, flat[...]).astype(BF)


def expert(x, u, w1, w2, hidden, grad, store):
    for lo, hi in cuts(hidden.shape[1], 256):
        v = mm(x, w1[:, lo:hi])
        square = v * v
        t = jnp.tanh(0.7978845608 * v * (1.0 + 0.044715 * square))
        gate = 0.5 + 0.5 * t
        hidden[:, lo:hi] = (v * gate).astype(BF)
        slope = gate + 0.5 * v * (1.0 - t * t) * (0.7978845608 * (1.0 + 0.134145 * square))
        grad[:, lo:hi] = (mm_t(u, w2[lo:hi, :]) * slope).astype(BF)
    for lo, hi in cuts(w2.shape[1], 512):
        store(0, lo, hi, mm(hidden[...], w2[:, lo:hi]))
        store(1, lo, hi, mm_t(grad[...], w1[lo:hi, :]))


def near_kernel(rows, w1, w2, *rest):
    part, hidden, grad = rest[-3:]
    half = rows.shape[0] // 2

    def store(stream, lo, hi, value):
        part[stream * half : (stream + 1) * half, lo:hi] = value.astype(part.dtype)

    expert(rows[:half, :], rows[half:, :], w1, w2, hidden, grad, store)


def far_kernel(ours, theirs, w1, w2, keep, send, rows, hidden, grad):
    half = ours.shape[0] // 2
    for stream in range(2):
        at = slice(stream * half, (stream + 1) * half)
        rows[2 * stream * half : (2 * stream + 1) * half, :] = ours[at, :]
        rows[(2 * stream + 1) * half : (2 * stream + 2) * half, :] = theirs[at, :]

    def store(stream, lo, hi, value):
        at = slice(stream * half, (stream + 1) * half)
        keep[at, lo:hi] = value[:half, :]
        send[at, lo:hi] = value[half:, :].astype(send.dtype)

    expert(rows[: 2 * half, :], rows[2 * half :, :], w1, w2, hidden, grad, store)


def combine_kernel(keep, got, *outs):
    block = outs[0].shape[0] // 2
    for stream in range(2):
        for i, out in enumerate(outs):
            lo = (stream * len(outs) + i) * block
            at = slice(lo, lo + block)
            total = keep[at, :] + got[at, :].astype(F32)
            out[stream * block : (stream + 1) * block, :] = total.astype(out.dtype)


def add_kernel(a, b, after, out):
    out[...] = (a[...].astype(F32) + b[...].astype(F32)).astype(BF)


def final_kernel(mine, theirs, merge_high, merge_low, stream, gain, upstream, layer_out, stream_grad, back):
    rows, width = stream.shape
    n = mine.shape[0]
    rest = width - WIDE
    total = stream[...]
    centered, inverse = statistics(total)
    x_hat = centered * inverse
    for group in range(4):
        at = slice(group * rows, (group + 1) * rows)
        summed = mm(merge_high[at, :n], mine[...]) + mm(merge_high[at, n:], theirs[...])
        summed += mm(merge_low[at, :n], mine[...]) + mm(merge_low[at, n:], theirs[...])
        cols = slice(0, WIDE) if group < 2 else slice(WIDE, width)
        summed = summed if group < 2 else summed[:, :rest]
        if group % 2 == 0:
            layer_out[:, cols] = (total[:, cols] + summed).astype(BF)
        else:
            back[:, cols] = summed
    scaled = gain[...] * back[...]
    mean = jnp.mean(scaled, axis=-1, keepdims=True)
    along = jnp.mean(scaled * x_hat, axis=-1, keepdims=True)
    pulled = inverse * (scaled - mean - x_hat * along)
    stream_grad[...] = (upstream[...].astype(F32) + pulled).astype(BF)


def per_device(
    context,
    out_weight,
    residual,
    norm_gain,
    expert_in,
    expert_out,
    patch_index,
    patch_count,
    gate_value,
    upstream,
):
    rows, width = residual.shape
    experts, capacity = patch_index.shape
    shards = lax.axis_size("y")
    packed = experts * PACK
    block = experts * HALF
    units = expert_in.shape[2]
    sds = jax.ShapeDtypeStruct
    core = lax.axis_index("core")
    index = lax.axis_index("xz") * shards + lax.axis_index("y")
    ids = jnp.stack([core, index * (2 * rows)]).astype(I32)
    gain = norm_gain.reshape(1, width)

    def swap_core(x):
        return lax.ppermute(x, "core", [(0, 1), (1, 0)])

    def ring(x, way):
        pairs = []
        for y in range(shards):
            for c in range(2):
                step = way if c == 0 else -way
                pairs.append((y * 2 + c, (y + step) % shards * 2 + c))
        return lax.ppermute(x, ("y", "core"), pairs)

    def exchange(x):
        got = lax.all_to_all(
            x.reshape(experts, PACK, WIDE), "xz", split_axis=0, concat_axis=0, tiled=True
        )
        return got.reshape(packed, WIDE)

    weight_in = expert_in[0]
    weight_out = expert_out[0]

    with jax.named_scope("routing"):
        pick_keep, pick_send, slots = call(
            routing_kernel,
            [sds((packed, 4 * rows), BF)] * 2 + [sds((3 * experts, 128), BF)],
            [SMEM] + [VMEM] * 3,
            flops=10**9,
            moved=10**6,
        )(ids, patch_index, patch_count.reshape(1, experts), gate_value)
    with jax.named_scope("attend"):
        att_send, att_keep = call(
            attend_kernel,
            [sds((rows, width), F32)] * 2,
            [SMEM, VMEM, VMEM, ANY],
            flops=4 * rows * width * context.shape[1],
            moved=5 * 10**6,
        )(ids, context.T, out_weight, slots)
        att_got = swap_core(att_send)
    with jax.named_scope("norm"):
        stream, keep, send = call(
            norm_kernel,
            [sds((rows, width), F32)] + [sds((packed, WIDE), BF)] * 2,
            [VMEM] * 7,
            [pltpu.VMEM((2 * rows, width), BF)],
            flops=10**9,
            moved=3 * 10**6,
        )(att_keep, att_got, residual, gain, upstream, pick_keep, pick_send)
    with jax.named_scope("merge"):
        merge_high, merge_low = call(
            merge_kernel,
            [sds((4 * rows, 2 * packed), BF)] * 2,
            [SMEM, VMEM],
            flops=10**8,
            moved=10**6,
        )(ids, slots)
    pair = (2 * block, width)
    with jax.named_scope("dispatch"):
        own = call(unpack_kernel, sds(pair, BF), [VMEM], flops=10**8, moved=10**6)(
            exchange(keep + swap_core(send))
        )

    def near_part(x, kind, *after):
        tall = x.shape[0] // 2
        return call(
            near_kernel,
            sds(x.shape, kind),
            [VMEM] * 3 + [ANY] * len(after),
            [pltpu.VMEM((tall, units), BF)] * 2,
            flops=24 * tall * width * units,
            moved=10**7,
            mib=20,
        )(x, weight_in, weight_out, *after)

    def combine(keep, got, *kinds):
        outs = [sds(pair, kind) for kind in kinds]
        return call(combine_kernel, outs, [VMEM] * 2, flops=10**6, moved=10**6)(keep, got)

    with jax.named_scope("gather"):
        one = ring(own, 1)
        two = ring(own, -1)
        far = ring(one, 1)
        near = call(
            stack_kernel, sds((6 * block, width), BF), [VMEM] * 3, flops=10**5, moved=10**6
        )(own, one, two)
        near_send = swap_core(near)
        far_send = swap_core(far)
    with jax.named_scope("near"):
        near_keep = near_part(near, F32)
        near_got = swap_core(near_part(near_send, BF, near_keep, far))
        own_sum, one_sum, two_sum = combine(near_keep, near_got, F32, F32, BF)
        from_two = ring(two_sum, 1)
    with jax.named_scope("far"):
        far_keep, far_out = call(
            far_kernel,
            [sds(pair, F32), sds(pair, BF)],
            [VMEM] * 4,
            [pltpu.VMEM((4 * block, width), BF)] + [pltpu.VMEM((2 * block, units), BF)] * 2,
            flops=48 * block * width * units,
            moved=10**7,
            mib=20,
        )(far, far_send, weight_in, weight_out)
        (far_sum,) = combine(far_keep, swap_core(far_out), BF)
        from_far = ring(far_sum, -1)
    with jax.named_scope("reduce"):
        one_sum = call(
            add_kernel, sds(pair, BF), [VMEM] * 2 + [ANY], flops=10**5, moved=10**6
        )(one_sum, from_far, from_two)
        from_one = ring(one_sum, -1)
    with jax.named_scope("collect"):
        ready = call(
            pack_kernel,
            sds((packed, WIDE), BF),
            [VMEM] * 3,
            [pltpu.VMEM((packed, WIDE), BF)],
            flops=10**8,
            moved=10**6,
        )(own_sum, from_one, from_two)
        mine = exchange(ready)
        theirs = swap_core(mine)
    with jax.named_scope("final"):
        layer_out, stream_grad = call(
            final_kernel,
            [sds((rows, width), BF)] * 2,
            [VMEM] * 7,
            [pltpu.VMEM((rows, width), F32)],
            flops=10**9,
            moved=4 * 10**6,
        )(mine, theirs, merge_high, merge_low, stream, gain, upstream)
    return (layer_out, stream_grad)


def solution(mesh):
    sizes = mesh.devices.shape
    shards = 4
    split = Mesh(
        mesh.devices.reshape(sizes[0] // shards, shards, sizes[1]), ("xz", "y", "core")
    )
    return jax.shard_map(
        per_device,
        mesh=split,
        in_specs=(
            P(("xz", "y"), "core"),
            P("core", None),
            P(("xz", "y", "core"), None),
            P(),
            P(("xz", "y"), None, "core"),
            P(("xz", "y"), "core", None),
            P(),
            P(),
            P(),
            P(("xz", "y", "core"), None),
        ),
        out_specs=(P(("xz", "y", "core"), None), P(("xz", "y", "core"), None)),
        check_vma=False,
    )
```

time: 132 us -> 119 us (0.902)
  starting transfers between devices: 44.5 us -> 18.5 us
  blocking collectives: 20 us -> 40.1 us
  Pallas kernels: 24.4 us -> 19.2 us
  waiting for transfers between devices: 34.9 us -> 38 us
  other arithmetic: 2.11 us -> 0.13 us
  local copies, waits for them, and re-layouts: 4.5 us -> 2.52 us
    all_to_all x1 -> x2, blocking collectives: 20 us -> 40.1 us  [exchange(): lax.all_to_all(x.reshape(experts, PACK, WIDE), 'xz', split_axis=0, concat...]
    all_to_all x2 -> x0, starting transfers between devices: 16 us -> none  [exchange(): lax.all_to_all(x.reshape(experts, PACK, x.shape[1]), 'xz', split_axis=0,...]
    ppermute x9 -> x6, waiting for transfers between devices: 23.8 us -> 32.8 us  [ring(): return lax.ppermute(x, ('y', 'core'), pairs)]
    ppermute x9 -> x6, starting transfers between devices: 12.8 us -> 5.71 us  [ring(): return lax.ppermute(x, ('y', 'core'), pairs)]
    all_to_all x2 -> x0, waiting for transfers between devices: 5.99 us -> none  [exchange(): lax.all_to_all(x.reshape(experts, PACK, x.shape[1]), 'xz', split_axis=0,...]
    pallas_call x13 -> x9, Pallas kernels: 20.3 us -> 15.1 us  [the longest x2 7.46 us: near_part(): call(near_kernel, sds(x.shape, kind), [VMEM] * 3 + [ANY] * len(after), [p...]
    ppermute x9 -> x7, starting transfers between devices: 15.7 us -> 12.8 us  [swap_core(): return lax.ppermute(x, 'core', [(0, 1), (1, 0)])]
    reshape x1 -> x0, local copies, waits for them, and re-layouts: 1.33 us -> none  [per_device(): patch_count.reshape(experts, 1)]
  transfers between devices with their start and end apart: 20 -> 13, of which waited for: 13 -> 9; matrix products, arithmetic and copies ran while one was open for 1% -> 0% of each run, Pallas kernels for 10% -> 10%
where the time goes in v5:
time: 119 us
  blocking collectives  40.1 us (34%)
  waiting for transfers between devices  38 us (32%)
  Pallas kernels  19.2 us (16%)
  starting transfers between devices  18.5 us (16%)
  local copies, waits for them, and re-layouts  2.52 us (2%)
    all_to_all x2, blocking collectives, exchange(): lax.all_to_all(x.reshape(experts, PACK, WIDE), 'xz', split_axis=0, concat...  40.1 us
    ppermute x6, waiting for transfers between devices, ring(): return lax.ppermute(x, ('y', 'core'), pairs)  32.8 us
    ppermute x7, starting transfers between devices, swap_core(): return lax.ppermute(x, 'core', [(0, 1), (1, 0)])  12.8 us
    pallas_call x2, Pallas kernels, near_part(): call(near_kernel, sds(x.shape, kind), [VMEM] * 3 + [ANY] * len(after), [p...  7.46 us
    ppermute x6, starting transfers between devices, ring(): return lax.ppermute(x, ('y', 'core'), pairs)  5.71 us
    ppermute x7, waiting for transfers between devices, swap_core(): return lax.ppermute(x, 'core', [(0, 1), (1, 0)])  5.12 us
    pallas_call x1, Pallas kernels, per_device(): call(far_kernel, [sds(pair, F32), sds(pair, BF)], [VMEM] * 4, [pltpu.VMEM...  3.31 us
    unnamed x20, local copies, waits for them, and re-layouts  2.51 us
  transfers between devices with their start and end apart: 13, of which 9 were waited for; matrix products, arithmetic and copies ran while one was open for 0% of the time, Pallas kernels for 10%

profile of v5, /device:TPU:1, one launch (start us, length us, event | category | flops | bytes accessed | tf_op | source)
XLA Modules:
  0.0 119.3 jit_solution(13095385020454555398)
XLA Ops:
  0.7 1.0 copy-done.6
  1.7 0.8 copy-done.7
  2.6 0.7 copy-done.8
  3.2 1.2 %routing.1 = (bf16[256,512]{1,0:T(8,128)(2,1)S(1)}, bf16[256,512]{1,0:T(8,128)(2,1)S(1)}, bf16[96,128]{1,0:T(8,128)(2,1)S(1)}) custom-call(s32[2]{0:T(128)S(1)} %pad_add_fusion.ids, s32[32,512]{1,0:T(8,128)S(1)} %copy-done.6, s32[1,32]{1,0:T(1,128)S(1)} %bitcast.22, f32[32,512]{1,0:T(8,128)S(1)} %copy-done.7), custom_call_target="tpu_custom_call" | custom-call | flops 1000000000 | bytes 1000000 | tf_op jit(solution)/shard_map/routing/pallas_call | solution.py:318
  4.5 1.7 %attend.1 = (f32[128,1664]{1,0:T(8,128)S(1)}, f32[128,1664]{1,0:T(8,128)S(1)}) custom-call(s32[2]{0:T(128)S(1)} %pad_add_fusion.ids, bf16[832,256]{1,0:T(8,128)(2,1)S(1)} %bitcast.15, bf16[832,1664]{1,0:T(8,128)(2,1)S(1)} %copy-done, bf16[96,128]{1,0:T(8,128)(2,1)S(1)} %get-tuple-element.17.after.slots), custom_call_target="tpu_custom_call" | custom-call | flops 708837376 | bytes 5000000 | tf_op jit(solution)/shard_map/attend/pallas_call | solution.py:326
  6.2 3.3 %collective-permute-start = (f32[128,1664]{1,0:T(8,128)S(1)}, f32[128,1664]{1,0:T(8,128)S(1)}, u32[]{:S(2)}, u32[]{:S(2)}) collective-permute-start(f32[128,1664]{1,0:T(8,128)S(1)} %get-tuple-element.19), channel_id=1, source_target_pairs={{0,1},{1,0},{2,3},{3,2},{4,5},{5,4},{6,7},{7,6},{8,9},{9,8},{10,11... | collective-permute-start | bytes 2555912 | tf_op jit(solution)/shard_map/attend/ppermute | solution.py:298
  9.5 2.0 %collective-permute-done.att_got = f32[128,1664]{1,0:T(8,128)S(1)} collective-permute-done((f32[128,1664]{1,0:T(8,128)S(1)}, f32[128,1664]{1,0:T(8,128)S(1)}, u32[]{:S(2)}, u32[]{:S(2)}) %collective-permute-start) | collective-permute-done | bytes 852000 | tf_op jit(solution)/shard_map/attend/ppermute | solution.py:298
  11.5 1.0 norm.1
  12.5 0.5 collective-permute-start.1
  13.0 1.4 %collective-permute-done.1 = bf16[256,896]{1,0:T(8,128)(2,1)S(1)} collective-permute-done((bf16[256,896]{1,0:T(8,128)(2,1)S(1)}, bf16[256,896]{1,0:T(8,128)(2,1)S(1)}, u32[]{:S(2)}, u32[]{:S(2)}) %collective-permute-start.1) | collective-permute-done | bytes 458784 | tf_op jit(solution)/shard_map/dispatch/ppermute | solution.py:298
  14.5 22.5 %all_to_all.10 = bf16[32,8,896]{2,1,0:T(8,128)(2,1)S(1)} all-to-all(bf16[32,8,896]{2,1,0:T(8,128)(2,1)S(1)} %add_bitcast_fusion), channel_id=1, replica_groups=mesh['xz'=32,'y'=4,'core'=2] {'xz'}, dimensions={0} | all-to-all | bytes 917504 | tf_op jit(solution)/shard_map/dispatch/all_to_all | solution.py:309
  37.0 0.3 dispatch.1.refs_0_
  37.3 2.8 %collective-permute-start.2 = (bf16[128,1664]{1,0:T(8,128)(2,1)S(1)}, bf16[128,1664]{1,0:T(8,128)(2,1)S(1)}, u32[]{:S(2)}, u32[]{:S(2)}) collective-permute-start(bf16[128,1664]{1,0:T(8,128)(2,1)S(1)} %dispatch.1.refs_0_), channel_id=1, source_target_pairs={{0,2},{1,7},{2,4},{3,1},{4,6},{5,3},{6,0},{7,5},{8,10},{9,15},{10,... | collective-permute-start | bytes 1277960 | tf_op jit(solution)/shard_map/gather/ppermute | solution.py:306
  40.1 5.8 %collective-permute-done.2.refs_1_ = bf16[128,1664]{1,0:T(8,128)(2,1)S(1)} collective-permute-done((bf16[128,1664]{1,0:T(8,128)(2,1)S(1)}, bf16[128,1664]{1,0:T(8,128)(2,1)S(1)}, u32[]{:S(2)}, u32[]{:S(2)}) %collective-permute-start.2) | collective-permute-done | bytes 426016 | tf_op jit(solution)/shard_map/gather/ppermute | solution.py:306
  45.9 6.5 %collective-permute-done.3.refs_2_ = bf16[128,1664]{1,0:T(8,128)(2,1)S(1)} collective-permute-done((bf16[128,1664]{1,0:T(8,128)(2,1)S(1)}, bf16[128,1664]{1,0:T(8,128)(2,1)S(1)}, u32[]{:S(2)}, u32[]{:S(2)}) %collective-permute-start.3) | collective-permute-done | bytes 426016 | tf_op jit(solution)/shard_map/gather/ppermute | solution.py:306
  52.4 1.3 %collective-permute-start.4 = (bf16[384,1664]{1,0:T(8,128)(2,1)S(1)}, bf16[384,1664]{1,0:T(8,128)(2,1)S(1)}, u32[]{:S(2)}, u32[]{:S(2)}) collective-permute-start(bf16[384,1664]{1,0:T(8,128)(2,1)S(1)} %gather.1.rows), channel_id=1, source_target_pairs={{0,1},{1,0},{2,3},{3,2},{4,5},{5,4},{6,7},{7,6},{8,9},{9,8},{10,11... | collective-permute-start | bytes 3833864 | tf_op jit(solution)/shard_map/gather/ppermute | solution.py:298
  53.8 3.7 %near.3.rest_0_.keep = f32[384,1664]{1,0:T(8,128)S(1)} custom-call(bf16[384,1664]{1,0:T(8,128)(2,1)S(1)} %gather.1.rows, bf16[1664,1024]{1,0:T(8,128)(2,1)S(1)} %bitcast.16, bf16[1024,1664]{1,0:T(8,128)(2,1)S(1)} %bitcast.19), custom_call_target="tpu_custom_call" | custom-call | flops 7851737088 | bytes 10000000 | tf_op jit(solution)/shard_map/near/pallas_call | solution.py:359
  57.5 3.5 %collective-permute-done.5.rest_1_.ours = bf16[128,1664]{1,0:T(8,128)(2,1)S(1)} collective-permute-done((bf16[128,1664]{1,0:T(8,128)(2,1)S(1)}, bf16[128,1664]{1,0:T(8,128)(2,1)S(1)}, u32[]{:S(2)}, u32[]{:S(2)}) %collective-permute-start.5) | collective-permute-done | bytes 426016 | tf_op jit(solution)/shard_map/gather/ppermute | solution.py:306
  61.0 2.2 %collective-permute-start.7 = (bf16[128,1664]{1,0:T(8,128)(2,1)S(1)}, bf16[128,1664]{1,0:T(8,128)(2,1)S(1)}, u32[]{:S(2)}, u32[]{:S(2)}) collective-permute-start(bf16[128,1664]{1,0:T(8,128)(2,1)S(1)} %collective-permute-done.5.rest_1_.ours), channel_id=1, source_target_pairs={{0,1},{1,0},{2,3},{3,2},{4,5},{5,4},{6,7},{7,6},{8,9},{9,8},{10,11... | collective-permute-start | bytes 1277960 | tf_op jit(solution)/shard_map/gather/ppermute | solution.py:298
  63.2 3.7 %near.4 = bf16[384,1664]{1,0:T(8,128)(2,1)S(1)} custom-call(bf16[384,1664]{1,0:T(8,128)(2,1)S(1)} %collective-permute-done.4.rows, bf16[1664,1024]{1,0:T(8,128)(2,1)S(1)} %bitcast.17, bf16[1024,1664]{1,0:T(8,128)(2,1)S(1)} %bitcast.20, f32[384,1664]{1,0:T(8,128)S(1)} %near.3.rest_0_.keep, bf16[128,1664]{1,0:T(8,128)(2,1)S(1)} %collective-permute-done.5.rest_1_.ours), custom_call_target="tpu_custom_call" | custom-call | flops 7851737088 | bytes 10000000 | tf_op jit(solution)/shard_map/near/pallas_call | solution.py:359
  67.0 3.3 %far.2 = (f32[128,1664]{1,0:T(8,128)S(1)}, bf16[128,1664]{1,0:T(8,128)(2,1)S(1)}) custom-call(bf16[128,1664]{1,0:T(8,128)(2,1)S(1)} %collective-permute-done.5.rest_1_.ours, bf16[128,1664]{1,0:T(8,128)(2,1)S(1)} %collective-permute-done.7.theirs, bf16[1664,1024]{1,0:T(8,128)(2,1)S(1)} %bitcast.18, bf16[1024,1664]{1,0:T(8,128)(2,1)S(1)} %bitcast.21), custom_call_target="tpu_custom_call" | custom-call | flops 5234491392 | bytes 10000000 | tf_op jit(solution)/shard_map/far/pallas_call | solution.py:388
  70.3 0.6 collective-permute-start.8
  70.9 1.4 %collective-permute-done.8.got = bf16[128,1664]{1,0:T(8,128)(2,1)S(1)} collective-permute-done((bf16[128,1664]{1,0:T(8,128)(2,1)S(1)}, bf16[128,1664]{1,0:T(8,128)(2,1)S(1)}, u32[]{:S(2)}, u32[]{:S(2)}) %collective-permute-start.8) | collective-permute-done | bytes 426016 | tf_op jit(solution)/shard_map/far/ppermute | solution.py:298
  72.7 2.7 %collective-permute-start.10 = (bf16[128,1664]{1,0:T(8,128)(2,1)S(1)}, bf16[128,1664]{1,0:T(8,128)(2,1)S(1)}, u32[]{:S(2)}, u32[]{:S(2)}) collective-permute-start(bf16[128,1664]{1,0:T(8,128)(2,1)S(1)} %get-tuple-element.28), channel_id=1, source_target_pairs={{0,2},{1,7},{2,4},{3,1},{4,6},{5,3},{6,0},{7,5},{8,10},{9,15},{10,... | collective-permute-start | bytes 1277960 | tf_op jit(solution)/shard_map/near/ppermute | solution.py:306
  75.4 8.9 %collective-permute-done.9.b = bf16[128,1664]{1,0:T(8,128)(2,1)S(1)} collective-permute-done((bf16[128,1664]{1,0:T(8,128)(2,1)S(1)}, bf16[128,1664]{1,0:T(8,128)(2,1)S(1)}, u32[]{:S(2)}, u32[]{:S(2)}) %collective-permute-start.9) | collective-permute-done | bytes 426016 | tf_op jit(solution)/shard_map/far/ppermute | solution.py:306
  84.5 8.2 %collective-permute-done.11.one = bf16[128,1664]{1,0:T(8,128)(2,1)S(1)} collective-permute-done((bf16[128,1664]{1,0:T(8,128)(2,1)S(1)}, bf16[128,1664]{1,0:T(8,128)(2,1)S(1)}, u32[]{:S(2)}, u32[]{:S(2)}) %collective-permute-start.11) | collective-permute-done | bytes 426016 | tf_op jit(solution)/shard_map/reduce/ppermute | solution.py:306
  92.7 0.4 collect.1
  93.1 17.6 %all_to_all.11 = bf16[32,8,896]{2,1,0:T(8,128)(2,1)S(1)} all-to-all(bf16[32,8,896]{2,1,0:T(8,128)(2,1)S(1)} %bitcast.11), channel_id=1, replica_groups=mesh['xz'=32,'y'=4,'core'=2] {'xz'}, dimensions={0} | all-to-all | bytes 917504 | tf_op jit(solution)/shard_map/collect/all_to_all | solution.py:309
  110.7 4.9 %collective-permute-start.12 = (bf16[256,896]{1,0:T(8,128)(2,1)S(1)}, bf16[256,896]{1,0:T(8,128)(2,1)S(1)}, u32[]{:S(2)}, u32[]{:S(2)}) collective-permute-start(bf16[256,896]{1,0:T(8,128)(2,1)S(1)} %bitcast.13), channel_id=1, source_target_pairs={{0,1},{1,0},{2,3},{3,2},{4,5},{5,4},{6,7},{7,6},{8,9},{9,8},{10,11... | collective-permute-start | bytes 1376264 | tf_op jit(solution)/shard_map/collect/ppermute | solution.py:298
  115.6 1.2 merge.1
  116.8 0.3 collective-permute-done.12.theirs
  117.0 2.3 %final.1 = (bf16[128,1664]{1,0:T(8,128)(2,1)}, bf16[128,1664]{1,0:T(8,128)(2,1)}) custom-call(bf16[256,896]{1,0:T(8,128)(2,1)S(1)} %bitcast.14, bf16[256,896]{1,0:T(8,128)(2,1)S(1)} %collective-permute-done.12.theirs, bf16[512,512]{1,0:T(8,128)(2,1)S(1)} %get-tuple-element.29.merge_high, bf16[512,512]{1,0:T(8,128)(2,1)S(1)} %get-tuple-element.30.merge_low, ...), custom_call_target="tpu_custom_call" | custom-call | flops 1000000000 | bytes 4000000 | tf_op jit(solution)/shard_map/final/pallas_call | solution.py:416
  (33 shorter events, 0.9 us)
Async XLA Ops:
  0.6 3.8 %copy-start.1 = (bf16[256,832]{0,1:T(8,128)(2,1)S(1)}, bf16[256,832]{0,1:T(8,128)(2,1)}, u32[]{:S(2)}) copy-start(bf16[256,832]{0,1:T(8,128)(2,1)} %param.10) | copy-start | bytes 1277956
  0.6 3.8 %copy-start = (bf16[832,1664]{1,0:T(8,128)(2,1)S(1)}, bf16[832,1664]{1,0:T(8,128)(2,1)}, u32[]{:S(2)}) copy-start(bf16[832,1664]{1,0:T(8,128)(2,1)} %weight.1) | copy-start | bytes 8306692
  0.7 1.0 copy-start.6
  1.7 0.8 copy-start.7
  2.6 0.7 copy-start.8
  3.2 6.3 %copy-start.9 = (f32[1664]{0:T(1024)S(1)}, f32[1664]{0:T(1024)}, u32[]{:S(2)}) copy-start(f32[1664]{0:T(1024)} %param.13) | copy-start | bytes 19972
  3.2 8.3 %copy-start.4 = (bf16[128,1664]{1,0:T(8,128)(2,1)S(1)}, bf16[128,1664]{1,0:T(8,128)(2,1)}, u32[]{:S(2)}) copy-start(bf16[128,1664]{1,0:T(8,128)(2,1)} %residual.1) | copy-start | bytes 1277956
  3.2 8.3 %copy-start.5 = (bf16[128,1664]{1,0:T(8,128)(2,1)S(1)}, bf16[128,1664]{1,0:T(8,128)(2,1)}, u32[]{:S(2)}) copy-start(bf16[128,1664]{1,0:T(8,128)(2,1)} %upstream.3) | copy-start | bytes 1277956
  6.2 5.3 %collective-permute-start = (f32[128,1664]{1,0:T(8,128)S(1)}, f32[128,1664]{1,0:T(8,128)S(1)}, u32[]{:S(2)}, u32[]{:S(2)}) collective-permute-start(f32[128,1664]{1,0:T(8,128)S(1)} %get-tuple-element.19), channel_id=1, source_target_pairs={{0,1},{1,0},{2,3},{3,2},{4,5},{5,4},{6,7},{7,6},{8,9},{9,8},{10,11... | collective-permute-start | bytes 2555912 | tf_op jit(solution)/shard_map/attend/ppermute | solution.py:298
  11.5 42.2 %copy-start.3 = (bf16[1,1024,1664]{2,1,0:T(8,128)(2,1)S(1)}, bf16[1,1024,1664]{2,1,0:T(8,128)(2,1)}, u32[]{:S(2)}) copy-start(bf16[1,1024,1664]{2,1,0:T(8,128)(2,1)} %param.15) | copy-start | bytes 10223620
  12.5 1.9 %collective-permute-start.1 = (bf16[256,896]{1,0:T(8,128)(2,1)S(1)}, bf16[256,896]{1,0:T(8,128)(2,1)S(1)}, u32[]{:S(2)}, u32[]{:S(2)}) collective-permute-start(bf16[256,896]{1,0:T(8,128)(2,1)S(1)} %get-tuple-element.23), channel_id=1, source_target_pairs={{0,1},{1,0},{2,3},{3,2},{4,5},{5,4},{6,7},{7,6},{8,9},{9,8},{10,11... | collective-permute-start | bytes 1376264 | tf_op jit(solution)/shard_map/dispatch/ppermute | solution.py:298
  14.4 39.3 %copy-start.2 = (bf16[1,1664,1024]{2,1,0:T(8,128)(2,1)S(1)}, bf16[1,1664,1024]{2,1,0:T(8,128)(2,1)}, u32[]{:S(2)}) copy-start(bf16[1,1664,1024]{2,1,0:T(8,128)(2,1)} %param.14) | copy-start | bytes 10223620
  37.3 8.6 %collective-permute-start.2 = (bf16[128,1664]{1,0:T(8,128)(2,1)S(1)}, bf16[128,1664]{1,0:T(8,128)(2,1)S(1)}, u32[]{:S(2)}, u32[]{:S(2)}) collective-permute-start(bf16[128,1664]{1,0:T(8,128)(2,1)S(1)} %dispatch.1.refs_0_), channel_id=1, source_target_pairs={{0,2},{1,7},{2,4},{3,1},{4,6},{5,3},{6,0},{7,5},{8,10},{9,15},{10,... | collective-permute-start | bytes 1277960 | tf_op jit(solution)/shard_map/gather/ppermute | solution.py:306
  40.1 12.2 %collective-permute-start.3 = (bf16[128,1664]{1,0:T(8,128)(2,1)S(1)}, bf16[128,1664]{1,0:T(8,128)(2,1)S(1)}, u32[]{:S(2)}, u32[]{:S(2)}) collective-permute-start(bf16[128,1664]{1,0:T(8,128)(2,1)S(1)} %dispatch.1.refs_0_), channel_id=1, source_target_pairs={{0,6},{1,3},{2,0},{3,5},{4,2},{5,7},{6,4},{7,1},{8,14},{9,11},{10,... | collective-permute-start | bytes 1277960 | tf_op jit(solution)/shard_map/gather/ppermute | solution.py:306
  52.4 10.7 %collective-permute-start.4 = (bf16[384,1664]{1,0:T(8,128)(2,1)S(1)}, bf16[384,1664]{1,0:T(8,128)(2,1)S(1)}, u32[]{:S(2)}, u32[]{:S(2)}) collective-permute-start(bf16[384,1664]{1,0:T(8,128)(2,1)S(1)} %gather.1.rows), channel_id=1, source_target_pairs={{0,1},{1,0},{2,3},{3,2},{4,5},{5,4},{6,7},{7,6},{8,9},{9,8},{10,11... | collective-permute-start | bytes 3833864 | tf_op jit(solution)/shard_map/gather/ppermute | solution.py:298
  53.7 7.3 %collective-permute-start.5 = (bf16[128,1664]{1,0:T(8,128)(2,1)S(1)}, bf16[128,1664]{1,0:T(8,128)(2,1)S(1)}, u32[]{:S(2)}, u32[]{:S(2)}) collective-permute-start(bf16[128,1664]{1,0:T(8,128)(2,1)S(1)} %collective-permute-done.2.refs_1_), channel_id=1, source_target_pairs={{0,2},{1,7},{2,4},{3,1},{4,6},{5,3},{6,0},{7,5},{8,10},{9,15},{10,... | collective-permute-start | bytes 1277960 | tf_op jit(solution)/shard_map/gather/ppermute | solution.py:306
  61.0 6.0 %collective-permute-start.7 = (bf16[128,1664]{1,0:T(8,128)(2,1)S(1)}, bf16[128,1664]{1,0:T(8,128)(2,1)S(1)}, u32[]{:S(2)}, u32[]{:S(2)}) collective-permute-start(bf16[128,1664]{1,0:T(8,128)(2,1)S(1)} %collective-permute-done.5.rest_1_.ours), channel_id=1, source_target_pairs={{0,1},{1,0},{2,3},{3,2},{4,5},{5,4},{6,7},{7,6},{8,9},{9,8},{10,11... | collective-permute-start | bytes 1277960 | tf_op jit(solution)/shard_map/gather/ppermute | solution.py:298
  66.9 5.6 %collective-permute-start.6 = (bf16[384,1664]{1,0:T(8,128)(2,1)S(1)}, bf16[384,1664]{1,0:T(8,128)(2,1)S(1)}, u32[]{:S(2)}, u32[]{:S(2)}) collective-permute-start(bf16[384,1664]{1,0:T(8,128)(2,1)S(1)} %near.4), channel_id=1, source_target_pairs={{0,1},{1,0},{2,3},{3,2},{4,5},{5,4},{6,7},{7,6},{8,9},{9,8},{10,11... | collective-permute-start | bytes 3833864 | tf_op jit(solution)/shard_map/near/ppermute | solution.py:298
  70.3 2.0 %collective-permute-start.8 = (bf16[128,1664]{1,0:T(8,128)(2,1)S(1)}, bf16[128,1664]{1,0:T(8,128)(2,1)S(1)}, u32[]{:S(2)}, u32[]{:S(2)}) collective-permute-start(bf16[128,1664]{1,0:T(8,128)(2,1)S(1)} %get-tuple-element.27), channel_id=1, source_target_pairs={{0,1},{1,0},{2,3},{3,2},{4,5},{5,4},{6,7},{7,6},{8,9},{9,8},{10,11... | collective-permute-start | bytes 1277960 | tf_op jit(solution)/shard_map/far/ppermute | solution.py:298
  72.4 12.0 %collective-permute-start.9 = (bf16[128,1664]{1,0:T(8,128)(2,1)S(1)}, bf16[128,1664]{1,0:T(8,128)(2,1)S(1)}, u32[]{:S(2)}, u32[]{:S(2)}) collective-permute-start(bf16[128,1664]{1,0:T(8,128)(2,1)S(1)} %far.3), channel_id=1, source_target_pairs={{0,6},{1,3},{2,0},{3,5},{4,2},{5,7},{6,4},{7,1},{8,14},{9,11},{10,... | collective-permute-start | bytes 1277960 | tf_op jit(solution)/shard_map/far/ppermute | solution.py:306
  72.7 11.6 %collective-permute-start.10 = (bf16[128,1664]{1,0:T(8,128)(2,1)S(1)}, bf16[128,1664]{1,0:T(8,128)(2,1)S(1)}, u32[]{:S(2)}, u32[]{:S(2)}) collective-permute-start(bf16[128,1664]{1,0:T(8,128)(2,1)S(1)} %get-tuple-element.28), channel_id=1, source_target_pairs={{0,2},{1,7},{2,4},{3,1},{4,6},{5,3},{6,0},{7,5},{8,10},{9,15},{10,... | collective-permute-start | bytes 1277960 | tf_op jit(solution)/shard_map/near/ppermute | solution.py:306
  84.4 8.3 %collective-permute-start.11 = (bf16[128,1664]{1,0:T(8,128)(2,1)S(1)}, bf16[128,1664]{1,0:T(8,128)(2,1)S(1)}, u32[]{:S(2)}, u32[]{:S(2)}) collective-permute-start(bf16[128,1664]{1,0:T(8,128)(2,1)S(1)} %reduce.1), channel_id=1, source_target_pairs={{0,6},{1,3},{2,0},{3,5},{4,2},{5,7},{6,4},{7,1},{8,14},{9,11},{10,... | collective-permute-start | bytes 1277960 | tf_op jit(solution)/shard_map/reduce/ppermute | solution.py:306
  110.7 6.3 %collective-permute-start.12 = (bf16[256,896]{1,0:T(8,128)(2,1)S(1)}, bf16[256,896]{1,0:T(8,128)(2,1)S(1)}, u32[]{:S(2)}, u32[]{:S(2)}) collective-permute-start(bf16[256,896]{1,0:T(8,128)(2,1)S(1)} %bitcast.13), channel_id=1, source_target_pairs={{0,1},{1,0},{2,3},{3,2},{4,5},{5,4},{6,7},{7,6},{8,9},{9,8},{10,11... | collective-permute-start | bytes 1376264 | tf_op jit(solution)/shard_map/collect/ppermute | solution.py:298

commit v6 on v2

--- a/solution.py
+++ b/solution.py
@@ -12,6 +12,7 @@
 I32 = jnp.int32
 VMEM = pl.BlockSpec(memory_space=pltpu.VMEM)
 SMEM = pl.BlockSpec(memory_space=pltpu.SMEM)
+ANY = pl.BlockSpec(memory_space=pl.ANY)
 WIDE = 896
 PACK = 8
 
@@ -22,6 +23,10 @@
 
 def mm_t(a, b):
     return lax.dot_general(a, b, (((1,), (1,)), ((), ())), preferred_element_type=F32)
+
+
+def mm_a(a, b):
+    return lax.dot_general(a, b, (((0,), (0,)), ((), ())), preferred_element_type=F32)
 
 
 def cuts(size, step):
@@ -48,9 +53,9 @@
     core = ids[0]
     rows = send.shape[0]
     for out, at in ((send, 1 - core), (keep, core)):
-        block = context[pl.ds(pl.multiple_of(at * rows, rows), rows), :]
+        block = context[:, pl.ds(pl.multiple_of(at * rows, rows), rows)]
         for lo, hi in cuts(out.shape[1], 512):
-            out[:, lo:hi] = mm(block, weight[:, lo:hi])
+            out[:, lo:hi] = mm_a(block, weight[:, lo:hi])
 
 
 def routing_kernel(ids, index, count, gate, pick_keep, pick_send, merge_high, merge_low):
@@ -161,7 +166,8 @@
     out[...] = mm(order, flat[...]).astype(BF)
 
 
-def forward_kernel(x0, x1, x2, x3, w1, w2, slope, part, x, hidden):
+def forward_kernel(x0, x1, x2, x3, w1, w2, *rest):
+    slope, part, x, hidden = rest[-4:]
     block = x0.shape[0]
     for i, ref in enumerate((x0, x1, x2, x3)):
         x[i * block : (i + 1) * block, :] = ref[...]
@@ -176,7 +182,8 @@
         part[:, lo:hi] = mm(hidden[...], w2[:, lo:hi]).astype(part.dtype)
 
 
-def backward_kernel(x0, x1, x2, x3, w1, w2, slope, part, x, grad):
+def backward_kernel(x0, x1, x2, x3, w1, w2, slope, *rest):
+    part, x, grad = rest[-3:]
     block = x0.shape[0]
     for i, ref in enumerate((x0, x1, x2, x3)):
         x[i * block : (i + 1) * block, :] = ref[...]
@@ -269,7 +276,7 @@
             [SMEM, VMEM, VMEM],
             flops=4 * rows * width * context.shape[1],
             moved=5 * 10**6,
-        )(ids, context, out_weight)
+        )(ids, context.T, out_weight)
         att_got = swap_core(att_send)
     with jax.named_scope("routing"):
         pick_keep, pick_send, merge_high, merge_low = call(
@@ -320,42 +327,43 @@
     weight_in = expert_in[0]
     weight_out = expert_out[0]
     tall = shards * block
-    flops = 4 * tall * width * units
-
-    def forward(xs, kind):
+    flops = 16 * tall * width * units
+
+    def forward(xs, kind, *after):
         return call(
             forward_kernel,
             [sds((tall, units), F32), sds((tall, width), kind)],
-            [VMEM] * 6,
+            [VMEM] * 6 + [ANY] * len(after),
             [pltpu.VMEM((tall, width), BF), pltpu.VMEM((tall, units), BF)],
             flops=flops,
             moved=10**7,
             mib=24,
-        )(*xs, weight_in, weight_out)
-
-    def backward(xs, slope, kind):
+        )(*xs, weight_in, weight_out, *after)
+
+    def backward(xs, slope, kind, *after):
         return call(
             backward_kernel,
             sds((tall, width), kind),
-            [VMEM] * 7,
+            [VMEM] * 7 + [ANY] * len(after),
             [pltpu.VMEM((tall, width), BF), pltpu.VMEM((tall, units), BF)],
             flops=flops,
             moved=10**7,
             mib=24,
-        )(*xs, weight_in, weight_out, slope)
+        )(*xs, weight_in, weight_out, slope, *after)
 
     with jax.named_scope("gather_normed"):
         keeps, sends = gather_y(normed_rows)
     with jax.named_scope("gather_down"):
         down_keeps, down_sends = gather_y(down_rows)
     with jax.named_scope("forward"):
-        slope_send, part_send = forward(sends, BF)
         slope_keep, part_keep = forward(keeps, F32)
+        slope_send, part_send = forward(sends, BF, slope_keep)
     with jax.named_scope("return_result"):
-        result = reduce_y(combine(part_keep, part_send))
+        parts = combine(part_keep, part_send)
+        result = reduce_y(parts)
     with jax.named_scope("backward"):
         back_send = backward(down_sends, slope_send, BF)
-        back_keep = backward(down_keeps, slope_keep, F32)
+        back_keep = backward(down_keeps, slope_keep, F32, parts[3])
     with jax.named_scope("return_back"):
         back = reduce_y(combine(back_keep, back_send))
     with jax.named_scope("collect"):

time: 114 us -> 110 us (0.965)
  starting transfers between devices: 36.2 us -> 32.2 us
  blocking collectives: 38.8 us -> 40.5 us
    ppermute x13, starting transfers between devices: 25.8 us -> 21.4 us  [swap_core(): return lax.ppermute(x, 'core', [(0, 1), (1, 0)])]
    all_to_all x2, blocking collectives: 38.8 us -> 40.5 us  [exchange(): lax.all_to_all(x.reshape(experts, PACK, WIDE), 'xz', split_axis=0, concat...]
    unnamed x19 -> x20, local copies, waits for them, and re-layouts: 3.94 us -> 3.66 us
  transfers between devices with their start and end apart: 25 -> 25, of which waited for: 8 -> 8; matrix products, arithmetic and copies ran while one was open for 0% -> 0% of each run, Pallas kernels for 10% -> 11%
where the time goes in v6:
time: 110 us
  blocking collectives  40.5 us (37%)
  starting transfers between devices  32.2 us (29%)
  Pallas kernels  17.3 us (16%)
  waiting for transfers between devices  15.3 us (14%)
  local copies, waits for them, and re-layouts  3.75 us (3%)
    all_to_all x2, blocking collectives, exchange(): lax.all_to_all(x.reshape(experts, PACK, WIDE), 'xz', split_axis=0, concat...  40.5 us
    ppermute x13, starting transfers between devices, swap_core(): return lax.ppermute(x, 'core', [(0, 1), (1, 0)])  21.4 us
    ppermute x12, waiting for transfers between devices, ring(): return lax.ppermute(x, ('y', 'core'), pairs)  12 us
    ppermute x12, starting transfers between devices, ring(): return lax.ppermute(x, ('y', 'core'), pairs)  10.7 us
    pallas_call x2, Pallas kernels, forward(): call(forward_kernel, [sds((tall, units), F32), sds((tall, width), kind)],...  5.15 us
    pallas_call x2, Pallas kernels, backward(): call(backward_kernel, sds((tall, width), kind), [VMEM] * 7 + [ANY] * len(...  4.45 us
    unnamed x20, local copies, waits for them, and re-layouts  3.66 us
    ppermute x13, waiting for transfers between devices, swap_core(): return lax.ppermute(x, 'core', [(0, 1), (1, 0)])  3.26 us
  transfers between devices with their start and end apart: 25, of which 8 were waited for; matrix products, arithmetic and copies ran while one was open for 0% of the time, Pallas kernels for 11%

profile of v6, /device:TPU:1, one launch (start us, length us, event | category | flops | bytes accessed | tf_op | source)
XLA Modules:
  0.0 110.0 jit_solution(10532862221509101630)
XLA Ops:
  0.7 1.8 %copy-done = bf16[832,1664]{1,0:T(8,128)(2,1)S(1)} copy-done((bf16[832,1664]{1,0:T(8,128)(2,1)S(1)}, bf16[832,1664]{1,0:T(8,128)(2,1)}, u32[]{:S(2)}) %copy-start) | copy-done | bytes 2768920
  2.5 1.0 copy-done.1
  3.5 1.7 %attend.1 = (f32[128,1664]{1,0:T(8,128)S(1)}, f32[128,1664]{1,0:T(8,128)S(1)}) custom-call(s32[2]{0:T(128)S(1)} %pad_add_fusion.ids, bf16[832,256]{1,0:T(8,128)(2,1)S(1)} %bitcast.15, bf16[832,1664]{1,0:T(8,128)(2,1)S(1)} %copy-done), custom_call_target="tpu_custom_call" | custom-call | flops 708837376 | bytes 5000000 | tf_op jit(solution)/shard_map/attend/pallas_call | solution.py:273
  5.3 3.3 %collective-permute-start = (f32[128,1664]{1,0:T(8,128)S(1)}, f32[128,1664]{1,0:T(8,128)S(1)}, u32[]{:S(2)}, u32[]{:S(2)}) collective-permute-start(f32[128,1664]{1,0:T(8,128)S(1)} %get-tuple-element.26), channel_id=1, source_target_pairs={{0,1},{1,0},{2,3},{3,2},{4,5},{5,4},{6,7},{7,6},{8,9},{9,8},{10,11... | collective-permute-start | bytes 2555912 | tf_op jit(solution)/shard_map/attend/ppermute | solution.py:256
  8.7 0.8 copy-done.7
  9.5 1.7 %routing.1 = (bf16[256,512]{1,0:T(8,128)(2,1)S(1)}, bf16[256,512]{1,0:T(8,128)(2,1)S(1)}, bf16[512,512]{1,0:T(8,128)(2,1)S(1)}, bf16[512,512]{1,0:T(8,128)(2,1)S(1)}) custom-call(s32[2]{0:T(128)S(1)} %pad_add_fusion.ids, s32[32,512]{1,0:T(8,128)S(1)} %copy-done.6, s32[32,1]{1,0:T(8,128)S(1)} %copy.12.count, f32[32,512]{1,0:T(8,128)S(1)} %copy-done.7), custom_call_target="tpu_custom_call" | custom-call | flops 1000000000 | bytes 2000000 | tf_op jit(solution)/shard_map/routing/pallas_call | solution.py:282
  11.2 1.0 norm.1
  12.4 1.8 %collective-permute-done.1 = bf16[256,896]{1,0:T(8,128)(2,1)S(1)} collective-permute-done((bf16[256,896]{1,0:T(8,128)(2,1)S(1)}, bf16[256,896]{1,0:T(8,128)(2,1)S(1)}, u32[]{:S(2)}, u32[]{:S(2)}) %collective-permute-start.1) | collective-permute-done | bytes 458784 | tf_op jit(solution)/shard_map/dispatch/ppermute | solution.py:256
  14.2 22.2 %all_to_all.10 = bf16[32,8,896]{2,1,0:T(8,128)(2,1)S(1)} all-to-all(bf16[32,8,896]{2,1,0:T(8,128)(2,1)S(1)} %add_bitcast_fusion), channel_id=1, replica_groups=mesh['xz'=32,'y'=4,'core'=2] {'xz'}, dimensions={0} | all-to-all | bytes 917504 | tf_op jit(solution)/shard_map/dispatch/all_to_all | solution.py:267
  36.7 2.8 %collective-permute-start.2 = (bf16[64,1664]{1,0:T(8,128)(2,1)S(1)}, bf16[64,1664]{1,0:T(8,128)(2,1)S(1)}, u32[]{:S(2)}, u32[]{:S(2)}) collective-permute-start(bf16[64,1664]{1,0:T(8,128)(2,1)S(1)} %get-tuple-element.31.x0), channel_id=1, source_target_pairs={{0,2},{1,7},{2,4},{3,1},{4,6},{5,3},{6,0},{7,5},{8,10},{9,15},{10,... | collective-permute-start | bytes 638984 | tf_op jit(solution)/shard_map/gather_normed/ppermute | solution.py:264
  39.5 3.8 %collective-permute-start.5 = (bf16[64,1664]{1,0:T(8,128)(2,1)S(1)}, bf16[64,1664]{1,0:T(8,128)(2,1)S(1)}, u32[]{:S(2)}, u32[]{:S(2)}) collective-permute-start(bf16[64,1664]{1,0:T(8,128)(2,1)S(1)} %get-tuple-element.31.x0), channel_id=1, source_target_pairs={{0,1},{1,0},{2,3},{3,2},{4,5},{5,4},{6,7},{7,6},{8,9},{9,8},{10,11... | collective-permute-start | bytes 638984 | tf_op jit(solution)/shard_map/gather_normed/ppermute | solution.py:256
  43.3 1.5 %collective-permute-start.13 = (bf16[64,1664]{1,0:T(8,128)(2,1)S(1)}, bf16[64,1664]{1,0:T(8,128)(2,1)S(1)}, u32[]{:S(2)}, u32[]{:S(2)}) collective-permute-start(bf16[64,1664]{1,0:T(8,128)(2,1)S(1)} %get-tuple-element.39.x0), channel_id=1, source_target_pairs={{0,2},{1,7},{2,4},{3,1},{4,6},{5,3},{6,0},{7,5},{8,10},{9,15},{10,... | collective-permute-start | bytes 638984 | tf_op jit(solution)/shard_map/gather_down/ppermute | solution.py:264
  44.9 0.6 collective-permute-start.4
  45.4 0.9 collective-permute-start.14
  46.3 0.6 collective-permute-done.3.x2
  47.0 4.7 %collective-permute-start.6 = (bf16[64,1664]{1,0:T(8,128)(2,1)S(1)}, bf16[64,1664]{1,0:T(8,128)(2,1)S(1)}, u32[]{:S(2)}, u32[]{:S(2)}) collective-permute-start(bf16[64,1664]{1,0:T(8,128)(2,1)S(1)} %collective-permute-done.2.x1), channel_id=1, source_target_pairs={{0,1},{1,0},{2,3},{3,2},{4,5},{5,4},{6,7},{7,6},{8,9},{9,8},{10,11... | collective-permute-start | bytes 638984 | tf_op jit(solution)/shard_map/gather_normed/ppermute | solution.py:256
  51.8 3.7 %collective-permute-start.8 = (bf16[64,1664]{1,0:T(8,128)(2,1)S(1)}, bf16[64,1664]{1,0:T(8,128)(2,1)S(1)}, u32[]{:S(2)}, u32[]{:S(2)}) collective-permute-start(bf16[64,1664]{1,0:T(8,128)(2,1)S(1)} %collective-permute-done.4.x3), channel_id=1, source_target_pairs={{0,1},{1,0},{2,3},{3,2},{4,5},{5,4},{6,7},{7,6},{8,9},{9,8},{10,11... | collective-permute-start | bytes 638984 | tf_op jit(solution)/shard_map/gather_normed/ppermute | solution.py:256
  55.5 2.6 %forward.2 = (f32[256,1024]{1,0:T(8,128)S(1)}, f32[256,1664]{1,0:T(8,128)S(1)}) custom-call(bf16[64,1664]{1,0:T(8,128)(2,1)S(1)} %get-tuple-element.31.x0, bf16[64,1664]{1,0:T(8,128)(2,1)S(1)} %collective-permute-done.2.x1, bf16[64,1664]{1,0:T(8,128)(2,1)S(1)} %collective-permute-done.3.x2, bf16[64,1664]{1,0:T(8,128)(2,1)S(1)} %collective-permute-done.4.x3, ...), custom_call_target="tpu_custom_call" | custom-call | flops 6979321856 | bytes 10000000 | tf_op jit(solution)/shard_map/forward/pallas_call | solution.py:333
  59.2 2.6 %forward.3 = (f32[256,1024]{1,0:T(8,128)S(1)}, bf16[256,1664]{1,0:T(8,128)(2,1)S(1)}) custom-call(bf16[64,1664]{1,0:T(8,128)(2,1)S(1)} %collective-permute-done.5.x0, bf16[64,1664]{1,0:T(8,128)(2,1)S(1)} %collective-permute-done.6.x1, bf16[64,1664]{1,0:T(8,128)(2,1)S(1)} %collective-permute-done.7.x2, bf16[64,1664]{1,0:T(8,128)(2,1)S(1)} %collective-permute-done.8.x3, ...), custom_call_target="tpu_custom_call" | custom-call | flops 6979321856 | bytes 10000000 | tf_op jit(solution)/shard_map/forward/pallas_call | solution.py:333
  62.0 2.2 %backward.3 = bf16[256,1664]{1,0:T(8,128)(2,1)S(1)} custom-call(bf16[64,1664]{1,0:T(8,128)(2,1)S(1)} %collective-permute-done.16.x0, bf16[64,1664]{1,0:T(8,128)(2,1)S(1)} %collective-permute-done.17.x1, bf16[64,1664]{1,0:T(8,128)(2,1)S(1)} %collective-permute-done.18.x2, bf16[64,1664]{1,0:T(8,128)(2,1)S(1)} %collective-permute-done.19.x3, ...), custom_call_target="tpu_custom_call" | custom-call | flops 6979321856 | bytes 10000000 | tf_op jit(solution)/shard_map/backward/pallas_call | solution.py:344
  65.0 2.2 %backward.2.keep = f32[256,1664]{1,0:T(8,128)S(1)} custom-call(bf16[64,1664]{1,0:T(8,128)(2,1)S(1)} %get-tuple-element.39.x0, bf16[64,1664]{1,0:T(8,128)(2,1)S(1)} %collective-permute-done.13.x1, bf16[64,1664]{1,0:T(8,128)(2,1)S(1)} %collective-permute-done.14.x2, bf16[64,1664]{1,0:T(8,128)(2,1)S(1)} %collective-permute-done.15.x3, ...), custom_call_target="tpu_custom_call" | custom-call | flops 6979321856 | bytes 10000000 | tf_op jit(solution)/shard_map/backward/pallas_call | solution.py:344
  67.7 2.7 %collective-permute-start.12 = (bf16[64,1664]{1,0:T(8,128)(2,1)S(1)}, bf16[64,1664]{1,0:T(8,128)(2,1)S(1)}, u32[]{:S(2)}, u32[]{:S(2)}) collective-permute-start(bf16[64,1664]{1,0:T(8,128)(2,1)S(1)} %get-tuple-element.38), channel_id=1, source_target_pairs={{0,2},{1,7},{2,4},{3,1},{4,6},{5,3},{6,0},{7,5},{8,10},{9,15},{10,... | collective-permute-start | bytes 638984 | tf_op jit(solution)/shard_map/return_result/ppermute | solution.py:264
  70.4 1.4 %collective-permute-start.23 = (bf16[64,1664]{1,0:T(8,128)(2,1)S(1)}, bf16[64,1664]{1,0:T(8,128)(2,1)S(1)}, u32[]{:S(2)}, u32[]{:S(2)}) collective-permute-start(bf16[64,1664]{1,0:T(8,128)(2,1)S(1)} %get-tuple-element.44), channel_id=1, source_target_pairs={{0,2},{1,7},{2,4},{3,1},{4,6},{5,3},{6,0},{7,5},{8,10},{9,15},{10,... | collective-permute-start | bytes 638984 | tf_op jit(solution)/shard_map/return_back/ppermute | solution.py:264
  72.0 1.6 %collective-permute-done.21.b = bf16[64,1664]{1,0:T(8,128)(2,1)S(1)} collective-permute-done((bf16[64,1664]{1,0:T(8,128)(2,1)S(1)}, bf16[64,1664]{1,0:T(8,128)(2,1)S(1)}, u32[]{:S(2)}, u32[]{:S(2)}) %collective-permute-start.21) | collective-permute-done | bytes 213024 | tf_op jit(solution)/shard_map/return_back/ppermute | solution.py:264
  73.9 1.4 %collective-permute-done.12.two_r = bf16[64,1664]{1,0:T(8,128)(2,1)S(1)} collective-permute-done((bf16[64,1664]{1,0:T(8,128)(2,1)S(1)}, bf16[64,1664]{1,0:T(8,128)(2,1)S(1)}, u32[]{:S(2)}, u32[]{:S(2)}) %collective-permute-start.12) | collective-permute-done | bytes 213024 | tf_op jit(solution)/shard_map/return_result/ppermute | solution.py:264
  75.3 3.7 %collective-permute-done.23.two_b = bf16[64,1664]{1,0:T(8,128)(2,1)S(1)} collective-permute-done((bf16[64,1664]{1,0:T(8,128)(2,1)S(1)}, bf16[64,1664]{1,0:T(8,128)(2,1)S(1)}, u32[]{:S(2)}, u32[]{:S(2)}) %collective-permute-start.23) | collective-permute-done | bytes 213024 | tf_op jit(solution)/shard_map/return_back/ppermute | solution.py:264
  79.1 1.3 %collective-permute-done.11.one_r = bf16[64,1664]{1,0:T(8,128)(2,1)S(1)} collective-permute-done((bf16[64,1664]{1,0:T(8,128)(2,1)S(1)}, bf16[64,1664]{1,0:T(8,128)(2,1)S(1)}, u32[]{:S(2)}, u32[]{:S(2)}) %collective-permute-start.11) | collective-permute-done | bytes 213024 | tf_op jit(solution)/shard_map/return_result/ppermute | solution.py:264
  80.4 3.3 %collective-permute-done.22.one_b = bf16[64,1664]{1,0:T(8,128)(2,1)S(1)} collective-permute-done((bf16[64,1664]{1,0:T(8,128)(2,1)S(1)}, bf16[64,1664]{1,0:T(8,128)(2,1)S(1)}, u32[]{:S(2)}, u32[]{:S(2)}) %collective-permute-start.22) | collective-permute-done | bytes 213024 | tf_op jit(solution)/shard_map/return_back/ppermute | solution.py:264
  84.1 18.4 %all_to_all.11 = bf16[32,8,896]{2,1,0:T(8,128)(2,1)S(1)} all-to-all(bf16[32,8,896]{2,1,0:T(8,128)(2,1)S(1)} %bitcast.11), channel_id=1, replica_groups=mesh['xz'=32,'y'=4,'core'=2] {'xz'}, dimensions={0} | all-to-all | bytes 917504 | tf_op jit(solution)/shard_map/collect/all_to_all | solution.py:267
  102.4 3.9 %collective-permute-start.24 = (bf16[256,896]{1,0:T(8,128)(2,1)S(1)}, bf16[256,896]{1,0:T(8,128)(2,1)S(1)}, u32[]{:S(2)}, u32[]{:S(2)}) collective-permute-start(bf16[256,896]{1,0:T(8,128)(2,1)S(1)} %bitcast.13), channel_id=1, source_target_pairs={{0,1},{1,0},{2,3},{3,2},{4,5},{5,4},{6,7},{7,6},{8,9},{9,8},{10,11... | collective-permute-start | bytes 1376264 | tf_op jit(solution)/shard_map/collect/ppermute | solution.py:256
  106.3 1.4 %collective-permute-done.24.theirs = bf16[256,896]{1,0:T(8,128)(2,1)S(1)} collective-permute-done((bf16[256,896]{1,0:T(8,128)(2,1)S(1)}, bf16[256,896]{1,0:T(8,128)(2,1)S(1)}, u32[]{:S(2)}, u32[]{:S(2)}) %collective-permute-start.24) | collective-permute-done | bytes 458784 | tf_op jit(solution)/shard_map/collect/ppermute | solution.py:256
  107.7 2.3 %final.1 = (bf16[128,1664]{1,0:T(8,128)(2,1)}, bf16[128,1664]{1,0:T(8,128)(2,1)}) custom-call(bf16[256,896]{1,0:T(8,128)(2,1)S(1)} %bitcast.14, bf16[256,896]{1,0:T(8,128)(2,1)S(1)} %collective-permute-done.24.theirs, bf16[512,512]{1,0:T(8,128)(2,1)S(1)} %get-tuple-element.45.merge_high, bf16[512,512]{1,0:T(8,128)(2,1)S(1)} %get-tuple-element.46.merge_low, ...), custom_call_target="tpu_custom_call" | custom-call | flops 1000000000 | bytes 4000000 | tf_op jit(solution)/shard_map/final/pallas_call | solution.py:381
  (58 shorter events, 4.2 us)
Async XLA Ops:
  0.6 7.9 %copy-start.8 = (f32[1664]{0:T(1024)S(1)}, f32[1664]{0:T(1024)}, u32[]{:S(2)}) copy-start(f32[1664]{0:T(1024)} %param.13) | copy-start | bytes 19972
  0.6 8.0 %copy-start.9 = (s32[32]{0:T(128)S(1)}, s32[32]{0:T(128)}, u32[]{:S(2)}) copy-start(s32[32]{0:T(128)} %param.17) | copy-start | bytes 388
  3.5 5.2 %copy-start.6 = (s32[32,512]{1,0:T(8,128)S(1)}, s32[32,512]{1,0:T(8,128)}, u32[]{:S(2)}) copy-start(s32[32,512]{1,0:T(8,128)} %index.1) | copy-start | bytes 196612
  3.5 7.7 %copy-start.4 = (bf16[128,1664]{1,0:T(8,128)(2,1)S(1)}, bf16[128,1664]{1,0:T(8,128)(2,1)}, u32[]{:S(2)}) copy-start(bf16[128,1664]{1,0:T(8,128)(2,1)} %residual.1) | copy-start | bytes 1277956
  3.5 7.7 %copy-start.5 = (bf16[128,1664]{1,0:T(8,128)(2,1)S(1)}, bf16[128,1664]{1,0:T(8,128)(2,1)}, u32[]{:S(2)}) copy-start(bf16[128,1664]{1,0:T(8,128)(2,1)} %upstream.3) | copy-start | bytes 1277956
  5.3 6.0 %collective-permute-start = (f32[128,1664]{1,0:T(8,128)S(1)}, f32[128,1664]{1,0:T(8,128)S(1)}, u32[]{:S(2)}, u32[]{:S(2)}) collective-permute-start(f32[128,1664]{1,0:T(8,128)S(1)} %get-tuple-element.26), channel_id=1, source_target_pairs={{0,1},{1,0},{2,3},{3,2},{4,5},{5,4},{6,7},{7,6},{8,9},{9,8},{10,11... | collective-permute-start | bytes 2555912 | tf_op jit(solution)/shard_map/attend/ppermute | solution.py:256
  9.5 45.9 %copy-start.3 = (bf16[1,1024,1664]{2,1,0:T(8,128)(2,1)S(1)}, bf16[1,1024,1664]{2,1,0:T(8,128)(2,1)}, u32[]{:S(2)}) copy-start(bf16[1,1024,1664]{2,1,0:T(8,128)(2,1)} %param.15) | copy-start | bytes 10223620
  11.2 44.2 %copy-start.2 = (bf16[1,1664,1024]{2,1,0:T(8,128)(2,1)S(1)}, bf16[1,1664,1024]{2,1,0:T(8,128)(2,1)}, u32[]{:S(2)}) copy-start(bf16[1,1664,1024]{2,1,0:T(8,128)(2,1)} %param.14) | copy-start | bytes 10223620
  12.3 1.9 %collective-permute-start.1 = (bf16[256,896]{1,0:T(8,128)(2,1)S(1)}, bf16[256,896]{1,0:T(8,128)(2,1)S(1)}, u32[]{:S(2)}, u32[]{:S(2)}) collective-permute-start(bf16[256,896]{1,0:T(8,128)(2,1)S(1)} %get-tuple-element.30), channel_id=1, source_target_pairs={{0,1},{1,0},{2,3},{3,2},{4,5},{5,4},{6,7},{7,6},{8,9},{9,8},{10,11... | collective-permute-start | bytes 1376264 | tf_op jit(solution)/shard_map/dispatch/ppermute | solution.py:256
  36.7 8.2 %collective-permute-start.2 = (bf16[64,1664]{1,0:T(8,128)(2,1)S(1)}, bf16[64,1664]{1,0:T(8,128)(2,1)S(1)}, u32[]{:S(2)}, u32[]{:S(2)}) collective-permute-start(bf16[64,1664]{1,0:T(8,128)(2,1)S(1)} %get-tuple-element.31.x0), channel_id=1, source_target_pairs={{0,2},{1,7},{2,4},{3,1},{4,6},{5,3},{6,0},{7,5},{8,10},{9,15},{10,... | collective-permute-start | bytes 638984 | tf_op jit(solution)/shard_map/gather_normed/ppermute | solution.py:264
  39.5 7.4 %collective-permute-start.3 = (bf16[64,1664]{1,0:T(8,128)(2,1)S(1)}, bf16[64,1664]{1,0:T(8,128)(2,1)S(1)}, u32[]{:S(2)}, u32[]{:S(2)}) collective-permute-start(bf16[64,1664]{1,0:T(8,128)(2,1)S(1)} %get-tuple-element.31.x0), channel_id=1, source_target_pairs={{0,6},{1,3},{2,0},{3,5},{4,2},{5,7},{6,4},{7,1},{8,14},{9,11},{10,... | collective-permute-start | bytes 638984 | tf_op jit(solution)/shard_map/gather_normed/ppermute | solution.py:264
  39.5 12.1 %collective-permute-start.5 = (bf16[64,1664]{1,0:T(8,128)(2,1)S(1)}, bf16[64,1664]{1,0:T(8,128)(2,1)S(1)}, u32[]{:S(2)}, u32[]{:S(2)}) collective-permute-start(bf16[64,1664]{1,0:T(8,128)(2,1)S(1)} %get-tuple-element.31.x0), channel_id=1, source_target_pairs={{0,1},{1,0},{2,3},{3,2},{4,5},{5,4},{6,7},{7,6},{8,9},{9,8},{10,11... | collective-permute-start | bytes 638984 | tf_op jit(solution)/shard_map/gather_normed/ppermute | solution.py:256
  43.3 8.4 %collective-permute-start.13 = (bf16[64,1664]{1,0:T(8,128)(2,1)S(1)}, bf16[64,1664]{1,0:T(8,128)(2,1)S(1)}, u32[]{:S(2)}, u32[]{:S(2)}) collective-permute-start(bf16[64,1664]{1,0:T(8,128)(2,1)S(1)} %get-tuple-element.39.x0), channel_id=1, source_target_pairs={{0,2},{1,7},{2,4},{3,1},{4,6},{5,3},{6,0},{7,5},{8,10},{9,15},{10,... | collective-permute-start | bytes 638984 | tf_op jit(solution)/shard_map/gather_down/ppermute | solution.py:264
  44.9 6.9 %collective-permute-start.4 = (bf16[64,1664]{1,0:T(8,128)(2,1)S(1)}, bf16[64,1664]{1,0:T(8,128)(2,1)S(1)}, u32[]{:S(2)}, u32[]{:S(2)}) collective-permute-start(bf16[64,1664]{1,0:T(8,128)(2,1)S(1)} %collective-permute-done.2.x1), channel_id=1, source_target_pairs={{0,2},{1,7},{2,4},{3,1},{4,6},{5,3},{6,0},{7,5},{8,10},{9,15},{10,... | collective-permute-start | bytes 638984 | tf_op jit(solution)/shard_map/gather_normed/ppermute | solution.py:264
  45.4 12.6 %collective-permute-start.14 = (bf16[64,1664]{1,0:T(8,128)(2,1)S(1)}, bf16[64,1664]{1,0:T(8,128)(2,1)S(1)}, u32[]{:S(2)}, u32[]{:S(2)}) collective-permute-start(bf16[64,1664]{1,0:T(8,128)(2,1)S(1)} %get-tuple-element.39.x0), channel_id=1, source_target_pairs={{0,6},{1,3},{2,0},{3,5},{4,2},{5,7},{6,4},{7,1},{8,14},{9,11},{10,... | collective-permute-start | bytes 638984 | tf_op jit(solution)/shard_map/gather_down/ppermute | solution.py:264
  47.0 11.2 %collective-permute-start.6 = (bf16[64,1664]{1,0:T(8,128)(2,1)S(1)}, bf16[64,1664]{1,0:T(8,128)(2,1)S(1)}, u32[]{:S(2)}, u32[]{:S(2)}) collective-permute-start(bf16[64,1664]{1,0:T(8,128)(2,1)S(1)} %collective-permute-done.2.x1), channel_id=1, source_target_pairs={{0,1},{1,0},{2,3},{3,2},{4,5},{5,4},{6,7},{7,6},{8,9},{9,8},{10,11... | collective-permute-start | bytes 638984 | tf_op jit(solution)/shard_map/gather_normed/ppermute | solution.py:256
  51.6 7.0 %collective-permute-start.7 = (bf16[64,1664]{1,0:T(8,128)(2,1)S(1)}, bf16[64,1664]{1,0:T(8,128)(2,1)S(1)}, u32[]{:S(2)}, u32[]{:S(2)}) collective-permute-start(bf16[64,1664]{1,0:T(8,128)(2,1)S(1)} %collective-permute-done.3.x2), channel_id=1, source_target_pairs={{0,1},{1,0},{2,3},{3,2},{4,5},{5,4},{6,7},{7,6},{8,9},{9,8},{10,11... | collective-permute-start | bytes 638984 | tf_op jit(solution)/shard_map/gather_normed/ppermute | solution.py:256
  51.7 7.0 %collective-permute-start.15 = (bf16[64,1664]{1,0:T(8,128)(2,1)S(1)}, bf16[64,1664]{1,0:T(8,128)(2,1)S(1)}, u32[]{:S(2)}, u32[]{:S(2)}) collective-permute-start(bf16[64,1664]{1,0:T(8,128)(2,1)S(1)} %collective-permute-done.13.x1), channel_id=1, source_target_pairs={{0,2},{1,7},{2,4},{3,1},{4,6},{5,3},{6,0},{7,5},{8,10},{9,15},{10,... | collective-permute-start | bytes 638984 | tf_op jit(solution)/shard_map/gather_down/ppermute | solution.py:264
  51.8 7.5 %collective-permute-start.8 = (bf16[64,1664]{1,0:T(8,128)(2,1)S(1)}, bf16[64,1664]{1,0:T(8,128)(2,1)S(1)}, u32[]{:S(2)}, u32[]{:S(2)}) collective-permute-start(bf16[64,1664]{1,0:T(8,128)(2,1)S(1)} %collective-permute-done.4.x3), channel_id=1, source_target_pairs={{0,1},{1,0},{2,3},{3,2},{4,5},{5,4},{6,7},{7,6},{8,9},{9,8},{10,11... | collective-permute-start | bytes 638984 | tf_op jit(solution)/shard_map/gather_normed/ppermute | solution.py:256
  58.1 3.9 %collective-permute-start.16 = (bf16[64,1664]{1,0:T(8,128)(2,1)S(1)}, bf16[64,1664]{1,0:T(8,128)(2,1)S(1)}, u32[]{:S(2)}, u32[]{:S(2)}) collective-permute-start(bf16[64,1664]{1,0:T(8,128)(2,1)S(1)} %get-tuple-element.39.x0), channel_id=1, source_target_pairs={{0,1},{1,0},{2,3},{3,2},{4,5},{5,4},{6,7},{7,6},{8,9},{9,8},{10,11... | collective-permute-start | bytes 638984 | tf_op jit(solution)/shard_map/gather_down/ppermute | solution.py:256
  58.2 3.8 %collective-permute-start.17 = (bf16[64,1664]{1,0:T(8,128)(2,1)S(1)}, bf16[64,1664]{1,0:T(8,128)(2,1)S(1)}, u32[]{:S(2)}, u32[]{:S(2)}) collective-permute-start(bf16[64,1664]{1,0:T(8,128)(2,1)S(1)} %collective-permute-done.13.x1), channel_id=1, source_target_pairs={{0,1},{1,0},{2,3},{3,2},{4,5},{5,4},{6,7},{7,6},{8,9},{9,8},{10,11... | collective-permute-start | bytes 638984 | tf_op jit(solution)/shard_map/gather_down/ppermute | solution.py:256
  58.7 3.3 %collective-permute-start.18 = (bf16[64,1664]{1,0:T(8,128)(2,1)S(1)}, bf16[64,1664]{1,0:T(8,128)(2,1)S(1)}, u32[]{:S(2)}, u32[]{:S(2)}) collective-permute-start(bf16[64,1664]{1,0:T(8,128)(2,1)S(1)} %collective-permute-done.14.x2), channel_id=1, source_target_pairs={{0,1},{1,0},{2,3},{3,2},{4,5},{5,4},{6,7},{7,6},{8,9},{9,8},{10,11... | collective-permute-start | bytes 638984 | tf_op jit(solution)/shard_map/gather_down/ppermute | solution.py:256
  58.8 3.2 %collective-permute-start.19 = (bf16[64,1664]{1,0:T(8,128)(2,1)S(1)}, bf16[64,1664]{1,0:T(8,128)(2,1)S(1)}, u32[]{:S(2)}, u32[]{:S(2)}) collective-permute-start(bf16[64,1664]{1,0:T(8,128)(2,1)S(1)} %collective-permute-done.15.x3), channel_id=1, source_target_pairs={{0,1},{1,0},{2,3},{3,2},{4,5},{5,4},{6,7},{7,6},{8,9},{9,8},{10,11... | collective-permute-start | bytes 638984 | tf_op jit(solution)/shard_map/gather_down/ppermute | solution.py:256
  61.8 2.9 %collective-permute-start.9 = (bf16[256,1664]{1,0:T(8,128)(2,1)S(1)}, bf16[256,1664]{1,0:T(8,128)(2,1)S(1)}, u32[]{:S(2)}, u32[]{:S(2)}) collective-permute-start(bf16[256,1664]{1,0:T(8,128)(2,1)S(1)} %get-tuple-element.34), channel_id=1, source_target_pairs={{0,1},{1,0},{2,3},{3,2},{4,5},{5,4},{6,7},{7,6},{8,9},{9,8},{10,11... | collective-permute-start | bytes 2555912 | tf_op jit(solution)/shard_map/return_result/ppermute | solution.py:256
  64.2 3.0 %collective-permute-start.20 = (bf16[256,1664]{1,0:T(8,128)(2,1)S(1)}, bf16[256,1664]{1,0:T(8,128)(2,1)S(1)}, u32[]{:S(2)}, u32[]{:S(2)}) collective-permute-start(bf16[256,1664]{1,0:T(8,128)(2,1)S(1)} %backward.3), channel_id=1, source_target_pairs={{0,1},{1,0},{2,3},{3,2},{4,5},{5,4},{6,7},{7,6},{8,9},{9,8},{10,11... | collective-permute-start | bytes 2555912 | tf_op jit(solution)/shard_map/return_back/ppermute | solution.py:256
  64.9 6.9 %collective-permute-start.10 = (bf16[64,1664]{1,0:T(8,128)(2,1)S(1)}, bf16[64,1664]{1,0:T(8,128)(2,1)S(1)}, u32[]{:S(2)}, u32[]{:S(2)}) collective-permute-start(bf16[64,1664]{1,0:T(8,128)(2,1)S(1)} %get-tuple-element.37.rest_0_), channel_id=1, source_target_pairs={{0,6},{1,3},{2,0},{3,5},{4,2},{5,7},{6,4},{7,1},{8,14},{9,11},{10,... | collective-permute-start | bytes 638984 | tf_op jit(solution)/shard_map/return_result/ppermute | solution.py:264
  67.4 6.2 %collective-permute-start.21 = (bf16[64,1664]{1,0:T(8,128)(2,1)S(1)}, bf16[64,1664]{1,0:T(8,128)(2,1)S(1)}, u32[]{:S(2)}, u32[]{:S(2)}) collective-permute-start(bf16[64,1664]{1,0:T(8,128)(2,1)S(1)} %get-tuple-element.43), channel_id=1, source_target_pairs={{0,6},{1,3},{2,0},{3,5},{4,2},{5,7},{6,4},{7,1},{8,14},{9,11},{10,... | collective-permute-start | bytes 638984 | tf_op jit(solution)/shard_map/return_back/ppermute | solution.py:264
  67.7 7.6 %collective-permute-start.12 = (bf16[64,1664]{1,0:T(8,128)(2,1)S(1)}, bf16[64,1664]{1,0:T(8,128)(2,1)S(1)}, u32[]{:S(2)}, u32[]{:S(2)}) collective-permute-start(bf16[64,1664]{1,0:T(8,128)(2,1)S(1)} %get-tuple-element.38), channel_id=1, source_target_pairs={{0,2},{1,7},{2,4},{3,1},{4,6},{5,3},{6,0},{7,5},{8,10},{9,15},{10,... | collective-permute-start | bytes 638984 | tf_op jit(solution)/shard_map/return_result/ppermute | solution.py:264
  70.4 8.7 %collective-permute-start.23 = (bf16[64,1664]{1,0:T(8,128)(2,1)S(1)}, bf16[64,1664]{1,0:T(8,128)(2,1)S(1)}, u32[]{:S(2)}, u32[]{:S(2)}) collective-permute-start(bf16[64,1664]{1,0:T(8,128)(2,1)S(1)} %get-tuple-element.44), channel_id=1, source_target_pairs={{0,2},{1,7},{2,4},{3,1},{4,6},{5,3},{6,0},{7,5},{8,10},{9,15},{10,... | collective-permute-start | bytes 638984 | tf_op jit(solution)/shard_map/return_back/ppermute | solution.py:264
  71.8 8.6 %collective-permute-start.11 = (bf16[64,1664]{1,0:T(8,128)(2,1)S(1)}, bf16[64,1664]{1,0:T(8,128)(2,1)S(1)}, u32[]{:S(2)}, u32[]{:S(2)}) collective-permute-start(bf16[64,1664]{1,0:T(8,128)(2,1)S(1)} %return_result.3), channel_id=1, source_target_pairs={{0,6},{1,3},{2,0},{3,5},{4,2},{5,7},{6,4},{7,1},{8,14},{9,11},{10,... | collective-permute-start | bytes 638984 | tf_op jit(solution)/shard_map/return_result/ppermute | solution.py:264
  73.6 10.1 %collective-permute-start.22 = (bf16[64,1664]{1,0:T(8,128)(2,1)S(1)}, bf16[64,1664]{1,0:T(8,128)(2,1)S(1)}, u32[]{:S(2)}, u32[]{:S(2)}) collective-permute-start(bf16[64,1664]{1,0:T(8,128)(2,1)S(1)} %return_back.3), channel_id=1, source_target_pairs={{0,6},{1,3},{2,0},{3,5},{4,2},{5,7},{6,4},{7,1},{8,14},{9,11},{10,... | collective-permute-start | bytes 638984 | tf_op jit(solution)/shard_map/return_back/ppermute | solution.py:264
  102.4 5.3 %collective-permute-start.24 = (bf16[256,896]{1,0:T(8,128)(2,1)S(1)}, bf16[256,896]{1,0:T(8,128)(2,1)S(1)}, u32[]{:S(2)}, u32[]{:S(2)}) collective-permute-start(bf16[256,896]{1,0:T(8,128)(2,1)S(1)} %bitcast.13), channel_id=1, source_target_pairs={{0,1},{1,0},{2,3},{3,2},{4,5},{5,4},{6,7},{7,6},{8,9},{9,8},{10,11... | collective-permute-start | bytes 1376264 | tf_op jit(solution)/shard_map/collect/ppermute | solution.py:256
  (3 other events, 3.6 us)

commit v7 on v6

--- a/solution.py
+++ b/solution.py
@@ -1,3 +1,5 @@
+import functools
+
 import jax
 import jax.numpy as jnp
 from jax import lax
@@ -166,11 +168,24 @@
     out[...] = mm(order, flat[...]).astype(BF)
 
 
-def forward_kernel(x0, x1, x2, x3, w1, w2, *rest):
-    slope, part, x, hidden = rest[-4:]
-    block = x0.shape[0]
-    for i, ref in enumerate((x0, x1, x2, x3)):
+def gathered(refs, x):
+    block = refs[0].shape[0]
+    for i, ref in enumerate(refs):
         x[i * block : (i + 1) * block, :] = ref[...]
+
+
+def scatter(value, parts, lo, hi):
+    at = 0
+    for part in parts:
+        rows = part.shape[0]
+        part[:, lo:hi] = value[at : at + rows, :].astype(part.dtype)
+        at += rows
+
+
+def forward_kernel(count, n_parts, *refs):
+    w1, w2 = refs[count : count + 2]
+    slope, *parts, x, hidden = refs[-3 - n_parts :]
+    gathered(refs[:count], x)
     for lo, hi in cuts(hidden.shape[1], 256):
         v = mm(x[...], w1[:, lo:hi])
         square = v * v
@@ -178,43 +193,54 @@
         gate = 0.5 + 0.5 * t
         hidden[:, lo:hi] = (v * gate).astype(BF)
         slope[:, lo:hi] = gate + 0.5 * v * (1.0 - t * t) * (0.7978845608 * (1.0 + 0.134145 * square))
-    for lo, hi in cuts(part.shape[1], 512):
-        part[:, lo:hi] = mm(hidden[...], w2[:, lo:hi]).astype(part.dtype)
-
-
-def backward_kernel(x0, x1, x2, x3, w1, w2, slope, *rest):
-    part, x, grad = rest[-3:]
-    block = x0.shape[0]
-    for i, ref in enumerate((x0, x1, x2, x3)):
-        x[i * block : (i + 1) * block, :] = ref[...]
+    for lo, hi in cuts(w2.shape[1], 512):
+        scatter(mm(hidden[...], w2[:, lo:hi]), parts, lo, hi)
+
+
+def backward_kernel(count, n_parts, *refs):
+    w1, w2, slope = refs[count : count + 3]
+    *parts, x, grad = refs[-2 - n_parts :]
+    gathered(refs[:count], x)
     for lo, hi in cuts(grad.shape[1], 256):
         grad[:, lo:hi] = (mm_t(x[...], w2[lo:hi, :]) * slope[:, lo:hi]).astype(BF)
-    for lo, hi in cuts(part.shape[1], 512):
-        part[:, lo:hi] = mm_t(grad[...], w1[lo:hi, :]).astype(part.dtype)
-
-
-def combine_kernel(keep, got, own, one, two, far):
-    block = own.shape[0]
-    for i, out in enumerate((own, one, two, far)):
+    for lo, hi in cuts(w2.shape[1], 512):
+        scatter(mm_t(grad[...], w1[lo:hi, :]), parts, lo, hi)
+
+
+def combine_kernel(keep, got, *outs):
+    block = outs[0].shape[0]
+    for i, out in enumerate(outs):
         at = slice(i * block, (i + 1) * block)
         out[...] = (keep[at, :] + got[at, :].astype(F32)).astype(out.dtype)
 
 
-def add_kernel(a, b, out):
+def add_kernel(a, b, *rest):
+    out = rest[-1]
     out[...] = (a[...].astype(F32) + b[...].astype(F32)).astype(BF)
 
 
-def final_kernel(mine, theirs, merge_high, merge_low, stream, gain, upstream, layer_out, stream_grad, back):
+def merged(rows, merge_high, merge_low, group, size, lo):
+    at = (slice(group * size, (group + 1) * size), slice(lo, lo + rows.shape[0]))
+    return mm(merge_high[at], rows[...]) + mm(merge_low[at], rows[...])
+
+
+def first_kernel(mine, merge_high, merge_low, out):
+    size = out.shape[0] // 4
+    for group in range(4):
+        at = slice(group * size, (group + 1) * size)
+        out[at, :] = merged(mine, merge_high, merge_low, group, size, 0)
+
+
+def final_kernel(first, theirs, merge_high, merge_low, stream, gain, upstream, layer_out, stream_grad, back):
     rows, width = stream.shape
-    n = mine.shape[0]
+    n = theirs.shape[0]
     rest = width - WIDE
     total = stream[...]
     centered, inverse = statistics(total)
     x_hat = centered * inverse
     for group in range(4):
         at = slice(group * rows, (group + 1) * rows)
-        summed = mm(merge_high[at, :n], mine[...]) + mm(merge_high[at, n:], theirs[...])
-        summed += mm(merge_low[at, :n], mine[...]) + mm(merge_low[at, n:], theirs[...])
+        summed = first[at, :] + merged(theirs, merge_high, merge_low, group, rows, n)
         cols = slice(0, WIDE) if group < 2 else slice(WIDE, width)
         summed = summed if group < 2 else summed[:, :rest]
         if group % 2 == 0:
@@ -301,71 +327,72 @@
             unpack_kernel, [sds((block, width), BF)] * 2, [VMEM], flops=10**8, moved=10**6
         )(got)
 
+    weight_in = expert_in[0]
+    weight_out = expert_out[0]
+    single = (block, width)
+
     def gather_y(own):
         one = ring(own, 1)
         two = ring(own, -1)
         far = ring(one, 1)
-        keeps = [own, one, two, far]
-        return keeps, [swap_core(x) for x in keeps]
-
-    def combine(keep_part, send_part):
-        return call(
-            combine_kernel,
-            [sds((block, width), F32)] * 2 + [sds((block, width), BF)] * 2,
-            [VMEM] * 2,
-            flops=10**6,
-            moved=4 * 10**6,
-        )(keep_part, swap_core(send_part))
-
-    def reduce_y(parts):
-        own, one, two, far = parts
+        near = [own, one, two]
+        return near, [swap_core(x) for x in near], [far, swap_core(far)]
+
+    def combine(keep_part, got_part, *kinds):
+        outs = [sds(single, kind) for kind in kinds]
+        return call(combine_kernel, outs, [VMEM] * 2, flops=10**6, moved=10**6)(keep_part, got_part)
+
+    def reduce_y(own, one, two, far, *after):
         from_two = ring(two, 1)
         from_far = ring(far, -1)
-        one = call(add_kernel, sds((block, width), BF), [VMEM] * 2, flops=10**5, moved=10**6)(one, from_far)
+        specs = [VMEM] * 2 + [ANY] * (1 + len(after))
+        one = call(add_kernel, sds(single, BF), specs, flops=10**5, moved=10**6)(
+            one, from_far, from_two, *after
+        )
         return own, ring(one, -1), from_two
 
-    weight_in = expert_in[0]
-    weight_out = expert_out[0]
-    tall = shards * block
-    flops = 16 * tall * width * units
-
-    def forward(xs, kind, *after):
+    def expert(kernel, xs, weights, outs, after):
+        tall = len(xs) * block
+        parts = [sds((rows_of, width), kind) for rows_of, kind in outs]
+        slope = [sds((tall, units), F32)] if kernel is forward_kernel else []
         return call(
-            forward_kernel,
-            [sds((tall, units), F32), sds((tall, width), kind)],
-            [VMEM] * 6 + [ANY] * len(after),
+            functools.partial(kernel, len(xs), len(parts)),
+            slope + parts,
+            [VMEM] * (len(xs) + len(weights)) + [ANY] * len(after),
             [pltpu.VMEM((tall, width), BF), pltpu.VMEM((tall, units), BF)],
-            flops=flops,
+            flops=16 * tall * width * units,
             moved=10**7,
             mib=24,
-        )(*xs, weight_in, weight_out, *after)
-
-    def backward(xs, slope, kind, *after):
-        return call(
-            backward_kernel,
-            sds((tall, width), kind),
-            [VMEM] * 7 + [ANY] * len(after),
-            [pltpu.VMEM((tall, width), BF), pltpu.VMEM((tall, units), BF)],
-            flops=flops,
-            moved=10**7,
-            mib=24,
-        )(*xs, weight_in, weight_out, slope, *after)
-
+        )(*xs, *weights, *after)
+
+    def forward(xs, outs, *after):
+        return expert(forward_kernel, xs, (weight_in, weight_out), outs, after)
+
+    def backward(xs, slope, outs, *after):
+        return expert(backward_kernel, xs, (weight_in, weight_out, slope), outs, after)
+
+    near_f32 = [(3 * block, F32)]
+    near_bf = [(3 * block, BF)]
+    far_both = [(block, F32), (block, BF)]
     with jax.named_scope("gather_normed"):
-        keeps, sends = gather_y(normed_rows)
+        near, near_send, far = gather_y(normed_rows)
     with jax.named_scope("gather_down"):
-        down_keeps, down_sends = gather_y(down_rows)
+        down, down_send, down_far = gather_y(down_rows)
     with jax.named_scope("forward"):
-        slope_keep, part_keep = forward(keeps, F32)
-        slope_send, part_send = forward(sends, BF, slope_keep)
-    with jax.named_scope("return_result"):
-        parts = combine(part_keep, part_send)
-        result = reduce_y(parts)
+        slope_keep, near_keep = forward(near, near_f32)
+        slope_send, near_out = forward(near_send, near_bf, slope_keep)
+        slope_far, far_keep, far_out = forward(far, far_both, slope_send)
+        near_sums = combine(near_keep, swap_core(near_out), F32, F32, BF)
+        far_sums = combine(far_keep, swap_core(far_out), BF)
     with jax.named_scope("backward"):
-        back_send = backward(down_sends, slope_send, BF)
-        back_keep = backward(down_keeps, slope_keep, F32, parts[3])
-    with jax.named_scope("return_back"):
-        back = reduce_y(combine(back_keep, back_send))
+        (back_out,) = backward(down_send, slope_send, near_bf, slope_far)
+        (back_keep,) = backward(down, slope_keep, near_f32, *far_sums)
+        back_far, back_far_out = backward(down_far, slope_far, far_both)
+        back_sums = combine(back_keep, swap_core(back_out), F32, F32, BF)
+        back_far_sums = combine(back_far, swap_core(back_far_out), BF)
+    with jax.named_scope("reduce"):
+        result = reduce_y(*near_sums, *far_sums, back_sums[2])
+        back = reduce_y(*back_sums, *back_far_sums)
     with jax.named_scope("collect"):
         ready = call(
             pack_kernel,
@@ -378,6 +405,9 @@
         mine = exchange(ready)
         theirs = swap_core(mine)
     with jax.named_scope("final"):
+        first = call(first_kernel, sds((4 * rows, WIDE), F32), [VMEM] * 3, flops=10**9, moved=4 * 10**6)(
+            mine, merge_high, merge_low
+        )
         layer_out, stream_grad = call(
             final_kernel,
             [sds((rows, width), BF)] * 2,
@@ -385,7 +415,7 @@
             [pltpu.VMEM((rows, width), F32)],
             flops=10**9,
             moved=4 * 10**6,
-        )(mine, theirs, merge_high, merge_low, stream, gain, upstream)
+        )(first, theirs, merge_high, merge_low, stream, gain, upstream)
     return (layer_out, stream_grad)
 
 

time: 110 us -> 113 us (1.027)
  Pallas kernels: 17.3 us -> 20.3 us
  starting transfers between devices: 32.2 us -> 35.2 us
  waiting for transfers between devices: 15.3 us -> 13.7 us
  blocking collectives: 40.5 us -> 39.2 us
    pallas_call x8 -> x13, Pallas kernels: 9.97 us -> 13.5 us  [the longest x6 12.4 us: expert(): call(functools.partial(kernel, len(xs), len(parts)), slope + parts, [VMEM...]
    ppermute x12, starting transfers between devices: 10.7 us -> 12.5 us  [ring(): return lax.ppermute(x, ('y', 'core'), pairs)]
    ppermute x12, waiting for transfers between devices: 12 us -> 10.6 us  [ring(): return lax.ppermute(x, ('y', 'core'), pairs)]
    ppermute x13 -> x15, starting transfers between devices: 21.4 us -> 22.7 us  [swap_core(): return lax.ppermute(x, 'core', [(0, 1), (1, 0)])]
    all_to_all x2, blocking collectives: 40.5 us -> 39.2 us  [exchange(): lax.all_to_all(x.reshape(experts, PACK, WIDE), 'xz', split_axis=0, concat...]
    ppermute x13 -> x15, waiting for transfers between devices: 3.26 us -> 3.05 us  [swap_core(): return lax.ppermute(x, 'core', [(0, 1), (1, 0)])]
  transfers between devices with their start and end apart: 25 -> 27, of which waited for: 8 -> 8; matrix products, arithmetic and copies ran while one was open for 0% -> 0% of each run, Pallas kernels for 11% -> 13%
where the time goes in v7:
time: 113 us
  blocking collectives  39.2 us (35%)
  starting transfers between devices  35.2 us (31%)
  Pallas kernels  20.3 us (18%)
  waiting for transfers between devices  13.7 us (12%)
  local copies, waits for them, and re-layouts  3.75 us (3%)
    all_to_all x2, blocking collectives, exchange(): lax.all_to_all(x.reshape(experts, PACK, WIDE), 'xz', split_axis=0, concat...  39.2 us
    ppermute x15, starting transfers between devices, swap_core(): return lax.ppermute(x, 'core', [(0, 1), (1, 0)])  22.7 us
    ppermute x12, starting transfers between devices, ring(): return lax.ppermute(x, ('y', 'core'), pairs)  12.5 us
    pallas_call x6, Pallas kernels, expert(): call(functools.partial(kernel, len(xs), len(parts)), slope + parts, [VMEM...  12.4 us
    ppermute x12, waiting for transfers between devices, ring(): return lax.ppermute(x, ('y', 'core'), pairs)  10.6 us
    unnamed x20, local copies, waits for them, and re-layouts  3.66 us
    ppermute x15, waiting for transfers between devices, swap_core(): return lax.ppermute(x, 'core', [(0, 1), (1, 0)])  3.05 us
  transfers between devices with their start and end apart: 27, of which 8 were waited for; matrix products, arithmetic and copies ran while one was open for 0% of the time, Pallas kernels for 13%

profile of v7, /device:TPU:1, one launch (start us, length us, event | category | flops | bytes accessed | tf_op | source)
XLA Modules:
  0.0 113.2 jit_solution(17419885581228464674)
XLA Ops:
  0.7 1.8 %copy-done = bf16[832,1664]{1,0:T(8,128)(2,1)S(1)} copy-done((bf16[832,1664]{1,0:T(8,128)(2,1)S(1)}, bf16[832,1664]{1,0:T(8,128)(2,1)}, u32[]{:S(2)}) %copy-start) | copy-done | bytes 2768920
  2.5 1.0 copy-done.2
  3.5 1.7 %attend.1 = (f32[128,1664]{1,0:T(8,128)S(1)}, f32[128,1664]{1,0:T(8,128)S(1)}) custom-call(s32[2]{0:T(128)S(1)} %pad_add_fusion.ids, bf16[832,256]{1,0:T(8,128)(2,1)S(1)} %bitcast.15, bf16[832,1664]{1,0:T(8,128)(2,1)S(1)} %copy-done), custom_call_target="tpu_custom_call" | custom-call | flops 708837376 | bytes 5000000 | tf_op jit(solution)/shard_map/attend/pallas_call | solution.py:299
  5.3 3.3 %collective-permute-start = (f32[128,1664]{1,0:T(8,128)S(1)}, f32[128,1664]{1,0:T(8,128)S(1)}, u32[]{:S(2)}, u32[]{:S(2)}) collective-permute-start(f32[128,1664]{1,0:T(8,128)S(1)} %get-tuple-element.29), channel_id=1, source_target_pairs={{0,1},{1,0},{2,3},{3,2},{4,5},{5,4},{6,7},{7,6},{8,9},{9,8},{10,11... | collective-permute-start | bytes 2555912 | tf_op jit(solution)/shard_map/attend/ppermute | solution.py:282
  9.5 1.7 %routing.1 = (bf16[256,512]{1,0:T(8,128)(2,1)S(1)}, bf16[256,512]{1,0:T(8,128)(2,1)S(1)}, bf16[512,512]{1,0:T(8,128)(2,1)S(1)}, bf16[512,512]{1,0:T(8,128)(2,1)S(1)}) custom-call(s32[2]{0:T(128)S(1)} %pad_add_fusion.ids, s32[32,512]{1,0:T(8,128)S(1)} %copy-done.6, s32[32,1]{1,0:T(8,128)S(1)} %copy.12.count, f32[32,512]{1,0:T(8,128)S(1)} %copy-done.7), custom_call_target="tpu_custom_call" | custom-call | flops 1000000000 | bytes 2000000 | tf_op jit(solution)/shard_map/routing/pallas_call | solution.py:308
  11.2 1.0 norm.1
  12.3 1.8 %collective-permute-done.1 = bf16[256,896]{1,0:T(8,128)(2,1)S(1)} collective-permute-done((bf16[256,896]{1,0:T(8,128)(2,1)S(1)}, bf16[256,896]{1,0:T(8,128)(2,1)S(1)}, u32[]{:S(2)}, u32[]{:S(2)}) %collective-permute-start.1) | collective-permute-done | bytes 458784 | tf_op jit(solution)/shard_map/dispatch/ppermute | solution.py:282
  14.2 22.2 %all_to_all.10 = bf16[32,8,896]{2,1,0:T(8,128)(2,1)S(1)} all-to-all(bf16[32,8,896]{2,1,0:T(8,128)(2,1)S(1)} %add_bitcast_fusion), channel_id=1, replica_groups=mesh['xz'=32,'y'=4,'core'=2] {'xz'}, dimensions={0} | all-to-all | bytes 917504 | tf_op jit(solution)/shard_map/dispatch/all_to_all | solution.py:293
  36.7 2.8 %collective-permute-start.2 = (bf16[64,1664]{1,0:T(8,128)(2,1)S(1)}, bf16[64,1664]{1,0:T(8,128)(2,1)S(1)}, u32[]{:S(2)}, u32[]{:S(2)}) collective-permute-start(bf16[64,1664]{1,0:T(8,128)(2,1)S(1)} %get-tuple-element.34.refs_0_), channel_id=1, source_target_pairs={{0,2},{1,7},{2,4},{3,1},{4,6},{5,3},{6,0},{7,5},{8,10},{9,15},{10,... | collective-permute-start | bytes 638984 | tf_op jit(solution)/shard_map/gather_normed/ppermute | solution.py:290
  39.5 3.8 %collective-permute-start.4 = (bf16[64,1664]{1,0:T(8,128)(2,1)S(1)}, bf16[64,1664]{1,0:T(8,128)(2,1)S(1)}, u32[]{:S(2)}, u32[]{:S(2)}) collective-permute-start(bf16[64,1664]{1,0:T(8,128)(2,1)S(1)} %get-tuple-element.34.refs_0_), channel_id=1, source_target_pairs={{0,1},{1,0},{2,3},{3,2},{4,5},{5,4},{6,7},{7,6},{8,9},{9,8},{10,11... | collective-permute-start | bytes 638984 | tf_op jit(solution)/shard_map/gather_normed/ppermute | solution.py:282
  43.3 1.5 %collective-permute-start.13 = (bf16[64,1664]{1,0:T(8,128)(2,1)S(1)}, bf16[64,1664]{1,0:T(8,128)(2,1)S(1)}, u32[]{:S(2)}, u32[]{:S(2)}) collective-permute-start(bf16[64,1664]{1,0:T(8,128)(2,1)S(1)} %get-tuple-element.44.refs_0_), channel_id=1, source_target_pairs={{0,2},{1,7},{2,4},{3,1},{4,6},{5,3},{6,0},{7,5},{8,10},{9,15},{10,... | collective-permute-start | bytes 638984 | tf_op jit(solution)/shard_map/gather_down/ppermute | solution.py:290
  44.8 3.5 %collective-permute-start.5 = (bf16[64,1664]{1,0:T(8,128)(2,1)S(1)}, bf16[64,1664]{1,0:T(8,128)(2,1)S(1)}, u32[]{:S(2)}, u32[]{:S(2)}) collective-permute-start(bf16[64,1664]{1,0:T(8,128)(2,1)S(1)} %collective-permute-done.2.refs_1_), channel_id=1, source_target_pairs={{0,1},{1,0},{2,3},{3,2},{4,5},{5,4},{6,7},{7,6},{8,9},{9,8},{10,11... | collective-permute-start | bytes 638984 | tf_op jit(solution)/shard_map/gather_normed/ppermute | solution.py:282
  48.8 2.5 %collective-permute-start.6 = (bf16[64,1664]{1,0:T(8,128)(2,1)S(1)}, bf16[64,1664]{1,0:T(8,128)(2,1)S(1)}, u32[]{:S(2)}, u32[]{:S(2)}) collective-permute-start(bf16[64,1664]{1,0:T(8,128)(2,1)S(1)} %collective-permute-done.3.refs_2_), channel_id=1, source_target_pairs={{0,1},{1,0},{2,3},{3,2},{4,5},{5,4},{6,7},{7,6},{8,9},{9,8},{10,11... | collective-permute-start | bytes 638984 | tf_op jit(solution)/shard_map/gather_normed/ppermute | solution.py:282
  51.4 2.0 %forward.5 = (f32[192,1024]{1,0:T(8,128)S(1)}, f32[192,1664]{1,0:T(8,128)S(1)}) custom-call(bf16[64,1664]{1,0:T(8,128)(2,1)S(1)} %get-tuple-element.34.refs_0_, bf16[64,1664]{1,0:T(8,128)(2,1)S(1)} %collective-permute-done.2.refs_1_, bf16[64,1664]{1,0:T(8,128)(2,1)S(1)} %collective-permute-done.3.refs_2_, bf16[1664,1024]{1,0:T(8,128)(2,1)S(1)} %bitcast.16, ...), custom_call_target="tpu_custom_call" | custom-call | flops 5234491392 | bytes 10000000 | tf_op jit(solution)/shard_map/forward/pallas_call | solution.py:358
  54.2 1.5 %collective-permute-start.20 = (bf16[64,1664]{1,0:T(8,128)(2,1)S(1)}, bf16[64,1664]{1,0:T(8,128)(2,1)S(1)}, u32[]{:S(2)}, u32[]{:S(2)}) collective-permute-start(bf16[64,1664]{1,0:T(8,128)(2,1)S(1)} %collective-permute-done.13.refs_1_), channel_id=1, source_target_pairs={{0,2},{1,7},{2,4},{3,1},{4,6},{5,3},{6,0},{7,5},{8,10},{9,15},{10,... | collective-permute-start | bytes 638984 | tf_op jit(solution)/shard_map/gather_down/ppermute | solution.py:290
  56.2 2.0 %forward.6 = (f32[192,1024]{1,0:T(8,128)S(1)}, bf16[192,1664]{1,0:T(8,128)(2,1)S(1)}) custom-call(bf16[64,1664]{1,0:T(8,128)(2,1)S(1)} %collective-permute-done.4.refs_0_, bf16[64,1664]{1,0:T(8,128)(2,1)S(1)} %collective-permute-done.5.refs_1_, bf16[64,1664]{1,0:T(8,128)(2,1)S(1)} %collective-permute-done.6.refs_2_, bf16[1664,1024]{1,0:T(8,128)(2,1)S(1)} %bitcast.17, ...), custom_call_target="tpu_custom_call" | custom-call | flops 5234491392 | bytes 10000000 | tf_op jit(solution)/shard_map/forward/pallas_call | solution.py:358
  59.2 2.2 %collective-permute-start.7 = (bf16[192,1664]{1,0:T(8,128)(2,1)S(1)}, bf16[192,1664]{1,0:T(8,128)(2,1)S(1)}, u32[]{:S(2)}, u32[]{:S(2)}) collective-permute-start(bf16[192,1664]{1,0:T(8,128)(2,1)S(1)} %get-tuple-element.37), channel_id=1, source_target_pairs={{0,1},{1,0},{2,3},{3,2},{4,5},{5,4},{6,7},{7,6},{8,9},{9,8},{10,11... | collective-permute-start | bytes 1916936 | tf_op jit(solution)/shard_map/forward/ppermute | solution.py:282
  61.4 1.5 %forward.8 = (f32[128,1024]{1,0:T(8,128)S(1)}, f32[64,1664]{1,0:T(8,128)S(1)}, bf16[64,1664]{1,0:T(8,128)(2,1)S(1)}) custom-call(bf16[64,1664]{1,0:T(8,128)(2,1)S(1)} %collective-permute-done.8.refs_0_, bf16[64,1664]{1,0:T(8,128)(2,1)S(1)} %collective-permute-done.9.refs_1_, bf16[1664,1024]{1,0:T(8,128)(2,1)S(1)} %bitcast.18, ...), custom_call_target="tpu_custom_call" | custom-call | flops 3489660928 | bytes 10000000 | tf_op jit(solution)/shard_map/forward/pallas_call | solution.py:358
  63.7 2.2 %backward.8 = (f32[64,1664]{1,0:T(8,128)S(1)}, bf16[64,1664]{1,0:T(8,128)(2,1)S(1)}) custom-call(bf16[64,1664]{1,0:T(8,128)(2,1)S(1)} %collective-permute-done.20.refs_0_, bf16[64,1664]{1,0:T(8,128)(2,1)S(1)} %collective-permute-done.21.refs_1_, bf16[1664,1024]{1,0:T(8,128)(2,1)S(1)} %bitcast.19, bf16[1024,1664]{1,0:T(8,128)(2,1)S(1)} %bitcast.25, ...), custom_call_target="tpu_custom_call" | custom-call | flops 3489660928 | bytes 10000000 | tf_op jit(solution)/shard_map/backward/pallas_call | solution.py:358
  66.2 2.3 %backward.6 = bf16[192,1664]{1,0:T(8,128)(2,1)S(1)} custom-call(bf16[64,1664]{1,0:T(8,128)(2,1)S(1)} %collective-permute-done.15.refs_0_, bf16[64,1664]{1,0:T(8,128)(2,1)S(1)} %collective-permute-done.16.refs_1_, bf16[64,1664]{1,0:T(8,128)(2,1)S(1)} %collective-permute-done.17.refs_2_, bf16[1664,1024]{1,0:T(8,128)(2,1)S(1)} %bitcast.20, ...), custom_call_target="tpu_custom_call" | custom-call | flops 5234491392 | bytes 10000000 | tf_op jit(solution)/shard_map/backward/pallas_call | solution.py:358
  69.3 1.0 collective-permute-start.23
  70.4 2.0 %collective-permute-start.12 = (bf16[64,1664]{1,0:T(8,128)(2,1)S(1)}, bf16[64,1664]{1,0:T(8,128)(2,1)S(1)}, u32[]{:S(2)}, u32[]{:S(2)}) collective-permute-start(bf16[64,1664]{1,0:T(8,128)(2,1)S(1)} %get-tuple-element.43), channel_id=1, source_target_pairs={{0,2},{1,7},{2,4},{3,1},{4,6},{5,3},{6,0},{7,5},{8,10},{9,15},{10,... | collective-permute-start | bytes 638984 | tf_op jit(solution)/shard_map/reduce/ppermute | solution.py:290
  72.5 2.3 %backward.5.keep = f32[192,1664]{1,0:T(8,128)S(1)} custom-call(bf16[64,1664]{1,0:T(8,128)(2,1)S(1)} %get-tuple-element.44.refs_0_, bf16[64,1664]{1,0:T(8,128)(2,1)S(1)} %collective-permute-done.13.refs_1_, bf16[64,1664]{1,0:T(8,128)(2,1)S(1)} %collective-permute-done.14.refs_2_, bf16[1664,1024]{1,0:T(8,128)(2,1)S(1)} %bitcast.21, ...), custom_call_target="tpu_custom_call" | custom-call | flops 5234491392 | bytes 10000000 | tf_op jit(solution)/shard_map/backward/pallas_call | solution.py:358
  74.9 1.4 %collective-permute-start.24 = (bf16[64,1664]{1,0:T(8,128)(2,1)S(1)}, bf16[64,1664]{1,0:T(8,128)(2,1)S(1)}, u32[]{:S(2)}, u32[]{:S(2)}) collective-permute-start(bf16[64,1664]{1,0:T(8,128)(2,1)S(1)} %get-tuple-element.46.rest_1_), channel_id=1, source_target_pairs={{0,2},{1,7},{2,4},{3,1},{4,6},{5,3},{6,0},{7,5},{8,10},{9,15},{10,... | collective-permute-start | bytes 638984 | tf_op jit(solution)/shard_map/reduce/ppermute | solution.py:290
  76.3 1.4 %collective-permute-done.12.rest_0_.two_r = bf16[64,1664]{1,0:T(8,128)(2,1)S(1)} collective-permute-done((bf16[64,1664]{1,0:T(8,128)(2,1)S(1)}, bf16[64,1664]{1,0:T(8,128)(2,1)S(1)}, u32[]{:S(2)}, u32[]{:S(2)}) %collective-permute-start.12) | collective-permute-done | bytes 213024 | tf_op jit(solution)/shard_map/reduce/ppermute | solution.py:290
  77.8 1.4 %collective-permute-start.19 = (bf16[64,1664]{1,0:T(8,128)(2,1)S(1)}, bf16[64,1664]{1,0:T(8,128)(2,1)S(1)}, u32[]{:S(2)}, u32[]{:S(2)}) collective-permute-start(bf16[64,1664]{1,0:T(8,128)(2,1)S(1)} %reduce.2), channel_id=1, source_target_pairs={{0,6},{1,3},{2,0},{3,5},{4,2},{5,7},{6,4},{7,1},{8,14},{9,11},{10,... | collective-permute-start | bytes 638984 | tf_op jit(solution)/shard_map/reduce/ppermute | solution.py:290
  79.2 2.3 %collective-permute-done.24.rest_0_.two_b = bf16[64,1664]{1,0:T(8,128)(2,1)S(1)} collective-permute-done((bf16[64,1664]{1,0:T(8,128)(2,1)S(1)}, bf16[64,1664]{1,0:T(8,128)(2,1)S(1)}, u32[]{:S(2)}, u32[]{:S(2)}) %collective-permute-start.24) | collective-permute-done | bytes 213024 | tf_op jit(solution)/shard_map/reduce/ppermute | solution.py:290
  81.7 2.7 %collective-permute-done.19.one_r = bf16[64,1664]{1,0:T(8,128)(2,1)S(1)} collective-permute-done((bf16[64,1664]{1,0:T(8,128)(2,1)S(1)}, bf16[64,1664]{1,0:T(8,128)(2,1)S(1)}, u32[]{:S(2)}, u32[]{:S(2)}) %collective-permute-start.19) | collective-permute-done | bytes 213024 | tf_op jit(solution)/shard_map/reduce/ppermute | solution.py:290
  84.4 3.2 %collective-permute-done.25.one_b = bf16[64,1664]{1,0:T(8,128)(2,1)S(1)} collective-permute-done((bf16[64,1664]{1,0:T(8,128)(2,1)S(1)}, bf16[64,1664]{1,0:T(8,128)(2,1)S(1)}, u32[]{:S(2)}, u32[]{:S(2)}) %collective-permute-start.25) | collective-permute-done | bytes 213024 | tf_op jit(solution)/shard_map/reduce/ppermute | solution.py:290
  87.9 17.1 %all_to_all.11 = bf16[32,8,896]{2,1,0:T(8,128)(2,1)S(1)} all-to-all(bf16[32,8,896]{2,1,0:T(8,128)(2,1)S(1)} %bitcast.11), channel_id=1, replica_groups=mesh['xz'=32,'y'=4,'core'=2] {'xz'}, dimensions={0} | all-to-all | bytes 917504 | tf_op jit(solution)/shard_map/collect/all_to_all | solution.py:293
  105.0 4.9 %collective-permute-start.26 = (bf16[256,896]{1,0:T(8,128)(2,1)S(1)}, bf16[256,896]{1,0:T(8,128)(2,1)S(1)}, u32[]{:S(2)}, u32[]{:S(2)}) collective-permute-start(bf16[256,896]{1,0:T(8,128)(2,1)S(1)} %bitcast.13), channel_id=1, source_target_pairs={{0,1},{1,0},{2,3},{3,2},{4,5},{5,4},{6,7},{7,6},{8,9},{9,8},{10,11... | collective-permute-start | bytes 1376264 | tf_op jit(solution)/shard_map/collect/ppermute | solution.py:282
  111.4 1.8 %final.3 = (bf16[128,1664]{1,0:T(8,128)(2,1)}, bf16[128,1664]{1,0:T(8,128)(2,1)}) custom-call(f32[512,896]{1,0:T(8,128)S(1)} %final.2.first, bf16[256,896]{1,0:T(8,128)(2,1)S(1)} %collective-permute-done.26.theirs, bf16[512,512]{1,0:T(8,128)(2,1)S(1)} %get-tuple-element.51.merge_high, bf16[512,512]{1,0:T(8,128)(2,1)S(1)} %get-tuple-element.52.merge_low, ...), custom_call_target="tpu_custom_call" | custom-call | flops 1000000000 | bytes 4000000 | tf_op jit(solution)/shard_map/final/pallas_call | solution.py:411
  (67 shorter events, 8.3 us)
Async XLA Ops:
  0.6 7.9 %copy-start.8 = (f32[1664]{0:T(1024)S(1)}, f32[1664]{0:T(1024)}, u32[]{:S(2)}) copy-start(f32[1664]{0:T(1024)} %param.13) | copy-start | bytes 19972
  0.6 8.0 %copy-start.9 = (s32[32]{0:T(128)S(1)}, s32[32]{0:T(128)}, u32[]{:S(2)}) copy-start(s32[32]{0:T(128)} %param.17) | copy-start | bytes 388
  3.5 7.7 %copy-start.5 = (bf16[128,1664]{1,0:T(8,128)(2,1)S(1)}, bf16[128,1664]{1,0:T(8,128)(2,1)}, u32[]{:S(2)}) copy-start(bf16[128,1664]{1,0:T(8,128)(2,1)} %residual.1) | copy-start | bytes 1277956
  5.3 6.0 %collective-permute-start = (f32[128,1664]{1,0:T(8,128)S(1)}, f32[128,1664]{1,0:T(8,128)S(1)}, u32[]{:S(2)}, u32[]{:S(2)}) collective-permute-start(f32[128,1664]{1,0:T(8,128)S(1)} %get-tuple-element.29), channel_id=1, source_target_pairs={{0,1},{1,0},{2,3},{3,2},{4,5},{5,4},{6,7},{7,6},{8,9},{9,8},{10,11... | collective-permute-start | bytes 2555912 | tf_op jit(solution)/shard_map/attend/ppermute | solution.py:282
  9.5 41.8 %copy-start.4 = (bf16[1,1024,1664]{2,1,0:T(8,128)(2,1)S(1)}, bf16[1,1024,1664]{2,1,0:T(8,128)(2,1)}, u32[]{:S(2)}) copy-start(bf16[1,1024,1664]{2,1,0:T(8,128)(2,1)} %param.15) | copy-start | bytes 10223620
  11.2 40.1 %copy-start.3 = (bf16[1,1664,1024]{2,1,0:T(8,128)(2,1)S(1)}, bf16[1,1664,1024]{2,1,0:T(8,128)(2,1)}, u32[]{:S(2)}) copy-start(bf16[1,1664,1024]{2,1,0:T(8,128)(2,1)} %param.14) | copy-start | bytes 10223620
  12.2 1.9 %collective-permute-start.1 = (bf16[256,896]{1,0:T(8,128)(2,1)S(1)}, bf16[256,896]{1,0:T(8,128)(2,1)S(1)}, u32[]{:S(2)}, u32[]{:S(2)}) collective-permute-start(bf16[256,896]{1,0:T(8,128)(2,1)S(1)} %get-tuple-element.33), channel_id=1, source_target_pairs={{0,1},{1,0},{2,3},{3,2},{4,5},{5,4},{6,7},{7,6},{8,9},{9,8},{10,11... | collective-permute-start | bytes 1376264 | tf_op jit(solution)/shard_map/dispatch/ppermute | solution.py:282
  36.7 8.2 %collective-permute-start.2 = (bf16[64,1664]{1,0:T(8,128)(2,1)S(1)}, bf16[64,1664]{1,0:T(8,128)(2,1)S(1)}, u32[]{:S(2)}, u32[]{:S(2)}) collective-permute-start(bf16[64,1664]{1,0:T(8,128)(2,1)S(1)} %get-tuple-element.34.refs_0_), channel_id=1, source_target_pairs={{0,2},{1,7},{2,4},{3,1},{4,6},{5,3},{6,0},{7,5},{8,10},{9,15},{10,... | collective-permute-start | bytes 638984 | tf_op jit(solution)/shard_map/gather_normed/ppermute | solution.py:290
  39.5 8.9 %collective-permute-start.3 = (bf16[64,1664]{1,0:T(8,128)(2,1)S(1)}, bf16[64,1664]{1,0:T(8,128)(2,1)S(1)}, u32[]{:S(2)}, u32[]{:S(2)}) collective-permute-start(bf16[64,1664]{1,0:T(8,128)(2,1)S(1)} %get-tuple-element.34.refs_0_), channel_id=1, source_target_pairs={{0,6},{1,3},{2,0},{3,5},{4,2},{5,7},{6,4},{7,1},{8,14},{9,11},{10,... | collective-permute-start | bytes 638984 | tf_op jit(solution)/shard_map/gather_normed/ppermute | solution.py:290
  39.5 9.4 %collective-permute-start.4 = (bf16[64,1664]{1,0:T(8,128)(2,1)S(1)}, bf16[64,1664]{1,0:T(8,128)(2,1)S(1)}, u32[]{:S(2)}, u32[]{:S(2)}) collective-permute-start(bf16[64,1664]{1,0:T(8,128)(2,1)S(1)} %get-tuple-element.34.refs_0_), channel_id=1, source_target_pairs={{0,1},{1,0},{2,3},{3,2},{4,5},{5,4},{6,7},{7,6},{8,9},{9,8},{10,11... | collective-permute-start | bytes 638984 | tf_op jit(solution)/shard_map/gather_normed/ppermute | solution.py:282
  43.3 10.1 %collective-permute-start.13 = (bf16[64,1664]{1,0:T(8,128)(2,1)S(1)}, bf16[64,1664]{1,0:T(8,128)(2,1)S(1)}, u32[]{:S(2)}, u32[]{:S(2)}) collective-permute-start(bf16[64,1664]{1,0:T(8,128)(2,1)S(1)} %get-tuple-element.44.refs_0_), channel_id=1, source_target_pairs={{0,2},{1,7},{2,4},{3,1},{4,6},{5,3},{6,0},{7,5},{8,10},{9,15},{10,... | collective-permute-start | bytes 638984 | tf_op jit(solution)/shard_map/gather_down/ppermute | solution.py:290
  44.8 8.8 %collective-permute-start.14 = (bf16[64,1664]{1,0:T(8,128)(2,1)S(1)}, bf16[64,1664]{1,0:T(8,128)(2,1)S(1)}, u32[]{:S(2)}, u32[]{:S(2)}) collective-permute-start(bf16[64,1664]{1,0:T(8,128)(2,1)S(1)} %get-tuple-element.44.refs_0_), channel_id=1, source_target_pairs={{0,6},{1,3},{2,0},{3,5},{4,2},{5,7},{6,4},{7,1},{8,14},{9,11},{10,... | collective-permute-start | bytes 638984 | tf_op jit(solution)/shard_map/gather_down/ppermute | solution.py:290
  44.8 9.3 %collective-permute-start.5 = (bf16[64,1664]{1,0:T(8,128)(2,1)S(1)}, bf16[64,1664]{1,0:T(8,128)(2,1)S(1)}, u32[]{:S(2)}, u32[]{:S(2)}) collective-permute-start(bf16[64,1664]{1,0:T(8,128)(2,1)S(1)} %collective-permute-done.2.refs_1_), channel_id=1, source_target_pairs={{0,1},{1,0},{2,3},{3,2},{4,5},{5,4},{6,7},{7,6},{8,9},{9,8},{10,11... | collective-permute-start | bytes 638984 | tf_op jit(solution)/shard_map/gather_normed/ppermute | solution.py:282
  48.4 7.6 %collective-permute-start.8 = (bf16[64,1664]{1,0:T(8,128)(2,1)S(1)}, bf16[64,1664]{1,0:T(8,128)(2,1)S(1)}, u32[]{:S(2)}, u32[]{:S(2)}) collective-permute-start(bf16[64,1664]{1,0:T(8,128)(2,1)S(1)} %collective-permute-done.2.refs_1_), channel_id=1, source_target_pairs={{0,2},{1,7},{2,4},{3,1},{4,6},{5,3},{6,0},{7,5},{8,10},{9,15},{10,... | collective-permute-start | bytes 638984 | tf_op jit(solution)/shard_map/gather_normed/ppermute | solution.py:290
  48.8 6.8 %collective-permute-start.6 = (bf16[64,1664]{1,0:T(8,128)(2,1)S(1)}, bf16[64,1664]{1,0:T(8,128)(2,1)S(1)}, u32[]{:S(2)}, u32[]{:S(2)}) collective-permute-start(bf16[64,1664]{1,0:T(8,128)(2,1)S(1)} %collective-permute-done.3.refs_2_), channel_id=1, source_target_pairs={{0,1},{1,0},{2,3},{3,2},{4,5},{5,4},{6,7},{7,6},{8,9},{9,8},{10,11... | collective-permute-start | bytes 638984 | tf_op jit(solution)/shard_map/gather_normed/ppermute | solution.py:282
  53.4 12.5 %collective-permute-start.15 = (bf16[64,1664]{1,0:T(8,128)(2,1)S(1)}, bf16[64,1664]{1,0:T(8,128)(2,1)S(1)}, u32[]{:S(2)}, u32[]{:S(2)}) collective-permute-start(bf16[64,1664]{1,0:T(8,128)(2,1)S(1)} %get-tuple-element.44.refs_0_), channel_id=1, source_target_pairs={{0,1},{1,0},{2,3},{3,2},{4,5},{5,4},{6,7},{7,6},{8,9},{9,8},{10,11... | collective-permute-start | bytes 638984 | tf_op jit(solution)/shard_map/gather_down/ppermute | solution.py:282
  53.7 12.5 %collective-permute-start.16 = (bf16[64,1664]{1,0:T(8,128)(2,1)S(1)}, bf16[64,1664]{1,0:T(8,128)(2,1)S(1)}, u32[]{:S(2)}, u32[]{:S(2)}) collective-permute-start(bf16[64,1664]{1,0:T(8,128)(2,1)S(1)} %collective-permute-done.13.refs_1_), channel_id=1, source_target_pairs={{0,1},{1,0},{2,3},{3,2},{4,5},{5,4},{6,7},{7,6},{8,9},{9,8},{10,11... | collective-permute-start | bytes 638984 | tf_op jit(solution)/shard_map/gather_down/ppermute | solution.py:282
  54.2 5.0 %collective-permute-start.20 = (bf16[64,1664]{1,0:T(8,128)(2,1)S(1)}, bf16[64,1664]{1,0:T(8,128)(2,1)S(1)}, u32[]{:S(2)}, u32[]{:S(2)}) collective-permute-start(bf16[64,1664]{1,0:T(8,128)(2,1)S(1)} %collective-permute-done.13.refs_1_), channel_id=1, source_target_pairs={{0,2},{1,7},{2,4},{3,1},{4,6},{5,3},{6,0},{7,5},{8,10},{9,15},{10,... | collective-permute-start | bytes 638984 | tf_op jit(solution)/shard_map/gather_down/ppermute | solution.py:290
  55.7 10.5 %collective-permute-start.17 = (bf16[64,1664]{1,0:T(8,128)(2,1)S(1)}, bf16[64,1664]{1,0:T(8,128)(2,1)S(1)}, u32[]{:S(2)}, u32[]{:S(2)}) collective-permute-start(bf16[64,1664]{1,0:T(8,128)(2,1)S(1)} %collective-permute-done.14.refs_2_), channel_id=1, source_target_pairs={{0,1},{1,0},{2,3},{3,2},{4,5},{5,4},{6,7},{7,6},{8,9},{9,8},{10,11... | collective-permute-start | bytes 638984 | tf_op jit(solution)/shard_map/gather_down/ppermute | solution.py:282
  55.9 5.4 %collective-permute-start.9 = (bf16[64,1664]{1,0:T(8,128)(2,1)S(1)}, bf16[64,1664]{1,0:T(8,128)(2,1)S(1)}, u32[]{:S(2)}, u32[]{:S(2)}) collective-permute-start(bf16[64,1664]{1,0:T(8,128)(2,1)S(1)} %collective-permute-done.8.refs_0_), channel_id=1, source_target_pairs={{0,1},{1,0},{2,3},{3,2},{4,5},{5,4},{6,7},{7,6},{8,9},{9,8},{10,11... | collective-permute-start | bytes 638984 | tf_op jit(solution)/shard_map/gather_normed/ppermute | solution.py:282
  59.2 11.2 %collective-permute-start.7 = (bf16[192,1664]{1,0:T(8,128)(2,1)S(1)}, bf16[192,1664]{1,0:T(8,128)(2,1)S(1)}, u32[]{:S(2)}, u32[]{:S(2)}) collective-permute-start(bf16[192,1664]{1,0:T(8,128)(2,1)S(1)} %get-tuple-element.37), channel_id=1, source_target_pairs={{0,1},{1,0},{2,3},{3,2},{4,5},{5,4},{6,7},{7,6},{8,9},{9,8},{10,11... | collective-permute-start | bytes 1916936 | tf_op jit(solution)/shard_map/forward/ppermute | solution.py:282
  61.4 2.0 %collective-permute-start.21 = (bf16[64,1664]{1,0:T(8,128)(2,1)S(1)}, bf16[64,1664]{1,0:T(8,128)(2,1)S(1)}, u32[]{:S(2)}, u32[]{:S(2)}) collective-permute-start(bf16[64,1664]{1,0:T(8,128)(2,1)S(1)} %collective-permute-done.20.refs_0_), channel_id=1, source_target_pairs={{0,1},{1,0},{2,3},{3,2},{4,5},{5,4},{6,7},{7,6},{8,9},{9,8},{10,11... | collective-permute-start | bytes 638984 | tf_op jit(solution)/shard_map/gather_down/ppermute | solution.py:282
  63.4 5.6 %collective-permute-start.10 = (bf16[64,1664]{1,0:T(8,128)(2,1)S(1)}, bf16[64,1664]{1,0:T(8,128)(2,1)S(1)}, u32[]{:S(2)}, u32[]{:S(2)}) collective-permute-start(bf16[64,1664]{1,0:T(8,128)(2,1)S(1)} %get-tuple-element.42), channel_id=1, source_target_pairs={{0,1},{1,0},{2,3},{3,2},{4,5},{5,4},{6,7},{7,6},{8,9},{9,8},{10,11... | collective-permute-start | bytes 638984 | tf_op jit(solution)/shard_map/forward/ppermute | solution.py:282
  66.0 3.3 %collective-permute-start.22 = (bf16[64,1664]{1,0:T(8,128)(2,1)S(1)}, bf16[64,1664]{1,0:T(8,128)(2,1)S(1)}, u32[]{:S(2)}, u32[]{:S(2)}) collective-permute-start(bf16[64,1664]{1,0:T(8,128)(2,1)S(1)} %get-tuple-element.50), channel_id=1, source_target_pairs={{0,1},{1,0},{2,3},{3,2},{4,5},{5,4},{6,7},{7,6},{8,9},{9,8},{10,11... | collective-permute-start | bytes 638984 | tf_op jit(solution)/shard_map/backward/ppermute | solution.py:282
  68.5 6.3 %collective-permute-start.18 = (bf16[192,1664]{1,0:T(8,128)(2,1)S(1)}, bf16[192,1664]{1,0:T(8,128)(2,1)S(1)}, u32[]{:S(2)}, u32[]{:S(2)}) collective-permute-start(bf16[192,1664]{1,0:T(8,128)(2,1)S(1)} %backward.6), channel_id=1, source_target_pairs={{0,1},{1,0},{2,3},{3,2},{4,5},{5,4},{6,7},{7,6},{8,9},{9,8},{10,11... | collective-permute-start | bytes 1916936 | tf_op jit(solution)/shard_map/backward/ppermute | solution.py:282
  69.0 7.3 %collective-permute-start.11 = (bf16[64,1664]{1,0:T(8,128)(2,1)S(1)}, bf16[64,1664]{1,0:T(8,128)(2,1)S(1)}, u32[]{:S(2)}, u32[]{:S(2)}) collective-permute-start(bf16[64,1664]{1,0:T(8,128)(2,1)S(1)} %forward.9.refs_6_), channel_id=1, source_target_pairs={{0,6},{1,3},{2,0},{3,5},{4,2},{5,7},{6,4},{7,1},{8,14},{9,11},{10,... | collective-permute-start | bytes 638984 | tf_op jit(solution)/shard_map/reduce/ppermute | solution.py:290
  69.3 9.9 %collective-permute-start.23 = (bf16[64,1664]{1,0:T(8,128)(2,1)S(1)}, bf16[64,1664]{1,0:T(8,128)(2,1)S(1)}, u32[]{:S(2)}, u32[]{:S(2)}) collective-permute-start(bf16[64,1664]{1,0:T(8,128)(2,1)S(1)} %backward.9), channel_id=1, source_target_pairs={{0,6},{1,3},{2,0},{3,5},{4,2},{5,7},{6,4},{7,1},{8,14},{9,11},{10,... | collective-permute-start | bytes 638984 | tf_op jit(solution)/shard_map/reduce/ppermute | solution.py:290
  70.4 7.3 %collective-permute-start.12 = (bf16[64,1664]{1,0:T(8,128)(2,1)S(1)}, bf16[64,1664]{1,0:T(8,128)(2,1)S(1)}, u32[]{:S(2)}, u32[]{:S(2)}) collective-permute-start(bf16[64,1664]{1,0:T(8,128)(2,1)S(1)} %get-tuple-element.43), channel_id=1, source_target_pairs={{0,2},{1,7},{2,4},{3,1},{4,6},{5,3},{6,0},{7,5},{8,10},{9,15},{10,... | collective-permute-start | bytes 638984 | tf_op jit(solution)/shard_map/reduce/ppermute | solution.py:290
  74.9 6.6 %collective-permute-start.24 = (bf16[64,1664]{1,0:T(8,128)(2,1)S(1)}, bf16[64,1664]{1,0:T(8,128)(2,1)S(1)}, u32[]{:S(2)}, u32[]{:S(2)}) collective-permute-start(bf16[64,1664]{1,0:T(8,128)(2,1)S(1)} %get-tuple-element.46.rest_1_), channel_id=1, source_target_pairs={{0,2},{1,7},{2,4},{3,1},{4,6},{5,3},{6,0},{7,5},{8,10},{9,15},{10,... | collective-permute-start | bytes 638984 | tf_op jit(solution)/shard_map/reduce/ppermute | solution.py:290
  77.8 6.6 %collective-permute-start.19 = (bf16[64,1664]{1,0:T(8,128)(2,1)S(1)}, bf16[64,1664]{1,0:T(8,128)(2,1)S(1)}, u32[]{:S(2)}, u32[]{:S(2)}) collective-permute-start(bf16[64,1664]{1,0:T(8,128)(2,1)S(1)} %reduce.2), channel_id=1, source_target_pairs={{0,6},{1,3},{2,0},{3,5},{4,2},{5,7},{6,4},{7,1},{8,14},{9,11},{10,... | collective-permute-start | bytes 638984 | tf_op jit(solution)/shard_map/reduce/ppermute | solution.py:290
  81.6 6.0 %collective-permute-start.25 = (bf16[64,1664]{1,0:T(8,128)(2,1)S(1)}, bf16[64,1664]{1,0:T(8,128)(2,1)S(1)}, u32[]{:S(2)}, u32[]{:S(2)}) collective-permute-start(bf16[64,1664]{1,0:T(8,128)(2,1)S(1)} %reduce.3), channel_id=1, source_target_pairs={{0,6},{1,3},{2,0},{3,5},{4,2},{5,7},{6,4},{7,1},{8,14},{9,11},{10,... | collective-permute-start | bytes 638984 | tf_op jit(solution)/shard_map/reduce/ppermute | solution.py:290
  105.0 6.4 %collective-permute-start.26 = (bf16[256,896]{1,0:T(8,128)(2,1)S(1)}, bf16[256,896]{1,0:T(8,128)(2,1)S(1)}, u32[]{:S(2)}, u32[]{:S(2)}) collective-permute-start(bf16[256,896]{1,0:T(8,128)(2,1)S(1)} %bitcast.13), channel_id=1, source_target_pairs={{0,1},{1,0},{2,3},{3,2},{4,5},{5,4},{6,7},{7,6},{8,9},{9,8},{10,11... | collective-permute-start | bytes 1376264 | tf_op jit(solution)/shard_map/collect/ppermute | solution.py:282
  (5 other events, 16.5 us)

commit v8 on v6

--- a/solution.py
+++ b/solution.py
@@ -200,21 +200,33 @@
         out[...] = (keep[at, :] + got[at, :].astype(F32)).astype(out.dtype)
 
 
-def add_kernel(a, b, out):
+def add_kernel(a, b, *rest):
+    out = rest[-1]
     out[...] = (a[...].astype(F32) + b[...].astype(F32)).astype(BF)
 
 
-def final_kernel(mine, theirs, merge_high, merge_low, stream, gain, upstream, layer_out, stream_grad, back):
+def merged(rows, merge_high, merge_low, group, size, lo):
+    at = (slice(group * size, (group + 1) * size), slice(lo, lo + rows.shape[0]))
+    return mm(merge_high[at], rows[...]) + mm(merge_low[at], rows[...])
+
+
+def first_kernel(mine, merge_high, merge_low, out):
+    size = out.shape[0] // 4
+    for group in range(4):
+        at = slice(group * size, (group + 1) * size)
+        out[at, :] = merged(mine, merge_high, merge_low, group, size, 0)
+
+
+def final_kernel(first, theirs, merge_high, merge_low, stream, gain, upstream, layer_out, stream_grad, back):
     rows, width = stream.shape
-    n = mine.shape[0]
+    n = theirs.shape[0]
     rest = width - WIDE
     total = stream[...]
     centered, inverse = statistics(total)
     x_hat = centered * inverse
     for group in range(4):
         at = slice(group * rows, (group + 1) * rows)
-        summed = mm(merge_high[at, :n], mine[...]) + mm(merge_high[at, n:], theirs[...])
-        summed += mm(merge_low[at, :n], mine[...]) + mm(merge_low[at, n:], theirs[...])
+        summed = first[at, :] + merged(theirs, merge_high, merge_low, group, rows, n)
         cols = slice(0, WIDE) if group < 2 else slice(WIDE, width)
         summed = summed if group < 2 else summed[:, :rest]
         if group % 2 == 0:
@@ -317,11 +329,14 @@
             moved=4 * 10**6,
         )(keep_part, swap_core(send_part))
 
-    def reduce_y(parts):
+    def reduce_y(parts, early):
         own, one, two, far = parts
+        from_far = ring(far, -1)
         from_two = ring(two, 1)
-        from_far = ring(far, -1)
-        one = call(add_kernel, sds((block, width), BF), [VMEM] * 2, flops=10**5, moved=10**6)(one, from_far)
+        after = [from_two] if early else []
+        one = call(
+            add_kernel, sds((block, width), BF), [VMEM] * 2 + [ANY] * len(after), flops=10**5, moved=10**6
+        )(one, from_far, *after)
         return own, ring(one, -1), from_two
 
     weight_in = expert_in[0]
@@ -360,12 +375,12 @@
         slope_send, part_send = forward(sends, BF, slope_keep)
     with jax.named_scope("return_result"):
         parts = combine(part_keep, part_send)
-        result = reduce_y(parts)
+        result = reduce_y(parts, True)
     with jax.named_scope("backward"):
         back_send = backward(down_sends, slope_send, BF)
         back_keep = backward(down_keeps, slope_keep, F32, parts[3])
     with jax.named_scope("return_back"):
-        back = reduce_y(combine(back_keep, back_send))
+        back = reduce_y(combine(back_keep, back_send), False)
     with jax.named_scope("collect"):
         ready = call(
             pack_kernel,
@@ -378,6 +393,9 @@
         mine = exchange(ready)
         theirs = swap_core(mine)
     with jax.named_scope("final"):
+        first = call(first_kernel, sds((4 * rows, WIDE), F32), [VMEM] * 3, flops=10**9, moved=4 * 10**6)(
+            mine, merge_high, merge_low
+        )
         layer_out, stream_grad = call(
             final_kernel,
             [sds((rows, width), BF)] * 2,
@@ -385,7 +403,7 @@
             [pltpu.VMEM((rows, width), F32)],
             flops=10**9,
             moved=4 * 10**6,
-        )(mine, theirs, merge_high, merge_low, stream, gain, upstream)
+        )(first, theirs, merge_high, merge_low, stream, gain, upstream)
     return (layer_out, stream_grad)
 
 

time: 110 us -> 110 us (level)
  starting transfers between devices: 32.2 us -> 33.9 us
  waiting for transfers between devices: 15.3 us -> 13.9 us
  transfers between devices with their start and end apart: 25 -> 25, of which waited for: 8 -> 7; matrix products, arithmetic and copies ran while one was open for 0% -> 0% of each run, Pallas kernels for 11% -> 11%
where the time goes in v8:
time: 110 us
  blocking collectives  39.9 us (36%)
  starting transfers between devices  33.9 us (31%)
  Pallas kernels  17.5 us (16%)
  waiting for transfers between devices  13.9 us (13%)
  local copies, waits for them, and re-layouts  3.75 us (3%)
    all_to_all x2, blocking collectives, exchange(): lax.all_to_all(x.reshape(experts, PACK, WIDE), 'xz', split_axis=0, concat...  39.9 us
    ppermute x13, starting transfers between devices, swap_core(): return lax.ppermute(x, 'core', [(0, 1), (1, 0)])  22.4 us
    ppermute x12, starting transfers between devices, ring(): return lax.ppermute(x, ('y', 'core'), pairs)  11.5 us
    ppermute x12, waiting for transfers between devices, ring(): return lax.ppermute(x, ('y', 'core'), pairs)  11.4 us
    pallas_call x2, Pallas kernels, forward(): call(forward_kernel, [sds((tall, units), F32), sds((tall, width), kind)],...  5.14 us
    pallas_call x2, Pallas kernels, backward(): call(backward_kernel, sds((tall, width), kind), [VMEM] * 7 + [ANY] * len(...  4.44 us
    unnamed x20, local copies, waits for them, and re-layouts  3.66 us
    ppermute x13, waiting for transfers between devices, swap_core(): return lax.ppermute(x, 'core', [(0, 1), (1, 0)])  2.54 us
  transfers between devices with their start and end apart: 25, of which 7 were waited for; matrix products, arithmetic and copies ran while one was open for 0% of the time, Pallas kernels for 11%

profile of v8, /device:TPU:1, one launch (start us, length us, event | category | flops | bytes accessed | tf_op | source)
XLA Modules:
  0.0 110.0 jit_solution(5975509841633803865)
XLA Ops:
  0.7 1.8 %copy-done = bf16[832,1664]{1,0:T(8,128)(2,1)S(1)} copy-done((bf16[832,1664]{1,0:T(8,128)(2,1)S(1)}, bf16[832,1664]{1,0:T(8,128)(2,1)}, u32[]{:S(2)}) %copy-start) | copy-done | bytes 2768920
  2.5 1.0 copy-done.2
  3.5 1.7 %attend.1 = (f32[128,1664]{1,0:T(8,128)S(1)}, f32[128,1664]{1,0:T(8,128)S(1)}) custom-call(s32[2]{0:T(128)S(1)} %pad_add_fusion.ids, bf16[832,256]{1,0:T(8,128)(2,1)S(1)} %bitcast.15, bf16[832,1664]{1,0:T(8,128)(2,1)S(1)} %copy-done), custom_call_target="tpu_custom_call" | custom-call | flops 708837376 | bytes 5000000 | tf_op jit(solution)/shard_map/attend/pallas_call | solution.py:285
  5.3 3.3 %collective-permute-start = (f32[128,1664]{1,0:T(8,128)S(1)}, f32[128,1664]{1,0:T(8,128)S(1)}, u32[]{:S(2)}, u32[]{:S(2)}) collective-permute-start(f32[128,1664]{1,0:T(8,128)S(1)} %get-tuple-element.26), channel_id=1, source_target_pairs={{0,1},{1,0},{2,3},{3,2},{4,5},{5,4},{6,7},{7,6},{8,9},{9,8},{10,11... | collective-permute-start | bytes 2555912 | tf_op jit(solution)/shard_map/attend/ppermute | solution.py:268
  8.7 0.8 copy-done.7
  9.5 1.7 %routing.1 = (bf16[256,512]{1,0:T(8,128)(2,1)S(1)}, bf16[256,512]{1,0:T(8,128)(2,1)S(1)}, bf16[512,512]{1,0:T(8,128)(2,1)S(1)}, bf16[512,512]{1,0:T(8,128)(2,1)S(1)}) custom-call(s32[2]{0:T(128)S(1)} %pad_add_fusion.ids, s32[32,512]{1,0:T(8,128)S(1)} %copy-done.6, s32[32,1]{1,0:T(8,128)S(1)} %copy.12.count, f32[32,512]{1,0:T(8,128)S(1)} %copy-done.7), custom_call_target="tpu_custom_call" | custom-call | flops 1000000000 | bytes 2000000 | tf_op jit(solution)/shard_map/routing/pallas_call | solution.py:294
  11.2 1.0 norm.1
  12.3 1.8 %collective-permute-done.1 = bf16[256,896]{1,0:T(8,128)(2,1)S(1)} collective-permute-done((bf16[256,896]{1,0:T(8,128)(2,1)S(1)}, bf16[256,896]{1,0:T(8,128)(2,1)S(1)}, u32[]{:S(2)}, u32[]{:S(2)}) %collective-permute-start.1) | collective-permute-done | bytes 458784 | tf_op jit(solution)/shard_map/dispatch/ppermute | solution.py:268
  14.2 22.2 %all_to_all.10 = bf16[32,8,896]{2,1,0:T(8,128)(2,1)S(1)} all-to-all(bf16[32,8,896]{2,1,0:T(8,128)(2,1)S(1)} %add_bitcast_fusion), channel_id=1, replica_groups=mesh['xz'=32,'y'=4,'core'=2] {'xz'}, dimensions={0} | all-to-all | bytes 917504 | tf_op jit(solution)/shard_map/dispatch/all_to_all | solution.py:279
  36.7 2.8 %collective-permute-start.2 = (bf16[64,1664]{1,0:T(8,128)(2,1)S(1)}, bf16[64,1664]{1,0:T(8,128)(2,1)S(1)}, u32[]{:S(2)}, u32[]{:S(2)}) collective-permute-start(bf16[64,1664]{1,0:T(8,128)(2,1)S(1)} %get-tuple-element.31.x0), channel_id=1, source_target_pairs={{0,2},{1,7},{2,4},{3,1},{4,6},{5,3},{6,0},{7,5},{8,10},{9,15},{10,... | collective-permute-start | bytes 638984 | tf_op jit(solution)/shard_map/gather_normed/ppermute | solution.py:276
  39.5 3.8 %collective-permute-start.5 = (bf16[64,1664]{1,0:T(8,128)(2,1)S(1)}, bf16[64,1664]{1,0:T(8,128)(2,1)S(1)}, u32[]{:S(2)}, u32[]{:S(2)}) collective-permute-start(bf16[64,1664]{1,0:T(8,128)(2,1)S(1)} %get-tuple-element.31.x0), channel_id=1, source_target_pairs={{0,1},{1,0},{2,3},{3,2},{4,5},{5,4},{6,7},{7,6},{8,9},{9,8},{10,11... | collective-permute-start | bytes 638984 | tf_op jit(solution)/shard_map/gather_normed/ppermute | solution.py:268
  43.3 1.5 %collective-permute-start.13 = (bf16[64,1664]{1,0:T(8,128)(2,1)S(1)}, bf16[64,1664]{1,0:T(8,128)(2,1)S(1)}, u32[]{:S(2)}, u32[]{:S(2)}) collective-permute-start(bf16[64,1664]{1,0:T(8,128)(2,1)S(1)} %get-tuple-element.39.x0), channel_id=1, source_target_pairs={{0,2},{1,7},{2,4},{3,1},{4,6},{5,3},{6,0},{7,5},{8,10},{9,15},{10,... | collective-permute-start | bytes 638984 | tf_op jit(solution)/shard_map/gather_down/ppermute | solution.py:276
  44.8 0.6 collective-permute-start.4
  45.4 0.9 collective-permute-start.14
  46.3 0.6 collective-permute-done.3.x2
  46.9 4.7 %collective-permute-start.6 = (bf16[64,1664]{1,0:T(8,128)(2,1)S(1)}, bf16[64,1664]{1,0:T(8,128)(2,1)S(1)}, u32[]{:S(2)}, u32[]{:S(2)}) collective-permute-start(bf16[64,1664]{1,0:T(8,128)(2,1)S(1)} %collective-permute-done.2.x1), channel_id=1, source_target_pairs={{0,1},{1,0},{2,3},{3,2},{4,5},{5,4},{6,7},{7,6},{8,9},{9,8},{10,11... | collective-permute-start | bytes 638984 | tf_op jit(solution)/shard_map/gather_normed/ppermute | solution.py:268
  51.7 3.7 %collective-permute-start.8 = (bf16[64,1664]{1,0:T(8,128)(2,1)S(1)}, bf16[64,1664]{1,0:T(8,128)(2,1)S(1)}, u32[]{:S(2)}, u32[]{:S(2)}) collective-permute-start(bf16[64,1664]{1,0:T(8,128)(2,1)S(1)} %collective-permute-done.4.x3), channel_id=1, source_target_pairs={{0,1},{1,0},{2,3},{3,2},{4,5},{5,4},{6,7},{7,6},{8,9},{9,8},{10,11... | collective-permute-start | bytes 638984 | tf_op jit(solution)/shard_map/gather_normed/ppermute | solution.py:268
  55.4 2.6 %forward.2 = (f32[256,1024]{1,0:T(8,128)S(1)}, f32[256,1664]{1,0:T(8,128)S(1)}) custom-call(bf16[64,1664]{1,0:T(8,128)(2,1)S(1)} %get-tuple-element.31.x0, bf16[64,1664]{1,0:T(8,128)(2,1)S(1)} %collective-permute-done.2.x1, bf16[64,1664]{1,0:T(8,128)(2,1)S(1)} %collective-permute-done.3.x2, bf16[64,1664]{1,0:T(8,128)(2,1)S(1)} %collective-permute-done.4.x3, ...), custom_call_target="tpu_custom_call" | custom-call | flops 6979321856 | bytes 10000000 | tf_op jit(solution)/shard_map/forward/pallas_call | solution.py:348
  59.2 2.6 %forward.3 = (f32[256,1024]{1,0:T(8,128)S(1)}, bf16[256,1664]{1,0:T(8,128)(2,1)S(1)}) custom-call(bf16[64,1664]{1,0:T(8,128)(2,1)S(1)} %collective-permute-done.5.x0, bf16[64,1664]{1,0:T(8,128)(2,1)S(1)} %collective-permute-done.6.x1, bf16[64,1664]{1,0:T(8,128)(2,1)S(1)} %collective-permute-done.7.x2, bf16[64,1664]{1,0:T(8,128)(2,1)S(1)} %collective-permute-done.8.x3, ...), custom_call_target="tpu_custom_call" | custom-call | flops 6979321856 | bytes 10000000 | tf_op jit(solution)/shard_map/forward/pallas_call | solution.py:348
  61.9 2.2 %backward.3 = bf16[256,1664]{1,0:T(8,128)(2,1)S(1)} custom-call(bf16[64,1664]{1,0:T(8,128)(2,1)S(1)} %collective-permute-done.16.x0, bf16[64,1664]{1,0:T(8,128)(2,1)S(1)} %collective-permute-done.17.x1, bf16[64,1664]{1,0:T(8,128)(2,1)S(1)} %collective-permute-done.18.x2, bf16[64,1664]{1,0:T(8,128)(2,1)S(1)} %collective-permute-done.19.x3, ...), custom_call_target="tpu_custom_call" | custom-call | flops 6979321856 | bytes 10000000 | tf_op jit(solution)/shard_map/backward/pallas_call | solution.py:359
  64.9 2.7 %collective-permute-start.11 = (bf16[64,1664]{1,0:T(8,128)(2,1)S(1)}, bf16[64,1664]{1,0:T(8,128)(2,1)S(1)}, u32[]{:S(2)}, u32[]{:S(2)}) collective-permute-start(bf16[64,1664]{1,0:T(8,128)(2,1)S(1)} %get-tuple-element.38), channel_id=1, source_target_pairs={{0,2},{1,7},{2,4},{3,1},{4,6},{5,3},{6,0},{7,5},{8,10},{9,15},{10,... | collective-permute-start | bytes 638984 | tf_op jit(solution)/shard_map/return_result/ppermute | solution.py:276
  67.6 2.2 %backward.2.keep = f32[256,1664]{1,0:T(8,128)S(1)} custom-call(bf16[64,1664]{1,0:T(8,128)(2,1)S(1)} %get-tuple-element.39.x0, bf16[64,1664]{1,0:T(8,128)(2,1)S(1)} %collective-permute-done.13.x1, bf16[64,1664]{1,0:T(8,128)(2,1)S(1)} %collective-permute-done.14.x2, bf16[64,1664]{1,0:T(8,128)(2,1)S(1)} %collective-permute-done.15.x3, ...), custom_call_target="tpu_custom_call" | custom-call | flops 6979321856 | bytes 10000000 | tf_op jit(solution)/shard_map/backward/pallas_call | solution.py:359
  70.1 2.7 %collective-permute-start.23 = (bf16[64,1664]{1,0:T(8,128)(2,1)S(1)}, bf16[64,1664]{1,0:T(8,128)(2,1)S(1)}, u32[]{:S(2)}, u32[]{:S(2)}) collective-permute-start(bf16[64,1664]{1,0:T(8,128)(2,1)S(1)} %get-tuple-element.44), channel_id=1, source_target_pairs={{0,2},{1,7},{2,4},{3,1},{4,6},{5,3},{6,0},{7,5},{8,10},{9,15},{10,... | collective-permute-start | bytes 638984 | tf_op jit(solution)/shard_map/return_back/ppermute | solution.py:276
  72.9 3.4 %collective-permute-done.21.b = bf16[64,1664]{1,0:T(8,128)(2,1)S(1)} collective-permute-done((bf16[64,1664]{1,0:T(8,128)(2,1)S(1)}, bf16[64,1664]{1,0:T(8,128)(2,1)S(1)}, u32[]{:S(2)}, u32[]{:S(2)}) %collective-permute-start.21) | collective-permute-done | bytes 213024 | tf_op jit(solution)/shard_map/return_back/ppermute | solution.py:276
  76.4 0.7 collective-permute-done.23.two_b
  77.1 4.3 %collective-permute-done.12.one_r = bf16[64,1664]{1,0:T(8,128)(2,1)S(1)} collective-permute-done((bf16[64,1664]{1,0:T(8,128)(2,1)S(1)}, bf16[64,1664]{1,0:T(8,128)(2,1)S(1)}, u32[]{:S(2)}, u32[]{:S(2)}) %collective-permute-start.12) | collective-permute-done | bytes 213024 | tf_op jit(solution)/shard_map/return_result/ppermute | solution.py:276
  81.4 2.4 %collective-permute-done.22.one_b = bf16[64,1664]{1,0:T(8,128)(2,1)S(1)} collective-permute-done((bf16[64,1664]{1,0:T(8,128)(2,1)S(1)}, bf16[64,1664]{1,0:T(8,128)(2,1)S(1)}, u32[]{:S(2)}, u32[]{:S(2)}) %collective-permute-start.22) | collective-permute-done | bytes 213024 | tf_op jit(solution)/shard_map/return_back/ppermute | solution.py:276
  84.1 17.7 %all_to_all.11 = bf16[32,8,896]{2,1,0:T(8,128)(2,1)S(1)} all-to-all(bf16[32,8,896]{2,1,0:T(8,128)(2,1)S(1)} %bitcast.11), channel_id=1, replica_groups=mesh['xz'=32,'y'=4,'core'=2] {'xz'}, dimensions={0} | all-to-all | bytes 917504 | tf_op jit(solution)/shard_map/collect/all_to_all | solution.py:279
  101.9 4.9 %collective-permute-start.24 = (bf16[256,896]{1,0:T(8,128)(2,1)S(1)}, bf16[256,896]{1,0:T(8,128)(2,1)S(1)}, u32[]{:S(2)}, u32[]{:S(2)}) collective-permute-start(bf16[256,896]{1,0:T(8,128)(2,1)S(1)} %bitcast.13), channel_id=1, source_target_pairs={{0,1},{1,0},{2,3},{3,2},{4,5},{5,4},{6,7},{7,6},{8,9},{9,8},{10,11... | collective-permute-start | bytes 1376264 | tf_op jit(solution)/shard_map/collect/ppermute | solution.py:268
  106.7 0.7 final.2.first
  107.5 0.7 collective-permute-done.24.theirs
  108.2 1.8 %final.3 = (bf16[128,1664]{1,0:T(8,128)(2,1)}, bf16[128,1664]{1,0:T(8,128)(2,1)}) custom-call(f32[512,896]{1,0:T(8,128)S(1)} %final.2.first, bf16[256,896]{1,0:T(8,128)(2,1)S(1)} %collective-permute-done.24.theirs, bf16[512,512]{1,0:T(8,128)(2,1)S(1)} %get-tuple-element.45.merge_high, bf16[512,512]{1,0:T(8,128)(2,1)S(1)} %get-tuple-element.46.merge_low, ...), custom_call_target="tpu_custom_call" | custom-call | flops 1000000000 | bytes 4000000 | tf_op jit(solution)/shard_map/final/pallas_call | solution.py:399
  (59 shorter events, 3.7 us)
Async XLA Ops:
  0.6 7.9 %copy-start.8 = (f32[1664]{0:T(1024)S(1)}, f32[1664]{0:T(1024)}, u32[]{:S(2)}) copy-start(f32[1664]{0:T(1024)} %param.13) | copy-start | bytes 19972
  0.6 8.0 %copy-start.9 = (s32[32]{0:T(128)S(1)}, s32[32]{0:T(128)}, u32[]{:S(2)}) copy-start(s32[32]{0:T(128)} %param.17) | copy-start | bytes 388
  3.5 5.2 %copy-start.6 = (s32[32,512]{1,0:T(8,128)S(1)}, s32[32,512]{1,0:T(8,128)}, u32[]{:S(2)}) copy-start(s32[32,512]{1,0:T(8,128)} %index.1) | copy-start | bytes 196612
  3.5 7.7 %copy-start.1 = (bf16[128,1664]{1,0:T(8,128)(2,1)S(1)}, bf16[128,1664]{1,0:T(8,128)(2,1)}, u32[]{:S(2)}) copy-start(bf16[128,1664]{1,0:T(8,128)(2,1)} %upstream.3) | copy-start | bytes 1277956
  3.5 7.7 %copy-start.5 = (bf16[128,1664]{1,0:T(8,128)(2,1)S(1)}, bf16[128,1664]{1,0:T(8,128)(2,1)}, u32[]{:S(2)}) copy-start(bf16[128,1664]{1,0:T(8,128)(2,1)} %residual.1) | copy-start | bytes 1277956
  5.3 6.0 %collective-permute-start = (f32[128,1664]{1,0:T(8,128)S(1)}, f32[128,1664]{1,0:T(8,128)S(1)}, u32[]{:S(2)}, u32[]{:S(2)}) collective-permute-start(f32[128,1664]{1,0:T(8,128)S(1)} %get-tuple-element.26), channel_id=1, source_target_pairs={{0,1},{1,0},{2,3},{3,2},{4,5},{5,4},{6,7},{7,6},{8,9},{9,8},{10,11... | collective-permute-start | bytes 2555912 | tf_op jit(solution)/shard_map/attend/ppermute | solution.py:268
  9.5 45.9 %copy-start.4 = (bf16[1,1024,1664]{2,1,0:T(8,128)(2,1)S(1)}, bf16[1,1024,1664]{2,1,0:T(8,128)(2,1)}, u32[]{:S(2)}) copy-start(bf16[1,1024,1664]{2,1,0:T(8,128)(2,1)} %param.15) | copy-start | bytes 10223620
  11.2 44.2 %copy-start.3 = (bf16[1,1664,1024]{2,1,0:T(8,128)(2,1)S(1)}, bf16[1,1664,1024]{2,1,0:T(8,128)(2,1)}, u32[]{:S(2)}) copy-start(bf16[1,1664,1024]{2,1,0:T(8,128)(2,1)} %param.14) | copy-start | bytes 10223620
  12.2 1.9 %collective-permute-start.1 = (bf16[256,896]{1,0:T(8,128)(2,1)S(1)}, bf16[256,896]{1,0:T(8,128)(2,1)S(1)}, u32[]{:S(2)}, u32[]{:S(2)}) collective-permute-start(bf16[256,896]{1,0:T(8,128)(2,1)S(1)} %get-tuple-element.30), channel_id=1, source_target_pairs={{0,1},{1,0},{2,3},{3,2},{4,5},{5,4},{6,7},{7,6},{8,9},{9,8},{10,11... | collective-permute-start | bytes 1376264 | tf_op jit(solution)/shard_map/dispatch/ppermute | solution.py:268
  36.7 8.2 %collective-permute-start.2 = (bf16[64,1664]{1,0:T(8,128)(2,1)S(1)}, bf16[64,1664]{1,0:T(8,128)(2,1)S(1)}, u32[]{:S(2)}, u32[]{:S(2)}) collective-permute-start(bf16[64,1664]{1,0:T(8,128)(2,1)S(1)} %get-tuple-element.31.x0), channel_id=1, source_target_pairs={{0,2},{1,7},{2,4},{3,1},{4,6},{5,3},{6,0},{7,5},{8,10},{9,15},{10,... | collective-permute-start | bytes 638984 | tf_op jit(solution)/shard_map/gather_normed/ppermute | solution.py:276
  39.5 7.4 %collective-permute-start.3 = (bf16[64,1664]{1,0:T(8,128)(2,1)S(1)}, bf16[64,1664]{1,0:T(8,128)(2,1)S(1)}, u32[]{:S(2)}, u32[]{:S(2)}) collective-permute-start(bf16[64,1664]{1,0:T(8,128)(2,1)S(1)} %get-tuple-element.31.x0), channel_id=1, source_target_pairs={{0,6},{1,3},{2,0},{3,5},{4,2},{5,7},{6,4},{7,1},{8,14},{9,11},{10,... | collective-permute-start | bytes 638984 | tf_op jit(solution)/shard_map/gather_normed/ppermute | solution.py:276
  39.5 12.1 %collective-permute-start.5 = (bf16[64,1664]{1,0:T(8,128)(2,1)S(1)}, bf16[64,1664]{1,0:T(8,128)(2,1)S(1)}, u32[]{:S(2)}, u32[]{:S(2)}) collective-permute-start(bf16[64,1664]{1,0:T(8,128)(2,1)S(1)} %get-tuple-element.31.x0), channel_id=1, source_target_pairs={{0,1},{1,0},{2,3},{3,2},{4,5},{5,4},{6,7},{7,6},{8,9},{9,8},{10,11... | collective-permute-start | bytes 638984 | tf_op jit(solution)/shard_map/gather_normed/ppermute | solution.py:268
  43.3 8.4 %collective-permute-start.13 = (bf16[64,1664]{1,0:T(8,128)(2,1)S(1)}, bf16[64,1664]{1,0:T(8,128)(2,1)S(1)}, u32[]{:S(2)}, u32[]{:S(2)}) collective-permute-start(bf16[64,1664]{1,0:T(8,128)(2,1)S(1)} %get-tuple-element.39.x0), channel_id=1, source_target_pairs={{0,2},{1,7},{2,4},{3,1},{4,6},{5,3},{6,0},{7,5},{8,10},{9,15},{10,... | collective-permute-start | bytes 638984 | tf_op jit(solution)/shard_map/gather_down/ppermute | solution.py:276
  44.8 6.9 %collective-permute-start.4 = (bf16[64,1664]{1,0:T(8,128)(2,1)S(1)}, bf16[64,1664]{1,0:T(8,128)(2,1)S(1)}, u32[]{:S(2)}, u32[]{:S(2)}) collective-permute-start(bf16[64,1664]{1,0:T(8,128)(2,1)S(1)} %collective-permute-done.2.x1), channel_id=1, source_target_pairs={{0,2},{1,7},{2,4},{3,1},{4,6},{5,3},{6,0},{7,5},{8,10},{9,15},{10,... | collective-permute-start | bytes 638984 | tf_op jit(solution)/shard_map/gather_normed/ppermute | solution.py:276
  45.4 12.6 %collective-permute-start.14 = (bf16[64,1664]{1,0:T(8,128)(2,1)S(1)}, bf16[64,1664]{1,0:T(8,128)(2,1)S(1)}, u32[]{:S(2)}, u32[]{:S(2)}) collective-permute-start(bf16[64,1664]{1,0:T(8,128)(2,1)S(1)} %get-tuple-element.39.x0), channel_id=1, source_target_pairs={{0,6},{1,3},{2,0},{3,5},{4,2},{5,7},{6,4},{7,1},{8,14},{9,11},{10,... | collective-permute-start | bytes 638984 | tf_op jit(solution)/shard_map/gather_down/ppermute | solution.py:276
  46.9 11.2 %collective-permute-start.6 = (bf16[64,1664]{1,0:T(8,128)(2,1)S(1)}, bf16[64,1664]{1,0:T(8,128)(2,1)S(1)}, u32[]{:S(2)}, u32[]{:S(2)}) collective-permute-start(bf16[64,1664]{1,0:T(8,128)(2,1)S(1)} %collective-permute-done.2.x1), channel_id=1, source_target_pairs={{0,1},{1,0},{2,3},{3,2},{4,5},{5,4},{6,7},{7,6},{8,9},{9,8},{10,11... | collective-permute-start | bytes 638984 | tf_op jit(solution)/shard_map/gather_normed/ppermute | solution.py:268
  51.6 7.0 %collective-permute-start.7 = (bf16[64,1664]{1,0:T(8,128)(2,1)S(1)}, bf16[64,1664]{1,0:T(8,128)(2,1)S(1)}, u32[]{:S(2)}, u32[]{:S(2)}) collective-permute-start(bf16[64,1664]{1,0:T(8,128)(2,1)S(1)} %collective-permute-done.3.x2), channel_id=1, source_target_pairs={{0,1},{1,0},{2,3},{3,2},{4,5},{5,4},{6,7},{7,6},{8,9},{9,8},{10,11... | collective-permute-start | bytes 638984 | tf_op jit(solution)/shard_map/gather_normed/ppermute | solution.py:268
  51.7 7.0 %collective-permute-start.15 = (bf16[64,1664]{1,0:T(8,128)(2,1)S(1)}, bf16[64,1664]{1,0:T(8,128)(2,1)S(1)}, u32[]{:S(2)}, u32[]{:S(2)}) collective-permute-start(bf16[64,1664]{1,0:T(8,128)(2,1)S(1)} %collective-permute-done.13.x1), channel_id=1, source_target_pairs={{0,2},{1,7},{2,4},{3,1},{4,6},{5,3},{6,0},{7,5},{8,10},{9,15},{10,... | collective-permute-start | bytes 638984 | tf_op jit(solution)/shard_map/gather_down/ppermute | solution.py:276
  51.7 7.5 %collective-permute-start.8 = (bf16[64,1664]{1,0:T(8,128)(2,1)S(1)}, bf16[64,1664]{1,0:T(8,128)(2,1)S(1)}, u32[]{:S(2)}, u32[]{:S(2)}) collective-permute-start(bf16[64,1664]{1,0:T(8,128)(2,1)S(1)} %collective-permute-done.4.x3), channel_id=1, source_target_pairs={{0,1},{1,0},{2,3},{3,2},{4,5},{5,4},{6,7},{7,6},{8,9},{9,8},{10,11... | collective-permute-start | bytes 638984 | tf_op jit(solution)/shard_map/gather_normed/ppermute | solution.py:268
  58.0 3.9 %collective-permute-start.16 = (bf16[64,1664]{1,0:T(8,128)(2,1)S(1)}, bf16[64,1664]{1,0:T(8,128)(2,1)S(1)}, u32[]{:S(2)}, u32[]{:S(2)}) collective-permute-start(bf16[64,1664]{1,0:T(8,128)(2,1)S(1)} %get-tuple-element.39.x0), channel_id=1, source_target_pairs={{0,1},{1,0},{2,3},{3,2},{4,5},{5,4},{6,7},{7,6},{8,9},{9,8},{10,11... | collective-permute-start | bytes 638984 | tf_op jit(solution)/shard_map/gather_down/ppermute | solution.py:268
  58.1 3.8 %collective-permute-start.17 = (bf16[64,1664]{1,0:T(8,128)(2,1)S(1)}, bf16[64,1664]{1,0:T(8,128)(2,1)S(1)}, u32[]{:S(2)}, u32[]{:S(2)}) collective-permute-start(bf16[64,1664]{1,0:T(8,128)(2,1)S(1)} %collective-permute-done.13.x1), channel_id=1, source_target_pairs={{0,1},{1,0},{2,3},{3,2},{4,5},{5,4},{6,7},{7,6},{8,9},{9,8},{10,11... | collective-permute-start | bytes 638984 | tf_op jit(solution)/shard_map/gather_down/ppermute | solution.py:268
  58.6 3.3 %collective-permute-start.18 = (bf16[64,1664]{1,0:T(8,128)(2,1)S(1)}, bf16[64,1664]{1,0:T(8,128)(2,1)S(1)}, u32[]{:S(2)}, u32[]{:S(2)}) collective-permute-start(bf16[64,1664]{1,0:T(8,128)(2,1)S(1)} %collective-permute-done.14.x2), channel_id=1, source_target_pairs={{0,1},{1,0},{2,3},{3,2},{4,5},{5,4},{6,7},{7,6},{8,9},{9,8},{10,11... | collective-permute-start | bytes 638984 | tf_op jit(solution)/shard_map/gather_down/ppermute | solution.py:268
  58.7 3.2 %collective-permute-start.19 = (bf16[64,1664]{1,0:T(8,128)(2,1)S(1)}, bf16[64,1664]{1,0:T(8,128)(2,1)S(1)}, u32[]{:S(2)}, u32[]{:S(2)}) collective-permute-start(bf16[64,1664]{1,0:T(8,128)(2,1)S(1)} %collective-permute-done.15.x3), channel_id=1, source_target_pairs={{0,1},{1,0},{2,3},{3,2},{4,5},{5,4},{6,7},{7,6},{8,9},{9,8},{10,11... | collective-permute-start | bytes 638984 | tf_op jit(solution)/shard_map/gather_down/ppermute | solution.py:268
  61.8 2.9 %collective-permute-start.9 = (bf16[256,1664]{1,0:T(8,128)(2,1)S(1)}, bf16[256,1664]{1,0:T(8,128)(2,1)S(1)}, u32[]{:S(2)}, u32[]{:S(2)}) collective-permute-start(bf16[256,1664]{1,0:T(8,128)(2,1)S(1)} %get-tuple-element.34), channel_id=1, source_target_pairs={{0,1},{1,0},{2,3},{3,2},{4,5},{5,4},{6,7},{7,6},{8,9},{9,8},{10,11... | collective-permute-start | bytes 2555912 | tf_op jit(solution)/shard_map/return_result/ppermute | solution.py:268
  64.2 5.6 %collective-permute-start.20 = (bf16[256,1664]{1,0:T(8,128)(2,1)S(1)}, bf16[256,1664]{1,0:T(8,128)(2,1)S(1)}, u32[]{:S(2)}, u32[]{:S(2)}) collective-permute-start(bf16[256,1664]{1,0:T(8,128)(2,1)S(1)} %backward.3), channel_id=1, source_target_pairs={{0,1},{1,0},{2,3},{3,2},{4,5},{5,4},{6,7},{7,6},{8,9},{9,8},{10,11... | collective-permute-start | bytes 2555912 | tf_op jit(solution)/shard_map/return_back/ppermute | solution.py:268
  64.8 7.9 %collective-permute-start.10 = (bf16[64,1664]{1,0:T(8,128)(2,1)S(1)}, bf16[64,1664]{1,0:T(8,128)(2,1)S(1)}, u32[]{:S(2)}, u32[]{:S(2)}) collective-permute-start(bf16[64,1664]{1,0:T(8,128)(2,1)S(1)} %get-tuple-element.37.rest_0_), channel_id=1, source_target_pairs={{0,6},{1,3},{2,0},{3,5},{4,2},{5,7},{6,4},{7,1},{8,14},{9,11},{10,... | collective-permute-start | bytes 638984 | tf_op jit(solution)/shard_map/return_result/ppermute | solution.py:276
  64.9 7.8 %collective-permute-start.11 = (bf16[64,1664]{1,0:T(8,128)(2,1)S(1)}, bf16[64,1664]{1,0:T(8,128)(2,1)S(1)}, u32[]{:S(2)}, u32[]{:S(2)}) collective-permute-start(bf16[64,1664]{1,0:T(8,128)(2,1)S(1)} %get-tuple-element.38), channel_id=1, source_target_pairs={{0,2},{1,7},{2,4},{3,1},{4,6},{5,3},{6,0},{7,5},{8,10},{9,15},{10,... | collective-permute-start | bytes 638984 | tf_op jit(solution)/shard_map/return_result/ppermute | solution.py:276
  70.0 6.3 %collective-permute-start.21 = (bf16[64,1664]{1,0:T(8,128)(2,1)S(1)}, bf16[64,1664]{1,0:T(8,128)(2,1)S(1)}, u32[]{:S(2)}, u32[]{:S(2)}) collective-permute-start(bf16[64,1664]{1,0:T(8,128)(2,1)S(1)} %get-tuple-element.43), channel_id=1, source_target_pairs={{0,6},{1,3},{2,0},{3,5},{4,2},{5,7},{6,4},{7,1},{8,14},{9,11},{10,... | collective-permute-start | bytes 638984 | tf_op jit(solution)/shard_map/return_back/ppermute | solution.py:276
  70.1 7.0 %collective-permute-start.23 = (bf16[64,1664]{1,0:T(8,128)(2,1)S(1)}, bf16[64,1664]{1,0:T(8,128)(2,1)S(1)}, u32[]{:S(2)}, u32[]{:S(2)}) collective-permute-start(bf16[64,1664]{1,0:T(8,128)(2,1)S(1)} %get-tuple-element.44), channel_id=1, source_target_pairs={{0,2},{1,7},{2,4},{3,1},{4,6},{5,3},{6,0},{7,5},{8,10},{9,15},{10,... | collective-permute-start | bytes 638984 | tf_op jit(solution)/shard_map/return_back/ppermute | solution.py:276
  72.8 8.6 %collective-permute-start.12 = (bf16[64,1664]{1,0:T(8,128)(2,1)S(1)}, bf16[64,1664]{1,0:T(8,128)(2,1)S(1)}, u32[]{:S(2)}, u32[]{:S(2)}) collective-permute-start(bf16[64,1664]{1,0:T(8,128)(2,1)S(1)} %return_result.3), channel_id=1, source_target_pairs={{0,6},{1,3},{2,0},{3,5},{4,2},{5,7},{6,4},{7,1},{8,14},{9,11},{10,... | collective-permute-start | bytes 638984 | tf_op jit(solution)/shard_map/return_result/ppermute | solution.py:276
  76.3 7.4 %collective-permute-start.22 = (bf16[64,1664]{1,0:T(8,128)(2,1)S(1)}, bf16[64,1664]{1,0:T(8,128)(2,1)S(1)}, u32[]{:S(2)}, u32[]{:S(2)}) collective-permute-start(bf16[64,1664]{1,0:T(8,128)(2,1)S(1)} %return_back.3), channel_id=1, source_target_pairs={{0,6},{1,3},{2,0},{3,5},{4,2},{5,7},{6,4},{7,1},{8,14},{9,11},{10,... | collective-permute-start | bytes 638984 | tf_op jit(solution)/shard_map/return_back/ppermute | solution.py:276
  101.9 6.3 %collective-permute-start.24 = (bf16[256,896]{1,0:T(8,128)(2,1)S(1)}, bf16[256,896]{1,0:T(8,128)(2,1)S(1)}, u32[]{:S(2)}, u32[]{:S(2)}) collective-permute-start(bf16[256,896]{1,0:T(8,128)(2,1)S(1)} %bitcast.13), channel_id=1, source_target_pairs={{0,1},{1,0},{2,3},{3,2},{4,5},{5,4},{6,7},{7,6},{8,9},{9,8},{10,11... | collective-permute-start | bytes 1376264 | tf_op jit(solution)/shard_map/collect/ppermute | solution.py:268
  (3 other events, 3.6 us)

commit v9 on v8

--- a/solution.py
+++ b/solution.py
@@ -1,3 +1,5 @@
+import functools
+
 import jax
 import jax.numpy as jnp
 from jax import lax
@@ -49,60 +51,80 @@
     )
 
 
-def attend_kernel(ids, context, weight, send, keep):
-    core = ids[0]
-    rows = send.shape[0]
-    for out, at in ((send, 1 - core), (keep, core)):
-        block = context[:, pl.ds(pl.multiple_of(at * rows, rows), rows)]
-        for lo, hi in cuts(out.shape[1], 512):
-            out[:, lo:hi] = mm_a(block, weight[:, lo:hi])
-
-
-def routing_kernel(ids, index, count, gate, pick_keep, pick_send, merge_high, merge_low):
+def attend_kernel(other, ids, context, weight, out):
+    at = (1 - ids[0]) if other else ids[0]
+    rows = out.shape[0]
+    block = context[:, pl.ds(pl.multiple_of(at * rows, rows), rows)]
+    for lo, hi in cuts(out.shape[1], 512):
+        out[:, lo:hi] = mm_a(block, weight[:, lo:hi])
+
+
+def routing_kernel(ids, index, count, gate, pick_keep, pick_send, slots):
     core = ids[0]
     experts, capacity = index.shape
     packed = experts * PACK
-    own_rows = 128
+    rows = pick_keep.shape[1] // 4
     local = index[...] - ids[1]
-    listed = iota((experts, capacity), 1) < count[...]
-    mine = listed & (local >= 0) & (local < 2 * own_rows)
+    diagonal = iota((experts, experts), 0) == iota((experts, experts), 1)
+    counts = jnp.sum(jnp.where(diagonal, count[...].astype(F32), 0.0), axis=1, keepdims=True)
+    listed = iota((experts, capacity), 1).astype(F32) < counts
+    mine = listed & (local >= 0) & (local < 2 * rows)
     upto = jnp.where(iota((capacity, capacity), 0) <= iota((capacity, capacity), 1), 1.0, 0.0)
     rank = mm(jnp.where(mine, 1.0, 0.0).astype(BF), upto.astype(BF))
     lane = iota((experts, 128), 1)
-    rows = jnp.zeros((experts, 128), F32)
+    at_row = jnp.zeros((experts, 128), F32)
     gates = jnp.zeros((experts, 128), F32)
     shifted = (local + 1).astype(F32)
     for slot in range(SLOTS):
         here = mine & (rank == slot + 1.0)
         row = jnp.sum(jnp.where(here, shifted, 0.0), axis=1, keepdims=True) - 1.0
-        rows = jnp.where(lane == slot, row, rows)
-        weight = jnp.sum(jnp.where(here, gate[...], 0.0), axis=1, keepdims=True)
-        gates = jnp.where(lane == slot, weight, gates)
-    rows = rows.astype(BF)
+        at_row = jnp.where(lane == slot, row, at_row)
+        value = jnp.sum(jnp.where(here, gate[...], 0.0), axis=1, keepdims=True)
+        gates = jnp.where(lane == slot, value, gates)
+    at_row = at_row.astype(BF)
     gate_high = gates.astype(BF)
-    gate_low = (gates - gate_high.astype(F32)).astype(BF)
-    spread = jnp.where(iota((packed, experts), 0) // PACK == iota((packed, experts), 1), 1.0, 0.0).astype(BF)
-    down = mm(spread, rows)
+    slots[:experts, :] = at_row
+    slots[experts : 2 * experts, :] = gate_high
+    slots[2 * experts :, :] = (gates - gate_high.astype(F32)).astype(BF)
+    down = mm(spread_of(experts), at_row)
     r_col = iota((packed, 128), 0) % PACK
     lane_id = iota((packed, 128), 1)
-    k = iota((packed, 2 * own_rows), 1)
-    r_wide = iota((packed, 2 * own_rows), 0) % PACK
-    same_stream = (r_wide // 2) % 2 == k // own_rows
-    patch = (core * own_rows + k % own_rows).astype(F32)
+    k = iota((packed, 2 * rows), 1)
+    r_wide = iota((packed, 2 * rows), 0) % PACK
+    same_stream = (r_wide // 2) % 2 == k // rows
+    patch = (core * rows + k % rows).astype(F32)
     for out, side in ((pick_keep, core), (pick_send, 1 - core)):
         slot = 2 * side + r_col % 2
         row = jnp.sum(jnp.where(lane_id == slot, down, 0.0), axis=1, keepdims=True)
         hot = same_stream & (row == patch)
-        out[:, : 2 * own_rows] = jnp.where(hot & (r_wide < 4), 1.0, 0.0).astype(BF)
-        out[:, 2 * own_rows :] = jnp.where(hot & (r_wide >= 4), 1.0, 0.0).astype(BF)
-    along = (((0,), (1,)), ((), ()))
+        out[:, : 2 * rows] = jnp.where(hot & (r_wide < 4), 1.0, 0.0).astype(BF)
+        out[:, 2 * rows :] = jnp.where(hot & (r_wide >= 4), 1.0, 0.0).astype(BF)
+
+
+def spread_of(experts):
+    shape = (experts * PACK, experts)
+    return jnp.where(iota(shape, 0) // PACK == iota(shape, 1), 1.0, 0.0).astype(BF)
+
+
+def merge_kernel(ids, slots, merge_high, merge_low):
+    core = ids[0]
+    experts = slots.shape[0] // 3
+    packed = experts * PACK
+    rows = merge_high.shape[0] // 4
+    spread = spread_of(experts)
     across = [
-        lax.dot_general(part, spread, along, preferred_element_type=F32)
-        for part in (rows, gate_high, gate_low)
+        lax.dot_general(
+            slots[i * experts : (i + 1) * experts, :],
+            spread,
+            (((0,), (1,)), ((), ())),
+            preferred_element_type=F32,
+        )
+        for i in range(3)
     ]
     q = iota((128, packed), 1) % PACK
     sub = iota((128, packed), 0)
-    own = (core * own_rows + iota((own_rows, packed), 0)).astype(F32)
+    own = (core * rows + iota((rows, packed), 0)).astype(F32)
+    q_rows = iota((rows, packed), 1) % PACK
     for which, side in ((0, core), (1, 1 - core)):
         slot = 2 * side + q % 2
         row, high, low = (
@@ -110,8 +132,8 @@
         )
         hot = row == own
         for group in range(4):
-            here = hot & (q // 2 == group)
-            at = (slice(group * own_rows, (group + 1) * own_rows), slice(which * packed, (which + 1) * packed))
+            here = hot & (q_rows // 2 == group)
+            at = (slice(group * rows, (group + 1) * rows), slice(which * packed, (which + 1) * packed))
             merge_high[at] = jnp.where(here, high, 0.0).astype(BF)
             merge_low[at] = jnp.where(here, low, 0.0).astype(BF)
 
@@ -200,8 +222,7 @@
         out[...] = (keep[at, :] + got[at, :].astype(F32)).astype(out.dtype)
 
 
-def add_kernel(a, b, *rest):
-    out = rest[-1]
+def add_kernel(a, b, out):
     out[...] = (a[...].astype(F32) + b[...].astype(F32)).astype(BF)
 
 
@@ -281,23 +302,34 @@
         )
         return got.reshape(packed, WIDE)
 
+    def attend(other):
+        return call(
+            functools.partial(attend_kernel, other),
+            sds((rows, width), F32),
+            [SMEM, VMEM, VMEM],
+            flops=2 * rows * width * context.shape[1],
+            moved=4 * 10**6,
+        )(ids, context.T, out_weight)
+
     with jax.named_scope("attend"):
-        att_send, att_keep = call(
-            attend_kernel,
-            [sds((rows, width), F32)] * 2,
-            [SMEM, VMEM, VMEM],
-            flops=4 * rows * width * context.shape[1],
-            moved=5 * 10**6,
-        )(ids, context.T, out_weight)
-        att_got = swap_core(att_send)
+        att_got = swap_core(attend(True))
+        att_keep = attend(False)
     with jax.named_scope("routing"):
-        pick_keep, pick_send, merge_high, merge_low = call(
+        pick_keep, pick_send, slots = call(
             routing_kernel,
-            [sds((packed, 4 * rows), BF)] * 2 + [sds((4 * rows, 2 * packed), BF)] * 2,
+            [sds((packed, 4 * rows), BF)] * 2 + [sds((3 * experts, 128), BF)],
             [SMEM] + [VMEM] * 3,
             flops=10**9,
-            moved=2 * 10**6,
-        )(ids, patch_index, patch_count.reshape(experts, 1), gate_value)
+            moved=10**6,
+        )(ids, patch_index, patch_count.reshape(1, experts), gate_value)
+    with jax.named_scope("merge"):
+        merge_high, merge_low = call(
+            merge_kernel,
+            [sds((4 * rows, 2 * packed), BF)] * 2,
+            [SMEM, VMEM],
+            flops=10**8,
+            moved=10**6,
+        )(ids, slots)
     with jax.named_scope("norm"):
         stream, keep, send = call(
             norm_kernel,
@@ -329,14 +361,11 @@
             moved=4 * 10**6,
         )(keep_part, swap_core(send_part))
 
-    def reduce_y(parts, early):
+    def reduce_y(parts):
         own, one, two, far = parts
+        from_two = ring(two, 1)
         from_far = ring(far, -1)
-        from_two = ring(two, 1)
-        after = [from_two] if early else []
-        one = call(
-            add_kernel, sds((block, width), BF), [VMEM] * 2 + [ANY] * len(after), flops=10**5, moved=10**6
-        )(one, from_far, *after)
+        one = call(add_kernel, sds((block, width), BF), [VMEM] * 2, flops=10**5, moved=10**6)(one, from_far)
         return own, ring(one, -1), from_two
 
     weight_in = expert_in[0]
@@ -375,12 +404,12 @@
         slope_send, part_send = forward(sends, BF, slope_keep)
     with jax.named_scope("return_result"):
         parts = combine(part_keep, part_send)
-        result = reduce_y(parts, True)
+        result = reduce_y(parts)
     with jax.named_scope("backward"):
         back_send = backward(down_sends, slope_send, BF)
         back_keep = backward(down_keeps, slope_keep, F32, parts[3])
     with jax.named_scope("return_back"):
-        back = reduce_y(combine(back_keep, back_send), False)
+        back = reduce_y(combine(back_keep, back_send))
     with jax.named_scope("collect"):
         ready = call(
             pack_kernel,

time: 110 us -> 110 us (level)
  Pallas kernels: 17.5 us -> 19.3 us
  starting transfers between devices: 33.9 us -> 32.2 us
    pallas_call x4 -> x6, Pallas kernels: 3.45 us -> 4.89 us  [the longest x2 2.44 us: attend(): call(functools.partial(attend_kernel, other), sds((rows, width), F32), [S...]
  transfers between devices with their start and end apart: 25 -> 25, of which waited for: 7 -> 7; matrix products, arithmetic and copies ran while one was open for 0% -> 0% of each run, Pallas kernels for 11% -> 13%
where the time goes in v9:
time: 110 us
  blocking collectives  40.6 us (37%)
  starting transfers between devices  32.2 us (29%)
  Pallas kernels  19.3 us (18%)
  waiting for transfers between devices  13.8 us (13%)
  local copies, waits for them, and re-layouts  2.84 us (3%)
    all_to_all x2, blocking collectives, exchange(): lax.all_to_all(x.reshape(experts, PACK, WIDE), 'xz', split_axis=0, concat...  40.6 us
    ppermute x13, starting transfers between devices, swap_core(): return lax.ppermute(x, 'core', [(0, 1), (1, 0)])  21.4 us
    ppermute x12, waiting for transfers between devices, ring(): return lax.ppermute(x, ('y', 'core'), pairs)  11.9 us
    ppermute x12, starting transfers between devices, ring(): return lax.ppermute(x, ('y', 'core'), pairs)  10.8 us
    pallas_call x2, Pallas kernels, forward(): call(forward_kernel, [sds((tall, units), F32), sds((tall, width), kind)],...  5.26 us
    pallas_call x2, Pallas kernels, backward(): call(backward_kernel, sds((tall, width), kind), [VMEM] * 7 + [ANY] * len(...  4.62 us
    unnamed x20, local copies, waits for them, and re-layouts  2.84 us
    pallas_call x2, Pallas kernels, attend(): call(functools.partial(attend_kernel, other), sds((rows, width), F32), [S...  2.44 us
  transfers between devices with their start and end apart: 25, of which 7 were waited for; matrix products, arithmetic and copies ran while one was open for 0% of the time, Pallas kernels for 13%

profile of v9, /device:TPU:1, one launch (start us, length us, event | category | flops | bytes accessed | tf_op | source)
XLA Modules:
  0.0 109.7 jit_solution(3099273439436445362)
XLA Ops:
  0.7 1.8 %copy-done = bf16[832,1664]{1,0:T(8,128)(2,1)S(1)} copy-done((bf16[832,1664]{1,0:T(8,128)(2,1)S(1)}, bf16[832,1664]{1,0:T(8,128)(2,1)}, u32[]{:S(2)}) %copy-start) | copy-done | bytes 2768920
  2.5 1.0 copy-done.1
  3.5 1.2 %attend.3 = f32[128,1664]{1,0:T(8,128)S(1)} custom-call(s32[2]{0:T(128)S(1)} %pad_add_fusion.ids, bf16[832,256]{1,0:T(8,128)(2,1)S(1)} %bitcast.13, bf16[832,1664]{1,0:T(8,128)(2,1)S(1)} %copy-done), custom_call_target="tpu_custom_call" | custom-call | flops 354418688 | bytes 4000000 | tf_op jit(solution)/shard_map/attend/pallas_call | solution.py:306
  4.8 3.3 %collective-permute-start = (f32[128,1664]{1,0:T(8,128)S(1)}, f32[128,1664]{1,0:T(8,128)S(1)}, u32[]{:S(2)}, u32[]{:S(2)}) collective-permute-start(f32[128,1664]{1,0:T(8,128)S(1)} %attend.3), channel_id=1, source_target_pairs={{0,1},{1,0},{2,3},{3,2},{4,5},{5,4},{6,7},{7,6},{8,9},{9,8},{10,11... | collective-permute-start | bytes 2555912 | tf_op jit(solution)/shard_map/attend/ppermute | solution.py:289
  8.1 1.2 %attend.2.att_keep = f32[128,1664]{1,0:T(8,128)S(1)} custom-call(s32[2]{0:T(128)S(1)} %pad_add_fusion.ids, bf16[832,256]{1,0:T(8,128)(2,1)S(1)} %bitcast.14, bf16[832,1664]{1,0:T(8,128)(2,1)S(1)} %copy-done), custom_call_target="tpu_custom_call" | custom-call | flops 354418688 | bytes 4000000 | tf_op jit(solution)/shard_map/attend/pallas_call | solution.py:306
  9.4 1.2 %routing.1 = (bf16[256,512]{1,0:T(8,128)(2,1)S(1)}, bf16[256,512]{1,0:T(8,128)(2,1)S(1)}, bf16[96,128]{1,0:T(8,128)(2,1)S(1)}) custom-call(s32[2]{0:T(128)S(1)} %pad_add_fusion.ids, s32[32,512]{1,0:T(8,128)S(1)} %copy-done.6, s32[1,32]{1,0:T(1,128)S(1)} %bitcast.25, f32[32,512]{1,0:T(8,128)S(1)} %copy-done.7), custom_call_target="tpu_custom_call" | custom-call | flops 1000000000 | bytes 1000000 | tf_op jit(solution)/shard_map/routing/pallas_call | solution.py:318
  10.7 1.0 norm.1
  11.8 1.8 %collective-permute-done.1 = bf16[256,896]{1,0:T(8,128)(2,1)S(1)} collective-permute-done((bf16[256,896]{1,0:T(8,128)(2,1)S(1)}, bf16[256,896]{1,0:T(8,128)(2,1)S(1)}, u32[]{:S(2)}, u32[]{:S(2)}) %collective-permute-start.1) | collective-permute-done | bytes 458784 | tf_op jit(solution)/shard_map/dispatch/ppermute | solution.py:289
  13.7 22.2 %all_to_all.10 = bf16[32,8,896]{2,1,0:T(8,128)(2,1)S(1)} all-to-all(bf16[32,8,896]{2,1,0:T(8,128)(2,1)S(1)} %add_bitcast_fusion), channel_id=1, replica_groups=mesh['xz'=32,'y'=4,'core'=2] {'xz'}, dimensions={0} | all-to-all | bytes 917504 | tf_op jit(solution)/shard_map/dispatch/all_to_all | solution.py:300
  36.1 2.8 %collective-permute-start.2 = (bf16[64,1664]{1,0:T(8,128)(2,1)S(1)}, bf16[64,1664]{1,0:T(8,128)(2,1)S(1)}, u32[]{:S(2)}, u32[]{:S(2)}) collective-permute-start(bf16[64,1664]{1,0:T(8,128)(2,1)S(1)} %get-tuple-element.28.x0), channel_id=1, source_target_pairs={{0,2},{1,7},{2,4},{3,1},{4,6},{5,3},{6,0},{7,5},{8,10},{9,15},{10,... | collective-permute-start | bytes 638984 | tf_op jit(solution)/shard_map/gather_normed/ppermute | solution.py:297
  38.9 3.8 %collective-permute-start.5 = (bf16[64,1664]{1,0:T(8,128)(2,1)S(1)}, bf16[64,1664]{1,0:T(8,128)(2,1)S(1)}, u32[]{:S(2)}, u32[]{:S(2)}) collective-permute-start(bf16[64,1664]{1,0:T(8,128)(2,1)S(1)} %get-tuple-element.28.x0), channel_id=1, source_target_pairs={{0,1},{1,0},{2,3},{3,2},{4,5},{5,4},{6,7},{7,6},{8,9},{9,8},{10,11... | collective-permute-start | bytes 638984 | tf_op jit(solution)/shard_map/gather_normed/ppermute | solution.py:289
  42.8 1.5 %collective-permute-start.13 = (bf16[64,1664]{1,0:T(8,128)(2,1)S(1)}, bf16[64,1664]{1,0:T(8,128)(2,1)S(1)}, u32[]{:S(2)}, u32[]{:S(2)}) collective-permute-start(bf16[64,1664]{1,0:T(8,128)(2,1)S(1)} %get-tuple-element.36.x0), channel_id=1, source_target_pairs={{0,2},{1,7},{2,4},{3,1},{4,6},{5,3},{6,0},{7,5},{8,10},{9,15},{10,... | collective-permute-start | bytes 638984 | tf_op jit(solution)/shard_map/gather_down/ppermute | solution.py:297
  44.9 0.9 collective-permute-start.14
  45.8 0.6 collective-permute-done.3.x2
  46.4 4.7 %collective-permute-start.6 = (bf16[64,1664]{1,0:T(8,128)(2,1)S(1)}, bf16[64,1664]{1,0:T(8,128)(2,1)S(1)}, u32[]{:S(2)}, u32[]{:S(2)}) collective-permute-start(bf16[64,1664]{1,0:T(8,128)(2,1)S(1)} %collective-permute-done.2.x1), channel_id=1, source_target_pairs={{0,1},{1,0},{2,3},{3,2},{4,5},{5,4},{6,7},{7,6},{8,9},{9,8},{10,11... | collective-permute-start | bytes 638984 | tf_op jit(solution)/shard_map/gather_normed/ppermute | solution.py:289
  51.2 3.7 %collective-permute-start.8 = (bf16[64,1664]{1,0:T(8,128)(2,1)S(1)}, bf16[64,1664]{1,0:T(8,128)(2,1)S(1)}, u32[]{:S(2)}, u32[]{:S(2)}) collective-permute-start(bf16[64,1664]{1,0:T(8,128)(2,1)S(1)} %collective-permute-done.4.x3), channel_id=1, source_target_pairs={{0,1},{1,0},{2,3},{3,2},{4,5},{5,4},{6,7},{7,6},{8,9},{9,8},{10,11... | collective-permute-start | bytes 638984 | tf_op jit(solution)/shard_map/gather_normed/ppermute | solution.py:289
  54.9 2.6 %forward.2 = (f32[256,1024]{1,0:T(8,128)S(1)}, f32[256,1664]{1,0:T(8,128)S(1)}) custom-call(bf16[64,1664]{1,0:T(8,128)(2,1)S(1)} %get-tuple-element.28.x0, bf16[64,1664]{1,0:T(8,128)(2,1)S(1)} %collective-permute-done.2.x1, bf16[64,1664]{1,0:T(8,128)(2,1)S(1)} %collective-permute-done.3.x2, bf16[64,1664]{1,0:T(8,128)(2,1)S(1)} %collective-permute-done.4.x3, ...), custom_call_target="tpu_custom_call" | custom-call | flops 6979321856 | bytes 10000000 | tf_op jit(solution)/shard_map/forward/pallas_call | solution.py:377
  58.7 2.6 %forward.3 = (f32[256,1024]{1,0:T(8,128)S(1)}, bf16[256,1664]{1,0:T(8,128)(2,1)S(1)}) custom-call(bf16[64,1664]{1,0:T(8,128)(2,1)S(1)} %collective-permute-done.5.x0, bf16[64,1664]{1,0:T(8,128)(2,1)S(1)} %collective-permute-done.6.x1, bf16[64,1664]{1,0:T(8,128)(2,1)S(1)} %collective-permute-done.7.x2, bf16[64,1664]{1,0:T(8,128)(2,1)S(1)} %collective-permute-done.8.x3, ...), custom_call_target="tpu_custom_call" | custom-call | flops 6979321856 | bytes 10000000 | tf_op jit(solution)/shard_map/forward/pallas_call | solution.py:377
  61.5 2.3 %backward.3 = bf16[256,1664]{1,0:T(8,128)(2,1)S(1)} custom-call(bf16[64,1664]{1,0:T(8,128)(2,1)S(1)} %collective-permute-done.16.x0, bf16[64,1664]{1,0:T(8,128)(2,1)S(1)} %collective-permute-done.17.x1, bf16[64,1664]{1,0:T(8,128)(2,1)S(1)} %collective-permute-done.18.x2, bf16[64,1664]{1,0:T(8,128)(2,1)S(1)} %collective-permute-done.19.x3, ...), custom_call_target="tpu_custom_call" | custom-call | flops 6979321856 | bytes 10000000 | tf_op jit(solution)/shard_map/backward/pallas_call | solution.py:388
  64.6 2.3 %backward.2.keep = f32[256,1664]{1,0:T(8,128)S(1)} custom-call(bf16[64,1664]{1,0:T(8,128)(2,1)S(1)} %get-tuple-element.36.x0, bf16[64,1664]{1,0:T(8,128)(2,1)S(1)} %collective-permute-done.13.x1, bf16[64,1664]{1,0:T(8,128)(2,1)S(1)} %collective-permute-done.14.x2, bf16[64,1664]{1,0:T(8,128)(2,1)S(1)} %collective-permute-done.15.x3, ...), custom_call_target="tpu_custom_call" | custom-call | flops 6979321856 | bytes 10000000 | tf_op jit(solution)/shard_map/backward/pallas_call | solution.py:388
  67.3 2.7 %collective-permute-start.12 = (bf16[64,1664]{1,0:T(8,128)(2,1)S(1)}, bf16[64,1664]{1,0:T(8,128)(2,1)S(1)}, u32[]{:S(2)}, u32[]{:S(2)}) collective-permute-start(bf16[64,1664]{1,0:T(8,128)(2,1)S(1)} %get-tuple-element.35), channel_id=1, source_target_pairs={{0,2},{1,7},{2,4},{3,1},{4,6},{5,3},{6,0},{7,5},{8,10},{9,15},{10,... | collective-permute-start | bytes 638984 | tf_op jit(solution)/shard_map/return_result/ppermute | solution.py:297
  70.1 1.4 %collective-permute-start.23 = (bf16[64,1664]{1,0:T(8,128)(2,1)S(1)}, bf16[64,1664]{1,0:T(8,128)(2,1)S(1)}, u32[]{:S(2)}, u32[]{:S(2)}) collective-permute-start(bf16[64,1664]{1,0:T(8,128)(2,1)S(1)} %get-tuple-element.41), channel_id=1, source_target_pairs={{0,2},{1,7},{2,4},{3,1},{4,6},{5,3},{6,0},{7,5},{8,10},{9,15},{10,... | collective-permute-start | bytes 638984 | tf_op jit(solution)/shard_map/return_back/ppermute | solution.py:297
  71.7 1.5 %collective-permute-done.21.b = bf16[64,1664]{1,0:T(8,128)(2,1)S(1)} collective-permute-done((bf16[64,1664]{1,0:T(8,128)(2,1)S(1)}, bf16[64,1664]{1,0:T(8,128)(2,1)S(1)}, u32[]{:S(2)}, u32[]{:S(2)}) %collective-permute-start.21) | collective-permute-done | bytes 213024 | tf_op jit(solution)/shard_map/return_back/ppermute | solution.py:297
  73.6 1.5 %collective-permute-done.12.two_r = bf16[64,1664]{1,0:T(8,128)(2,1)S(1)} collective-permute-done((bf16[64,1664]{1,0:T(8,128)(2,1)S(1)}, bf16[64,1664]{1,0:T(8,128)(2,1)S(1)}, u32[]{:S(2)}, u32[]{:S(2)}) %collective-permute-start.12) | collective-permute-done | bytes 213024 | tf_op jit(solution)/shard_map/return_result/ppermute | solution.py:297
  75.0 3.7 %collective-permute-done.23.two_b = bf16[64,1664]{1,0:T(8,128)(2,1)S(1)} collective-permute-done((bf16[64,1664]{1,0:T(8,128)(2,1)S(1)}, bf16[64,1664]{1,0:T(8,128)(2,1)S(1)}, u32[]{:S(2)}, u32[]{:S(2)}) %collective-permute-start.23) | collective-permute-done | bytes 213024 | tf_op jit(solution)/shard_map/return_back/ppermute | solution.py:297
  78.8 1.3 %collective-permute-done.11.one_r = bf16[64,1664]{1,0:T(8,128)(2,1)S(1)} collective-permute-done((bf16[64,1664]{1,0:T(8,128)(2,1)S(1)}, bf16[64,1664]{1,0:T(8,128)(2,1)S(1)}, u32[]{:S(2)}, u32[]{:S(2)}) %collective-permute-start.11) | collective-permute-done | bytes 213024 | tf_op jit(solution)/shard_map/return_result/ppermute | solution.py:297
  80.1 3.3 %collective-permute-done.22.one_b = bf16[64,1664]{1,0:T(8,128)(2,1)S(1)} collective-permute-done((bf16[64,1664]{1,0:T(8,128)(2,1)S(1)}, bf16[64,1664]{1,0:T(8,128)(2,1)S(1)}, u32[]{:S(2)}, u32[]{:S(2)}) %collective-permute-start.22) | collective-permute-done | bytes 213024 | tf_op jit(solution)/shard_map/return_back/ppermute | solution.py:297
  83.7 18.4 %all_to_all.11 = bf16[32,8,896]{2,1,0:T(8,128)(2,1)S(1)} all-to-all(bf16[32,8,896]{2,1,0:T(8,128)(2,1)S(1)} %bitcast.11), channel_id=1, replica_groups=mesh['xz'=32,'y'=4,'core'=2] {'xz'}, dimensions={0} | all-to-all | bytes 917504 | tf_op jit(solution)/shard_map/collect/all_to_all | solution.py:300
  102.1 3.9 %collective-permute-start.24 = (bf16[256,896]{1,0:T(8,128)(2,1)S(1)}, bf16[256,896]{1,0:T(8,128)(2,1)S(1)}, u32[]{:S(2)}, u32[]{:S(2)}) collective-permute-start(bf16[256,896]{1,0:T(8,128)(2,1)S(1)} %bitcast.15), channel_id=1, source_target_pairs={{0,1},{1,0},{2,3},{3,2},{4,5},{5,4},{6,7},{7,6},{8,9},{9,8},{10,11... | collective-permute-start | bytes 1376264 | tf_op jit(solution)/shard_map/collect/ppermute | solution.py:289
  105.9 1.2 %merge.1 = (bf16[512,512]{1,0:T(8,128)(2,1)S(1)}, bf16[512,512]{1,0:T(8,128)(2,1)S(1)}) custom-call(s32[2]{0:T(128)S(1)} %pad_add_fusion.ids, bf16[96,128]{1,0:T(8,128)(2,1)S(1)} %get-tuple-element.42.slots), custom_call_target="tpu_custom_call" | custom-call | flops 100000000 | bytes 1000000 | tf_op jit(solution)/shard_map/merge/pallas_call | solution.py:326
  107.1 0.7 final.2.first
  107.8 1.8 %final.3 = (bf16[128,1664]{1,0:T(8,128)(2,1)}, bf16[128,1664]{1,0:T(8,128)(2,1)}) custom-call(f32[512,896]{1,0:T(8,128)S(1)} %final.2.first, bf16[256,896]{1,0:T(8,128)(2,1)S(1)} %collective-permute-done.24.theirs, bf16[512,512]{1,0:T(8,128)(2,1)S(1)} %get-tuple-element.43.merge_high, bf16[512,512]{1,0:T(8,128)(2,1)S(1)} %get-tuple-element.44.merge_low, ...), custom_call_target="tpu_custom_call" | custom-call | flops 1000000000 | bytes 4000000 | tf_op jit(solution)/shard_map/final/pallas_call | solution.py:428
  (60 shorter events, 4.7 us)
Async XLA Ops:
  0.6 7.5 %copy-start.9 = (f32[1664]{0:T(1024)S(1)}, f32[1664]{0:T(1024)}, u32[]{:S(2)}) copy-start(f32[1664]{0:T(1024)} %param.13) | copy-start | bytes 19972
  0.7 1.8 %copy-start = (bf16[832,1664]{1,0:T(8,128)(2,1)S(1)}, bf16[832,1664]{1,0:T(8,128)(2,1)}, u32[]{:S(2)}) copy-start(bf16[832,1664]{1,0:T(8,128)(2,1)} %weight.3) | copy-start | bytes 8306692
  4.7 4.6 %copy-start.6 = (s32[32,512]{1,0:T(8,128)S(1)}, s32[32,512]{1,0:T(8,128)}, u32[]{:S(2)}) copy-start(s32[32,512]{1,0:T(8,128)} %index.1) | copy-start | bytes 196612
  4.7 4.6 %copy-start.7 = (f32[32,512]{1,0:T(8,128)S(1)}, f32[32,512]{1,0:T(8,128)}, u32[]{:S(2)}) copy-start(f32[32,512]{1,0:T(8,128)} %gate.1) | copy-start | bytes 196612
  4.8 4.6 %copy-start.8 = (s32[32]{0:T(128)S(1)}, s32[32]{0:T(128)}, u32[]{:S(2)}) copy-start(s32[32]{0:T(128)} %param.17) | copy-start | bytes 388
  4.8 5.9 %collective-permute-start = (f32[128,1664]{1,0:T(8,128)S(1)}, f32[128,1664]{1,0:T(8,128)S(1)}, u32[]{:S(2)}, u32[]{:S(2)}) collective-permute-start(f32[128,1664]{1,0:T(8,128)S(1)} %attend.3), channel_id=1, source_target_pairs={{0,1},{1,0},{2,3},{3,2},{4,5},{5,4},{6,7},{7,6},{8,9},{9,8},{10,11... | collective-permute-start | bytes 2555912 | tf_op jit(solution)/shard_map/attend/ppermute | solution.py:289
  9.4 45.5 %copy-start.4 = (bf16[1,1024,1664]{2,1,0:T(8,128)(2,1)S(1)}, bf16[1,1024,1664]{2,1,0:T(8,128)(2,1)}, u32[]{:S(2)}) copy-start(bf16[1,1024,1664]{2,1,0:T(8,128)(2,1)} %param.15) | copy-start | bytes 10223620
  10.7 44.2 %copy-start.3 = (bf16[1,1664,1024]{2,1,0:T(8,128)(2,1)S(1)}, bf16[1,1664,1024]{2,1,0:T(8,128)(2,1)}, u32[]{:S(2)}) copy-start(bf16[1,1664,1024]{2,1,0:T(8,128)(2,1)} %param.14) | copy-start | bytes 10223620
  11.7 1.9 %collective-permute-start.1 = (bf16[256,896]{1,0:T(8,128)(2,1)S(1)}, bf16[256,896]{1,0:T(8,128)(2,1)S(1)}, u32[]{:S(2)}, u32[]{:S(2)}) collective-permute-start(bf16[256,896]{1,0:T(8,128)(2,1)S(1)} %get-tuple-element.27), channel_id=1, source_target_pairs={{0,1},{1,0},{2,3},{3,2},{4,5},{5,4},{6,7},{7,6},{8,9},{9,8},{10,11... | collective-permute-start | bytes 1376264 | tf_op jit(solution)/shard_map/dispatch/ppermute | solution.py:289
  36.1 8.2 %collective-permute-start.2 = (bf16[64,1664]{1,0:T(8,128)(2,1)S(1)}, bf16[64,1664]{1,0:T(8,128)(2,1)S(1)}, u32[]{:S(2)}, u32[]{:S(2)}) collective-permute-start(bf16[64,1664]{1,0:T(8,128)(2,1)S(1)} %get-tuple-element.28.x0), channel_id=1, source_target_pairs={{0,2},{1,7},{2,4},{3,1},{4,6},{5,3},{6,0},{7,5},{8,10},{9,15},{10,... | collective-permute-start | bytes 638984 | tf_op jit(solution)/shard_map/gather_normed/ppermute | solution.py:297
  38.9 7.4 %collective-permute-start.3 = (bf16[64,1664]{1,0:T(8,128)(2,1)S(1)}, bf16[64,1664]{1,0:T(8,128)(2,1)S(1)}, u32[]{:S(2)}, u32[]{:S(2)}) collective-permute-start(bf16[64,1664]{1,0:T(8,128)(2,1)S(1)} %get-tuple-element.28.x0), channel_id=1, source_target_pairs={{0,6},{1,3},{2,0},{3,5},{4,2},{5,7},{6,4},{7,1},{8,14},{9,11},{10,... | collective-permute-start | bytes 638984 | tf_op jit(solution)/shard_map/gather_normed/ppermute | solution.py:297
  38.9 12.1 %collective-permute-start.5 = (bf16[64,1664]{1,0:T(8,128)(2,1)S(1)}, bf16[64,1664]{1,0:T(8,128)(2,1)S(1)}, u32[]{:S(2)}, u32[]{:S(2)}) collective-permute-start(bf16[64,1664]{1,0:T(8,128)(2,1)S(1)} %get-tuple-element.28.x0), channel_id=1, source_target_pairs={{0,1},{1,0},{2,3},{3,2},{4,5},{5,4},{6,7},{7,6},{8,9},{9,8},{10,11... | collective-permute-start | bytes 638984 | tf_op jit(solution)/shard_map/gather_normed/ppermute | solution.py:289
  42.8 8.4 %collective-permute-start.13 = (bf16[64,1664]{1,0:T(8,128)(2,1)S(1)}, bf16[64,1664]{1,0:T(8,128)(2,1)S(1)}, u32[]{:S(2)}, u32[]{:S(2)}) collective-permute-start(bf16[64,1664]{1,0:T(8,128)(2,1)S(1)} %get-tuple-element.36.x0), channel_id=1, source_target_pairs={{0,2},{1,7},{2,4},{3,1},{4,6},{5,3},{6,0},{7,5},{8,10},{9,15},{10,... | collective-permute-start | bytes 638984 | tf_op jit(solution)/shard_map/gather_down/ppermute | solution.py:297
  44.3 6.9 %collective-permute-start.4 = (bf16[64,1664]{1,0:T(8,128)(2,1)S(1)}, bf16[64,1664]{1,0:T(8,128)(2,1)S(1)}, u32[]{:S(2)}, u32[]{:S(2)}) collective-permute-start(bf16[64,1664]{1,0:T(8,128)(2,1)S(1)} %collective-permute-done.2.x1), channel_id=1, source_target_pairs={{0,2},{1,7},{2,4},{3,1},{4,6},{5,3},{6,0},{7,5},{8,10},{9,15},{10,... | collective-permute-start | bytes 638984 | tf_op jit(solution)/shard_map/gather_normed/ppermute | solution.py:297
  44.9 12.7 %collective-permute-start.14 = (bf16[64,1664]{1,0:T(8,128)(2,1)S(1)}, bf16[64,1664]{1,0:T(8,128)(2,1)S(1)}, u32[]{:S(2)}, u32[]{:S(2)}) collective-permute-start(bf16[64,1664]{1,0:T(8,128)(2,1)S(1)} %get-tuple-element.36.x0), channel_id=1, source_target_pairs={{0,6},{1,3},{2,0},{3,5},{4,2},{5,7},{6,4},{7,1},{8,14},{9,11},{10,... | collective-permute-start | bytes 638984 | tf_op jit(solution)/shard_map/gather_down/ppermute | solution.py:297
  46.4 11.3 %collective-permute-start.6 = (bf16[64,1664]{1,0:T(8,128)(2,1)S(1)}, bf16[64,1664]{1,0:T(8,128)(2,1)S(1)}, u32[]{:S(2)}, u32[]{:S(2)}) collective-permute-start(bf16[64,1664]{1,0:T(8,128)(2,1)S(1)} %collective-permute-done.2.x1), channel_id=1, source_target_pairs={{0,1},{1,0},{2,3},{3,2},{4,5},{5,4},{6,7},{7,6},{8,9},{9,8},{10,11... | collective-permute-start | bytes 638984 | tf_op jit(solution)/shard_map/gather_normed/ppermute | solution.py:289
  51.1 7.1 %collective-permute-start.7 = (bf16[64,1664]{1,0:T(8,128)(2,1)S(1)}, bf16[64,1664]{1,0:T(8,128)(2,1)S(1)}, u32[]{:S(2)}, u32[]{:S(2)}) collective-permute-start(bf16[64,1664]{1,0:T(8,128)(2,1)S(1)} %collective-permute-done.3.x2), channel_id=1, source_target_pairs={{0,1},{1,0},{2,3},{3,2},{4,5},{5,4},{6,7},{7,6},{8,9},{9,8},{10,11... | collective-permute-start | bytes 638984 | tf_op jit(solution)/shard_map/gather_normed/ppermute | solution.py:289
  51.2 7.1 %collective-permute-start.15 = (bf16[64,1664]{1,0:T(8,128)(2,1)S(1)}, bf16[64,1664]{1,0:T(8,128)(2,1)S(1)}, u32[]{:S(2)}, u32[]{:S(2)}) collective-permute-start(bf16[64,1664]{1,0:T(8,128)(2,1)S(1)} %collective-permute-done.13.x1), channel_id=1, source_target_pairs={{0,2},{1,7},{2,4},{3,1},{4,6},{5,3},{6,0},{7,5},{8,10},{9,15},{10,... | collective-permute-start | bytes 638984 | tf_op jit(solution)/shard_map/gather_down/ppermute | solution.py:297
  51.2 7.4 %collective-permute-start.8 = (bf16[64,1664]{1,0:T(8,128)(2,1)S(1)}, bf16[64,1664]{1,0:T(8,128)(2,1)S(1)}, u32[]{:S(2)}, u32[]{:S(2)}) collective-permute-start(bf16[64,1664]{1,0:T(8,128)(2,1)S(1)} %collective-permute-done.4.x3), channel_id=1, source_target_pairs={{0,1},{1,0},{2,3},{3,2},{4,5},{5,4},{6,7},{7,6},{8,9},{9,8},{10,11... | collective-permute-start | bytes 638984 | tf_op jit(solution)/shard_map/gather_normed/ppermute | solution.py:289
  57.5 4.0 %collective-permute-start.16 = (bf16[64,1664]{1,0:T(8,128)(2,1)S(1)}, bf16[64,1664]{1,0:T(8,128)(2,1)S(1)}, u32[]{:S(2)}, u32[]{:S(2)}) collective-permute-start(bf16[64,1664]{1,0:T(8,128)(2,1)S(1)} %get-tuple-element.36.x0), channel_id=1, source_target_pairs={{0,1},{1,0},{2,3},{3,2},{4,5},{5,4},{6,7},{7,6},{8,9},{9,8},{10,11... | collective-permute-start | bytes 638984 | tf_op jit(solution)/shard_map/gather_down/ppermute | solution.py:289
  57.6 3.9 %collective-permute-start.17 = (bf16[64,1664]{1,0:T(8,128)(2,1)S(1)}, bf16[64,1664]{1,0:T(8,128)(2,1)S(1)}, u32[]{:S(2)}, u32[]{:S(2)}) collective-permute-start(bf16[64,1664]{1,0:T(8,128)(2,1)S(1)} %collective-permute-done.13.x1), channel_id=1, source_target_pairs={{0,1},{1,0},{2,3},{3,2},{4,5},{5,4},{6,7},{7,6},{8,9},{9,8},{10,11... | collective-permute-start | bytes 638984 | tf_op jit(solution)/shard_map/gather_down/ppermute | solution.py:289
  58.1 3.4 %collective-permute-start.18 = (bf16[64,1664]{1,0:T(8,128)(2,1)S(1)}, bf16[64,1664]{1,0:T(8,128)(2,1)S(1)}, u32[]{:S(2)}, u32[]{:S(2)}) collective-permute-start(bf16[64,1664]{1,0:T(8,128)(2,1)S(1)} %collective-permute-done.14.x2), channel_id=1, source_target_pairs={{0,1},{1,0},{2,3},{3,2},{4,5},{5,4},{6,7},{7,6},{8,9},{9,8},{10,11... | collective-permute-start | bytes 638984 | tf_op jit(solution)/shard_map/gather_down/ppermute | solution.py:289
  58.2 3.3 %collective-permute-start.19 = (bf16[64,1664]{1,0:T(8,128)(2,1)S(1)}, bf16[64,1664]{1,0:T(8,128)(2,1)S(1)}, u32[]{:S(2)}, u32[]{:S(2)}) collective-permute-start(bf16[64,1664]{1,0:T(8,128)(2,1)S(1)} %collective-permute-done.15.x3), channel_id=1, source_target_pairs={{0,1},{1,0},{2,3},{3,2},{4,5},{5,4},{6,7},{7,6},{8,9},{9,8},{10,11... | collective-permute-start | bytes 638984 | tf_op jit(solution)/shard_map/gather_down/ppermute | solution.py:289
  61.3 3.0 %collective-permute-start.9 = (bf16[256,1664]{1,0:T(8,128)(2,1)S(1)}, bf16[256,1664]{1,0:T(8,128)(2,1)S(1)}, u32[]{:S(2)}, u32[]{:S(2)}) collective-permute-start(bf16[256,1664]{1,0:T(8,128)(2,1)S(1)} %get-tuple-element.31), channel_id=1, source_target_pairs={{0,1},{1,0},{2,3},{3,2},{4,5},{5,4},{6,7},{7,6},{8,9},{9,8},{10,11... | collective-permute-start | bytes 2555912 | tf_op jit(solution)/shard_map/return_result/ppermute | solution.py:289
  63.8 3.0 %collective-permute-start.20 = (bf16[256,1664]{1,0:T(8,128)(2,1)S(1)}, bf16[256,1664]{1,0:T(8,128)(2,1)S(1)}, u32[]{:S(2)}, u32[]{:S(2)}) collective-permute-start(bf16[256,1664]{1,0:T(8,128)(2,1)S(1)} %backward.3), channel_id=1, source_target_pairs={{0,1},{1,0},{2,3},{3,2},{4,5},{5,4},{6,7},{7,6},{8,9},{9,8},{10,11... | collective-permute-start | bytes 2555912 | tf_op jit(solution)/shard_map/return_back/ppermute | solution.py:289
  64.5 7.0 %collective-permute-start.10 = (bf16[64,1664]{1,0:T(8,128)(2,1)S(1)}, bf16[64,1664]{1,0:T(8,128)(2,1)S(1)}, u32[]{:S(2)}, u32[]{:S(2)}) collective-permute-start(bf16[64,1664]{1,0:T(8,128)(2,1)S(1)} %get-tuple-element.34.rest_0_), channel_id=1, source_target_pairs={{0,6},{1,3},{2,0},{3,5},{4,2},{5,7},{6,4},{7,1},{8,14},{9,11},{10,... | collective-permute-start | bytes 638984 | tf_op jit(solution)/shard_map/return_result/ppermute | solution.py:297
  67.0 6.2 %collective-permute-start.21 = (bf16[64,1664]{1,0:T(8,128)(2,1)S(1)}, bf16[64,1664]{1,0:T(8,128)(2,1)S(1)}, u32[]{:S(2)}, u32[]{:S(2)}) collective-permute-start(bf16[64,1664]{1,0:T(8,128)(2,1)S(1)} %get-tuple-element.40), channel_id=1, source_target_pairs={{0,6},{1,3},{2,0},{3,5},{4,2},{5,7},{6,4},{7,1},{8,14},{9,11},{10,... | collective-permute-start | bytes 638984 | tf_op jit(solution)/shard_map/return_back/ppermute | solution.py:297
  67.3 7.7 %collective-permute-start.12 = (bf16[64,1664]{1,0:T(8,128)(2,1)S(1)}, bf16[64,1664]{1,0:T(8,128)(2,1)S(1)}, u32[]{:S(2)}, u32[]{:S(2)}) collective-permute-start(bf16[64,1664]{1,0:T(8,128)(2,1)S(1)} %get-tuple-element.35), channel_id=1, source_target_pairs={{0,2},{1,7},{2,4},{3,1},{4,6},{5,3},{6,0},{7,5},{8,10},{9,15},{10,... | collective-permute-start | bytes 638984 | tf_op jit(solution)/shard_map/return_result/ppermute | solution.py:297
  70.1 8.7 %collective-permute-start.23 = (bf16[64,1664]{1,0:T(8,128)(2,1)S(1)}, bf16[64,1664]{1,0:T(8,128)(2,1)S(1)}, u32[]{:S(2)}, u32[]{:S(2)}) collective-permute-start(bf16[64,1664]{1,0:T(8,128)(2,1)S(1)} %get-tuple-element.41), channel_id=1, source_target_pairs={{0,2},{1,7},{2,4},{3,1},{4,6},{5,3},{6,0},{7,5},{8,10},{9,15},{10,... | collective-permute-start | bytes 638984 | tf_op jit(solution)/shard_map/return_back/ppermute | solution.py:297
  71.5 8.6 %collective-permute-start.11 = (bf16[64,1664]{1,0:T(8,128)(2,1)S(1)}, bf16[64,1664]{1,0:T(8,128)(2,1)S(1)}, u32[]{:S(2)}, u32[]{:S(2)}) collective-permute-start(bf16[64,1664]{1,0:T(8,128)(2,1)S(1)} %return_result.3), channel_id=1, source_target_pairs={{0,6},{1,3},{2,0},{3,5},{4,2},{5,7},{6,4},{7,1},{8,14},{9,11},{10,... | collective-permute-start | bytes 638984 | tf_op jit(solution)/shard_map/return_result/ppermute | solution.py:297
  73.3 10.0 %collective-permute-start.22 = (bf16[64,1664]{1,0:T(8,128)(2,1)S(1)}, bf16[64,1664]{1,0:T(8,128)(2,1)S(1)}, u32[]{:S(2)}, u32[]{:S(2)}) collective-permute-start(bf16[64,1664]{1,0:T(8,128)(2,1)S(1)} %return_back.3), channel_id=1, source_target_pairs={{0,6},{1,3},{2,0},{3,5},{4,2},{5,7},{6,4},{7,1},{8,14},{9,11},{10,... | collective-permute-start | bytes 638984 | tf_op jit(solution)/shard_map/return_back/ppermute | solution.py:297
  102.1 5.7 %collective-permute-start.24 = (bf16[256,896]{1,0:T(8,128)(2,1)S(1)}, bf16[256,896]{1,0:T(8,128)(2,1)S(1)}, u32[]{:S(2)}, u32[]{:S(2)}) collective-permute-start(bf16[256,896]{1,0:T(8,128)(2,1)S(1)} %bitcast.15), channel_id=1, source_target_pairs={{0,1},{1,0},{2,3},{3,2},{4,5},{5,4},{6,7},{7,6},{8,9},{9,8},{10,11... | collective-permute-start | bytes 1376264 | tf_op jit(solution)/shard_map/collect/ppermute | solution.py:289
  (3 other events, 3.6 us)

commit v10 on v9

--- a/solution.py
+++ b/solution.py
@@ -145,18 +145,22 @@
     return centered, lax.rsqrt(variance + 1e-06)
 
 
-def norm_kernel(att_keep, att_got, residual, gain, upstream, pick_keep, pick_send, stream, keep, send, both):
-    rows, width = residual.shape
+def select(pick, both, out):
+    count = both.shape[0]
+    rest = both.shape[1] - WIDE
+    first, second = pick[:, :count], pick[:, count:]
+    out[:, :rest] = (mm(first, both[:, :rest]) + mm(second, both[:, WIDE:])).astype(BF)
+    out[:, rest:] = mm(first, both[:, rest:WIDE]).astype(BF)
+
+
+def norm_kernel(att_keep, att_got, residual, gain, upstream, pick_send, stream, both, send):
+    rows = residual.shape[0]
     total = residual[...].astype(F32) + (att_keep[...] + att_got[...])
     stream[...] = total
     centered, inverse = statistics(total)
     both[:rows, :] = (gain[...] * centered * inverse).astype(BF)
     both[rows:, :] = upstream[...]
-    rest = width - WIDE
-    for pick, out in ((pick_send, send), (pick_keep, keep)):
-        first, second = pick[:, : 2 * rows], pick[:, 2 * rows :]
-        out[:, :rest] = (mm(first, both[:, :rest]) + mm(second, both[:, WIDE:])).astype(BF)
-        out[:, rest:] = mm(first, both[:, rest:WIDE]).astype(BF)
+    select(pick_send, both, send)
 
 
 def place(packed):
@@ -331,14 +335,16 @@
             moved=10**6,
         )(ids, slots)
     with jax.named_scope("norm"):
-        stream, keep, send = call(
+        stream, both, send = call(
             norm_kernel,
-            [sds((rows, width), F32)] + [sds((packed, WIDE), BF)] * 2,
-            [VMEM] * 7,
-            [pltpu.VMEM((2 * rows, width), BF)],
+            [sds((rows, width), F32), sds((2 * rows, width), BF), sds((packed, WIDE), BF)],
+            [VMEM] * 6,
             flops=10**9,
             moved=3 * 10**6,
-        )(att_keep, att_got, residual, gain, upstream, pick_keep, pick_send)
+        )(att_keep, att_got, residual, gain, upstream, pick_send)
+        keep = call(select, sds((packed, WIDE), BF), [VMEM] * 2, flops=10**9, moved=10**6)(
+            pick_keep, both
+        )
     with jax.named_scope("dispatch"):
         got = exchange(keep + swap_core(send))
         normed_rows, down_rows = call(

time: 110 us -> 110 us (level)
  transfers between devices with their start and end apart: 25 -> 25, of which waited for: 7 -> 7; matrix products, arithmetic and copies ran while one was open for 0% -> 0% of each run, Pallas kernels for 13% -> 14%
where the time goes in v10:
time: 110 us; the launch traced here: 109 us
  blocking collectives  40.6 us (37%)
  starting transfers between devices  32.1 us (29%)
  Pallas kernels  19.5 us (18%)
  waiting for transfers between devices  13.4 us (12%)
  local copies, waits for them, and re-layouts  2.84 us (3%)
    all_to_all x2, blocking collectives, exchange(): lax.all_to_all(x.reshape(experts, PACK, WIDE), 'xz', split_axis=0, concat...  40.6 us
    ppermute x13, starting transfers between devices, swap_core(): return lax.ppermute(x, 'core', [(0, 1), (1, 0)])  21.3 us
    ppermute x12, waiting for transfers between devices, ring(): return lax.ppermute(x, ('y', 'core'), pairs)  12 us
    ppermute x12, starting transfers between devices, ring(): return lax.ppermute(x, ('y', 'core'), pairs)  10.8 us
    pallas_call x2, Pallas kernels, forward(): call(forward_kernel, [sds((tall, units), F32), sds((tall, width), kind)],...  5.27 us
    pallas_call x2, Pallas kernels, backward(): call(backward_kernel, sds((tall, width), kind), [VMEM] * 7 + [ANY] * len(...  4.62 us
    unnamed x20, local copies, waits for them, and re-layouts  2.83 us
    pallas_call x2, Pallas kernels, attend(): call(functools.partial(attend_kernel, other), sds((rows, width), F32), [S...  2.44 us
  transfers between devices with their start and end apart: 25, of which 7 were waited for; matrix products, arithmetic and copies ran while one was open for 0% of the time, Pallas kernels for 14%

profile of v10, /device:TPU:1, one launch (start us, length us, event | category | flops | bytes accessed | tf_op | source)
XLA Modules:
  0.0 109.4 jit_solution(14145669293836920713)
XLA Ops:
  0.7 1.8 %copy-done = bf16[832,1664]{1,0:T(8,128)(2,1)S(1)} copy-done((bf16[832,1664]{1,0:T(8,128)(2,1)S(1)}, bf16[832,1664]{1,0:T(8,128)(2,1)}, u32[]{:S(2)}) %copy-start) | copy-done | bytes 2768920
  2.5 1.0 copy-done.1
  3.5 1.2 %attend.3 = f32[128,1664]{1,0:T(8,128)S(1)} custom-call(s32[2]{0:T(128)S(1)} %pad_add_fusion.ids, bf16[832,256]{1,0:T(8,128)(2,1)S(1)} %bitcast.13, bf16[832,1664]{1,0:T(8,128)(2,1)S(1)} %copy-done), custom_call_target="tpu_custom_call" | custom-call | flops 354418688 | bytes 4000000 | tf_op jit(solution)/shard_map/attend/pallas_call | solution.py:310
  4.8 3.3 %collective-permute-start = (f32[128,1664]{1,0:T(8,128)S(1)}, f32[128,1664]{1,0:T(8,128)S(1)}, u32[]{:S(2)}, u32[]{:S(2)}) collective-permute-start(f32[128,1664]{1,0:T(8,128)S(1)} %attend.3), channel_id=1, source_target_pairs={{0,1},{1,0},{2,3},{3,2},{4,5},{5,4},{6,7},{7,6},{8,9},{9,8},{10,11... | collective-permute-start | bytes 2555912 | tf_op jit(solution)/shard_map/attend/ppermute | solution.py:293
  8.1 1.2 %attend.2.att_keep = f32[128,1664]{1,0:T(8,128)S(1)} custom-call(s32[2]{0:T(128)S(1)} %pad_add_fusion.ids, bf16[832,256]{1,0:T(8,128)(2,1)S(1)} %bitcast.14, bf16[832,1664]{1,0:T(8,128)(2,1)S(1)} %copy-done), custom_call_target="tpu_custom_call" | custom-call | flops 354418688 | bytes 4000000 | tf_op jit(solution)/shard_map/attend/pallas_call | solution.py:310
  9.4 1.2 %routing.1 = (bf16[256,512]{1,0:T(8,128)(2,1)S(1)}, bf16[256,512]{1,0:T(8,128)(2,1)S(1)}, bf16[96,128]{1,0:T(8,128)(2,1)S(1)}) custom-call(s32[2]{0:T(128)S(1)} %pad_add_fusion.ids, s32[32,512]{1,0:T(8,128)S(1)} %copy-done.6, s32[1,32]{1,0:T(1,128)S(1)} %bitcast.25, f32[32,512]{1,0:T(8,128)S(1)} %copy-done.7), custom_call_target="tpu_custom_call" | custom-call | flops 1000000000 | bytes 1000000 | tf_op jit(solution)/shard_map/routing/pallas_call | solution.py:322
  10.7 0.8 norm.2
  12.0 1.4 %collective-permute-done.1 = bf16[256,896]{1,0:T(8,128)(2,1)S(1)} collective-permute-done((bf16[256,896]{1,0:T(8,128)(2,1)S(1)}, bf16[256,896]{1,0:T(8,128)(2,1)S(1)}, u32[]{:S(2)}, u32[]{:S(2)}) %collective-permute-start.1) | collective-permute-done | bytes 458784 | tf_op jit(solution)/shard_map/dispatch/ppermute | solution.py:293
  13.4 22.2 %all_to_all.10 = bf16[32,8,896]{2,1,0:T(8,128)(2,1)S(1)} all-to-all(bf16[32,8,896]{2,1,0:T(8,128)(2,1)S(1)} %add_bitcast_fusion), channel_id=1, replica_groups=mesh['xz'=32,'y'=4,'core'=2] {'xz'}, dimensions={0} | all-to-all | bytes 917504 | tf_op jit(solution)/shard_map/dispatch/all_to_all | solution.py:304
  35.9 2.8 %collective-permute-start.2 = (bf16[64,1664]{1,0:T(8,128)(2,1)S(1)}, bf16[64,1664]{1,0:T(8,128)(2,1)S(1)}, u32[]{:S(2)}, u32[]{:S(2)}) collective-permute-start(bf16[64,1664]{1,0:T(8,128)(2,1)S(1)} %get-tuple-element.28.x0), channel_id=1, source_target_pairs={{0,2},{1,7},{2,4},{3,1},{4,6},{5,3},{6,0},{7,5},{8,10},{9,15},{10,... | collective-permute-start | bytes 638984 | tf_op jit(solution)/shard_map/gather_normed/ppermute | solution.py:301
  38.7 3.8 %collective-permute-start.5 = (bf16[64,1664]{1,0:T(8,128)(2,1)S(1)}, bf16[64,1664]{1,0:T(8,128)(2,1)S(1)}, u32[]{:S(2)}, u32[]{:S(2)}) collective-permute-start(bf16[64,1664]{1,0:T(8,128)(2,1)S(1)} %get-tuple-element.28.x0), channel_id=1, source_target_pairs={{0,1},{1,0},{2,3},{3,2},{4,5},{5,4},{6,7},{7,6},{8,9},{9,8},{10,11... | collective-permute-start | bytes 638984 | tf_op jit(solution)/shard_map/gather_normed/ppermute | solution.py:293
  42.5 1.5 %collective-permute-start.13 = (bf16[64,1664]{1,0:T(8,128)(2,1)S(1)}, bf16[64,1664]{1,0:T(8,128)(2,1)S(1)}, u32[]{:S(2)}, u32[]{:S(2)}) collective-permute-start(bf16[64,1664]{1,0:T(8,128)(2,1)S(1)} %get-tuple-element.36.x0), channel_id=1, source_target_pairs={{0,2},{1,7},{2,4},{3,1},{4,6},{5,3},{6,0},{7,5},{8,10},{9,15},{10,... | collective-permute-start | bytes 638984 | tf_op jit(solution)/shard_map/gather_down/ppermute | solution.py:301
  44.6 0.9 collective-permute-start.14
  45.5 0.6 collective-permute-done.3.x2
  46.1 4.7 %collective-permute-start.6 = (bf16[64,1664]{1,0:T(8,128)(2,1)S(1)}, bf16[64,1664]{1,0:T(8,128)(2,1)S(1)}, u32[]{:S(2)}, u32[]{:S(2)}) collective-permute-start(bf16[64,1664]{1,0:T(8,128)(2,1)S(1)} %collective-permute-done.2.x1), channel_id=1, source_target_pairs={{0,1},{1,0},{2,3},{3,2},{4,5},{5,4},{6,7},{7,6},{8,9},{9,8},{10,11... | collective-permute-start | bytes 638984 | tf_op jit(solution)/shard_map/gather_normed/ppermute | solution.py:293
  50.9 3.7 %collective-permute-start.8 = (bf16[64,1664]{1,0:T(8,128)(2,1)S(1)}, bf16[64,1664]{1,0:T(8,128)(2,1)S(1)}, u32[]{:S(2)}, u32[]{:S(2)}) collective-permute-start(bf16[64,1664]{1,0:T(8,128)(2,1)S(1)} %collective-permute-done.4.x3), channel_id=1, source_target_pairs={{0,1},{1,0},{2,3},{3,2},{4,5},{5,4},{6,7},{7,6},{8,9},{9,8},{10,11... | collective-permute-start | bytes 638984 | tf_op jit(solution)/shard_map/gather_normed/ppermute | solution.py:293
  54.6 2.6 %forward.2 = (f32[256,1024]{1,0:T(8,128)S(1)}, f32[256,1664]{1,0:T(8,128)S(1)}) custom-call(bf16[64,1664]{1,0:T(8,128)(2,1)S(1)} %get-tuple-element.28.x0, bf16[64,1664]{1,0:T(8,128)(2,1)S(1)} %collective-permute-done.2.x1, bf16[64,1664]{1,0:T(8,128)(2,1)S(1)} %collective-permute-done.3.x2, bf16[64,1664]{1,0:T(8,128)(2,1)S(1)} %collective-permute-done.4.x3, ...), custom_call_target="tpu_custom_call" | custom-call | flops 6979321856 | bytes 10000000 | tf_op jit(solution)/shard_map/forward/pallas_call | solution.py:383
  58.4 2.6 %forward.3 = (f32[256,1024]{1,0:T(8,128)S(1)}, bf16[256,1664]{1,0:T(8,128)(2,1)S(1)}) custom-call(bf16[64,1664]{1,0:T(8,128)(2,1)S(1)} %collective-permute-done.5.x0, bf16[64,1664]{1,0:T(8,128)(2,1)S(1)} %collective-permute-done.6.x1, bf16[64,1664]{1,0:T(8,128)(2,1)S(1)} %collective-permute-done.7.x2, bf16[64,1664]{1,0:T(8,128)(2,1)S(1)} %collective-permute-done.8.x3, ...), custom_call_target="tpu_custom_call" | custom-call | flops 6979321856 | bytes 10000000 | tf_op jit(solution)/shard_map/forward/pallas_call | solution.py:383
  61.3 2.3 %backward.3 = bf16[256,1664]{1,0:T(8,128)(2,1)S(1)} custom-call(bf16[64,1664]{1,0:T(8,128)(2,1)S(1)} %collective-permute-done.16.x0, bf16[64,1664]{1,0:T(8,128)(2,1)S(1)} %collective-permute-done.17.x1, bf16[64,1664]{1,0:T(8,128)(2,1)S(1)} %collective-permute-done.18.x2, bf16[64,1664]{1,0:T(8,128)(2,1)S(1)} %collective-permute-done.19.x3, ...), custom_call_target="tpu_custom_call" | custom-call | flops 6979321856 | bytes 10000000 | tf_op jit(solution)/shard_map/backward/pallas_call | solution.py:394
  64.3 2.3 %backward.2.keep = f32[256,1664]{1,0:T(8,128)S(1)} custom-call(bf16[64,1664]{1,0:T(8,128)(2,1)S(1)} %get-tuple-element.36.x0, bf16[64,1664]{1,0:T(8,128)(2,1)S(1)} %collective-permute-done.13.x1, bf16[64,1664]{1,0:T(8,128)(2,1)S(1)} %collective-permute-done.14.x2, bf16[64,1664]{1,0:T(8,128)(2,1)S(1)} %collective-permute-done.15.x3, ...), custom_call_target="tpu_custom_call" | custom-call | flops 6979321856 | bytes 10000000 | tf_op jit(solution)/shard_map/backward/pallas_call | solution.py:394
  67.1 2.7 %collective-permute-start.12 = (bf16[64,1664]{1,0:T(8,128)(2,1)S(1)}, bf16[64,1664]{1,0:T(8,128)(2,1)S(1)}, u32[]{:S(2)}, u32[]{:S(2)}) collective-permute-start(bf16[64,1664]{1,0:T(8,128)(2,1)S(1)} %get-tuple-element.35), channel_id=1, source_target_pairs={{0,2},{1,7},{2,4},{3,1},{4,6},{5,3},{6,0},{7,5},{8,10},{9,15},{10,... | collective-permute-start | bytes 638984 | tf_op jit(solution)/shard_map/return_result/ppermute | solution.py:301
  69.8 1.4 %collective-permute-start.23 = (bf16[64,1664]{1,0:T(8,128)(2,1)S(1)}, bf16[64,1664]{1,0:T(8,128)(2,1)S(1)}, u32[]{:S(2)}, u32[]{:S(2)}) collective-permute-start(bf16[64,1664]{1,0:T(8,128)(2,1)S(1)} %get-tuple-element.41), channel_id=1, source_target_pairs={{0,2},{1,7},{2,4},{3,1},{4,6},{5,3},{6,0},{7,5},{8,10},{9,15},{10,... | collective-permute-start | bytes 638984 | tf_op jit(solution)/shard_map/return_back/ppermute | solution.py:301
  71.5 1.5 %collective-permute-done.21.b = bf16[64,1664]{1,0:T(8,128)(2,1)S(1)} collective-permute-done((bf16[64,1664]{1,0:T(8,128)(2,1)S(1)}, bf16[64,1664]{1,0:T(8,128)(2,1)S(1)}, u32[]{:S(2)}, u32[]{:S(2)}) %collective-permute-start.21) | collective-permute-done | bytes 213024 | tf_op jit(solution)/shard_map/return_back/ppermute | solution.py:301
  73.3 1.5 %collective-permute-done.12.two_r = bf16[64,1664]{1,0:T(8,128)(2,1)S(1)} collective-permute-done((bf16[64,1664]{1,0:T(8,128)(2,1)S(1)}, bf16[64,1664]{1,0:T(8,128)(2,1)S(1)}, u32[]{:S(2)}, u32[]{:S(2)}) %collective-permute-start.12) | collective-permute-done | bytes 213024 | tf_op jit(solution)/shard_map/return_result/ppermute | solution.py:301
  74.8 3.7 %collective-permute-done.23.two_b = bf16[64,1664]{1,0:T(8,128)(2,1)S(1)} collective-permute-done((bf16[64,1664]{1,0:T(8,128)(2,1)S(1)}, bf16[64,1664]{1,0:T(8,128)(2,1)S(1)}, u32[]{:S(2)}, u32[]{:S(2)}) %collective-permute-start.23) | collective-permute-done | bytes 213024 | tf_op jit(solution)/shard_map/return_back/ppermute | solution.py:301
  78.5 1.3 %collective-permute-done.11.one_r = bf16[64,1664]{1,0:T(8,128)(2,1)S(1)} collective-permute-done((bf16[64,1664]{1,0:T(8,128)(2,1)S(1)}, bf16[64,1664]{1,0:T(8,128)(2,1)S(1)}, u32[]{:S(2)}, u32[]{:S(2)}) %collective-permute-start.11) | collective-permute-done | bytes 213024 | tf_op jit(solution)/shard_map/return_result/ppermute | solution.py:301
  79.8 3.3 %collective-permute-done.22.one_b = bf16[64,1664]{1,0:T(8,128)(2,1)S(1)} collective-permute-done((bf16[64,1664]{1,0:T(8,128)(2,1)S(1)}, bf16[64,1664]{1,0:T(8,128)(2,1)S(1)}, u32[]{:S(2)}, u32[]{:S(2)}) %collective-permute-start.22) | collective-permute-done | bytes 213024 | tf_op jit(solution)/shard_map/return_back/ppermute | solution.py:301
  83.5 18.4 %all_to_all.11 = bf16[32,8,896]{2,1,0:T(8,128)(2,1)S(1)} all-to-all(bf16[32,8,896]{2,1,0:T(8,128)(2,1)S(1)} %bitcast.11), channel_id=1, replica_groups=mesh['xz'=32,'y'=4,'core'=2] {'xz'}, dimensions={0} | all-to-all | bytes 917504 | tf_op jit(solution)/shard_map/collect/all_to_all | solution.py:304
  101.9 3.8 %collective-permute-start.24 = (bf16[256,896]{1,0:T(8,128)(2,1)S(1)}, bf16[256,896]{1,0:T(8,128)(2,1)S(1)}, u32[]{:S(2)}, u32[]{:S(2)}) collective-permute-start(bf16[256,896]{1,0:T(8,128)(2,1)S(1)} %bitcast.15), channel_id=1, source_target_pairs={{0,1},{1,0},{2,3},{3,2},{4,5},{5,4},{6,7},{7,6},{8,9},{9,8},{10,11... | collective-permute-start | bytes 1376264 | tf_op jit(solution)/shard_map/collect/ppermute | solution.py:293
  105.7 1.2 %merge.1 = (bf16[512,512]{1,0:T(8,128)(2,1)S(1)}, bf16[512,512]{1,0:T(8,128)(2,1)S(1)}) custom-call(s32[2]{0:T(128)S(1)} %pad_add_fusion.ids, bf16[96,128]{1,0:T(8,128)(2,1)S(1)} %get-tuple-element.42.slots), custom_call_target="tpu_custom_call" | custom-call | flops 100000000 | bytes 1000000 | tf_op jit(solution)/shard_map/merge/pallas_call | solution.py:330
  106.9 0.7 final.2.first
  107.6 1.8 %final.3 = (bf16[128,1664]{1,0:T(8,128)(2,1)}, bf16[128,1664]{1,0:T(8,128)(2,1)}) custom-call(f32[512,896]{1,0:T(8,128)S(1)} %final.2.first, bf16[256,896]{1,0:T(8,128)(2,1)S(1)} %collective-permute-done.24.theirs, bf16[512,512]{1,0:T(8,128)(2,1)S(1)} %get-tuple-element.43.merge_high, bf16[512,512]{1,0:T(8,128)(2,1)S(1)} %get-tuple-element.44.merge_low, ...), custom_call_target="tpu_custom_call" | custom-call | flops 1000000000 | bytes 4000000 | tf_op jit(solution)/shard_map/final/pallas_call | solution.py:434
  (61 shorter events, 5.1 us)
Async XLA Ops:
  0.6 7.5 %copy-start.9 = (f32[1664]{0:T(1024)S(1)}, f32[1664]{0:T(1024)}, u32[]{:S(2)}) copy-start(f32[1664]{0:T(1024)} %param.13) | copy-start | bytes 19972
  0.7 1.8 %copy-start = (bf16[832,1664]{1,0:T(8,128)(2,1)S(1)}, bf16[832,1664]{1,0:T(8,128)(2,1)}, u32[]{:S(2)}) copy-start(bf16[832,1664]{1,0:T(8,128)(2,1)} %weight.3) | copy-start | bytes 8306692
  4.7 4.6 %copy-start.6 = (s32[32,512]{1,0:T(8,128)S(1)}, s32[32,512]{1,0:T(8,128)}, u32[]{:S(2)}) copy-start(s32[32,512]{1,0:T(8,128)} %index.1) | copy-start | bytes 196612
  4.7 4.6 %copy-start.7 = (f32[32,512]{1,0:T(8,128)S(1)}, f32[32,512]{1,0:T(8,128)}, u32[]{:S(2)}) copy-start(f32[32,512]{1,0:T(8,128)} %gate.1) | copy-start | bytes 196612
  4.8 4.6 %copy-start.8 = (s32[32]{0:T(128)S(1)}, s32[32]{0:T(128)}, u32[]{:S(2)}) copy-start(s32[32]{0:T(128)} %param.17) | copy-start | bytes 388
  4.8 5.9 %collective-permute-start = (f32[128,1664]{1,0:T(8,128)S(1)}, f32[128,1664]{1,0:T(8,128)S(1)}, u32[]{:S(2)}, u32[]{:S(2)}) collective-permute-start(f32[128,1664]{1,0:T(8,128)S(1)} %attend.3), channel_id=1, source_target_pairs={{0,1},{1,0},{2,3},{3,2},{4,5},{5,4},{6,7},{7,6},{8,9},{9,8},{10,11... | collective-permute-start | bytes 2555912 | tf_op jit(solution)/shard_map/attend/ppermute | solution.py:293
  10.7 44.0 %copy-start.4 = (bf16[1,1024,1664]{2,1,0:T(8,128)(2,1)S(1)}, bf16[1,1024,1664]{2,1,0:T(8,128)(2,1)}, u32[]{:S(2)}) copy-start(bf16[1,1024,1664]{2,1,0:T(8,128)(2,1)} %param.15) | copy-start | bytes 10223620
  11.4 1.9 %collective-permute-start.1 = (bf16[256,896]{1,0:T(8,128)(2,1)S(1)}, bf16[256,896]{1,0:T(8,128)(2,1)S(1)}, u32[]{:S(2)}, u32[]{:S(2)}) collective-permute-start(bf16[256,896]{1,0:T(8,128)(2,1)S(1)} %get-tuple-element.27), channel_id=1, source_target_pairs={{0,1},{1,0},{2,3},{3,2},{4,5},{5,4},{6,7},{7,6},{8,9},{9,8},{10,11... | collective-permute-start | bytes 1376264 | tf_op jit(solution)/shard_map/dispatch/ppermute | solution.py:293
  11.6 43.1 %copy-start.3 = (bf16[1,1664,1024]{2,1,0:T(8,128)(2,1)S(1)}, bf16[1,1664,1024]{2,1,0:T(8,128)(2,1)}, u32[]{:S(2)}) copy-start(bf16[1,1664,1024]{2,1,0:T(8,128)(2,1)} %param.14) | copy-start | bytes 10223620
  35.9 8.2 %collective-permute-start.2 = (bf16[64,1664]{1,0:T(8,128)(2,1)S(1)}, bf16[64,1664]{1,0:T(8,128)(2,1)S(1)}, u32[]{:S(2)}, u32[]{:S(2)}) collective-permute-start(bf16[64,1664]{1,0:T(8,128)(2,1)S(1)} %get-tuple-element.28.x0), channel_id=1, source_target_pairs={{0,2},{1,7},{2,4},{3,1},{4,6},{5,3},{6,0},{7,5},{8,10},{9,15},{10,... | collective-permute-start | bytes 638984 | tf_op jit(solution)/shard_map/gather_normed/ppermute | solution.py:301
  38.7 7.4 %collective-permute-start.3 = (bf16[64,1664]{1,0:T(8,128)(2,1)S(1)}, bf16[64,1664]{1,0:T(8,128)(2,1)S(1)}, u32[]{:S(2)}, u32[]{:S(2)}) collective-permute-start(bf16[64,1664]{1,0:T(8,128)(2,1)S(1)} %get-tuple-element.28.x0), channel_id=1, source_target_pairs={{0,6},{1,3},{2,0},{3,5},{4,2},{5,7},{6,4},{7,1},{8,14},{9,11},{10,... | collective-permute-start | bytes 638984 | tf_op jit(solution)/shard_map/gather_normed/ppermute | solution.py:301
  38.7 12.1 %collective-permute-start.5 = (bf16[64,1664]{1,0:T(8,128)(2,1)S(1)}, bf16[64,1664]{1,0:T(8,128)(2,1)S(1)}, u32[]{:S(2)}, u32[]{:S(2)}) collective-permute-start(bf16[64,1664]{1,0:T(8,128)(2,1)S(1)} %get-tuple-element.28.x0), channel_id=1, source_target_pairs={{0,1},{1,0},{2,3},{3,2},{4,5},{5,4},{6,7},{7,6},{8,9},{9,8},{10,11... | collective-permute-start | bytes 638984 | tf_op jit(solution)/shard_map/gather_normed/ppermute | solution.py:293
  42.5 8.4 %collective-permute-start.13 = (bf16[64,1664]{1,0:T(8,128)(2,1)S(1)}, bf16[64,1664]{1,0:T(8,128)(2,1)S(1)}, u32[]{:S(2)}, u32[]{:S(2)}) collective-permute-start(bf16[64,1664]{1,0:T(8,128)(2,1)S(1)} %get-tuple-element.36.x0), channel_id=1, source_target_pairs={{0,2},{1,7},{2,4},{3,1},{4,6},{5,3},{6,0},{7,5},{8,10},{9,15},{10,... | collective-permute-start | bytes 638984 | tf_op jit(solution)/shard_map/gather_down/ppermute | solution.py:301
  44.0 6.9 %collective-permute-start.4 = (bf16[64,1664]{1,0:T(8,128)(2,1)S(1)}, bf16[64,1664]{1,0:T(8,128)(2,1)S(1)}, u32[]{:S(2)}, u32[]{:S(2)}) collective-permute-start(bf16[64,1664]{1,0:T(8,128)(2,1)S(1)} %collective-permute-done.2.x1), channel_id=1, source_target_pairs={{0,2},{1,7},{2,4},{3,1},{4,6},{5,3},{6,0},{7,5},{8,10},{9,15},{10,... | collective-permute-start | bytes 638984 | tf_op jit(solution)/shard_map/gather_normed/ppermute | solution.py:301
  44.6 12.7 %collective-permute-start.14 = (bf16[64,1664]{1,0:T(8,128)(2,1)S(1)}, bf16[64,1664]{1,0:T(8,128)(2,1)S(1)}, u32[]{:S(2)}, u32[]{:S(2)}) collective-permute-start(bf16[64,1664]{1,0:T(8,128)(2,1)S(1)} %get-tuple-element.36.x0), channel_id=1, source_target_pairs={{0,6},{1,3},{2,0},{3,5},{4,2},{5,7},{6,4},{7,1},{8,14},{9,11},{10,... | collective-permute-start | bytes 638984 | tf_op jit(solution)/shard_map/gather_down/ppermute | solution.py:301
  46.1 11.3 %collective-permute-start.6 = (bf16[64,1664]{1,0:T(8,128)(2,1)S(1)}, bf16[64,1664]{1,0:T(8,128)(2,1)S(1)}, u32[]{:S(2)}, u32[]{:S(2)}) collective-permute-start(bf16[64,1664]{1,0:T(8,128)(2,1)S(1)} %collective-permute-done.2.x1), channel_id=1, source_target_pairs={{0,1},{1,0},{2,3},{3,2},{4,5},{5,4},{6,7},{7,6},{8,9},{9,8},{10,11... | collective-permute-start | bytes 638984 | tf_op jit(solution)/shard_map/gather_normed/ppermute | solution.py:293
  50.8 7.1 %collective-permute-start.7 = (bf16[64,1664]{1,0:T(8,128)(2,1)S(1)}, bf16[64,1664]{1,0:T(8,128)(2,1)S(1)}, u32[]{:S(2)}, u32[]{:S(2)}) collective-permute-start(bf16[64,1664]{1,0:T(8,128)(2,1)S(1)} %collective-permute-done.3.x2), channel_id=1, source_target_pairs={{0,1},{1,0},{2,3},{3,2},{4,5},{5,4},{6,7},{7,6},{8,9},{9,8},{10,11... | collective-permute-start | bytes 638984 | tf_op jit(solution)/shard_map/gather_normed/ppermute | solution.py:293
  50.9 7.1 %collective-permute-start.15 = (bf16[64,1664]{1,0:T(8,128)(2,1)S(1)}, bf16[64,1664]{1,0:T(8,128)(2,1)S(1)}, u32[]{:S(2)}, u32[]{:S(2)}) collective-permute-start(bf16[64,1664]{1,0:T(8,128)(2,1)S(1)} %collective-permute-done.13.x1), channel_id=1, source_target_pairs={{0,2},{1,7},{2,4},{3,1},{4,6},{5,3},{6,0},{7,5},{8,10},{9,15},{10,... | collective-permute-start | bytes 638984 | tf_op jit(solution)/shard_map/gather_down/ppermute | solution.py:301
  50.9 7.5 %collective-permute-start.8 = (bf16[64,1664]{1,0:T(8,128)(2,1)S(1)}, bf16[64,1664]{1,0:T(8,128)(2,1)S(1)}, u32[]{:S(2)}, u32[]{:S(2)}) collective-permute-start(bf16[64,1664]{1,0:T(8,128)(2,1)S(1)} %collective-permute-done.4.x3), channel_id=1, source_target_pairs={{0,1},{1,0},{2,3},{3,2},{4,5},{5,4},{6,7},{7,6},{8,9},{9,8},{10,11... | collective-permute-start | bytes 638984 | tf_op jit(solution)/shard_map/gather_normed/ppermute | solution.py:293
  57.3 4.0 %collective-permute-start.16 = (bf16[64,1664]{1,0:T(8,128)(2,1)S(1)}, bf16[64,1664]{1,0:T(8,128)(2,1)S(1)}, u32[]{:S(2)}, u32[]{:S(2)}) collective-permute-start(bf16[64,1664]{1,0:T(8,128)(2,1)S(1)} %get-tuple-element.36.x0), channel_id=1, source_target_pairs={{0,1},{1,0},{2,3},{3,2},{4,5},{5,4},{6,7},{7,6},{8,9},{9,8},{10,11... | collective-permute-start | bytes 638984 | tf_op jit(solution)/shard_map/gather_down/ppermute | solution.py:293
  57.4 3.9 %collective-permute-start.17 = (bf16[64,1664]{1,0:T(8,128)(2,1)S(1)}, bf16[64,1664]{1,0:T(8,128)(2,1)S(1)}, u32[]{:S(2)}, u32[]{:S(2)}) collective-permute-start(bf16[64,1664]{1,0:T(8,128)(2,1)S(1)} %collective-permute-done.13.x1), channel_id=1, source_target_pairs={{0,1},{1,0},{2,3},{3,2},{4,5},{5,4},{6,7},{7,6},{8,9},{9,8},{10,11... | collective-permute-start | bytes 638984 | tf_op jit(solution)/shard_map/gather_down/ppermute | solution.py:293
  57.9 3.4 %collective-permute-start.18 = (bf16[64,1664]{1,0:T(8,128)(2,1)S(1)}, bf16[64,1664]{1,0:T(8,128)(2,1)S(1)}, u32[]{:S(2)}, u32[]{:S(2)}) collective-permute-start(bf16[64,1664]{1,0:T(8,128)(2,1)S(1)} %collective-permute-done.14.x2), channel_id=1, source_target_pairs={{0,1},{1,0},{2,3},{3,2},{4,5},{5,4},{6,7},{7,6},{8,9},{9,8},{10,11... | collective-permute-start | bytes 638984 | tf_op jit(solution)/shard_map/gather_down/ppermute | solution.py:293
  58.0 3.3 %collective-permute-start.19 = (bf16[64,1664]{1,0:T(8,128)(2,1)S(1)}, bf16[64,1664]{1,0:T(8,128)(2,1)S(1)}, u32[]{:S(2)}, u32[]{:S(2)}) collective-permute-start(bf16[64,1664]{1,0:T(8,128)(2,1)S(1)} %collective-permute-done.15.x3), channel_id=1, source_target_pairs={{0,1},{1,0},{2,3},{3,2},{4,5},{5,4},{6,7},{7,6},{8,9},{9,8},{10,11... | collective-permute-start | bytes 638984 | tf_op jit(solution)/shard_map/gather_down/ppermute | solution.py:293
  61.0 3.0 %collective-permute-start.9 = (bf16[256,1664]{1,0:T(8,128)(2,1)S(1)}, bf16[256,1664]{1,0:T(8,128)(2,1)S(1)}, u32[]{:S(2)}, u32[]{:S(2)}) collective-permute-start(bf16[256,1664]{1,0:T(8,128)(2,1)S(1)} %get-tuple-element.31), channel_id=1, source_target_pairs={{0,1},{1,0},{2,3},{3,2},{4,5},{5,4},{6,7},{7,6},{8,9},{9,8},{10,11... | collective-permute-start | bytes 2555912 | tf_op jit(solution)/shard_map/return_result/ppermute | solution.py:293
  63.6 3.0 %collective-permute-start.20 = (bf16[256,1664]{1,0:T(8,128)(2,1)S(1)}, bf16[256,1664]{1,0:T(8,128)(2,1)S(1)}, u32[]{:S(2)}, u32[]{:S(2)}) collective-permute-start(bf16[256,1664]{1,0:T(8,128)(2,1)S(1)} %backward.3), channel_id=1, source_target_pairs={{0,1},{1,0},{2,3},{3,2},{4,5},{5,4},{6,7},{7,6},{8,9},{9,8},{10,11... | collective-permute-start | bytes 2555912 | tf_op jit(solution)/shard_map/return_back/ppermute | solution.py:293
  64.2 7.0 %collective-permute-start.10 = (bf16[64,1664]{1,0:T(8,128)(2,1)S(1)}, bf16[64,1664]{1,0:T(8,128)(2,1)S(1)}, u32[]{:S(2)}, u32[]{:S(2)}) collective-permute-start(bf16[64,1664]{1,0:T(8,128)(2,1)S(1)} %get-tuple-element.34.rest_0_), channel_id=1, source_target_pairs={{0,6},{1,3},{2,0},{3,5},{4,2},{5,7},{6,4},{7,1},{8,14},{9,11},{10,... | collective-permute-start | bytes 638984 | tf_op jit(solution)/shard_map/return_result/ppermute | solution.py:301
  66.8 6.2 %collective-permute-start.21 = (bf16[64,1664]{1,0:T(8,128)(2,1)S(1)}, bf16[64,1664]{1,0:T(8,128)(2,1)S(1)}, u32[]{:S(2)}, u32[]{:S(2)}) collective-permute-start(bf16[64,1664]{1,0:T(8,128)(2,1)S(1)} %get-tuple-element.40), channel_id=1, source_target_pairs={{0,6},{1,3},{2,0},{3,5},{4,2},{5,7},{6,4},{7,1},{8,14},{9,11},{10,... | collective-permute-start | bytes 638984 | tf_op jit(solution)/shard_map/return_back/ppermute | solution.py:301
  67.1 7.7 %collective-permute-start.12 = (bf16[64,1664]{1,0:T(8,128)(2,1)S(1)}, bf16[64,1664]{1,0:T(8,128)(2,1)S(1)}, u32[]{:S(2)}, u32[]{:S(2)}) collective-permute-start(bf16[64,1664]{1,0:T(8,128)(2,1)S(1)} %get-tuple-element.35), channel_id=1, source_target_pairs={{0,2},{1,7},{2,4},{3,1},{4,6},{5,3},{6,0},{7,5},{8,10},{9,15},{10,... | collective-permute-start | bytes 638984 | tf_op jit(solution)/shard_map/return_result/ppermute | solution.py:301
  69.8 8.6 %collective-permute-start.23 = (bf16[64,1664]{1,0:T(8,128)(2,1)S(1)}, bf16[64,1664]{1,0:T(8,128)(2,1)S(1)}, u32[]{:S(2)}, u32[]{:S(2)}) collective-permute-start(bf16[64,1664]{1,0:T(8,128)(2,1)S(1)} %get-tuple-element.41), channel_id=1, source_target_pairs={{0,2},{1,7},{2,4},{3,1},{4,6},{5,3},{6,0},{7,5},{8,10},{9,15},{10,... | collective-permute-start | bytes 638984 | tf_op jit(solution)/shard_map/return_back/ppermute | solution.py:301
  71.3 8.6 %collective-permute-start.11 = (bf16[64,1664]{1,0:T(8,128)(2,1)S(1)}, bf16[64,1664]{1,0:T(8,128)(2,1)S(1)}, u32[]{:S(2)}, u32[]{:S(2)}) collective-permute-start(bf16[64,1664]{1,0:T(8,128)(2,1)S(1)} %return_result.3), channel_id=1, source_target_pairs={{0,6},{1,3},{2,0},{3,5},{4,2},{5,7},{6,4},{7,1},{8,14},{9,11},{10,... | collective-permute-start | bytes 638984 | tf_op jit(solution)/shard_map/return_result/ppermute | solution.py:301
  73.0 10.0 %collective-permute-start.22 = (bf16[64,1664]{1,0:T(8,128)(2,1)S(1)}, bf16[64,1664]{1,0:T(8,128)(2,1)S(1)}, u32[]{:S(2)}, u32[]{:S(2)}) collective-permute-start(bf16[64,1664]{1,0:T(8,128)(2,1)S(1)} %return_back.3), channel_id=1, source_target_pairs={{0,6},{1,3},{2,0},{3,5},{4,2},{5,7},{6,4},{7,1},{8,14},{9,11},{10,... | collective-permute-start | bytes 638984 | tf_op jit(solution)/shard_map/return_back/ppermute | solution.py:301
  101.9 5.7 %collective-permute-start.24 = (bf16[256,896]{1,0:T(8,128)(2,1)S(1)}, bf16[256,896]{1,0:T(8,128)(2,1)S(1)}, u32[]{:S(2)}, u32[]{:S(2)}) collective-permute-start(bf16[256,896]{1,0:T(8,128)(2,1)S(1)} %bitcast.15), channel_id=1, source_target_pairs={{0,1},{1,0},{2,3},{3,2},{4,5},{5,4},{6,7},{7,6},{8,9},{9,8},{10,11... | collective-permute-start | bytes 1376264 | tf_op jit(solution)/shard_map/collect/ppermute | solution.py:293
  (3 other events, 3.6 us)
